TPU v7x, 32 devices: a whole 2x2x4 slice. The times are simulated.
32 devices in a mesh: lat: 8 (over y, x, core), lon: 4 (over z).
Axes of the slice: x: 2, y: 2, z: 4, core: 2. Of those that a mesh axis runs over, the one named last changes fastest.
Arguments:
- control: float32 [128, 32, 512], P('lat', None, 'lon'), may hold values from -6 to 6
- background: float32 [128, 32, 512], P('lat', None, 'lon'), may hold values from -6 to 6
- lon_width: int32 [128], P('lat'), may hold values from 2 to 16
- block_cells: int32 [512, 4], P('lat', 'lon'), may hold values from 0 to 255, as said below
- block_owner: int32 [512, 4], P('lat', 'lon'), may hold values from -1 to 7, as said below
- channel_count: int32 [288, 4], P('lat', 'lon'), may hold values from 1 to 256
- radiance: bfloat16 [2048, 1152], P('lat', 'lon'), may hold values from -6 to 6
- in_weight: bfloat16 [32, 1024], replicated, may hold values from -1 to 1
- in_bias: float32 [1024], replicated, may hold values from -3 to 3
- mid_weight: bfloat16 [1024, 1024], replicated, may hold values from -0.1875 to 0.1875
- mid_bias: float32 [1024], replicated, may hold values from -3 to 3
- out_weight: bfloat16 [1024, 256], replicated, may hold values from -0.1875 to 0.1875
- out_bias: float32 [256], replicated, may hold values from -3 to 3
Outputs:
- gradient: float32 [128, 32, 512], P('lat', None, 'lon')
Inputs may be any that keep to these rules, and one draw needn't show every extreme that they name: `block_owner`: the live slots of a device come first, unused ones hold -1. Every device has at least 16 observed blocks, some device of every lon index has 64. One device sends at most 8 blocks to one owner, and an owner receives at most 36 blocks from its lon index; both bounds are reached in every draw. `block_cells`: the live slots of one device name distinct blocks.
All inputs are finite; a program needn't handle non-finite values.
Results may differ from a plain program's by a relative error of at most 0.0023.
Values may be sent and summed in bfloat16 or wider, within the bound.
No kernel may reach another device: no remote copies, remote signals or barrier semaphores. Data moves between devices by JAX's collectives and lax.ppermute only.
A program may use at most 64 MiB of HBM per device.

v0:
```python
import jax
import jax.numpy as jnp
from jax import lax
from jax.sharding import PartitionSpec as P

REACH = 16
BLOCK_COLS = 8


lat_sigma = 8.0


def padded_2(block, sides, width, periodic):
    for axis, dim in sides:
        count = lax.axis_size(axis)
        forward = [(i, i + 1) for i in range(count - 1)]
        if periodic:
            forward.append((count - 1, 0))
        backward = [(target, source) for source, target in forward]
        low = lax.ppermute(
            lax.slice_in_dim(block, block.shape[dim] - width, None, axis=dim), axis, forward
        )
        high = lax.ppermute(lax.slice_in_dim(block, 0, width, axis=dim), axis, backward)
        block = jnp.concatenate([low, block, high], axis=dim)
    return block


def lat_band(height, span):
    out_ids = lax.broadcasted_iota(jnp.int32, (height, span), 0)
    in_ids = lax.broadcasted_iota(jnp.int32, (height, span), 1)
    offsets = (in_ids - out_ids - REACH).astype(jnp.float32)
    steps_all = jnp.arange(-REACH, REACH + 1).astype(jnp.float32)
    norm_scale = jnp.sqrt(jnp.sum(jnp.exp(-steps_all * steps_all / (lat_sigma * lat_sigma))))
    raw_taps = jnp.exp(-offsets * offsets / (2.0 * lat_sigma * lat_sigma)) / norm_scale
    return jnp.where(jnp.abs(offsets) <= REACH, raw_taps, 0.0)


def smooth_lat(padded, height):
    band_matrix = lat_band(height, padded.shape[0])
    return jnp.einsum("rq,qlc->rlc", band_matrix, padded, precision=lax.Precision.HIGHEST)


def lon_band(widths, span, width_out):
    spread = jnp.maximum(widths, 1).astype(jnp.float32)[:, None, None]
    in_ids = lax.broadcasted_iota(jnp.int32, (1, span, width_out), 1)
    out_ids = lax.broadcasted_iota(jnp.int32, (1, span, width_out), 2)
    offsets = (in_ids - out_ids - REACH).astype(jnp.float32)
    steps_all = jnp.arange(-REACH, REACH + 1).astype(jnp.float32)[None, :]
    row_spread = spread[:, :, 0]
    norm_scale = jnp.sqrt(
        jnp.sum(jnp.exp(-steps_all * steps_all / (row_spread * row_spread)), axis=1)
    )
    raw_taps = jnp.exp(-offsets * offsets / (2.0 * spread * spread)) / norm_scale[:, None, None]
    return jnp.where(jnp.abs(offsets) <= REACH, raw_taps, 0.0)


def smooth_lon(padded, widths):
    band_matrix = lon_band(widths, padded.shape[2], padded.shape[2] - 2 * REACH)
    return jnp.einsum("rlq,rqc->rlc", padded, band_matrix, precision=lax.Precision.HIGHEST)


def lat_rims(values):
    return padded_2(values, (("lat", 0),), REACH, False)


def lon_rims(values):
    return padded_2(values, (("lon", 2),), REACH, True)


def radiate(
    inputs, observed, kept_mask, in_weight, in_bias, mid_weight, mid_bias, out_weight, out_bias
):
    first_pre = (
        jnp.einsum("lh,lm->hm", in_weight, inputs, preferred_element_type=jnp.float32)
        + in_bias[:, None]
    )
    act_one = jnp.tanh(first_pre).astype(jnp.bfloat16)
    second_pre = (
        jnp.einsum("hk,hm->km", mid_weight, act_one, preferred_element_type=jnp.float32)
        + mid_bias[:, None]
    )
    act_two = jnp.tanh(second_pre).astype(jnp.bfloat16)
    emitted = (
        jnp.einsum("kn,km->nm", out_weight, act_two, preferred_element_type=jnp.float32)
        + out_bias[:, None]
    )
    misfit = jnp.where(kept_mask, emitted - observed.astype(jnp.float32), 0.0).astype(jnp.bfloat16)
    back_two = jnp.einsum("kn,nm->km", out_weight, misfit, preferred_element_type=jnp.float32)
    two_val = act_two.astype(jnp.float32)
    grad_two = (back_two * (1.0 - two_val * two_val)).astype(jnp.bfloat16)
    back_one = jnp.einsum("hk,km->hm", mid_weight, grad_two, preferred_element_type=jnp.float32)
    one_val = act_one.astype(jnp.float32)
    grad_one = (back_one * (1.0 - one_val * one_val)).astype(jnp.bfloat16)
    return jnp.einsum("lh,hm->lm", in_weight, grad_one, preferred_element_type=jnp.float32).astype(
        jnp.bfloat16
    )


def observe(
    profile,
    block_cells,
    block_owner,
    channel_count,
    radiance,
    in_weight,
    in_bias,
    mid_weight,
    mid_bias,
    out_weight,
    out_bias,
    lat_count,
):
    height = profile.shape[0]
    levels = profile.shape[1]
    width_cols = profile.shape[2]
    groups = width_cols // BLOCK_COLS
    cell_count = height * groups
    block_size = levels * BLOCK_COLS
    cells = jnp.transpose(
        profile.reshape(height, levels, groups, BLOCK_COLS), (0, 2, 1, 3)
    ).reshape(cell_count, block_size)
    owners = block_owner[:, 0]
    picked = block_cells[:, 0]
    slot_count = owners.shape[0]
    send_cap = (slot_count + lat_count - 1) // lat_count
    slot_ids = lax.broadcasted_iota(jnp.int32, (slot_count, slot_count), 1)
    here_ids = lax.broadcasted_iota(jnp.int32, (slot_count, slot_count), 0)
    arrival = jnp.sum(
        ((owners[None, :] == owners[:, None]) & (slot_ids < here_ids)).astype(jnp.int32), axis=1
    )
    dest_ids = lax.broadcasted_iota(jnp.int32, (lat_count, send_cap, slot_count), 0)
    rank_ids = lax.broadcasted_iota(jnp.int32, (lat_count, send_cap, slot_count), 1)
    select = ((owners[None, None, :] == dest_ids) & (arrival[None, None, :] == rank_ids)).astype(
        jnp.float32
    )
    cell_match = (
        picked[:, None] == lax.broadcasted_iota(jnp.int32, (slot_count, cell_count), 1)
    ).astype(jnp.float32)
    routing = jnp.einsum("oks,sr->okr", select, cell_match).astype(jnp.bfloat16)
    outgoing = jnp.einsum("okr,re->oke", routing, cells, preferred_element_type=jnp.float32).astype(
        jnp.bfloat16
    )
    slot_flags = jnp.sum(select, axis=2).astype(jnp.bfloat16)
    arrived, arrived_flags = (
        lax.all_to_all(outgoing, "lat", split_axis=0, concat_axis=0, tiled=True),
        lax.all_to_all(slot_flags, "lat", split_axis=0, concat_axis=0, tiled=True),
    )
    recv_most = channel_count.shape[0]
    present = (arrived_flags.reshape(-1) > 0.5).astype(jnp.int32)
    position = jnp.cumsum(present) - present
    recv_ids = lax.broadcasted_iota(jnp.int32, (recv_most, present.shape[0]), 0)
    compact = ((present[None, :] == 1) & (position[None, :] == recv_ids)).astype(jnp.bfloat16)
    blocks = jnp.einsum(
        "mf,fe->me", compact, arrived.reshape(-1, block_size), preferred_element_type=jnp.float32
    ).astype(jnp.bfloat16)
    inputs = jnp.transpose(blocks.reshape(recv_most, levels, BLOCK_COLS), (1, 0, 2)).reshape(
        levels, recv_most * BLOCK_COLS
    )
    filled = lax.broadcasted_iota(jnp.int32, (recv_most,), 0) < jnp.sum(present)
    col_counts = jnp.broadcast_to(channel_count[:, 0][:, None], (recv_most, BLOCK_COLS)).reshape(-1)
    col_filled = jnp.broadcast_to(filled[:, None], (recv_most, BLOCK_COLS)).reshape(-1)
    channel_ids = lax.broadcasted_iota(jnp.int32, (radiance.shape[0], 1), 0)
    kept_mask = (channel_ids < col_counts[None, :]) & col_filled[None, :]
    sensitivity = radiate(
        inputs, radiance, kept_mask, in_weight, in_bias, mid_weight, mid_bias, out_weight, out_bias
    )
    sens_blocks = jnp.transpose(
        sensitivity.reshape(levels, recv_most, BLOCK_COLS), (1, 0, 2)
    ).reshape(recv_most, block_size)
    returning = jnp.einsum(
        "mf,me->fe", compact, sens_blocks, preferred_element_type=jnp.float32
    ).astype(jnp.bfloat16)
    returned = lax.all_to_all(
        returning.reshape(lat_count, send_cap, block_size),
        "lat",
        split_axis=0,
        concat_axis=0,
        tiled=True,
    )
    landed = jnp.einsum("okr,oke->re", routing, returned, preferred_element_type=jnp.float32)
    return jnp.transpose(landed.reshape(height, groups, levels, BLOCK_COLS), (0, 2, 1, 3)).reshape(
        height, levels, width_cols
    )


def shards(
    control,
    background,
    lon_width,
    block_cells,
    block_owner,
    channel_count,
    radiance,
    in_weight,
    in_bias,
    mid_weight,
    mid_bias,
    out_weight,
    out_bias,
):
    height = control.shape[0]
    lat_count = lax.axis_size("lat")
    increment = smooth_lon(lon_rims(smooth_lat(lat_rims(control), height)), lon_width)
    profile = (background + increment).astype(jnp.bfloat16)
    landing = observe(
        profile,
        block_cells,
        block_owner,
        channel_count,
        radiance,
        in_weight,
        in_bias,
        mid_weight,
        mid_bias,
        out_weight,
        out_bias,
        lat_count,
    )
    adjoint = smooth_lat(lat_rims(smooth_lon(lon_rims(landing), lon_width)), height)
    return control + adjoint


def solution(mesh):
    return jax.shard_map(
        shards,
        mesh=mesh,
        in_specs=(
            P("lat", None, "lon"),
            P("lat", None, "lon"),
            P("lat"),
            P("lat", "lon"),
            P("lat", "lon"),
            P("lat", "lon"),
            P("lat", "lon"),
            P(),
            P(),
            P(),
            P(),
            P(),
            P(),
        ),
        out_specs=P("lat", None, "lon"),
        check_vma=False,
    )
```

profile of v0, /device:TPU:1, one launch (start us, length us, event | category | flops | bytes accessed | tf_op | source)
XLA Modules:
  0.0 101.0 jit_solution(3956513606847236199)
XLA Ops:
  1.3 4.5 %collective-permute-start = (f32[16,32,128]{2,0,1:T(8,128)S(1)}, f32[16,32,128]{2,0,1:T(8,128)S(1)}, u32[]{:S(2)}, u32[]{:S(2)}) collective-permute-start(f32[16,32,128]{2,0,1:T(8,128)S(1)} %copy.88), channel_id=1, source_target_pairs={{0,4},{4,8},{8,12},{12,16},{16,20},{20,24},{24,28},{1,5},{5,9},{9,... | collective-permute-start | bytes 786440 | tf_op jit(solution)/shard_map/ppermute | solution.py:20
  5.8 1.9 %collective-permute-start.1 = (f32[16,32,128]{2,0,1:T(8,128)S(1)}, f32[16,32,128]{2,0,1:T(8,128)S(1)}, u32[]{:S(2)}, u32[]{:S(2)}) collective-permute-start(f32[16,32,128]{2,0,1:T(8,128)S(1)} %copy.88), channel_id=1, source_target_pairs={{4,0},{8,4},{12,8},{16,12},{20,16},{24,20},{28,24},{5,1},{9,5},{13... | collective-permute-start | bytes 786440 | tf_op jit(solution)/shard_map/ppermute | solution.py:23
  10.0 4.4 %all-to-all-start = ((bf16[8,1,8]{2,1,0:T(2,128)(2,1)}), bf16[8,1,8]{2,1,0:T(2,128)(2,1)S(1)}, u32[]{:S(2)}, u32[]{:S(2)}) async-start(bf16[8,1,8]{2,1,0:T(2,128)(2,1)} %copy.69), calls=%async_computation | async-start | bytes 8192 | tf_op jit(solution)/shard_map/all_to_all | solution.py:146
  21.1 2.1 %collective-permute-start.3 = (f32[16,32,16]{2,0,1:T(8,128)S(1)}, f32[16,32,16]{2,0,1:T(8,128)S(1)}, u32[]{:S(2)}, u32[]{:S(2)}) collective-permute-start(f32[16,32,16]{2,0,1:T(8,128)S(1)} %get-tuple-element.10), channel_id=1, source_target_pairs={{1,0},{2,1},{3,2},{0,3},{5,4},{6,5},{7,6},{4,7},{9,8},{10,9},{11,1... | collective-permute-start | bytes 98312 | tf_op jit(solution)/shard_map/ppermute | solution.py:23
  23.2 5.8 %collective-permute-done.2 = f32[16,32,16]{2,0,1:T(8,128)S(1)} collective-permute-done((f32[16,32,16]{2,0,1:T(8,128)S(1)}, f32[16,32,16]{2,0,1:T(8,128)S(1)}, u32[]{:S(2)}, u32[]{:S(2)}) %collective-permute-start.2) | collective-permute-done | bytes 32800 | tf_op jit(solution)/shard_map/ppermute | solution.py:20
  29.0 5.3 %collective-permute-done.3 = f32[16,32,16]{2,0,1:T(8,128)S(1)} collective-permute-done((f32[16,32,16]{2,0,1:T(8,128)S(1)}, f32[16,32,16]{2,0,1:T(8,128)S(1)}, u32[]{:S(2)}, u32[]{:S(2)}) %collective-permute-start.3) | collective-permute-done | bytes 32800 | tf_op jit(solution)/shard_map/ppermute | solution.py:23
  34.6 1.7 %fusion.16 = bf16[16,32,128]{2,1,0:T(8,128)(2,1)S(1)} fusion(f32[16,32,128]{2,1,0:T(8,128)S(1)} %copy-done.3, f32[16]{0:T(128)S(1)} %sqrt.13, f32[16]{0:T(128)S(1)} %get-tuple-element.11, f32[160,128]{1,0:T(8,128)S(1)} %negate_multiply_fusion, pred[160,128]{1,0:T(8,128)(4,1)S(1)} %abs_compare_fusion, f32[16,32,160]{2,0,1:T(8,128)S(1)} %pad_maximum_fusion.1), kind=kOutput, calls=%fused_computation.25 | convolution fusion | flops 126943232 | bytes 823424 | tf_op jit(solution)/shard_map/rlq,rqc->rlc/dot_general | solution.py:59
  37.3 2.9 %copy.76 = bf16[16,16,32,8]{1,0,3,2:T(8,128)(2,1)S(1)} copy(bf16[16,16,32,8]{2,3,1,0:T(8,128)(2,1)} %bitcast.73) | data formatting | bytes 262144 | tf_op jit(solution)/shard_map/transpose | solution.py:119
  42.0 4.9 %all-to-all-start.1 = ((bf16[8,8,256]{2,1,0:T(8,128)(2,1)}), bf16[8,8,256]{2,1,0:T(8,128)(2,1)S(1)}, u32[]{:S(2)}, u32[]{:S(2)}) async-start(bf16[8,8,256]{2,1,0:T(8,128)(2,1)} %convolution_convert_fusion.1), calls=%async_computation.1 | async-start | bytes 65536 | tf_op jit(solution)/shard_map/all_to_all | solution.py:145
  48.1 2.9 %all-to-all-done.1 = bf16[8,8,256]{2,1,0:T(8,128)(2,1)S(1)} async-done(((bf16[8,8,256]{2,1,0:T(8,128)(2,1)}), bf16[8,8,256]{2,1,0:T(8,128)(2,1)S(1)}, u32[]{:S(2)}, u32[]{:S(2)}) %all-to-all-start.1) | async-done | bytes 32800 | tf_op jit(solution)/shard_map/all_to_all | solution.py:145
  51.5 2.0 %fusion.5 = bf16[288,1024]{1,0:T(8,128)(2,1)} fusion(bf16[32,1024]{1,0:T(8,128)(2,1)} %param.20, f32[1024]{0:T(1024)S(1)} %copy-done.6, bf16[32,36,8]{0,2,1:T(8,128)(2,1)S(1)} %copy.79), kind=kOutput, calls=%fused_computation.9 | convolution fusion | flops 19464192 | bytes 677888 | tf_op jit(solution)/shard_map/lh,lm->hm/dot_general | solution.py:74
  53.4 2.8 %fusion.2 = bf16[288,1024]{1,0:T(8,128)(2,1)} fusion(bf16[288,1024]{1,0:T(8,128)(2,1)} %fusion.5, bf16[1024,1024]{1,0:T(8,128)(2,1)S(1)} %copy-done, f32[1024]{0:T(1024)S(1)} %copy-done.7), kind=kOutput, calls=%fused_computation.6 | convolution fusion | flops 604569600 | bytes 3280896 | tf_op jit(solution)/shard_map/hk,hm->km/dot_general | solution.py:79
  56.2 2.9 %fusion.3 = bf16[288,1024]{1,0:T(8,128)(2,1)} fusion(bf16[1024,256]{1,0:T(8,128)(2,1)S(1)} %copy-done.2, bf16[288,1024]{1,0:T(8,128)(2,1)} %fusion.2, bf16[256,288]{0,1:T(8,128)(2,1)S(1)} %copy-done.4, f32[256]{0:T(256)S(1)} %copy-done.8, s32[288]{0:T(512)S(1)} %lt.30, pred[288]{0:T(512)(128)(4,1)S(1)} %and.28), kind=kOutput, calls=%fused_computation.7 | convolution fusion | flops 303980544 | bytes 1853856 | tf_op jit(solution)/shard_map/kn,nm->km/dot_general | solution.py:88
  59.1 2.3 %fusion.19 = bf16[32,288]{1,0:T(8,128)(2,1)S(1)} fusion(bf16[32,1024]{1,0:T(8,128)(2,1)S(1)} %copy-done.5, bf16[288,1024]{1,0:T(8,128)(2,1)} %fusion.3, bf16[1024,1024]{1,0:T(8,128)(2,1)S(1)} %copy-done, bf16[288,1024]{1,0:T(8,128)(2,1)} %fusion.5), kind=kOutput, calls=%fused_computation.32 | convolution fusion | flops 624337920 | bytes 3360768 | tf_op jit(solution)/shard_map/lh,hm->lm/dot_general | solution.py:94
  61.9 7.2 %all_to_all.16 = bf16[8,8,256]{2,1,0:T(8,128)(2,1)S(1)} all-to-all(bf16[8,8,256]{2,1,0:T(8,128)(2,1)S(1)} %fusion.18), channel_id=1, replica_groups=mesh['lat'=8,'lon'=4] {'lat'}, dimensions={0} | all-to-all | bytes 65536 | tf_op jit(solution)/shard_map/all_to_all | solution.py:173
  69.3 2.0 %reshape.162 = f32[16,16,32,8]{1,0,3,2:T(8,128)} reshape(f32[256,256]{0,1:T(8,128)S(1)} %convolution_bitcast_fusion) | data formatting | bytes 524288 | tf_op jit(solution)/shard_map/reshape | solution.py:181
  71.3 2.8 %copy.83 = f32[16,32,16,8]{1,3,2,0:T(8,128)S(1)} copy(f32[16,32,16,8]{2,0,3,1:T(8,128)} %bitcast.71) | data formatting | bytes 524288 | tf_op jit(solution)/shard_map/transpose | solution.py:181
  75.5 2.4 %collective-permute-start.5 = (f32[16,32,16]{2,1,0:T(8,128)S(1)}, f32[16,32,16]{2,1,0:T(8,128)S(1)}, u32[]{:S(2)}, u32[]{:S(2)}) collective-permute-start(f32[16,32,16]{2,1,0:T(8,128)S(1)} %get-tuple-element.8), channel_id=1, source_target_pairs={{1,0},{2,1},{3,2},{0,3},{5,4},{6,5},{7,6},{4,7},{9,8},{10,9},{11,1... | collective-permute-start | bytes 98312 | tf_op jit(solution)/shard_map/ppermute | solution.py:23
  77.9 5.7 %collective-permute-done.4 = f32[16,32,16]{2,1,0:T(8,128)S(1)} collective-permute-done((f32[16,32,16]{2,1,0:T(8,128)S(1)}, f32[16,32,16]{2,1,0:T(8,128)S(1)}, u32[]{:S(2)}, u32[]{:S(2)}) %collective-permute-start.4) | collective-permute-done | bytes 32800 | tf_op jit(solution)/shard_map/ppermute | solution.py:20
  83.6 4.7 %collective-permute-done.5 = f32[16,32,16]{2,1,0:T(8,128)S(1)} collective-permute-done((f32[16,32,16]{2,1,0:T(8,128)S(1)}, f32[16,32,16]{2,1,0:T(8,128)S(1)}, u32[]{:S(2)}, u32[]{:S(2)}) %collective-permute-start.5) | collective-permute-done | bytes 32800 | tf_op jit(solution)/shard_map/ppermute | solution.py:23
  88.3 1.5 %fusion.27 = f32[16,32,128]{2,1,0:T(8,128)S(1)} fusion(f32[16]{0:T(128)S(1)} %sqrt.13, f32[16]{0:T(128)S(1)} %get-tuple-element.11, f32[160,128]{1,0:T(8,128)S(1)} %negate_multiply_fusion, pred[160,128]{1,0:T(8,128)(4,1)S(1)} %abs_compare_fusion, f32[16,32,16]{2,1,0:T(8,128)S(1)} %collective-permute-done.5, f32[16,32,128]{2,1,0:T(8,128)S(1)} %copy.84, ...), kind=kOutput, calls=%fused_computation.41 | convolution fusion | flops 126976000 | bytes 692352 | tf_op jit(solution)/shard_map/rlq,rqc->rlc/dot_general | solution.py:59
  89.8 3.6 %collective-permute-start.7 = (f32[16,32,128]{2,1,0:T(8,128)S(1)}, f32[16,32,128]{2,1,0:T(8,128)S(1)}, u32[]{:S(2)}, u32[]{:S(2)}) collective-permute-start(f32[16,32,128]{2,1,0:T(8,128)S(1)} %fusion.27), channel_id=1, source_target_pairs={{4,0},{8,4},{12,8},{16,12},{20,16},{24,20},{28,24},{5,1},{9,5},{13... | collective-permute-start | bytes 786440 | tf_op jit(solution)/shard_map/ppermute | solution.py:23
  93.4 2.4 %collective-permute-start.6 = (f32[16,32,128]{2,1,0:T(8,128)S(1)}, f32[16,32,128]{2,1,0:T(8,128)S(1)}, u32[]{:S(2)}, u32[]{:S(2)}) collective-permute-start(f32[16,32,128]{2,1,0:T(8,128)S(1)} %fusion.27), channel_id=1, source_target_pairs={{0,4},{4,8},{8,12},{12,16},{16,20},{20,24},{24,28},{1,5},{5,9},{9,... | collective-permute-start | bytes 786440 | tf_op jit(solution)/shard_map/ppermute | solution.py:20
  95.8 2.1 %collective-permute-done.7 = f32[16,32,128]{2,1,0:T(8,128)S(1)} collective-permute-done((f32[16,32,128]{2,1,0:T(8,128)S(1)}, f32[16,32,128]{2,1,0:T(8,128)S(1)}, u32[]{:S(2)}, u32[]{:S(2)}) %collective-permute-start.7) | collective-permute-done | bytes 262176 | tf_op jit(solution)/shard_map/ppermute | solution.py:23
  (67 shorter events, 19.2 us)
Async XLA Ops:
  0.0 53.4 %copy-start = (bf16[1024,1024]{1,0:T(8,128)(2,1)S(1)}, bf16[1024,1024]{1,0:T(8,128)(2,1)}, u32[]{:S(2)}) copy-start(bf16[1024,1024]{1,0:T(8,128)(2,1)} %param.22) | copy-start | bytes 6291460
  1.3 17.8 %collective-permute-start = (f32[16,32,128]{2,0,1:T(8,128)S(1)}, f32[16,32,128]{2,0,1:T(8,128)S(1)}, u32[]{:S(2)}, u32[]{:S(2)}) collective-permute-start(f32[16,32,128]{2,0,1:T(8,128)S(1)} %copy.88), channel_id=1, source_target_pairs={{0,4},{4,8},{8,12},{12,16},{16,20},{20,24},{24,28},{1,5},{5,9},{9,... | collective-permute-start | bytes 786440 | tf_op jit(solution)/shard_map/ppermute | solution.py:20
  5.8 13.3 %collective-permute-start.1 = (f32[16,32,128]{2,0,1:T(8,128)S(1)}, f32[16,32,128]{2,0,1:T(8,128)S(1)}, u32[]{:S(2)}, u32[]{:S(2)}) collective-permute-start(f32[16,32,128]{2,0,1:T(8,128)S(1)} %copy.88), channel_id=1, source_target_pairs={{4,0},{8,4},{12,8},{16,12},{20,16},{24,20},{28,24},{5,1},{9,5},{13... | collective-permute-start | bytes 786440 | tf_op jit(solution)/shard_map/ppermute | solution.py:23
  10.0 8.3 %all-to-all-start = ((bf16[8,1,8]{2,1,0:T(2,128)(2,1)}), bf16[8,1,8]{2,1,0:T(2,128)(2,1)S(1)}, u32[]{:S(2)}, u32[]{:S(2)}) async-start(bf16[8,1,8]{2,1,0:T(2,128)(2,1)} %copy.69), calls=%async_computation | async-start | bytes 8192 | tf_op jit(solution)/shard_map/all_to_all | solution.py:146
  19.6 15.0 %copy-start.3 = (f32[16,32,128]{2,1,0:T(8,128)S(1)}, f32[16,32,128]{2,1,0:T(8,128)}, u32[]{:S(2)}) copy-start(f32[16,32,128]{2,1,0:T(8,128)} %param.14) | copy-start | bytes 786436
  19.8 9.3 %collective-permute-start.2 = (f32[16,32,16]{2,0,1:T(8,128)S(1)}, f32[16,32,16]{2,0,1:T(8,128)S(1)}, u32[]{:S(2)}, u32[]{:S(2)}) collective-permute-start(f32[16,32,16]{2,0,1:T(8,128)S(1)} %get-tuple-element.9), channel_id=1, source_target_pairs={{0,1},{1,2},{2,3},{3,0},{4,5},{5,6},{6,7},{7,4},{8,9},{9,10},{10,1... | collective-permute-start | bytes 98312 | tf_op jit(solution)/shard_map/ppermute | solution.py:20
  21.1 13.2 %collective-permute-start.3 = (f32[16,32,16]{2,0,1:T(8,128)S(1)}, f32[16,32,16]{2,0,1:T(8,128)S(1)}, u32[]{:S(2)}, u32[]{:S(2)}) collective-permute-start(f32[16,32,16]{2,0,1:T(8,128)S(1)} %get-tuple-element.10), channel_id=1, source_target_pairs={{1,0},{2,1},{3,2},{0,3},{5,4},{6,5},{7,6},{4,7},{9,8},{10,9},{11,1... | collective-permute-start | bytes 98312 | tf_op jit(solution)/shard_map/ppermute | solution.py:23
  40.2 11.3 %copy-start.6 = (f32[1024]{0:T(1024)S(1)}, f32[1024]{0:T(1024)}, u32[]{:S(2)}) copy-start(f32[1024]{0:T(1024)} %param.21) | copy-start | bytes 12292
  40.2 13.2 %copy-start.7 = (f32[1024]{0:T(1024)S(1)}, f32[1024]{0:T(1024)}, u32[]{:S(2)}) copy-start(f32[1024]{0:T(1024)} %param.23) | copy-start | bytes 12292
  42.0 9.0 %all-to-all-start.1 = ((bf16[8,8,256]{2,1,0:T(8,128)(2,1)}), bf16[8,8,256]{2,1,0:T(8,128)(2,1)S(1)}, u32[]{:S(2)}, u32[]{:S(2)}) async-start(bf16[8,8,256]{2,1,0:T(8,128)(2,1)} %convolution_convert_fusion.1), calls=%async_computation.1 | async-start | bytes 65536 | tf_op jit(solution)/shard_map/all_to_all | solution.py:145
  53.4 2.8 %copy-start.2 = (bf16[1024,256]{1,0:T(8,128)(2,1)S(1)}, bf16[1024,256]{1,0:T(8,128)(2,1)}, u32[]{:S(2)}) copy-start(bf16[1024,256]{1,0:T(8,128)(2,1)} %param.24) | copy-start | bytes 1572868
  53.4 2.8 %copy-start.4 = (bf16[256,288]{0,1:T(8,128)(2,1)S(1)}, bf16[256,288]{0,1:T(8,128)(2,1)}, u32[]{:S(2)}) copy-start(bf16[256,288]{0,1:T(8,128)(2,1)} %param.19) | copy-start | bytes 442372
  53.4 2.8 %copy-start.8 = (f32[256]{0:T(256)S(1)}, f32[256]{0:T(256)}, u32[]{:S(2)}) copy-start(f32[256]{0:T(256)} %param.25) | copy-start | bytes 3076
  56.2 2.9 %copy-start.5 = (bf16[32,1024]{1,0:T(8,128)(2,1)S(1)}, bf16[32,1024]{1,0:T(8,128)(2,1)}, u32[]{:S(2)}) copy-start(bf16[32,1024]{1,0:T(8,128)(2,1)} %param.20) | copy-start | bytes 196612
  74.6 9.0 %collective-permute-start.4 = (f32[16,32,16]{2,1,0:T(8,128)S(1)}, f32[16,32,16]{2,1,0:T(8,128)S(1)}, u32[]{:S(2)}, u32[]{:S(2)}) collective-permute-start(f32[16,32,16]{2,1,0:T(8,128)S(1)} %get-tuple-element.7), channel_id=1, source_target_pairs={{0,1},{1,2},{2,3},{3,0},{4,5},{5,6},{6,7},{7,4},{8,9},{9,10},{10,1... | collective-permute-start | bytes 98312 | tf_op jit(solution)/shard_map/ppermute | solution.py:20
  75.5 12.8 %collective-permute-start.5 = (f32[16,32,16]{2,1,0:T(8,128)S(1)}, f32[16,32,16]{2,1,0:T(8,128)S(1)}, u32[]{:S(2)}, u32[]{:S(2)}) collective-permute-start(f32[16,32,16]{2,1,0:T(8,128)S(1)} %get-tuple-element.8), channel_id=1, source_target_pairs={{1,0},{2,1},{3,2},{0,3},{5,4},{6,5},{7,6},{4,7},{9,8},{10,9},{11,1... | collective-permute-start | bytes 98312 | tf_op jit(solution)/shard_map/ppermute | solution.py:23
  89.8 9.4 %copy-start.1 = (f32[16,32,128]{2,1,0:T(8,128)S(1)}, f32[16,32,128]{2,1,0:T(8,128)}, u32[]{:S(2)}) copy-start(f32[16,32,128]{2,1,0:T(8,128)} %param.13) | copy-start | bytes 786436
  89.8 8.1 %collective-permute-start.7 = (f32[16,32,128]{2,1,0:T(8,128)S(1)}, f32[16,32,128]{2,1,0:T(8,128)S(1)}, u32[]{:S(2)}, u32[]{:S(2)}) collective-permute-start(f32[16,32,128]{2,1,0:T(8,128)S(1)} %fusion.27), channel_id=1, source_target_pairs={{4,0},{8,4},{12,8},{16,12},{20,16},{24,20},{28,24},{5,1},{9,5},{13... | collective-permute-start | bytes 786440 | tf_op jit(solution)/shard_map/ppermute | solution.py:23
  93.4 5.7 %collective-permute-start.6 = (f32[16,32,128]{2,1,0:T(8,128)S(1)}, f32[16,32,128]{2,1,0:T(8,128)S(1)}, u32[]{:S(2)}, u32[]{:S(2)}) collective-permute-start(f32[16,32,128]{2,1,0:T(8,128)S(1)} %fusion.27), channel_id=1, source_target_pairs={{0,4},{4,8},{8,12},{12,16},{16,20},{20,24},{24,28},{1,5},{5,9},{9,... | collective-permute-start | bytes 786440 | tf_op jit(solution)/shard_map/ppermute | solution.py:20
where the time goes:
time: 102 us; the launch traced here: 101 us
  starting transfers between devices  28.5 us (28%)
  waiting for transfers between devices  27.8 us (27%)
  matrix products  16.8 us (16%)
  local copies, waits for them, and re-layouts  14.7 us (14%)
  blocking collectives  7.21 us (7%)
  other arithmetic  5.11 us (5%)
    ppermute x4, waiting for transfers between devices, padded_2(): lax.ppermute(lax.slice_in_dim(block, block.shape[dim] - width, None, axis...  12.7 us
    ppermute x4, waiting for transfers between devices, padded_2(): lax.ppermute(lax.slice_in_dim(block, 0, width, axis=dim), axis, backward)  12.1 us
    ppermute x4, starting transfers between devices, padded_2(): lax.ppermute(lax.slice_in_dim(block, 0, width, axis=dim), axis, backward)  10 us
    ppermute x4, starting transfers between devices, padded_2(): lax.ppermute(lax.slice_in_dim(block, block.shape[dim] - width, None, axis...  9.14 us
    all_to_all x1, blocking collectives, observe(): lax.all_to_all(returning.reshape(lat_count, send_cap, block_size), 'lat',...  7.21 us
    all_to_all x1, starting transfers between devices, observe(): lax.all_to_all(outgoing, 'lat', split_axis=0, concat_axis=0, tiled=True)  4.95 us
    all_to_all x1, starting transfers between devices, observe(): lax.all_to_all(slot_flags, 'lat', split_axis=0, concat_axis=0, tiled=True)  4.36 us
    dot_general x2, matrix products, smooth_lon(): jnp.einsum('rlq,rqc->rlc', padded, band_matrix, precision=lax.Precision.H...  3.18 us
  transfers between devices with their start and end apart: 10, of which 7 were waited for; matrix products, arithmetic and copies ran while one was open for 7% of the time, Pallas kernels for 0%

commit v1 on v0

v1 whole, which is shorter than its diff:
```python
import functools

import jax
import jax.numpy as jnp
import numpy as np
from jax import lax
from jax.experimental import pallas as pl
from jax.experimental.pallas import tpu as pltpu
from jax.sharding import PartitionSpec as P

REACH = 16
BLOCK_COLS = 8
LANES = 128
LAT_SIGMA = 8.0
VMEM_BYTES = 40 * 1024 * 1024

VMEM = pl.BlockSpec(memory_space=pltpu.VMEM)
SMEM = pl.BlockSpec(memory_space=pltpu.SMEM)
ANY = pl.BlockSpec(memory_space=pl.ANY)


def lat_taps():
    offsets = np.arange(-REACH, REACH + 1, dtype=np.float64)
    raw = np.exp(-offsets * offsets / (2.0 * LAT_SIGMA * LAT_SIGMA))
    return [float(v) for v in (raw / np.sqrt(np.sum(raw * raw))).astype(np.float32)]


def call(kernel, out_shape, in_specs, out_specs, flops, bytes_moved, scratch=(), name=None):
    return pl.pallas_call(
        kernel,
        out_shape=out_shape,
        in_specs=in_specs,
        out_specs=out_specs,
        scratch_shapes=list(scratch),
        compiler_params=pltpu.CompilerParams(vmem_limit_bytes=VMEM_BYTES),
        cost_estimate=pl.CostEstimate(flops=flops, bytes_accessed=bytes_moved, transcendentals=0),
        name=name,
    )


def lat_conv_row(row, low, own, high):
    taps = lat_taps()
    height = own.shape[0]
    acc = None
    for j in range(-REACH, REACH + 1):
        source = row + j
        if source < 0:
            part = low[source + REACH]
        elif source < height:
            part = own[source]
        else:
            part = high[source - height]
        term = taps[j + REACH] * part
        acc = term if acc is None else acc + term
    return acc


def lon_conv(padded, taps, tile, width):
    acc = taps[tile, 0:1, :] * padded[tile, pl.ds(REACH, width), :]
    for j in range(1, REACH + 1):
        both = padded[tile, pl.ds(REACH + j, width), :] + padded[tile, pl.ds(REACH - j, width), :]
        acc = acc + taps[tile, j : j + 1, :] * both
    return acc


def owner_kernel(radiance, block_owner, channel_count, slabs, meta):
    channels, columns = radiance.shape
    slots = columns // BLOCK_COLS
    halves = channels // LANES
    parts = []
    for half in range(halves):
        block = radiance[half * LANES : (half + 1) * LANES, :].astype(jnp.float32)
        parts.append(jnp.transpose(block).reshape(slots, BLOCK_COLS, LANES))
    slabs[...] = jnp.concatenate(parts, axis=1).astype(jnp.bfloat16)
    meta[...] = jnp.zeros_like(meta)
    meta[0:1, :] = jnp.full((1, LANES), -1, jnp.int32)
    meta[0:1, 0 : block_owner.shape[1]] = block_owner[...]
    meta[1:2, 0 : channel_count.shape[1]] = channel_count[...]


def prepare_kernel(lon_width, background, taps, turned):
    tiles = turned.shape[0]
    height, levels, width = background.shape
    per_tile = height // tiles
    lane_row = lax.broadcasted_iota(jnp.int32, (1, LANES), 1) // levels
    steps = lax.broadcasted_iota(jnp.int32, (taps.shape[1], LANES), 0)
    dist = steps.astype(jnp.float32)
    weight = jnp.where(steps == 0, 1.0, jnp.where(steps <= REACH, 2.0, 0.0))
    for tile in range(tiles):
        spread = jnp.zeros((1, LANES), jnp.int32)
        for sub in range(per_tile):
            spread = jnp.where(lane_row == sub, lon_width[tile * per_tile + sub], spread)
        spread = spread.astype(jnp.float32)
        raw = jnp.exp(-dist * dist / (2.0 * spread * spread))
        norm = jnp.sum(weight * raw * raw, axis=0, keepdims=True)
        taps[tile] = raw / jnp.sqrt(norm)
        rows = background[tile * per_tile : (tile + 1) * per_tile].reshape(per_tile * levels, width)
        turned[tile] = jnp.transpose(rows)


def routing_kernel(recv_most, slot_count, mine, everyone, table):
    count = everyone.shape[0]
    here = lax.axis_index("lat")
    rows = lax.broadcasted_iota(jnp.int32, (slot_count, LANES), 0)
    lanes = lax.broadcasted_iota(jnp.int32, (slot_count, LANES), 1)
    diagonal = rows == lanes
    owner = jnp.sum(jnp.where(diagonal, mine[0:1, :], 0), axis=1, keepdims=True)

    def rank(device, acc):
        before = (device < here) | ((device == here) & (lanes < rows))
        same = everyone[device, 0:1, :] == owner
        return acc + jnp.where(same & before, 1, 0)

    zero = jnp.zeros((slot_count, LANES), jnp.int32)
    arrival = jnp.sum(lax.fori_loop(0, count, rank, zero, unroll=count <= 8), axis=1, keepdims=True)

    def counted(device, acc):
        hit = (owner == device) & (lanes == arrival)
        return acc + jnp.where(hit, everyone[device, 1:2, :], 0)

    kept = jnp.sum(lax.fori_loop(0, count, counted, zero, unroll=count <= 8), axis=1, keepdims=True)
    target = jnp.where(owner >= 0, owner * recv_most + arrival, 0)
    table[...] = jnp.zeros_like(table)
    table[0:1, :] = jnp.sum(jnp.where(diagonal, target, 0), axis=0, keepdims=True)
    table[1:2, :] = jnp.sum(jnp.where(diagonal, kept, 0), axis=0, keepdims=True)


def lat_smooth_kernel(low, own, high, smoothed, edge_low, edge_high):
    tiles = smoothed.shape[0]
    height, levels, width = own.shape
    per_tile = height // tiles
    for tile in range(tiles):
        rows = [lat_conv_row(tile * per_tile + sub, low, own, high) for sub in range(per_tile)]
        turned = jnp.transpose(jnp.concatenate(rows, axis=0))
        smoothed[tile] = turned
        edge_low[tile] = turned[0:REACH]
        edge_high[tile] = turned[width - REACH : width]


def block_place(cells, slot, groups, per_tile, width):
    block = cells[slot]
    row = block // groups
    start = (row // per_tile) * width + (block % groups) * BLOCK_COLS
    return pl.multiple_of(start, BLOCK_COLS), row % per_tile


def net_kernel(
    cells,
    table,
    low,
    own,
    high,
    turned,
    taps,
    slabs,
    in_weight,
    in_bias,
    mid_weight,
    mid_bias,
    out_weight,
    out_bias,
    landing,
    edge_low,
    edge_high,
    padded,
    profile,
    picked,
    wide_in,
    emitted,
    misfit,
    observed,
    act_one,
    act_two,
    sem,
):
    tiles, width, _ = own.shape
    levels = in_weight.shape[0]
    per_tile = LANES // levels
    groups = width // BLOCK_COLS
    slot_count = cells.shape[0]
    channels = out_weight.shape[1]

    def fetch(slot, carry):
        pltpu.make_async_copy(slabs.at[table[0, slot]], observed.at[slot], sem).start()
        return carry

    lax.fori_loop(0, slot_count, fetch, 0, unroll=8)

    padded[:, 0:REACH, :] = low[...]
    padded[:, REACH : REACH + width, :] = own[...]
    padded[:, REACH + width :, :] = high[...]
    for tile in range(tiles):
        total = turned[tile] + lon_conv(padded, taps, tile, width)
        profile[tile * width : (tile + 1) * width, :] = total.astype(jnp.bfloat16).astype(jnp.float32)
    for sub in range(per_tile):
        wide_in[sub * levels : (sub + 1) * levels, :] = in_weight[...]

    lane_row = lax.broadcasted_iota(jnp.int32, (BLOCK_COLS, LANES), 1) // levels
    for slot in range(slot_count):
        start, sub = block_place(cells, slot, groups, per_tile, width)
        block = profile[pl.ds(start, BLOCK_COLS), :]
        picked[slot * BLOCK_COLS : (slot + 1) * BLOCK_COLS, :] = jnp.where(lane_row == sub, block, 0.0)

    def dot(a, b):
        return jnp.dot(a, b, preferred_element_type=jnp.float32)

    def dot_t(a, b):
        return lax.dot_general(a, b, (((1,), (1,)), ((), ())), preferred_element_type=jnp.float32)

    inputs = picked[...].astype(jnp.bfloat16)
    act_one[...] = jnp.tanh(dot(inputs, wide_in[...]) + in_bias[...]).astype(jnp.bfloat16)
    act_two[...] = jnp.tanh(dot(act_one[...], mid_weight[...]) + mid_bias[...]).astype(jnp.bfloat16)
    emitted[...] = dot(act_two[...], out_weight[...]) + out_bias[...]

    pltpu.make_async_copy(slabs.at[pl.ds(0, slot_count)], observed, sem).wait()
    channel = lax.broadcasted_iota(jnp.int32, (BLOCK_COLS, channels), 1)
    for slot in range(0, slot_count, 2):
        pair = []
        for at in (slot, slot + 1):
            slab = observed[at].astype(jnp.float32)
            seen = jnp.concatenate(
                [slab[h * BLOCK_COLS : (h + 1) * BLOCK_COLS] for h in range(channels // LANES)], axis=1
            )
            gap = emitted[at * BLOCK_COLS : (at + 1) * BLOCK_COLS, :] - seen
            pair.append(jnp.where(channel < table[1, at], gap, 0.0))
        misfit[slot * BLOCK_COLS : (slot + 2) * BLOCK_COLS, :] = jnp.concatenate(pair, axis=0).astype(
            jnp.bfloat16
        )

    two = act_two[...].astype(jnp.float32)
    grad_two = (dot_t(misfit[...], out_weight[...]) * (1.0 - two * two)).astype(jnp.bfloat16)
    one = act_one[...].astype(jnp.float32)
    grad_one = (dot_t(grad_two, mid_weight[...]) * (1.0 - one * one)).astype(jnp.bfloat16)
    picked[...] = dot_t(grad_one, wide_in[...]).astype(jnp.bfloat16).astype(jnp.float32)

    profile[...] = jnp.zeros_like(profile)
    for slot in range(slot_count):
        start, sub = block_place(cells, slot, groups, per_tile, width)
        block = picked[slot * BLOCK_COLS : (slot + 1) * BLOCK_COLS, :]
        profile[pl.ds(start, BLOCK_COLS), :] += jnp.where(lane_row == sub, block, 0.0)
    for tile in range(tiles):
        landing[tile] = profile[tile * width : (tile + 1) * width, :]
        edge_low[tile] = profile[tile * width : tile * width + REACH, :].astype(jnp.bfloat16)
        edge_high[tile] = profile[(tile + 1) * width - REACH : (tile + 1) * width, :].astype(jnp.bfloat16)


def lon_back_kernel(low, own, high, taps, back, padded):
    tiles, width, _ = own.shape
    height, levels, _ = back.shape
    per_tile = height // tiles
    padded[:, 0:REACH, :] = low[...].astype(jnp.float32)
    padded[:, REACH : REACH + width, :] = own[...]
    padded[:, REACH + width :, :] = high[...].astype(jnp.float32)
    for tile in range(tiles):
        rows = jnp.transpose(lon_conv(padded, taps, tile, width))
        back[tile * per_tile : (tile + 1) * per_tile] = rows.reshape(per_tile, levels, width)


def lat_back_kernel(low, own, high, control, gradient):
    for row in range(own.shape[0]):
        gradient[row] = control[row] + lat_conv_row(row, low, own, high)


def swap(forward_value, backward_value, axis, periodic):
    count = lax.axis_size(axis)
    forward = [(i, i + 1) for i in range(count - 1)]
    if periodic:
        forward.append((count - 1, 0))
    backward = [(target, source) for source, target in forward]
    return lax.ppermute(forward_value, axis, forward), lax.ppermute(backward_value, axis, backward)


def shards(
    control,
    background,
    lon_width,
    block_cells,
    block_owner,
    channel_count,
    radiance,
    in_weight,
    in_bias,
    mid_weight,
    mid_bias,
    out_weight,
    out_bias,
):
    height, levels, width = control.shape
    hidden = mid_weight.shape[0]
    channels, columns = radiance.shape
    slot_count = block_owner.shape[0]
    recv_most = channel_count.shape[0]
    per_tile = LANES // levels
    tiles = height // per_tile
    slab_rows = BLOCK_COLS * channels // LANES
    f32, bf16, i32 = jnp.float32, jnp.bfloat16, jnp.int32
    shape = jax.ShapeDtypeStruct
    field = height * levels * width
    conv_flops = 2 * 33 * field

    low, high = swap(control, control, "lat", False)

    slabs, meta = call(
        owner_kernel,
        (shape((recv_most, slab_rows, LANES), bf16), shape((8, LANES), i32)),
        [VMEM] * 3,
        (VMEM, VMEM),
        0,
        4 * channels * columns,
        name="owner_slabs",
    )(radiance, block_owner.reshape(1, slot_count), channel_count.reshape(1, recv_most))
    all_meta = lax.all_gather(meta, "lat", axis=0, tiled=False)
    all_slabs = lax.all_gather(slabs, "lat", axis=0, tiled=True)

    taps, turned = call(
        prepare_kernel,
        (shape((tiles, 24, LANES), f32), shape((tiles, width, LANES), f32)),
        [SMEM, VMEM],
        (VMEM, VMEM),
        0,
        8 * field,
        name="taps_background",
    )(lon_width, background)

    table = call(
        functools.partial(routing_kernel, recv_most, slot_count),
        shape((8, LANES), i32),
        [VMEM, VMEM],
        VMEM,
        0,
        32768,
        name="routing",
    )(meta, all_meta)

    smoothed, edge_low, edge_high = call(
        lat_smooth_kernel,
        (shape((tiles, width, LANES), f32),) + (shape((tiles, REACH, LANES), f32),) * 2,
        [VMEM] * 3,
        (VMEM,) * 3,
        conv_flops,
        16 * field,
        name="lat_smooth",
    )(low, control, high)
    low, high = swap(edge_high, edge_low, "lon", True)

    x_rows = slot_count * BLOCK_COLS
    landing, edge_low, edge_high = call(
        net_kernel,
        (shape((tiles, width, LANES), f32),) + (shape((tiles, REACH, LANES), bf16),) * 2,
        [SMEM, SMEM] + [VMEM] * 5 + [ANY] + [VMEM] * 6,
        (VMEM,) * 3,
        4 * x_rows * hidden * (LANES + hidden + channels),
        6 * 1024 * 1024,
        scratch=(
            pltpu.VMEM((tiles, width + 2 * REACH, LANES), f32),
            pltpu.VMEM((tiles * width, LANES), f32),
            pltpu.VMEM((x_rows, LANES), f32),
            pltpu.VMEM((LANES, hidden), bf16),
            pltpu.VMEM((x_rows, channels), f32),
            pltpu.VMEM((x_rows, channels), bf16),
            pltpu.VMEM((slot_count, slab_rows, LANES), bf16),
            pltpu.VMEM((x_rows, hidden), bf16),
            pltpu.VMEM((x_rows, hidden), bf16),
            pltpu.SemaphoreType.DMA,
        ),
        name="net",
    )(
        block_cells.reshape(slot_count),
        table,
        low,
        smoothed,
        high,
        turned,
        taps,
        all_slabs,
        in_weight,
        in_bias.reshape(1, hidden),
        mid_weight,
        mid_bias.reshape(1, hidden),
        out_weight,
        out_bias.reshape(1, channels),
    )
    low, high = swap(edge_high, edge_low, "lon", True)

    back = call(
        lon_back_kernel,
        shape((height, levels, width), f32),
        [VMEM] * 4,
        VMEM,
        conv_flops,
        8 * field,
        scratch=(pltpu.VMEM((tiles, width + 2 * REACH, LANES), f32),),
        name="lon_back",
    )(low, landing, high, taps)
    low, high = swap(back, back, "lat", False)

    return call(
        lat_back_kernel,
        shape((height, levels, width), f32),
        [VMEM] * 4,
        VMEM,
        conv_flops,
        20 * field,
        name="lat_back",
    )(low, back, high, control)


def solution(mesh):
    return jax.shard_map(
        shards,
        mesh=mesh,
        in_specs=(
            P("lat", None, "lon"),
            P("lat", None, "lon"),
            P("lat"),
            P("lat", "lon"),
            P("lat", "lon"),
            P("lat", "lon"),
            P("lat", "lon"),
            P(),
            P(),
            P(),
            P(),
            P(),
            P(),
        ),
        out_specs=P("lat", None, "lon"),
        check_vma=False,
    )
```

time: 102 us -> 78.3 us (0.77)
  waiting for transfers between devices: 27.8 us -> 8.07 us
  matrix products: 16.8 us -> 0 us
  between operations: 0.95 us -> 13.5 us
  Pallas kernels: 0 us -> 11.1 us
  starting transfers between devices: 28.5 us -> 18.7 us
  blocking collectives: 7.21 us -> 13.1 us
  other arithmetic: 5.11 us -> 0 us
  local copies, waits for them, and re-layouts: 14.7 us -> 12.4 us
    dot_general x13 -> x0, matrix products: 16.8 us -> none  [the longest x2 3.18 us: smooth_lon(): jnp.einsum('rlq,rqc->rlc', padded, band_matrix, precision=lax.Precision.H...]
    ppermute x8, waiting for transfers between devices: 24.8 us -> 8.03 us  [the longest x4 4.44 us: swap(): lax.ppermute(backward_value, axis, backward)]
    all_gather x0 -> x1, blocking collectives: none -> 13.1 us  [shards(): all_meta = lax.all_gather(meta, 'lat', axis=0, tiled=False)]
    pallas_call x0 -> x7, Pallas kernels: none -> 11.1 us  [the longest x1 6.63 us: shards(): call(net_kernel, (shape((tiles, width, LANES), f32),) + (shape((tiles, RE...]
    unnamed x19 -> x29, local copies, waits for them, and re-layouts: 1.3 us -> 12.4 us
    all_to_all x2 -> x0, starting transfers between devices: 9.3 us -> none  [the longest x1 4.95 us: observe(): lax.all_to_all(outgoing, 'lat', split_axis=0, concat_axis=0, tiled=True)]
    all_to_all x1 -> x0, blocking collectives: 7.21 us -> none  [observe(): lax.all_to_all(returning.reshape(lat_count, send_cap, block_size), 'lat',...]
    transpose x4 -> x0, local copies, waits for them, and re-layouts: 6.04 us -> none  [the longest x1 2.9 us: observe(): jnp.transpose(profile.reshape(height, levels, groups, BLOCK_COLS), (0, 2,...]
  transfers between devices with their start and end apart: 10 -> 9, of which waited for: 7 -> 5; matrix products, arithmetic and copies ran while one was open for 7% -> 0% of each run, Pallas kernels for 0% -> 2%
where the time goes in v1:
time: 78.3 us; the launch traced here: 76.9 us
  starting transfers between devices  18.7 us (24%)
  between operations  13.5 us (17%)
  blocking collectives  13.1 us (17%)
  local copies, waits for them, and re-layouts  12.4 us (16%)
  Pallas kernels  11.1 us (14%)
  waiting for transfers between devices  8.07 us (10%)
    all_gather x1, blocking collectives, shards(): all_meta = lax.all_gather(meta, 'lat', axis=0, tiled=False)  13.1 us
    unnamed x29, local copies, waits for them, and re-layouts  12.4 us
    ppermute x4, starting transfers between devices, swap(): lax.ppermute(backward_value, axis, backward)  10.6 us
    ppermute x4, starting transfers between devices, swap(): lax.ppermute(forward_value, axis, forward)  8.18 us
    pallas_call x1, Pallas kernels, shards(): call(net_kernel, (shape((tiles, width, LANES), f32),) + (shape((tiles, RE...  6.63 us
    ppermute x4, waiting for transfers between devices, swap(): lax.ppermute(backward_value, axis, backward)  4.44 us
    ppermute x4, waiting for transfers between devices, swap(): lax.ppermute(forward_value, axis, forward)  3.6 us
  transfers between devices with their start and end apart: 9, of which 5 were waited for; matrix products, arithmetic and copies ran while one was open for 0% of the time, Pallas kernels for 2%

profile of v1, /device:TPU:1, one launch (start us, length us, event | category | flops | bytes accessed | tf_op | source)
XLA Modules:
  0.0 76.9 jit_solution(1701305438553822000)
XLA Ops:
  6.5 1.1 %copy.15.radiance = bf16[256,288]{1,0:T(8,128)(2,1)S(1)} copy(bf16[256,288]{0,1:T(8,128)(2,1)} %param.19) | data formatting | bytes 294912 | tf_op args[6]
  8.9 0.8 %owner_slabs.1 = (bf16[36,16,128]{2,1,0:T(8,128)(2,1)}, s32[8,128]{1,0:T(8,128)S(1)}) custom-call(bf16[256,288]{1,0:T(8,128)(2,1)S(1)} %copy.15.radiance, s32[1,64]{1,0:T(1,128)S(1)} %bitcast.8, s32[1,36]{1,0:T(1,128)S(1)} %bitcast.9), custom_call_target="tpu_custom_call" | custom-call | bytes 294912 | tf_op jit(solution)/shard_map/owner_slabs/pallas_call | solution.py:303
  9.8 2.0 %collective-permute-start.1 = (f32[16,32,128]{2,1,0:T(8,128)}, f32[16,32,128]{2,1,0:T(8,128)S(1)}, u32[]{:S(2)}, u32[]{:S(2)}) collective-permute-start(f32[16,32,128]{2,1,0:T(8,128)} %control.1), channel_id=1, source_target_pairs={{4,0},{8,4},{12,8},{16,12},{20,16},{24,20},{28,24},{5,1},{9,5},{13... | collective-permute-start | bytes 786440 | tf_op jit(solution)/shard_map/ppermute | solution.py:270
  11.7 4.5 %collective-permute-start = (f32[16,32,128]{2,1,0:T(8,128)}, f32[16,32,128]{2,1,0:T(8,128)S(1)}, u32[]{:S(2)}, u32[]{:S(2)}) collective-permute-start(f32[16,32,128]{2,1,0:T(8,128)} %control.1), channel_id=1, source_target_pairs={{0,4},{4,8},{8,12},{12,16},{16,20},{20,24},{24,28},{1,5},{5,9},{9,... | collective-permute-start | bytes 786440 | tf_op jit(solution)/shard_map/ppermute | solution.py:270
  16.2 2.3 %collective-permute-done.1.high = f32[16,32,128]{2,1,0:T(8,128)S(1)} collective-permute-done((f32[16,32,128]{2,1,0:T(8,128)}, f32[16,32,128]{2,1,0:T(8,128)S(1)}, u32[]{:S(2)}, u32[]{:S(2)}) %collective-permute-start.1) | collective-permute-done | bytes 262176 | tf_op jit(solution)/shard_map/ppermute | solution.py:270
  18.5 1.3 %collective-permute-done.low = f32[16,32,128]{2,1,0:T(8,128)S(1)} collective-permute-done((f32[16,32,128]{2,1,0:T(8,128)}, f32[16,32,128]{2,1,0:T(8,128)S(1)}, u32[]{:S(2)}, u32[]{:S(2)}) %collective-permute-start) | collective-permute-done | bytes 262176 | tf_op jit(solution)/shard_map/ppermute | solution.py:270
  19.8 1.0 %copy-done = f32[16,32,128]{2,1,0:T(8,128)S(1)} copy-done((f32[16,32,128]{2,1,0:T(8,128)S(1)}, f32[16,32,128]{2,1,0:T(8,128)}, u32[]{:S(2)}) %copy-start) | copy-done | bytes 262168
  20.8 0.7 lat_smooth.1
  21.5 1.3 %collective-permute-start.2 = (f32[4,16,128]{2,1,0:T(8,128)S(1)}, f32[4,16,128]{2,1,0:T(8,128)S(1)}, u32[]{:S(2)}, u32[]{:S(2)}) collective-permute-start(f32[4,16,128]{2,1,0:T(8,128)S(1)} %get-tuple-element.16), channel_id=1, source_target_pairs={{0,1},{1,2},{2,3},{3,0},{4,5},{5,6},{6,7},{7,4},{8,9},{9,10},{10,1... | collective-permute-start | bytes 98312 | tf_op jit(solution)/shard_map/ppermute | solution.py:270
  22.8 2.1 %collective-permute-start.3 = (f32[4,16,128]{2,1,0:T(8,128)S(1)}, f32[4,16,128]{2,1,0:T(8,128)S(1)}, u32[]{:S(2)}, u32[]{:S(2)}) collective-permute-start(f32[4,16,128]{2,1,0:T(8,128)S(1)} %get-tuple-element.18), channel_id=1, source_target_pairs={{1,0},{2,1},{3,2},{0,3},{5,4},{6,5},{7,6},{4,7},{9,8},{10,9},{11,1... | collective-permute-start | bytes 98312 | tf_op jit(solution)/shard_map/ppermute | solution.py:270
  24.9 13.1 %all-gather = s32[64,128]{1,0:T(8,128)S(1)} all-gather(s32[8,128]{1,0:T(8,128)S(1)} %get-tuple-element.15.mine), channel_id=2, replica_groups=mesh['lat'=8,'lon'=4] {'lat'}, dimensions={0}, use_global_device_ids=true | all-gather | bytes 36864 | tf_op jit(solution)/shard_map/all_gather | solution.py:312
  38.4 0.9 %copy-done.2 = f32[16,32,128]{2,1,0:T(8,128)S(1)} copy-done((f32[16,32,128]{2,1,0:T(8,128)S(1)}, f32[16,32,128]{2,1,0:T(8,128)}, u32[]{:S(2)}) %copy-start.2) | copy-done | bytes 262168
  40.7 1.6 %copy-done.6 = bf16[1024,1024]{1,0:T(8,128)(2,1)S(1)} copy-done((bf16[1024,1024]{1,0:T(8,128)(2,1)S(1)}, bf16[1024,1024]{1,0:T(8,128)(2,1)}, u32[]{:S(2)}) %copy-start.6) | copy-done | bytes 2097176
  42.3 1.3 %copy-done.7 = bf16[288,16,128]{2,1,0:T(8,128)(2,1)S(1)} copy-done((bf16[288,16,128]{2,1,0:T(8,128)(2,1)S(1)}, bf16[288,16,128]{2,1,0:T(8,128)(2,1)}, u32[]{:S(2)}) %copy-start.7) | copy-done | bytes 1179672
  43.5 1.0 %copy-done.8 = bf16[1024,256]{1,0:T(8,128)(2,1)S(1)} copy-done((bf16[1024,256]{1,0:T(8,128)(2,1)S(1)}, bf16[1024,256]{1,0:T(8,128)(2,1)}, u32[]{:S(2)}) %copy-start.8) | copy-done | bytes 524312
  44.6 0.8 %copy-done.9 = bf16[32,1024]{1,0:T(8,128)(2,1)S(1)} copy-done((bf16[32,1024]{1,0:T(8,128)(2,1)S(1)}, bf16[32,1024]{1,0:T(8,128)(2,1)}, u32[]{:S(2)}) %copy-start.9) | copy-done | bytes 65560
  48.1 6.6 %net.1 = (f32[4,128,128]{2,1,0:T(8,128)S(1)}, bf16[4,16,128]{2,1,0:T(8,128)(2,1)S(1)}, bf16[4,16,128]{2,1,0:T(8,128)(2,1)S(1)}) custom-call(s32[64]{0:T(128)S(1)} %bitcast.13, s32[8,128]{1,0:T(8,128)S(1)} %routing.1.table, f32[4,16,128]{2,1,0:T(8,128)S(1)} %collective-permute-done.2.low, f32[4,128,128]{2,1,0:T(8,128)S(1)} %get-tuple-element.17.own, ...), custom_call_target="tpu_custom_call" | custom-call | flops 2952790016 | bytes 6291456 | tf_op jit(solution)/shard_map/net/pallas_call | solution.py:347
  54.8 3.3 %collective-permute-start.5 = (bf16[4,16,128]{2,1,0:T(8,128)(2,1)S(1)}, bf16[4,16,128]{2,1,0:T(8,128)(2,1)S(1)}, u32[]{:S(2)}, u32[]{:S(2)}) collective-permute-start(bf16[4,16,128]{2,1,0:T(8,128)(2,1)S(1)} %get-tuple-element.24), channel_id=1, source_target_pairs={{1,0},{2,1},{3,2},{0,3},{5,4},{6,5},{7,6},{4,7},{9,8},{10,9},{11,1... | collective-permute-start | bytes 49160 | tf_op jit(solution)/shard_map/ppermute | solution.py:270
  58.1 1.1 %collective-permute-done.4.low = bf16[4,16,128]{2,1,0:T(8,128)(2,1)S(1)} collective-permute-done((bf16[4,16,128]{2,1,0:T(8,128)(2,1)S(1)}, bf16[4,16,128]{2,1,0:T(8,128)(2,1)S(1)}, u32[]{:S(2)}, u32[]{:S(2)}) %collective-permute-start.4) | collective-permute-done | bytes 16416 | tf_op jit(solution)/shard_map/ppermute | solution.py:270
  59.9 3.2 %collective-permute-start.7 = (f32[16,32,128]{2,1,0:T(8,128)S(1)}, f32[16,32,128]{2,1,0:T(8,128)S(1)}, u32[]{:S(2)}, u32[]{:S(2)}) collective-permute-start(f32[16,32,128]{2,1,0:T(8,128)S(1)} %lon_back.1.own), channel_id=1, source_target_pairs={{4,0},{8,4},{12,8},{16,12},{20,16},{24,20},{28,24},{5,1},{9,5},{13... | collective-permute-start | bytes 786440 | tf_op jit(solution)/shard_map/ppermute | solution.py:270
  63.1 2.3 %collective-permute-start.6 = (f32[16,32,128]{2,1,0:T(8,128)S(1)}, f32[16,32,128]{2,1,0:T(8,128)S(1)}, u32[]{:S(2)}, u32[]{:S(2)}) collective-permute-start(f32[16,32,128]{2,1,0:T(8,128)S(1)} %lon_back.1.own), channel_id=1, source_target_pairs={{0,4},{4,8},{8,12},{12,16},{16,20},{20,24},{24,28},{1,5},{5,9},{9,... | collective-permute-start | bytes 786440 | tf_op jit(solution)/shard_map/ppermute | solution.py:270
  65.5 2.1 %collective-permute-done.7.high = f32[16,32,128]{2,1,0:T(8,128)S(1)} collective-permute-done((f32[16,32,128]{2,1,0:T(8,128)S(1)}, f32[16,32,128]{2,1,0:T(8,128)S(1)}, u32[]{:S(2)}, u32[]{:S(2)}) %collective-permute-start.7) | collective-permute-done | bytes 262176 | tf_op jit(solution)/shard_map/ppermute | solution.py:270
  67.6 1.2 %collective-permute-done.6.low = f32[16,32,128]{2,1,0:T(8,128)S(1)} collective-permute-done((f32[16,32,128]{2,1,0:T(8,128)S(1)}, f32[16,32,128]{2,1,0:T(8,128)S(1)}, u32[]{:S(2)}, u32[]{:S(2)}) %collective-permute-start.6) | collective-permute-done | bytes 262176 | tf_op jit(solution)/shard_map/ppermute | solution.py:270
  68.8 1.3 %lat_back.1 = f32[16,32,128]{2,1,0:T(8,128)} custom-call(f32[16,32,128]{2,1,0:T(8,128)S(1)} %collective-permute-done.6.low, f32[16,32,128]{2,1,0:T(8,128)S(1)} %lon_back.1.own, f32[16,32,128]{2,1,0:T(8,128)S(1)} %collective-permute-done.7.high, f32[16,32,128]{2,1,0:T(8,128)S(1)} %copy-done.1), custom_call_target="tpu_custom_call" | custom-call | flops 4325376 | bytes 1310720 | tf_op jit(solution)/shard_map/lat_back/pallas_call | solution.py:397
  (32 shorter events, 6.5 us)
Async XLA Ops:
  6.5 34.1 %all-gather.3.cloned.1.call-start = ((), (), s32[]{:S(2)}) async-start(), calls=%async_computation | async-start | bytes 1327104 | tf_op jit(solution)/shard_map/all_gather | solution.py:313
  7.6 0.7 copy-start.3
  8.3 0.7 copy-start.4
  9.8 8.8 %collective-permute-start.1 = (f32[16,32,128]{2,1,0:T(8,128)}, f32[16,32,128]{2,1,0:T(8,128)S(1)}, u32[]{:S(2)}, u32[]{:S(2)}) collective-permute-start(f32[16,32,128]{2,1,0:T(8,128)} %control.1), channel_id=1, source_target_pairs={{4,0},{8,4},{12,8},{16,12},{20,16},{24,20},{28,24},{5,1},{9,5},{13... | collective-permute-start | bytes 786440 | tf_op jit(solution)/shard_map/ppermute | solution.py:270
  11.7 8.1 %collective-permute-start = (f32[16,32,128]{2,1,0:T(8,128)}, f32[16,32,128]{2,1,0:T(8,128)S(1)}, u32[]{:S(2)}, u32[]{:S(2)}) collective-permute-start(f32[16,32,128]{2,1,0:T(8,128)} %control.1), channel_id=1, source_target_pairs={{0,4},{4,8},{8,12},{12,16},{16,20},{20,24},{24,28},{1,5},{5,9},{9,... | collective-permute-start | bytes 786440 | tf_op jit(solution)/shard_map/ppermute | solution.py:270
  19.8 1.0 %copy-start = (f32[16,32,128]{2,1,0:T(8,128)S(1)}, f32[16,32,128]{2,1,0:T(8,128)}, u32[]{:S(2)}) copy-start(f32[16,32,128]{2,1,0:T(8,128)} %control.1) | copy-start | bytes 786436
  21.5 19.2 %collective-permute-start.2 = (f32[4,16,128]{2,1,0:T(8,128)S(1)}, f32[4,16,128]{2,1,0:T(8,128)S(1)}, u32[]{:S(2)}, u32[]{:S(2)}) collective-permute-start(f32[4,16,128]{2,1,0:T(8,128)S(1)} %get-tuple-element.16), channel_id=1, source_target_pairs={{0,1},{1,2},{2,3},{3,0},{4,5},{5,6},{6,7},{7,4},{8,9},{9,10},{10,1... | collective-permute-start | bytes 98312 | tf_op jit(solution)/shard_map/ppermute | solution.py:270
  22.8 17.8 %collective-permute-start.3 = (f32[4,16,128]{2,1,0:T(8,128)S(1)}, f32[4,16,128]{2,1,0:T(8,128)S(1)}, u32[]{:S(2)}, u32[]{:S(2)}) collective-permute-start(f32[4,16,128]{2,1,0:T(8,128)S(1)} %get-tuple-element.18), channel_id=1, source_target_pairs={{1,0},{2,1},{3,2},{0,3},{5,4},{6,5},{7,6},{4,7},{9,8},{10,9},{11,1... | collective-permute-start | bytes 98312 | tf_op jit(solution)/shard_map/ppermute | solution.py:270
  38.3 1.0 %copy-start.2 = (f32[16,32,128]{2,1,0:T(8,128)S(1)}, f32[16,32,128]{2,1,0:T(8,128)}, u32[]{:S(2)}) copy-start(f32[16,32,128]{2,1,0:T(8,128)} %background.1) | copy-start | bytes 786436
  39.3 0.7 copy-start.5
  40.7 1.6 %copy-start.6 = (bf16[1024,1024]{1,0:T(8,128)(2,1)S(1)}, bf16[1024,1024]{1,0:T(8,128)(2,1)}, u32[]{:S(2)}) copy-start(bf16[1024,1024]{1,0:T(8,128)(2,1)} %mid_weight.1) | copy-start | bytes 6291460
  42.3 1.3 %copy-start.7 = (bf16[288,16,128]{2,1,0:T(8,128)(2,1)S(1)}, bf16[288,16,128]{2,1,0:T(8,128)(2,1)}, u32[]{:S(2)}) copy-start(bf16[288,16,128]{2,1,0:T(8,128)(2,1)} %all-gather.3.cloned.1.call-done.slabs) | copy-start | bytes 3538948
  43.5 1.0 %copy-start.8 = (bf16[1024,256]{1,0:T(8,128)(2,1)S(1)}, bf16[1024,256]{1,0:T(8,128)(2,1)}, u32[]{:S(2)}) copy-start(bf16[1024,256]{1,0:T(8,128)(2,1)} %out_weight.1) | copy-start | bytes 1572868
  44.6 0.8 %copy-start.9 = (bf16[32,1024]{1,0:T(8,128)(2,1)S(1)}, bf16[32,1024]{1,0:T(8,128)(2,1)}, u32[]{:S(2)}) copy-start(bf16[32,1024]{1,0:T(8,128)(2,1)} %in_weight.1) | copy-start | bytes 196612
  45.4 0.7 copy-start.10
  46.1 0.7 copy-start.11
  46.8 0.7 copy-start.12
  47.5 0.7 copy-start.13
  48.1 20.6 %copy-start.1 = (f32[16,32,128]{2,1,0:T(8,128)S(1)}, f32[16,32,128]{2,1,0:T(8,128)}, u32[]{:S(2)}) copy-start(f32[16,32,128]{2,1,0:T(8,128)} %control.1) | copy-start | bytes 786436
  54.8 4.4 %collective-permute-start.4 = (bf16[4,16,128]{2,1,0:T(8,128)(2,1)S(1)}, bf16[4,16,128]{2,1,0:T(8,128)(2,1)S(1)}, u32[]{:S(2)}, u32[]{:S(2)}) collective-permute-start(bf16[4,16,128]{2,1,0:T(8,128)(2,1)S(1)} %get-tuple-element.22), channel_id=1, source_target_pairs={{0,1},{1,2},{2,3},{3,0},{4,5},{5,6},{6,7},{7,4},{8,9},{9,10},{10,1... | collective-permute-start | bytes 49160 | tf_op jit(solution)/shard_map/ppermute | solution.py:270
  54.8 4.4 %collective-permute-start.5 = (bf16[4,16,128]{2,1,0:T(8,128)(2,1)S(1)}, bf16[4,16,128]{2,1,0:T(8,128)(2,1)S(1)}, u32[]{:S(2)}, u32[]{:S(2)}) collective-permute-start(bf16[4,16,128]{2,1,0:T(8,128)(2,1)S(1)} %get-tuple-element.24), channel_id=1, source_target_pairs={{1,0},{2,1},{3,2},{0,3},{5,4},{6,5},{7,6},{4,7},{9,8},{10,9},{11,1... | collective-permute-start | bytes 49160 | tf_op jit(solution)/shard_map/ppermute | solution.py:270
  59.9 7.7 %collective-permute-start.7 = (f32[16,32,128]{2,1,0:T(8,128)S(1)}, f32[16,32,128]{2,1,0:T(8,128)S(1)}, u32[]{:S(2)}, u32[]{:S(2)}) collective-permute-start(f32[16,32,128]{2,1,0:T(8,128)S(1)} %lon_back.1.own), channel_id=1, source_target_pairs={{4,0},{8,4},{12,8},{16,12},{20,16},{24,20},{28,24},{5,1},{9,5},{13... | collective-permute-start | bytes 786440 | tf_op jit(solution)/shard_map/ppermute | solution.py:270
  63.1 5.6 %collective-permute-start.6 = (f32[16,32,128]{2,1,0:T(8,128)S(1)}, f32[16,32,128]{2,1,0:T(8,128)S(1)}, u32[]{:S(2)}, u32[]{:S(2)}) collective-permute-start(f32[16,32,128]{2,1,0:T(8,128)S(1)} %lon_back.1.own), channel_id=1, source_target_pairs={{0,4},{4,8},{8,12},{12,16},{16,20},{20,24},{24,28},{1,5},{5,9},{9,... | collective-permute-start | bytes 786440 | tf_op jit(solution)/shard_map/ppermute | solution.py:270
Sparse Core Ops, SparseCore 0:
  9.9 27.0 all-gather.2

commit v2 on v1

v2 whole, which is shorter than its diff:
```python
import functools

import jax
import jax.numpy as jnp
import numpy as np
from jax import lax
from jax.experimental import pallas as pl
from jax.experimental.pallas import tpu as pltpu
from jax.sharding import PartitionSpec as P

REACH = 16
BLOCK_COLS = 8
LANES = 128
LAT_SIGMA = 8.0
VMEM_BYTES = 40 * 1024 * 1024

VMEM = pl.BlockSpec(memory_space=pltpu.VMEM)
SMEM = pl.BlockSpec(memory_space=pltpu.SMEM)
HBM = pl.BlockSpec(memory_space=pltpu.HBM)
ANY = pl.BlockSpec(memory_space=pl.ANY)


def lat_taps():
    offsets = np.arange(-REACH, REACH + 1, dtype=np.float64)
    raw = np.exp(-offsets * offsets / (2.0 * LAT_SIGMA * LAT_SIGMA))
    return [float(v) for v in (raw / np.sqrt(np.sum(raw * raw))).astype(np.float32)]


def call(kernel, out_shape, in_specs, out_specs, flops, bytes_moved, scratch=(), name=None):
    return pl.pallas_call(
        kernel,
        out_shape=out_shape,
        in_specs=in_specs,
        out_specs=out_specs,
        scratch_shapes=list(scratch),
        compiler_params=pltpu.CompilerParams(vmem_limit_bytes=VMEM_BYTES),
        cost_estimate=pl.CostEstimate(flops=flops, bytes_accessed=bytes_moved, transcendentals=0),
        name=name,
    )


def pinned(*values):
    return [pltpu.with_memory_space_constraint(value, pltpu.HBM) for value in values]


def lat_conv_row(row, low, own, high):
    taps = lat_taps()
    height = own.shape[0]
    acc = None
    for j in range(-REACH, REACH + 1):
        source = row + j
        if source < 0:
            part = low[source + REACH].astype(jnp.float32)
        elif source < height:
            part = own[source]
        else:
            part = high[source - height].astype(jnp.float32)
        term = taps[j + REACH] * part
        acc = term if acc is None else acc + term
    return acc


def lon_conv(padded, taps, tile, width):
    acc = taps[tile, 0:1, :] * padded[tile, pl.ds(REACH, width), :]
    for j in range(1, REACH + 1):
        both = padded[tile, pl.ds(REACH + j, width), :] + padded[tile, pl.ds(REACH - j, width), :]
        acc = acc + taps[tile, j : j + 1, :] * both
    return acc


def first_kernel(
    radiance, block_owner, channel_count, control, slabs, held, halved, owners, counts, rows, tables, sems
):
    recv_most = radiance.shape[0]
    moves = [
        pltpu.make_async_copy(radiance, slabs.at[pl.ds(0, recv_most)], sems.at[0]),
        pltpu.make_async_copy(block_owner, owners, sems.at[1]),
        pltpu.make_async_copy(channel_count, counts, sems.at[2]),
        pltpu.make_async_copy(control, held, sems.at[3]),
    ]
    for move in moves:
        move.start()
    rows[...] = jnp.full(rows.shape, -1.0, jnp.float32)
    moves[1].wait()
    moves[2].wait()
    rows[0:1, 0 : owners.shape[1]] = owners[...].astype(jnp.float32)
    rows[1:2, 0 : counts.shape[1]] = counts[...].astype(jnp.float32)
    tables[...] = rows[...].astype(jnp.bfloat16)
    last = pltpu.make_async_copy(tables, slabs.at[recv_most], sems.at[4])
    last.start()
    moves[3].wait()
    halved[...] = held[...].astype(jnp.bfloat16)
    moves[0].wait()
    last.wait()


def prepare_kernel(lon_width, background, taps, turned, widths, field, sems):
    moves = [
        pltpu.make_async_copy(lon_width, widths, sems.at[0]),
        pltpu.make_async_copy(background, field, sems.at[1]),
    ]
    for move in moves:
        move.start()
    tiles = turned.shape[0]
    height, levels, width = background.shape
    per_tile = height // tiles
    lane_row = lax.broadcasted_iota(jnp.int32, (1, LANES), 1) // levels
    steps = lax.broadcasted_iota(jnp.int32, (taps.shape[1], LANES), 0)
    dist = steps.astype(jnp.float32)
    weight = jnp.where(steps == 0, 1.0, jnp.where(steps <= REACH, 2.0, 0.0))
    moves[0].wait()
    for tile in range(tiles):
        spread = jnp.zeros((1, LANES), jnp.int32)
        for sub in range(per_tile):
            spread = jnp.where(lane_row == sub, widths[tile * per_tile + sub], spread)
        spread = spread.astype(jnp.float32)
        raw = jnp.exp(-dist * dist / (2.0 * spread * spread))
        norm = jnp.sum(weight * raw * raw, axis=0, keepdims=True)
        taps[tile] = raw / jnp.sqrt(norm)
    moves[1].wait()
    for tile in range(tiles):
        rows = field[tile * per_tile : (tile + 1) * per_tile].reshape(per_tile * levels, width)
        turned[tile] = jnp.transpose(rows)


def routing(recv_most, slot_count, near, far, table):
    half = near.shape[0]
    here = lax.axis_index("lat")
    parity = here % 2
    rows = lax.broadcasted_iota(jnp.int32, (slot_count, LANES), 0)
    lanes = lax.broadcasted_iota(jnp.int32, (slot_count, LANES), 1)
    diagonal = rows == lanes
    zero = jnp.zeros((slot_count, LANES), jnp.int32)

    def line(ref, k, row):
        return ref[k].astype(jnp.float32)[row : row + 1].astype(jnp.int32)

    mine = line(near, here // 2, 0)
    owner = jnp.sum(jnp.where(diagonal, mine, 0), axis=1, keepdims=True)

    def rank(k, acc):
        for ref, device in ((near, 2 * k + parity), (far, 2 * k + 1 - parity)):
            before = (device < here) | ((device == here) & (lanes < rows))
            acc = acc + jnp.where((line(ref, k, 0) == owner) & before, 1, 0)
        return acc

    unroll = half <= 4
    arrival = jnp.sum(lax.fori_loop(0, half, rank, zero, unroll=unroll), axis=1, keepdims=True)

    def counted(k, acc):
        for ref, device in ((near, 2 * k + parity), (far, 2 * k + 1 - parity)):
            hit = (owner == device) & (lanes == arrival)
            acc = acc + jnp.where(hit, line(ref, k, 1), 0)
        return acc

    kept = jnp.sum(lax.fori_loop(0, half, counted, zero, unroll=unroll), axis=1, keepdims=True)
    live = owner >= 0
    target = jnp.where(live, (owner // 2) * (recv_most + 1) + arrival, 0)
    close = jnp.where(live & (owner % 2 != parity), 0, 1)
    table[...] = jnp.zeros_like(table)
    for row, column in enumerate((target, kept, close)):
        table[row : row + 1, :] = jnp.sum(jnp.where(diagonal, column, 0), axis=0, keepdims=True)


def lat_smooth_kernel(low, own, high, smoothed, edge_low, edge_high):
    tiles = smoothed.shape[0]
    height, levels, width = own.shape
    per_tile = height // tiles
    for tile in range(tiles):
        rows = [lat_conv_row(tile * per_tile + sub, low, own, high) for sub in range(per_tile)]
        turned = jnp.transpose(jnp.concatenate(rows, axis=0))
        smoothed[tile] = turned
        edge_low[tile] = turned[0:REACH]
        edge_high[tile] = turned[width - REACH : width]


def block_place(cells, slot, groups, per_tile, width):
    block = cells[slot]
    row = block // groups
    start = (row // per_tile) * width + (block % groups) * BLOCK_COLS
    return pl.multiple_of(start, BLOCK_COLS), row % per_tile


def dot(a, b):
    return jnp.dot(a, b, preferred_element_type=jnp.float32)


def dot_t(a, b):
    return lax.dot_general(a, b, (((1,), (1,)), ((), ())), preferred_element_type=jnp.float32)


def forward_kernel(
    block_cells,
    low,
    own,
    high,
    turned,
    taps,
    in_weight,
    in_bias,
    mid_weight,
    mid_bias,
    out_weight,
    out_bias,
    act_one,
    act_two,
    emitted,
    wide_in,
    weight_two,
    weight_out,
    cells,
    padded,
    profile,
    picked,
    bias_one,
    bias_two,
    bias_out,
    sems,
):
    tiles, width, _ = own.shape
    levels = in_weight.shape[0]
    per_tile = LANES // levels
    groups = width // BLOCK_COLS
    slot_count = block_cells.shape[0]

    cells_in = pltpu.make_async_copy(block_cells, cells, sems.at[0])
    first_in = [
        pltpu.make_async_copy(in_weight, wide_in.at[pl.ds(sub * levels, levels)], sems.at[1 + sub])
        for sub in range(per_tile)
    ] + [pltpu.make_async_copy(in_bias, bias_one, sems.at[1 + per_tile])]
    mid_in = [
        pltpu.make_async_copy(mid_weight, weight_two, sems.at[2 + per_tile]),
        pltpu.make_async_copy(mid_bias, bias_two, sems.at[3 + per_tile]),
    ]
    out_in = [
        pltpu.make_async_copy(out_weight, weight_out, sems.at[4 + per_tile]),
        pltpu.make_async_copy(out_bias, bias_out, sems.at[5 + per_tile]),
    ]
    for move in [cells_in] + first_in + mid_in + out_in:
        move.start()

    padded[:, 0:REACH, :] = low[...]
    padded[:, REACH : REACH + width, :] = own[...]
    padded[:, REACH + width :, :] = high[...]
    for tile in range(tiles):
        total = turned[tile] + lon_conv(padded, taps, tile, width)
        profile[tile * width : (tile + 1) * width, :] = total.astype(jnp.bfloat16).astype(jnp.float32)

    lane_row = lax.broadcasted_iota(jnp.int32, (BLOCK_COLS, LANES), 1) // levels
    cells_in.wait()
    for slot in range(slot_count):
        start, sub = block_place(cells, slot, groups, per_tile, width)
        block = profile[pl.ds(start, BLOCK_COLS), :]
        picked[slot * BLOCK_COLS : (slot + 1) * BLOCK_COLS, :] = jnp.where(lane_row == sub, block, 0.0)

    for move in first_in:
        move.wait()
    inputs = picked[...].astype(jnp.bfloat16)
    act_one[...] = jnp.tanh(dot(inputs, wide_in[...]) + bias_one[...]).astype(jnp.bfloat16)
    for move in mid_in:
        move.wait()
    act_two[...] = jnp.tanh(dot(act_one[...], weight_two[...]) + bias_two[...]).astype(jnp.bfloat16)
    for move in out_in:
        move.wait()
    emitted[...] = dot(act_two[...], weight_out[...]) + bias_out[...]


def backward_kernel(
    per_tile,
    block_cells,
    near,
    far,
    act_one,
    act_two,
    emitted,
    wide_in,
    weight_two,
    weight_out,
    landing,
    edge_low,
    edge_high,
    cells,
    near_tables,
    far_tables,
    table_rows,
    table,
    field,
    picked,
    misfit,
    observed,
    sems,
):
    tiles, width, _ = landing.shape
    half = near_tables.shape[0]
    per_owner = near.shape[0] // half
    slot_count = block_cells.shape[0]
    channels = weight_out.shape[1]
    groups = width // BLOCK_COLS
    levels = LANES // per_tile

    def tables_in(ref, rows, sem):
        return [
            pltpu.make_async_copy(ref.at[k * per_owner + per_owner - 1], rows.at[k], sem.at[k])
            for k in range(half)
        ]

    routes = tables_in(near, near_tables, sems.at[0]) + tables_in(far, far_tables, sems.at[1])
    cells_in = pltpu.make_async_copy(block_cells, cells, sems.at[2, 0])
    for move in routes + [cells_in]:
        move.start()
    field[...] = jnp.zeros_like(field)
    for move in routes:
        move.wait()
    routing(per_owner - 1, slot_count, near_tables, far_tables, table_rows)
    table_in = pltpu.make_async_copy(table_rows, table, sems.at[2, 1])
    table_in.start()
    table_in.wait()

    def fetch(slot, carry):
        for ref, close in ((near, 1), (far, 0)):

            @pl.when(table[2, slot] == close)
            def _():
                pltpu.make_async_copy(ref.at[table[0, slot]], observed.at[slot], sems.at[2, 2]).start()

        return carry

    lax.fori_loop(0, slot_count, fetch, 0, unroll=8)
    pltpu.make_async_copy(near.at[pl.ds(0, slot_count)], observed, sems.at[2, 2]).wait()

    channel = lax.broadcasted_iota(jnp.int32, (BLOCK_COLS, channels), 1)
    for slot in range(0, slot_count, 2):
        pair = []
        for at in (slot, slot + 1):
            slab = observed[at].astype(jnp.float32)
            seen = jnp.concatenate(
                [slab[h * BLOCK_COLS : (h + 1) * BLOCK_COLS] for h in range(channels // LANES)], axis=1
            )
            gap = emitted[at * BLOCK_COLS : (at + 1) * BLOCK_COLS, :] - seen
            pair.append(jnp.where(channel < table[1, at], gap, 0.0))
        misfit[slot * BLOCK_COLS : (slot + 2) * BLOCK_COLS, :] = jnp.concatenate(pair, axis=0).astype(
            jnp.bfloat16
        )

    two = act_two[...].astype(jnp.float32)
    grad_two = (dot_t(misfit[...], weight_out[...]) * (1.0 - two * two)).astype(jnp.bfloat16)
    one = act_one[...].astype(jnp.float32)
    grad_one = (dot_t(grad_two, weight_two[...]) * (1.0 - one * one)).astype(jnp.bfloat16)
    picked[...] = dot_t(grad_one, wide_in[...]).astype(jnp.bfloat16).astype(jnp.float32)

    lane_row = lax.broadcasted_iota(jnp.int32, (BLOCK_COLS, LANES), 1) // levels
    cells_in.wait()
    for slot in range(slot_count):
        start, sub = block_place(cells, slot, groups, per_tile, width)
        block = picked[slot * BLOCK_COLS : (slot + 1) * BLOCK_COLS, :]
        field[pl.ds(start, BLOCK_COLS), :] += jnp.where(lane_row == sub, block, 0.0)
    for tile in range(tiles):
        landing[tile] = field[tile * width : (tile + 1) * width, :]
        edge_low[tile] = field[tile * width : tile * width + REACH, :].astype(jnp.bfloat16)
        edge_high[tile] = field[(tile + 1) * width - REACH : (tile + 1) * width, :].astype(jnp.bfloat16)


def lon_back_kernel(low, own, high, taps, back, halved, padded):
    tiles, width, _ = own.shape
    height, levels, _ = back.shape
    per_tile = height // tiles
    padded[:, 0:REACH, :] = low[...].astype(jnp.float32)
    padded[:, REACH : REACH + width, :] = own[...]
    padded[:, REACH + width :, :] = high[...].astype(jnp.float32)
    for tile in range(tiles):
        rows = jnp.transpose(lon_conv(padded, taps, tile, width))
        rows = rows.reshape(per_tile, levels, width)
        back[tile * per_tile : (tile + 1) * per_tile] = rows
        halved[tile * per_tile : (tile + 1) * per_tile] = rows.astype(jnp.bfloat16)


def lat_back_kernel(low, own, high, control, gradient):
    for row in range(own.shape[0]):
        gradient[row] = control[row] + lat_conv_row(row, low, own, high)


def swap(forward_value, backward_value, axis, periodic):
    count = lax.axis_size(axis)
    forward = [(i, i + 1) for i in range(count - 1)]
    if periodic:
        forward.append((count - 1, 0))
    backward = [(target, source) for source, target in forward]
    return lax.ppermute(forward_value, axis, forward), lax.ppermute(backward_value, axis, backward)


def shards(
    control,
    background,
    lon_width,
    block_cells,
    block_owner,
    channel_count,
    radiance,
    in_weight,
    in_bias,
    mid_weight,
    mid_bias,
    out_weight,
    out_bias,
):
    height, levels, width = control.shape
    hidden = mid_weight.shape[0]
    channels, columns = radiance.shape
    slot_count = block_owner.shape[0]
    recv_most = channel_count.shape[0]
    per_tile = LANES // levels
    tiles = height // per_tile
    slab_rows = BLOCK_COLS * channels // LANES
    f32, bf16, i32 = jnp.float32, jnp.bfloat16, jnp.int32
    shape = jax.ShapeDtypeStruct
    field = height * levels * width
    conv_flops = 2 * 33 * field

    halves = channels // LANES
    radiance = radiance.T.reshape(recv_most, BLOCK_COLS, halves, LANES)
    radiance = jnp.swapaxes(radiance, 1, 2).reshape(recv_most, slab_rows, LANES)
    slabs, held, halved = call(
        first_kernel,
        (
            shape((recv_most + 1, slab_rows, LANES), bf16),
            shape(control.shape, f32),
            shape(control.shape, bf16),
        ),
        [HBM] * 4,
        (HBM, VMEM, VMEM),
        0,
        16 * field,
        scratch=(
            pltpu.VMEM((1, slot_count), i32),
            pltpu.VMEM((1, recv_most), i32),
            pltpu.VMEM((slab_rows, LANES), f32),
            pltpu.VMEM((slab_rows, LANES), bf16),
            pltpu.SemaphoreType.DMA((5,)),
        ),
        name="slabs_halves",
    )(*pinned(radiance, block_owner.reshape(1, slot_count), channel_count.reshape(1, recv_most), control))

    lat_count = lax.axis_size("lat")
    parities = [list(range(start, lat_count, 2)) for start in range(2)]
    near = lax.all_gather(slabs, "lat", axis=0, tiled=True, axis_index_groups=parities)
    low, high = swap(halved, halved, "lat", False)

    taps, turned = call(
        prepare_kernel,
        (shape((tiles, 24, LANES), f32), shape((tiles, width, LANES), f32)),
        [HBM, HBM],
        (VMEM, VMEM),
        0,
        8 * field,
        scratch=(
            pltpu.SMEM((height,), i32),
            pltpu.VMEM((height, levels, width), f32),
            pltpu.SemaphoreType.DMA((2,)),
        ),
        name="taps_background",
    )(*pinned(lon_width, background))

    smoothed, edge_low, edge_high = call(
        lat_smooth_kernel,
        (shape((tiles, width, LANES), f32),) + (shape((tiles, REACH, LANES), f32),) * 2,
        [VMEM] * 3,
        (VMEM,) * 3,
        conv_flops,
        16 * field,
        name="lat_smooth",
    )(low, held, high)
    low, high = swap(edge_high, edge_low, "lon", True)
    near, low, high = lax.optimization_barrier((near, low, high))
    far = lax.ppermute(near, "lat", [(i, i ^ 1) for i in range(lat_count)])

    x_rows = slot_count * BLOCK_COLS
    net_flops = 2 * x_rows * hidden * (LANES + hidden + channels)
    cells = block_cells.reshape(slot_count)
    states = call(
        forward_kernel,
        (
            shape((x_rows, hidden), bf16),
            shape((x_rows, hidden), bf16),
            shape((x_rows, channels), f32),
            shape((LANES, hidden), bf16),
            shape((hidden, hidden), bf16),
            shape((hidden, channels), bf16),
        ),
        [HBM] + [VMEM] * 5 + [HBM] * 6,
        (VMEM,) * 6,
        net_flops,
        6 * 1024 * 1024,
        scratch=(
            pltpu.SMEM((slot_count,), i32),
            pltpu.VMEM((tiles, width + 2 * REACH, LANES), f32),
            pltpu.VMEM((tiles * width, LANES), f32),
            pltpu.VMEM((x_rows, LANES), f32),
            pltpu.VMEM((1, hidden), f32),
            pltpu.VMEM((1, hidden), f32),
            pltpu.VMEM((1, channels), f32),
            pltpu.SemaphoreType.DMA((6 + per_tile,)),
        ),
        name="net_forward",
    )(
        *pinned(cells),
        low,
        smoothed,
        high,
        turned,
        taps,
        *pinned(
            in_weight,
            in_bias.reshape(1, hidden),
            mid_weight,
            mid_bias.reshape(1, hidden),
            out_weight,
            out_bias.reshape(1, channels),
        ),
    )

    landing, edge_low, edge_high = call(
        functools.partial(backward_kernel, per_tile),
        (shape((tiles, width, LANES), f32),) + (shape((tiles, REACH, LANES), bf16),) * 2,
        [HBM, HBM, ANY] + [VMEM] * 6,
        (VMEM,) * 3,
        net_flops,
        6 * 1024 * 1024,
        scratch=(
            pltpu.SMEM((slot_count,), i32),
            pltpu.VMEM((lat_count // 2, slab_rows, LANES), bf16),
            pltpu.VMEM((lat_count // 2, slab_rows, LANES), bf16),
            pltpu.VMEM((8, LANES), i32),
            pltpu.SMEM((8, LANES), i32),
            pltpu.VMEM((tiles * width, LANES), f32),
            pltpu.VMEM((x_rows, LANES), f32),
            pltpu.VMEM((x_rows, channels), bf16),
            pltpu.VMEM((slot_count, slab_rows, LANES), bf16),
            pltpu.SemaphoreType.DMA((3, max(4, lat_count // 2))),
        ),
        name="net_backward",
    )(*pinned(cells, near), far, *states)
    low, high = swap(edge_high, edge_low, "lon", True)

    back, halved = call(
        lon_back_kernel,
        (shape((height, levels, width), f32), shape((height, levels, width), bf16)),
        [VMEM] * 4,
        (VMEM, VMEM),
        conv_flops,
        8 * field,
        scratch=(pltpu.VMEM((tiles, width + 2 * REACH, LANES), f32),),
        name="lon_back",
    )(low, landing, high, taps)
    low, high = swap(halved, halved, "lat", False)

    return call(
        lat_back_kernel,
        shape((height, levels, width), f32),
        [VMEM] * 4,
        VMEM,
        conv_flops,
        20 * field,
        name="lat_back",
    )(low, back, high, held)


def solution(mesh):
    return jax.shard_map(
        shards,
        mesh=mesh,
        in_specs=(
            P("lat", None, "lon"),
            P("lat", None, "lon"),
            P("lat"),
            P("lat", "lon"),
            P("lat", "lon"),
            P("lat", "lon"),
            P("lat", "lon"),
            P(),
            P(),
            P(),
            P(),
            P(),
            P(),
        ),
        out_specs=P("lat", None, "lon"),
        check_vma=False,
    )
```

time: 78.3 us -> 57.7 us (0.74)
  between operations: 13.5 us -> 0.13 us
  local copies, waits for them, and re-layouts: 12.4 us -> 0.01 us
  Pallas kernels: 11.1 us -> 16 us
  waiting for transfers between devices: 8.07 us -> 9.94 us
  blocking collectives: 13.1 us -> 11.3 us
  starting transfers between devices: 18.7 us -> 19.5 us
    unnamed x29 -> x2, local copies, waits for them, and re-layouts: 12.4 us -> 0.01 us
    pallas_call x4, Pallas kernels: 8.44 us -> 12.8 us  [the longest x1 6.87 us: shards(): call(functools.partial(backward_kernel, per_tile), (shape((tiles, width,...]
    ppermute x4, waiting for transfers between devices: 4.44 us -> 8.7 us  [swap(): lax.ppermute(backward_value, axis, backward)]
    ppermute x4, waiting for transfers between devices: 3.6 us -> 1.24 us  [swap(): lax.ppermute(forward_value, axis, forward)]
    all_gather x1, blocking collectives: 13.1 us -> 11.3 us  [shards(): lax.all_gather(slabs, 'lat', axis=0, tiled=True, axis_index_groups=parities)]
    ppermute x4, starting transfers between devices: 10.6 us -> 9.18 us  [swap(): lax.ppermute(backward_value, axis, backward)]
    ppermute x4, starting transfers between devices: 8.18 us -> 9.39 us  [swap(): lax.ppermute(forward_value, axis, forward)]
    ppermute x0 -> x1, starting transfers between devices: none -> 0.97 us  [shards(): far = lax.ppermute(near, 'lat', [(i, i ^ 1) for i in range(lat_count)])]
  transfers between devices with their start and end apart: 9 -> 9, of which waited for: 5 -> 3; matrix products, arithmetic and copies ran while one was open for 0% -> 0% of each run, Pallas kernels for 2% -> 9%
where the time goes in v2:
time: 57.7 us; the launch traced here: 57 us
  starting transfers between devices  19.5 us (34%)
  Pallas kernels  16 us (28%)
  blocking collectives  11.3 us (20%)
  waiting for transfers between devices  9.94 us (17%)
    all_gather x1, blocking collectives, shards(): lax.all_gather(slabs, 'lat', axis=0, tiled=True, axis_index_groups=parities)  11.3 us
    ppermute x4, starting transfers between devices, swap(): lax.ppermute(forward_value, axis, forward)  9.39 us
    ppermute x4, starting transfers between devices, swap(): lax.ppermute(backward_value, axis, backward)  9.18 us
    ppermute x4, waiting for transfers between devices, swap(): lax.ppermute(backward_value, axis, backward)  8.7 us
    pallas_call x1, Pallas kernels, shards(): call(functools.partial(backward_kernel, per_tile), (shape((tiles, width,...  6.87 us
    pallas_call x1, Pallas kernels, shards(): call(forward_kernel, (shape((x_rows, hidden), bf16), shape((x_rows, hidde...  4.15 us
    pallas_call x1, Pallas kernels, shards(): call(lat_back_kernel, shape((height, levels, width), f32), [VMEM] * 4, VM...  1.43 us
    ppermute x4, waiting for transfers between devices, swap(): lax.ppermute(forward_value, axis, forward)  1.24 us
  transfers between devices with their start and end apart: 9, of which 3 were waited for; matrix products, arithmetic and copies ran while one was open for 0% of the time, Pallas kernels for 9%

profile of v2, /device:TPU:1, one launch (start us, length us, event | category | flops | bytes accessed | tf_op | source)
XLA Modules:
  0.0 57.0 jit_solution(14654847791202238280)
XLA Ops:
  0.0 1.1 %slabs_halves.1 = (bf16[37,16,128]{2,1,0:T(8,128)(2,1)S(1)}, f32[16,32,128]{2,1,0:T(8,128)S(1)}, bf16[16,32,128]{2,1,0:T(8,128)(2,1)S(1)}) custom-call(bf16[36,16,128]{2,1,0:T(8,128)(2,1)} %bitcast.13, s32[1,64]{1,0:T(1,128)} %bitcast.14, s32[1,36]{1,0:T(1,128)} %bitcast.15, f32[16,32,128]{2,1,0:T(8,128)} %control.1), custom_call_target="tpu_custom_call" | custom-call | bytes 1048576 | tf_op jit(solution)/shard_map/slabs_halves/pallas_call | solution.py:422
  1.1 4.5 %collective-permute-start = (bf16[16,32,128]{2,1,0:T(8,128)(2,1)S(1)}, bf16[16,32,128]{2,1,0:T(8,128)(2,1)S(1)}, u32[]{:S(2)}, u32[]{:S(2)}) collective-permute-start(bf16[16,32,128]{2,1,0:T(8,128)(2,1)S(1)} %get-tuple-element.28), channel_id=1, source_target_pairs={{0,4},{4,8},{8,12},{12,16},{16,20},{20,24},{24,28},{1,5},{5,9},{9,... | collective-permute-start | bytes 393224 | tf_op jit(solution)/shard_map/ppermute | solution.py:388
  5.6 1.9 %collective-permute-start.1 = (bf16[16,32,128]{2,1,0:T(8,128)(2,1)S(1)}, bf16[16,32,128]{2,1,0:T(8,128)(2,1)S(1)}, u32[]{:S(2)}, u32[]{:S(2)}) collective-permute-start(bf16[16,32,128]{2,1,0:T(8,128)(2,1)S(1)} %get-tuple-element.28), channel_id=1, source_target_pairs={{4,0},{8,4},{12,8},{16,12},{20,16},{24,20},{28,24},{5,1},{9,5},{13... | collective-permute-start | bytes 393224 | tf_op jit(solution)/shard_map/ppermute | solution.py:388
  7.6 0.0 collective-permute-done.low
  7.6 4.3 %collective-permute-done.1.high = bf16[16,32,128]{2,1,0:T(8,128)(2,1)S(1)} collective-permute-done((bf16[16,32,128]{2,1,0:T(8,128)(2,1)S(1)}, bf16[16,32,128]{2,1,0:T(8,128)(2,1)S(1)}, u32[]{:S(2)}, u32[]{:S(2)}) %collective-permute-start.1) | collective-permute-done | bytes 131104 | tf_op jit(solution)/shard_map/ppermute | solution.py:388
  11.9 0.7 %lat_smooth.1 = (f32[4,128,128]{2,1,0:T(8,128)S(1)}, f32[4,16,128]{2,1,0:T(8,128)S(1)}, f32[4,16,128]{2,1,0:T(8,128)S(1)}) custom-call(bf16[16,32,128]{2,1,0:T(8,128)(2,1)S(1)} %collective-permute-done.low, f32[16,32,128]{2,1,0:T(8,128)S(1)} %get-tuple-element.29.own.control, bf16[16,32,128]{2,1,0:T(8,128)(2,1)S(1)} %collective-permute-done.1.high), custom_call_target="tpu_custom_call" | custom-call | flops 4325376 | bytes 1048576 | tf_op jit(solution)/shard_map/lat_smooth/pallas_call | solution.py:463
  12.6 1.3 %collective-permute-start.2 = (f32[4,16,128]{2,1,0:T(8,128)S(1)}, f32[4,16,128]{2,1,0:T(8,128)S(1)}, u32[]{:S(2)}, u32[]{:S(2)}) collective-permute-start(f32[4,16,128]{2,1,0:T(8,128)S(1)} %get-tuple-element.30), channel_id=1, source_target_pairs={{0,1},{1,2},{2,3},{3,0},{4,5},{5,6},{6,7},{7,4},{8,9},{9,10},{10,1... | collective-permute-start | bytes 98312 | tf_op jit(solution)/shard_map/ppermute | solution.py:388
  14.0 2.1 %collective-permute-start.3 = (f32[4,16,128]{2,1,0:T(8,128)S(1)}, f32[4,16,128]{2,1,0:T(8,128)S(1)}, u32[]{:S(2)}, u32[]{:S(2)}) collective-permute-start(f32[4,16,128]{2,1,0:T(8,128)S(1)} %get-tuple-element.31), channel_id=1, source_target_pairs={{1,0},{2,1},{3,2},{0,3},{5,4},{6,5},{7,6},{4,7},{9,8},{10,9},{11,1... | collective-permute-start | bytes 98312 | tf_op jit(solution)/shard_map/ppermute | solution.py:388
  16.1 11.3 %all_gather.3.near = bf16[148,16,128]{2,1,0:T(8,128)(2,1)S(1)} all-gather(bf16[37,16,128]{2,1,0:T(8,128)(2,1)S(1)} %get-tuple-element.27), channel_id=1, replica_groups={{0,8,16,24},{4,12,20,28},{1,9,17,25},{5,13,21,29},{2,10,18,26},{6,14,22..., dimensions={0}, use_global_device_ids=true | all-gather | bytes 757760 | tf_op jit(solution)/shard_map/all_gather | solution.py:445
  27.4 0.0 collective-permute-done.2.low
  27.4 0.0 collective-permute-done.3.high
  27.4 1.0 %collective-permute-start.4 = (bf16[148,16,128]{2,1,0:T(8,128)(2,1)S(1)}, bf16[148,16,128]{2,1,0:T(8,128)(2,1)S(1)}, u32[]{:S(2)}, u32[]{:S(2)}) collective-permute-start(bf16[148,16,128]{2,1,0:T(8,128)(2,1)S(1)} %all_gather.3.near), channel_id=1, source_target_pairs={{0,4},{4,0},{8,12},{12,8},{16,20},{20,16},{24,28},{28,24},{1,5},{5... | collective-permute-start | bytes 1818632 | tf_op jit(solution)/shard_map/ppermute | solution.py:474
  28.4 1.1 %taps_background.1 = (f32[4,24,128]{2,1,0:T(8,128)S(1)}, f32[4,128,128]{2,1,0:T(8,128)S(1)}) custom-call(s32[16]{0:T(128)} %lon_width.1, f32[16,32,128]{2,1,0:T(8,128)} %background.1), custom_call_target="tpu_custom_call" | custom-call | bytes 524288 | tf_op jit(solution)/shard_map/taps_background/pallas_call | solution.py:448
  29.5 4.1 %net_forward.1 = (bf16[512,1024]{1,0:T(8,128)(2,1)S(1)}, bf16[512,1024]{1,0:T(8,128)(2,1)S(1)}, f32[512,256]{1,0:T(8,128)S(1)}, bf16[128,1024]{1,0:T(8,128)(2,1)...) custom-call(s32[64]{0:T(128)} %bitcast.16, f32[4,16,128]{2,1,0:T(8,128)S(1)} %collective-permute-done.2.low, ...), custom_call_target="tpu_custom_call" | custom-call | flops 1476395008 | bytes 6291456 | tf_op jit(solution)/shard_map/net_forward/pallas_call | solution.py:479
  33.7 0.0 collective-permute-done.4.far
  33.7 6.9 %net_backward.1 = (f32[4,128,128]{2,1,0:T(8,128)S(1)}, bf16[4,16,128]{2,1,0:T(8,128)(2,1)S(1)}, bf16[4,16,128]{2,1,0:T(8,128)(2,1)S(1)}) custom-call(s32[64]{0:T(128)} %bitcast.17, bf16[148,16,128]{2,1,0:T(8,128)(2,1)} %copy-done, bf16[148,16,128]{2,1,0:T(8,128)(2,1)S(1)} %collective-permute-done.4.far, bf16[512,1024]{1,0:T(8,128)(2,1)S(1)} %get-tuple-element.38.act_one, ...), custom_call_target="tpu_custom_call" | custom-call | flops 1476395008 | bytes 6291456 | tf_op jit(solution)/shard_map/net_backward/pallas_call | solution.py:521
  40.6 0.1 collective-permute-start.5
  40.6 3.3 %collective-permute-start.6 = (bf16[4,16,128]{2,1,0:T(8,128)(2,1)S(1)}, bf16[4,16,128]{2,1,0:T(8,128)(2,1)S(1)}, u32[]{:S(2)}, u32[]{:S(2)}) collective-permute-start(bf16[4,16,128]{2,1,0:T(8,128)(2,1)S(1)} %get-tuple-element.46), channel_id=1, source_target_pairs={{1,0},{2,1},{3,2},{0,3},{5,4},{6,5},{7,6},{4,7},{9,8},{10,9},{11,1... | collective-permute-start | bytes 49160 | tf_op jit(solution)/shard_map/ppermute | solution.py:388
  43.9 1.2 %collective-permute-done.5.low = bf16[4,16,128]{2,1,0:T(8,128)(2,1)S(1)} collective-permute-done((bf16[4,16,128]{2,1,0:T(8,128)(2,1)S(1)}, bf16[4,16,128]{2,1,0:T(8,128)(2,1)S(1)}, u32[]{:S(2)}, u32[]{:S(2)}) %collective-permute-start.5) | collective-permute-done | bytes 16416 | tf_op jit(solution)/shard_map/ppermute | solution.py:388
  45.1 0.6 %lon_back.1 = (f32[16,32,128]{2,1,0:T(8,128)S(1)}, bf16[16,32,128]{2,1,0:T(8,128)(2,1)S(1)}) custom-call(bf16[4,16,128]{2,1,0:T(8,128)(2,1)S(1)} %collective-permute-done.5.low, f32[4,128,128]{2,1,0:T(8,128)S(1)} %get-tuple-element.45.own, bf16[4,16,128]{2,1,0:T(8,128)(2,1)S(1)} %collective-permute-done.6.high, f32[4,24,128]{2,1,0:T(8,128)S(1)} %get-tuple-element.37.taps), custom_call_target="tpu_custom_call" | custom-call | flops 4325376 | bytes 524288 | tf_op jit(solution)/shard_map/lon_back/pallas_call | solution.py:544
  45.8 3.5 %collective-permute-start.7 = (bf16[16,32,128]{2,1,0:T(8,128)(2,1)S(1)}, bf16[16,32,128]{2,1,0:T(8,128)(2,1)S(1)}, u32[]{:S(2)}, u32[]{:S(2)}) collective-permute-start(bf16[16,32,128]{2,1,0:T(8,128)(2,1)S(1)} %get-tuple-element.47), channel_id=1, source_target_pairs={{0,4},{4,8},{8,12},{12,16},{16,20},{20,24},{24,28},{1,5},{5,9},{9,... | collective-permute-start | bytes 393224 | tf_op jit(solution)/shard_map/ppermute | solution.py:388
  49.3 1.9 %collective-permute-start.8 = (bf16[16,32,128]{2,1,0:T(8,128)(2,1)S(1)}, bf16[16,32,128]{2,1,0:T(8,128)(2,1)S(1)}, u32[]{:S(2)}, u32[]{:S(2)}) collective-permute-start(bf16[16,32,128]{2,1,0:T(8,128)(2,1)S(1)} %get-tuple-element.47), channel_id=1, source_target_pairs={{4,0},{8,4},{12,8},{16,12},{20,16},{24,20},{28,24},{5,1},{9,5},{13... | collective-permute-start | bytes 393224 | tf_op jit(solution)/shard_map/ppermute | solution.py:388
  51.2 4.3 %collective-permute-done.8.high = bf16[16,32,128]{2,1,0:T(8,128)(2,1)S(1)} collective-permute-done((bf16[16,32,128]{2,1,0:T(8,128)(2,1)S(1)}, bf16[16,32,128]{2,1,0:T(8,128)(2,1)S(1)}, u32[]{:S(2)}, u32[]{:S(2)}) %collective-permute-start.8) | collective-permute-done | bytes 131104 | tf_op jit(solution)/shard_map/ppermute | solution.py:388
  55.5 1.4 %lat_back.1 = f32[16,32,128]{2,1,0:T(8,128)} custom-call(bf16[16,32,128]{2,1,0:T(8,128)(2,1)S(1)} %collective-permute-done.7.low, f32[16,32,128]{2,1,0:T(8,128)S(1)} %get-tuple-element.48.own, bf16[16,32,128]{2,1,0:T(8,128)(2,1)S(1)} %collective-permute-done.8.high, f32[16,32,128]{2,1,0:T(8,128)S(1)} %get-tuple-element.29.own.control), custom_call_target="tpu_custom_call" | custom-call | flops 4325376 | bytes 1310720 | tf_op jit(solution)/shard_map/lat_back/pallas_call | solution.py:556
  (4 shorter events, 0.0 us)
Async XLA Ops:
  1.1 6.4 %collective-permute-start = (bf16[16,32,128]{2,1,0:T(8,128)(2,1)S(1)}, bf16[16,32,128]{2,1,0:T(8,128)(2,1)S(1)}, u32[]{:S(2)}, u32[]{:S(2)}) collective-permute-start(bf16[16,32,128]{2,1,0:T(8,128)(2,1)S(1)} %get-tuple-element.28), channel_id=1, source_target_pairs={{0,4},{4,8},{8,12},{12,16},{16,20},{20,24},{24,28},{1,5},{5,9},{9,... | collective-permute-start | bytes 393224 | tf_op jit(solution)/shard_map/ppermute | solution.py:388
  5.6 6.3 %collective-permute-start.1 = (bf16[16,32,128]{2,1,0:T(8,128)(2,1)S(1)}, bf16[16,32,128]{2,1,0:T(8,128)(2,1)S(1)}, u32[]{:S(2)}, u32[]{:S(2)}) collective-permute-start(bf16[16,32,128]{2,1,0:T(8,128)(2,1)S(1)} %get-tuple-element.28), channel_id=1, source_target_pairs={{4,0},{8,4},{12,8},{16,12},{20,16},{24,20},{28,24},{5,1},{9,5},{13... | collective-permute-start | bytes 393224 | tf_op jit(solution)/shard_map/ppermute | solution.py:388
  12.6 14.8 %collective-permute-start.2 = (f32[4,16,128]{2,1,0:T(8,128)S(1)}, f32[4,16,128]{2,1,0:T(8,128)S(1)}, u32[]{:S(2)}, u32[]{:S(2)}) collective-permute-start(f32[4,16,128]{2,1,0:T(8,128)S(1)} %get-tuple-element.30), channel_id=1, source_target_pairs={{0,1},{1,2},{2,3},{3,0},{4,5},{5,6},{6,7},{7,4},{8,9},{9,10},{10,1... | collective-permute-start | bytes 98312 | tf_op jit(solution)/shard_map/ppermute | solution.py:388
  14.0 13.4 %collective-permute-start.3 = (f32[4,16,128]{2,1,0:T(8,128)S(1)}, f32[4,16,128]{2,1,0:T(8,128)S(1)}, u32[]{:S(2)}, u32[]{:S(2)}) collective-permute-start(f32[4,16,128]{2,1,0:T(8,128)S(1)} %get-tuple-element.31), channel_id=1, source_target_pairs={{1,0},{2,1},{3,2},{0,3},{5,4},{6,5},{7,6},{4,7},{9,8},{10,9},{11,1... | collective-permute-start | bytes 98312 | tf_op jit(solution)/shard_map/ppermute | solution.py:388
  27.4 6.3 %copy-start = (bf16[148,16,128]{2,1,0:T(8,128)(2,1)}, bf16[148,16,128]{2,1,0:T(8,128)(2,1)S(1)}, u32[]{:S(2)}) copy-start(bf16[148,16,128]{2,1,0:T(8,128)(2,1)S(1)} %all_gather.3.near) | copy-start | bytes 1818628
  27.4 6.2 %collective-permute-start.4 = (bf16[148,16,128]{2,1,0:T(8,128)(2,1)S(1)}, bf16[148,16,128]{2,1,0:T(8,128)(2,1)S(1)}, u32[]{:S(2)}, u32[]{:S(2)}) collective-permute-start(bf16[148,16,128]{2,1,0:T(8,128)(2,1)S(1)} %all_gather.3.near), channel_id=1, source_target_pairs={{0,4},{4,0},{8,12},{12,8},{16,20},{20,16},{24,28},{28,24},{1,5},{5... | collective-permute-start | bytes 1818632 | tf_op jit(solution)/shard_map/ppermute | solution.py:474
  40.6 4.5 %collective-permute-start.5 = (bf16[4,16,128]{2,1,0:T(8,128)(2,1)S(1)}, bf16[4,16,128]{2,1,0:T(8,128)(2,1)S(1)}, u32[]{:S(2)}, u32[]{:S(2)}) collective-permute-start(bf16[4,16,128]{2,1,0:T(8,128)(2,1)S(1)} %get-tuple-element.44), channel_id=1, source_target_pairs={{0,1},{1,2},{2,3},{3,0},{4,5},{5,6},{6,7},{7,4},{8,9},{9,10},{10,1... | collective-permute-start | bytes 49160 | tf_op jit(solution)/shard_map/ppermute | solution.py:388
  40.6 4.5 %collective-permute-start.6 = (bf16[4,16,128]{2,1,0:T(8,128)(2,1)S(1)}, bf16[4,16,128]{2,1,0:T(8,128)(2,1)S(1)}, u32[]{:S(2)}, u32[]{:S(2)}) collective-permute-start(bf16[4,16,128]{2,1,0:T(8,128)(2,1)S(1)} %get-tuple-element.46), channel_id=1, source_target_pairs={{1,0},{2,1},{3,2},{0,3},{5,4},{6,5},{7,6},{4,7},{9,8},{10,9},{11,1... | collective-permute-start | bytes 49160 | tf_op jit(solution)/shard_map/ppermute | solution.py:388
  45.8 5.4 %collective-permute-start.7 = (bf16[16,32,128]{2,1,0:T(8,128)(2,1)S(1)}, bf16[16,32,128]{2,1,0:T(8,128)(2,1)S(1)}, u32[]{:S(2)}, u32[]{:S(2)}) collective-permute-start(bf16[16,32,128]{2,1,0:T(8,128)(2,1)S(1)} %get-tuple-element.47), channel_id=1, source_target_pairs={{0,4},{4,8},{8,12},{12,16},{16,20},{20,24},{24,28},{1,5},{5,9},{9,... | collective-permute-start | bytes 393224 | tf_op jit(solution)/shard_map/ppermute | solution.py:388
  49.3 6.3 %collective-permute-start.8 = (bf16[16,32,128]{2,1,0:T(8,128)(2,1)S(1)}, bf16[16,32,128]{2,1,0:T(8,128)(2,1)S(1)}, u32[]{:S(2)}, u32[]{:S(2)}) collective-permute-start(bf16[16,32,128]{2,1,0:T(8,128)(2,1)S(1)} %get-tuple-element.47), channel_id=1, source_target_pairs={{4,0},{8,4},{12,8},{16,12},{20,16},{24,20},{28,24},{5,1},{9,5},{13... | collective-permute-start | bytes 393224 | tf_op jit(solution)/shard_map/ppermute | solution.py:388

commit v3 on v2

--- a/solution.py
+++ b/solution.py
@@ -50,14 +50,22 @@
     for j in range(-REACH, REACH + 1):
         source = row + j
         if source < 0:
-            part = low[source + REACH].astype(jnp.float32)
+            part = low[source + REACH]
         elif source < height:
             part = own[source]
         else:
-            part = high[source - height].astype(jnp.float32)
+            part = high[source - height]
         term = taps[j + REACH] * part
         acc = term if acc is None else acc + term
     return acc
+
+
+def fill_padded(padded, far, own, close):
+    width = own.shape[1]
+    low, high = sides(far[...], close[...], "lon")
+    padded[:, 0:REACH, :] = low
+    padded[:, REACH : REACH + width, :] = own[...]
+    padded[:, REACH + width :, :] = high
 
 
 def lon_conv(padded, taps, tile, width):
@@ -123,55 +131,71 @@
         turned[tile] = jnp.transpose(rows)
 
 
-def routing(recv_most, slot_count, near, far, table):
-    half = near.shape[0]
+def routing(recv_most, slot_count, tables, table):
+    count = tables.shape[0]
+    half = count // 2
     here = lax.axis_index("lat")
-    parity = here % 2
     rows = lax.broadcasted_iota(jnp.int32, (slot_count, LANES), 0)
     lanes = lax.broadcasted_iota(jnp.int32, (slot_count, LANES), 1)
     diagonal = rows == lanes
     zero = jnp.zeros((slot_count, LANES), jnp.int32)
 
-    def line(ref, k, row):
-        return ref[k].astype(jnp.float32)[row : row + 1].astype(jnp.int32)
-
-    mine = line(near, here // 2, 0)
-    owner = jnp.sum(jnp.where(diagonal, mine, 0), axis=1, keepdims=True)
+    def device_of(k):
+        return here ^ jnp.where(k < half, 2 * k, 2 * (k - half) + 1)
+
+    def line(k, row):
+        return tables[k].astype(jnp.float32)[row : row + 1].astype(jnp.int32)
+
+    owner = jnp.sum(jnp.where(diagonal, line(0, 0), 0), axis=1, keepdims=True)
 
     def rank(k, acc):
-        for ref, device in ((near, 2 * k + parity), (far, 2 * k + 1 - parity)):
-            before = (device < here) | ((device == here) & (lanes < rows))
-            acc = acc + jnp.where((line(ref, k, 0) == owner) & before, 1, 0)
-        return acc
-
-    unroll = half <= 4
-    arrival = jnp.sum(lax.fori_loop(0, half, rank, zero, unroll=unroll), axis=1, keepdims=True)
+        device = device_of(k)
+        before = (device < here) | ((device == here) & (lanes < rows))
+        return acc + jnp.where((line(k, 0) == owner) & before, 1, 0)
+
+    unroll = count <= 8
+    arrival = jnp.sum(lax.fori_loop(0, count, rank, zero, unroll=unroll), axis=1, keepdims=True)
 
     def counted(k, acc):
-        for ref, device in ((near, 2 * k + parity), (far, 2 * k + 1 - parity)):
-            hit = (owner == device) & (lanes == arrival)
-            acc = acc + jnp.where(hit, line(ref, k, 1), 0)
-        return acc
-
-    kept = jnp.sum(lax.fori_loop(0, half, counted, zero, unroll=unroll), axis=1, keepdims=True)
-    live = owner >= 0
-    target = jnp.where(live, (owner // 2) * (recv_most + 1) + arrival, 0)
-    close = jnp.where(live & (owner % 2 != parity), 0, 1)
+        hit = (owner == device_of(k)) & (lanes == arrival)
+        return acc + jnp.where(hit, line(k, 1), 0)
+
+    kept = jnp.sum(lax.fori_loop(0, count, counted, zero, unroll=unroll), axis=1, keepdims=True)
+    apart = owner ^ here
+    place = (apart >> 1) + (apart & 1) * half
+    target = jnp.where(owner >= 0, place * (recv_most + 1) + arrival, 0)
     table[...] = jnp.zeros_like(table)
-    for row, column in enumerate((target, kept, close)):
+    for row, column in enumerate((target, kept)):
         table[row : row + 1, :] = jnp.sum(jnp.where(diagonal, column, 0), axis=0, keepdims=True)
 
 
-def lat_smooth_kernel(low, own, high, smoothed, edge_low, edge_high):
+def odd_index(axis):
+    return lax.axis_index(axis) % 2 == 1
+
+
+def sides(far, close, axis):
+    odd = odd_index(axis)
+    far, close = far.astype(jnp.float32), close.astype(jnp.float32)
+    return jnp.where(odd, close, far), jnp.where(odd, far, close)
+
+
+def split_sides(low, high, axis):
+    odd = odd_index(axis)
+    return jnp.where(odd, high, low), jnp.where(odd, low, high)
+
+
+def lat_smooth_kernel(far, close, own, smoothed, to_far, to_close, halos):
     tiles = smoothed.shape[0]
     height, levels, width = own.shape
     per_tile = height // tiles
+    halos[0], halos[1] = sides(far[...], close[...], "lat")
     for tile in range(tiles):
-        rows = [lat_conv_row(tile * per_tile + sub, low, own, high) for sub in range(per_tile)]
+        rows = [
+            lat_conv_row(tile * per_tile + sub, halos.at[0], own, halos.at[1]) for sub in range(per_tile)
+        ]
         turned = jnp.transpose(jnp.concatenate(rows, axis=0))
         smoothed[tile] = turned
-        edge_low[tile] = turned[0:REACH]
-        edge_high[tile] = turned[width - REACH : width]
+        to_far[tile], to_close[tile] = split_sides(turned[0:REACH], turned[width - REACH : width], "lon")
 
 
 def block_place(cells, slot, groups, per_tile, width):
@@ -191,9 +215,9 @@
 
 def forward_kernel(
     block_cells,
-    low,
+    far,
+    close,
     own,
-    high,
     turned,
     taps,
     in_weight,
@@ -239,9 +263,7 @@
     for move in [cells_in] + first_in + mid_in + out_in:
         move.start()
 
-    padded[:, 0:REACH, :] = low[...]
-    padded[:, REACH : REACH + width, :] = own[...]
-    padded[:, REACH + width :, :] = high[...]
+    fill_padded(padded, far, own, close)
     for tile in range(tiles):
         total = turned[tile] + lon_conv(padded, taps, tile, width)
         profile[tile * width : (tile + 1) * width, :] = total.astype(jnp.bfloat16).astype(jnp.float32)
@@ -267,83 +289,61 @@
 
 def backward_kernel(
     per_tile,
+    parts,
     block_cells,
-    near,
-    far,
-    act_one,
-    act_two,
-    emitted,
-    wide_in,
-    weight_two,
-    weight_out,
-    landing,
-    edge_low,
-    edge_high,
-    cells,
-    near_tables,
-    far_tables,
-    table_rows,
-    table,
-    field,
-    picked,
-    misfit,
-    observed,
-    sems,
+    *refs,
 ):
+    slabs, refs = refs[:parts], refs[parts:]
+    (act_one, act_two, emitted, wide_in, weight_two, weight_out) = refs[:6]
+    (landing, to_far, to_close) = refs[6:9]
+    (cells, tables, table_rows, table, held, observed, field, picked, sems) = refs[9:]
     tiles, width, _ = landing.shape
-    half = near_tables.shape[0]
-    per_owner = near.shape[0] // half
+    owners = tables.shape[0]
+    per_owner = held.shape[0] // owners
     slot_count = block_cells.shape[0]
     channels = weight_out.shape[1]
     groups = width // BLOCK_COLS
     levels = LANES // per_tile
 
-    def tables_in(ref, rows, sem):
-        return [
-            pltpu.make_async_copy(ref.at[k * per_owner + per_owner - 1], rows.at[k], sem.at[k])
-            for k in range(half)
-        ]
-
-    routes = tables_in(near, near_tables, sems.at[0]) + tables_in(far, far_tables, sems.at[1])
-    cells_in = pltpu.make_async_copy(block_cells, cells, sems.at[2, 0])
-    for move in routes + [cells_in]:
+    routes, bulk = [], []
+    for part, ref in enumerate(slabs):
+        sets = ref.shape[0] // per_owner
+        for k in range(sets):
+            entry = len(routes)
+            source = ref.at[k * per_owner + per_owner - 1]
+            routes.append(pltpu.make_async_copy(source, tables.at[entry], sems.at[entry]))
+        start = len(routes) - sets
+        bulk.append(
+            pltpu.make_async_copy(
+                ref, held.at[pl.ds(start * per_owner, ref.shape[0])], sems.at[owners + part]
+            )
+        )
+    cells_in = pltpu.make_async_copy(block_cells, cells, sems.at[owners + parts])
+    for move in routes + [cells_in] + bulk:
         move.start()
     field[...] = jnp.zeros_like(field)
     for move in routes:
         move.wait()
-    routing(per_owner - 1, slot_count, near_tables, far_tables, table_rows)
-    table_in = pltpu.make_async_copy(table_rows, table, sems.at[2, 1])
+    routing(per_owner - 1, slot_count, tables, table_rows)
+    table_in = pltpu.make_async_copy(table_rows, table, sems.at[owners + parts + 1])
     table_in.start()
-    table_in.wait()
-
-    def fetch(slot, carry):
-        for ref, close in ((near, 1), (far, 0)):
-
-            @pl.when(table[2, slot] == close)
-            def _():
-                pltpu.make_async_copy(ref.at[table[0, slot]], observed.at[slot], sems.at[2, 2]).start()
-
-        return carry
-
-    lax.fori_loop(0, slot_count, fetch, 0, unroll=8)
-    pltpu.make_async_copy(near.at[pl.ds(0, slot_count)], observed, sems.at[2, 2]).wait()
-
-    channel = lax.broadcasted_iota(jnp.int32, (BLOCK_COLS, channels), 1)
-    for slot in range(0, slot_count, 2):
-        pair = []
-        for at in (slot, slot + 1):
-            slab = observed[at].astype(jnp.float32)
-            seen = jnp.concatenate(
-                [slab[h * BLOCK_COLS : (h + 1) * BLOCK_COLS] for h in range(channels // LANES)], axis=1
+    for move in bulk + [table_in]:
+        move.wait()
+
+    channel = lax.broadcasted_iota(jnp.int32, (BLOCK_COLS, LANES), 1)
+    for slot in range(slot_count):
+        slab = held[table[0, slot]].astype(jnp.float32)
+        for h in range(channels // LANES):
+            part = slab[h * BLOCK_COLS : (h + 1) * BLOCK_COLS]
+            kept = channel + h * LANES < table[1, slot]
+            observed[slot * BLOCK_COLS : (slot + 1) * BLOCK_COLS, h * LANES : (h + 1) * LANES] = jnp.where(
+                kept, part, jnp.inf
             )
-            gap = emitted[at * BLOCK_COLS : (at + 1) * BLOCK_COLS, :] - seen
-            pair.append(jnp.where(channel < table[1, at], gap, 0.0))
-        misfit[slot * BLOCK_COLS : (slot + 2) * BLOCK_COLS, :] = jnp.concatenate(pair, axis=0).astype(
-            jnp.bfloat16
-        )
-
+
+    seen = observed[...]
+    misfit = jnp.where(seen < jnp.inf, emitted[...] - seen, 0.0).astype(jnp.bfloat16)
     two = act_two[...].astype(jnp.float32)
-    grad_two = (dot_t(misfit[...], weight_out[...]) * (1.0 - two * two)).astype(jnp.bfloat16)
+    grad_two = (dot_t(misfit, weight_out[...]) * (1.0 - two * two)).astype(jnp.bfloat16)
     one = act_one[...].astype(jnp.float32)
     grad_one = (dot_t(grad_two, weight_two[...]) * (1.0 - one * one)).astype(jnp.bfloat16)
     picked[...] = dot_t(grad_one, wide_in[...]).astype(jnp.bfloat16).astype(jnp.float32)
@@ -356,17 +356,17 @@
         field[pl.ds(start, BLOCK_COLS), :] += jnp.where(lane_row == sub, block, 0.0)
     for tile in range(tiles):
         landing[tile] = field[tile * width : (tile + 1) * width, :]
-        edge_low[tile] = field[tile * width : tile * width + REACH, :].astype(jnp.bfloat16)
-        edge_high[tile] = field[(tile + 1) * width - REACH : (tile + 1) * width, :].astype(jnp.bfloat16)
-
-
-def lon_back_kernel(low, own, high, taps, back, halved, padded):
+        low = field[tile * width : tile * width + REACH, :]
+        high = field[(tile + 1) * width - REACH : (tile + 1) * width, :]
+        low, high = split_sides(low, high, "lon")
+        to_far[tile], to_close[tile] = low.astype(jnp.bfloat16), high.astype(jnp.bfloat16)
+
+
+def lon_back_kernel(far, close, own, taps, back, halved, padded):
     tiles, width, _ = own.shape
     height, levels, _ = back.shape
     per_tile = height // tiles
-    padded[:, 0:REACH, :] = low[...].astype(jnp.float32)
-    padded[:, REACH : REACH + width, :] = own[...]
-    padded[:, REACH + width :, :] = high[...].astype(jnp.float32)
+    fill_padded(padded, far, own, close)
     for tile in range(tiles):
         rows = jnp.transpose(lon_conv(padded, taps, tile, width))
         rows = rows.reshape(per_tile, levels, width)
@@ -374,18 +374,20 @@
         halved[tile * per_tile : (tile + 1) * per_tile] = rows.astype(jnp.bfloat16)
 
 
-def lat_back_kernel(low, own, high, control, gradient):
+def lat_back_kernel(far, close, own, control, gradient, halos):
+    halos[0], halos[1] = sides(far[...], close[...], "lat")
     for row in range(own.shape[0]):
-        gradient[row] = control[row] + lat_conv_row(row, low, own, high)
-
-
-def swap(forward_value, backward_value, axis, periodic):
+        gradient[row] = control[row] + lat_conv_row(row, halos.at[0], own, halos.at[1])
+
+
+def exchange(to_far, to_close, axis, periodic):
     count = lax.axis_size(axis)
-    forward = [(i, i + 1) for i in range(count - 1)]
-    if periodic:
-        forward.append((count - 1, 0))
-    backward = [(target, source) for source, target in forward]
-    return lax.ppermute(forward_value, axis, forward), lax.ppermute(backward_value, axis, backward)
+    far = []
+    for odd in range(1, count, 2):
+        if odd + 1 < count or periodic:
+            far += [(odd, (odd + 1) % count), ((odd + 1) % count, odd)]
+    close = [(i, i ^ 1) for i in range(count)]
+    return lax.ppermute(to_far, axis, far), lax.ppermute(to_close, axis, close)
 
 
 def shards(
@@ -441,9 +443,13 @@
     )(*pinned(radiance, block_owner.reshape(1, slot_count), channel_count.reshape(1, recv_most), control))
 
     lat_count = lax.axis_size("lat")
-    parities = [list(range(start, lat_count, 2)) for start in range(2)]
-    near = lax.all_gather(slabs, "lat", axis=0, tiled=True, axis_index_groups=parities)
-    low, high = swap(halved, halved, "lat", False)
+    near = [slabs]
+    for bit in range(1, lat_count.bit_length() - 1):
+        held_sets = near[0] if len(near) == 1 else jnp.concatenate(near, axis=0)
+        near = [held_sets, lax.ppermute(held_sets, "lat", [(i, i ^ (1 << bit)) for i in range(lat_count)])]
+        if bit == 1:
+            far, close = exchange(halved, halved, "lat", False)
+            near[1], far, close = lax.optimization_barrier((near[1], far, close))
 
     taps, turned = call(
         prepare_kernel,
@@ -460,18 +466,20 @@
         name="taps_background",
     )(*pinned(lon_width, background))
 
-    smoothed, edge_low, edge_high = call(
+    halos = pltpu.VMEM((2, REACH, levels, width), f32)
+    smoothed, to_far, to_close = call(
         lat_smooth_kernel,
         (shape((tiles, width, LANES), f32),) + (shape((tiles, REACH, LANES), f32),) * 2,
         [VMEM] * 3,
         (VMEM,) * 3,
         conv_flops,
         16 * field,
+        scratch=(halos,),
         name="lat_smooth",
-    )(low, held, high)
-    low, high = swap(edge_high, edge_low, "lon", True)
-    near, low, high = lax.optimization_barrier((near, low, high))
-    far = lax.ppermute(near, "lat", [(i, i ^ 1) for i in range(lat_count)])
+    )(far, close, held)
+    far, close = exchange(to_far, to_close, "lon", True)
+    near, far, close = lax.optimization_barrier((near, far, close))
+    across = [lax.ppermute(part, "lat", [(i, i ^ 1) for i in range(lat_count)]) for part in near]
 
     x_rows = slot_count * BLOCK_COLS
     net_flops = 2 * x_rows * hidden * (LANES + hidden + channels)
@@ -503,9 +511,9 @@
         name="net_forward",
     )(
         *pinned(cells),
-        low,
+        far,
+        close,
         smoothed,
-        high,
         turned,
         taps,
         *pinned(
@@ -518,28 +526,28 @@
         ),
     )
 
-    landing, edge_low, edge_high = call(
-        functools.partial(backward_kernel, per_tile),
+    slabs = [*near, *across]
+    landing, to_far, to_close = call(
+        functools.partial(backward_kernel, per_tile, len(slabs)),
         (shape((tiles, width, LANES), f32),) + (shape((tiles, REACH, LANES), bf16),) * 2,
-        [HBM, HBM, ANY] + [VMEM] * 6,
+        [HBM] + [ANY] * len(slabs) + [VMEM] * 6,
         (VMEM,) * 3,
         net_flops,
         6 * 1024 * 1024,
         scratch=(
             pltpu.SMEM((slot_count,), i32),
-            pltpu.VMEM((lat_count // 2, slab_rows, LANES), bf16),
-            pltpu.VMEM((lat_count // 2, slab_rows, LANES), bf16),
+            pltpu.VMEM((lat_count, slab_rows, LANES), bf16),
             pltpu.VMEM((8, LANES), i32),
             pltpu.SMEM((8, LANES), i32),
+            pltpu.VMEM((lat_count * (recv_most + 1), slab_rows, LANES), bf16),
+            pltpu.VMEM((x_rows, channels), f32),
             pltpu.VMEM((tiles * width, LANES), f32),
             pltpu.VMEM((x_rows, LANES), f32),
-            pltpu.VMEM((x_rows, channels), bf16),
-            pltpu.VMEM((slot_count, slab_rows, LANES), bf16),
-            pltpu.SemaphoreType.DMA((3, max(4, lat_count // 2))),
+            pltpu.SemaphoreType.DMA((lat_count + len(slabs) + 2,)),
         ),
         name="net_backward",
-    )(*pinned(cells, near), far, *states)
-    low, high = swap(edge_high, edge_low, "lon", True)
+    )(*pinned(cells), *slabs, *states)
+    far, close = exchange(to_far, to_close, "lon", True)
 
     back, halved = call(
         lon_back_kernel,
@@ -550,8 +558,8 @@
         8 * field,
         scratch=(pltpu.VMEM((tiles, width + 2 * REACH, LANES), f32),),
         name="lon_back",
-    )(low, landing, high, taps)
-    low, high = swap(halved, halved, "lat", False)
+    )(far, close, landing, taps)
+    far, close = exchange(halved, halved, "lat", False)
 
     return call(
         lat_back_kernel,
@@ -560,8 +568,9 @@
         VMEM,
         conv_flops,
         20 * field,
+        scratch=(halos,),
         name="lat_back",
-    )(low, back, high, held)
+    )(far, close, back, held)
 
 
 def solution(mesh):

time: 57.7 us -> 46.6 us (0.81); the launches traced: 57 us -> 46.4 us
  blocking collectives: 11.3 us -> 0 us
  waiting for transfers between devices: 9.94 us -> 13.4 us
  Pallas kernels: 16 us -> 13.3 us
    all_gather x1 -> x0, blocking collectives: 11.3 us -> none  [shards(): lax.all_gather(slabs, 'lat', axis=0, tiled=True, axis_index_groups=parities)]
    ppermute x9 -> x12, waiting for transfers between devices: 9.94 us -> 13.4 us  [the longest x4 11.7 us: exchange(): lax.ppermute(to_far, axis, far)]
    pallas_call x1, Pallas kernels: 6.87 us -> 4.16 us  [shards(): call(functools.partial(backward_kernel, per_tile, len(slabs)), (shape((ti...]
    ppermute x9 -> x12, starting transfers between devices: 19.5 us -> 19.5 us  [the longest x4 12.7 us: exchange(): lax.ppermute(to_far, axis, far)]
  transfers between devices with their start and end apart: 9 -> 12, of which waited for: 3 -> 5; matrix products, arithmetic and copies ran while one was open for 0% -> 0% of each run, Pallas kernels for 9% -> 13%
where the time goes in v3:
time: 46.6 us; the launch traced here: 46.4 us
  starting transfers between devices  19.5 us (42%)
  waiting for transfers between devices  13.4 us (29%)
  Pallas kernels  13.3 us (29%)
    ppermute x4, starting transfers between devices, exchange(): lax.ppermute(to_far, axis, far)  12.7 us
    ppermute x4, waiting for transfers between devices, exchange(): lax.ppermute(to_far, axis, far)  11.7 us
    pallas_call x1, Pallas kernels, shards(): call(functools.partial(backward_kernel, per_tile, len(slabs)), (shape((ti...  4.16 us
    pallas_call x1, Pallas kernels, shards(): call(forward_kernel, (shape((x_rows, hidden), bf16), shape((x_rows, hidde...  4.15 us
    ppermute x2, starting transfers between devices, shards(): lax.ppermute(held_sets, 'lat', [(i, i ^ 1 << bit) for i in range(lat_coun...  3.55 us
    ppermute x2, starting transfers between devices, shards(): lax.ppermute(part, 'lat', [(i, i ^ 1) for i in range(lat_count)])  3.16 us
    ppermute x4, waiting for transfers between devices, exchange(): lax.ppermute(to_close, axis, close)  1.76 us
    pallas_call x1, Pallas kernels, shards(): call(lat_back_kernel, shape((height, levels, width), f32), [VMEM] * 4, VM...  1.36 us
  transfers between devices with their start and end apart: 12, of which 5 were waited for; matrix products, arithmetic and copies ran while one was open for 0% of the time, Pallas kernels for 13%

profile of v3, /device:TPU:1, one launch (start us, length us, event | category | flops | bytes accessed | tf_op | source)
XLA Modules:
  0.0 46.4 jit_solution(13545717139402447137)
XLA Ops:
  0.0 1.1 %slabs_halves.1 = (bf16[37,16,128]{2,1,0:T(8,128)(2,1)S(1)}, f32[16,32,128]{2,1,0:T(8,128)S(1)}, bf16[16,32,128]{2,1,0:T(8,128)(2,1)S(1)}) custom-call(bf16[36,16,128]{2,1,0:T(8,128)(2,1)} %bitcast.13, s32[1,64]{1,0:T(1,128)} %bitcast.14, s32[1,36]{1,0:T(1,128)} %bitcast.15, f32[16,32,128]{2,1,0:T(8,128)} %control.1), custom_call_target="tpu_custom_call" | custom-call | bytes 1048576 | tf_op jit(solution)/shard_map/slabs_halves/pallas_call | solution.py:424
  1.1 2.1 %collective-permute-start = (bf16[37,16,128]{2,1,0:T(8,128)(2,1)S(1)}, bf16[37,16,128]{2,1,0:T(8,128)(2,1)S(1)}, u32[]{:S(2)}, u32[]{:S(2)}) collective-permute-start(bf16[37,16,128]{2,1,0:T(8,128)(2,1)S(1)} %get-tuple-element.31), channel_id=1, source_target_pairs={{0,8},{4,12},{8,0},{12,4},{16,24},{20,28},{24,16},{28,20},{1,9},{5... | collective-permute-start | bytes 454664 | tf_op jit(solution)/shard_map/ppermute | solution.py:449
  3.2 2.5 %collective-permute-start.1 = (bf16[16,32,128]{2,1,0:T(8,128)(2,1)S(1)}, bf16[16,32,128]{2,1,0:T(8,128)(2,1)S(1)}, u32[]{:S(2)}, u32[]{:S(2)}) collective-permute-start(bf16[16,32,128]{2,1,0:T(8,128)(2,1)S(1)} %get-tuple-element.32), channel_id=1, source_target_pairs={{4,8},{8,4},{12,16},{16,12},{20,24},{24,20},{5,9},{9,5},{13,17},{1... | collective-permute-start | bytes 393224 | tf_op jit(solution)/shard_map/ppermute | solution.py:390
  5.7 0.1 collective-permute-start.2
  5.8 3.8 %collective-permute-done.1.far = bf16[16,32,128]{2,1,0:T(8,128)(2,1)S(1)} collective-permute-done((bf16[16,32,128]{2,1,0:T(8,128)(2,1)S(1)}, bf16[16,32,128]{2,1,0:T(8,128)(2,1)S(1)}, u32[]{:S(2)}, u32[]{:S(2)}) %collective-permute-start.1) | collective-permute-done | bytes 131104 | tf_op jit(solution)/shard_map/ppermute | solution.py:390
  9.7 0.0 collective-permute-done.2.close
  9.7 1.4 %collective-permute-start.3 = (bf16[74,16,128]{2,1,0:T(8,128)(2,1)S(1)}, bf16[74,16,128]{2,1,0:T(8,128)(2,1)S(1)}, u32[]{:S(2)}, u32[]{:S(2)}) collective-permute-start(bf16[74,16,128]{2,1,0:T(8,128)(2,1)S(1)} %constant_dynamic-update-slice_fusion.refs_0_), channel_id=1, source_target_pairs={{0,16},{4,20},{8,24},{12,28},{16,0},{20,4},{24,8},{28,12},{1,17},{... | collective-permute-start | bytes 909320 | tf_op jit(solution)/shard_map/ppermute | solution.py:449
  11.1 0.7 %lat_smooth.1 = (f32[4,128,128]{2,1,0:T(8,128)S(1)}, f32[4,16,128]{2,1,0:T(8,128)S(1)}, f32[4,16,128]{2,1,0:T(8,128)S(1)}) custom-call(bf16[16,32,128]{2,1,0:T(8,128)(2,1)S(1)} %collective-permute-done.1.far, bf16[16,32,128]{2,1,0:T(8,128)(2,1)S(1)} %collective-permute-done.2.close, f32[16,32,128]{2,1,0:T(8,128)S(1)} %get-tuple-element.36.own.control), custom_call_target="tpu_custom_call" | custom-call | flops 4325376 | bytes 1048576 | tf_op jit(solution)/shard_map/lat_smooth/pallas_call | solution.py:470
  11.9 3.4 %collective-permute-start.4 = (f32[4,16,128]{2,1,0:T(8,128)S(1)}, f32[4,16,128]{2,1,0:T(8,128)S(1)}, u32[]{:S(2)}, u32[]{:S(2)}) collective-permute-start(f32[4,16,128]{2,1,0:T(8,128)S(1)} %get-tuple-element.37), channel_id=1, source_target_pairs={{1,2},{2,1},{3,0},{0,3},{5,6},{6,5},{7,4},{4,7},{9,10},{10,9},{11,... | collective-permute-start | bytes 98312 | tf_op jit(solution)/shard_map/ppermute | solution.py:390
  15.3 0.0 collective-permute-start.5
  15.3 1.3 %collective-permute-done.4.far = f32[4,16,128]{2,1,0:T(8,128)S(1)} collective-permute-done((f32[4,16,128]{2,1,0:T(8,128)S(1)}, f32[4,16,128]{2,1,0:T(8,128)S(1)}, u32[]{:S(2)}, u32[]{:S(2)}) %collective-permute-start.4) | collective-permute-done | bytes 32800 | tf_op jit(solution)/shard_map/ppermute | solution.py:390
  16.6 1.8 %collective-permute-done.5.close = f32[4,16,128]{2,1,0:T(8,128)S(1)} collective-permute-done((f32[4,16,128]{2,1,0:T(8,128)S(1)}, f32[4,16,128]{2,1,0:T(8,128)S(1)}, u32[]{:S(2)}, u32[]{:S(2)}) %collective-permute-start.5) | collective-permute-done | bytes 32800 | tf_op jit(solution)/shard_map/ppermute | solution.py:390
  18.3 3.2 %collective-permute-start.6 = (bf16[74,16,128]{2,1,0:T(8,128)(2,1)S(1)}, bf16[74,16,128]{2,1,0:T(8,128)(2,1)S(1)}, u32[]{:S(2)}, u32[]{:S(2)}) collective-permute-start(bf16[74,16,128]{2,1,0:T(8,128)(2,1)S(1)} %constant_dynamic-update-slice_fusion.refs_0_), channel_id=1, source_target_pairs={{0,4},{4,0},{8,12},{12,8},{16,20},{20,16},{24,28},{28,24},{1,5},{5... | collective-permute-start | bytes 909320 | tf_op jit(solution)/shard_map/ppermute | solution.py:482
  21.5 0.0 collective-permute-start.7
  21.5 1.1 %taps_background.1 = (f32[4,24,128]{2,1,0:T(8,128)S(1)}, f32[4,128,128]{2,1,0:T(8,128)S(1)}) custom-call(s32[16]{0:T(128)} %lon_width.1, f32[16,32,128]{2,1,0:T(8,128)} %background.1), custom_call_target="tpu_custom_call" | custom-call | bytes 524288 | tf_op jit(solution)/shard_map/taps_background/pallas_call | solution.py:454
  22.6 4.2 %net_forward.1 = (bf16[512,1024]{1,0:T(8,128)(2,1)S(1)}, bf16[512,1024]{1,0:T(8,128)(2,1)S(1)}, f32[512,256]{1,0:T(8,128)S(1)}, bf16[128,1024]{1,0:T(8,128)(2,1)...) custom-call(s32[64]{0:T(128)} %bitcast.16, f32[4,16,128]{2,1,0:T(8,128)S(1)} %collective-permute-done.4.far, ...), custom_call_target="tpu_custom_call" | custom-call | flops 1476395008 | bytes 6291456 | tf_op jit(solution)/shard_map/net_forward/pallas_call | solution.py:487
  26.8 4.2 %net_backward.1 = (f32[4,128,128]{2,1,0:T(8,128)S(1)}, bf16[4,16,128]{2,1,0:T(8,128)(2,1)S(1)}, bf16[4,16,128]{2,1,0:T(8,128)(2,1)S(1)}) custom-call(s32[64]{0:T(128)} %bitcast.17, bf16[74,16,128]{2,1,0:T(8,128)(2,1)S(1)} %constant_dynamic-update-slice_fusion.refs_0_, bf16[74,16,128]{2,1,0:T(8,128)(2,1)S(1)} %collective-permute-done.3.refs_1_, ...), custom_call_target="tpu_custom_call" | custom-call | flops 1476395008 | bytes 6291456 | tf_op jit(solution)/shard_map/net_backward/pallas_call | solution.py:530
  30.9 1.7 %collective-permute-start.8 = (bf16[4,16,128]{2,1,0:T(8,128)(2,1)S(1)}, bf16[4,16,128]{2,1,0:T(8,128)(2,1)S(1)}, u32[]{:S(2)}, u32[]{:S(2)}) collective-permute-start(bf16[4,16,128]{2,1,0:T(8,128)(2,1)S(1)} %get-tuple-element.52), channel_id=1, source_target_pairs={{1,2},{2,1},{3,0},{0,3},{5,6},{6,5},{7,4},{4,7},{9,10},{10,9},{11,... | collective-permute-start | bytes 49160 | tf_op jit(solution)/shard_map/ppermute | solution.py:390
  32.6 2.8 %collective-permute-done.8.far = bf16[4,16,128]{2,1,0:T(8,128)(2,1)S(1)} collective-permute-done((bf16[4,16,128]{2,1,0:T(8,128)(2,1)S(1)}, bf16[4,16,128]{2,1,0:T(8,128)(2,1)S(1)}, u32[]{:S(2)}, u32[]{:S(2)}) %collective-permute-start.8) | collective-permute-done | bytes 16416 | tf_op jit(solution)/shard_map/ppermute | solution.py:390
  35.4 0.7 %lon_back.1 = (f32[16,32,128]{2,1,0:T(8,128)S(1)}, bf16[16,32,128]{2,1,0:T(8,128)(2,1)S(1)}) custom-call(bf16[4,16,128]{2,1,0:T(8,128)(2,1)S(1)} %collective-permute-done.8.far, bf16[4,16,128]{2,1,0:T(8,128)(2,1)S(1)} %collective-permute-done.9.close, f32[4,128,128]{2,1,0:T(8,128)S(1)} %get-tuple-element.54.own, f32[4,24,128]{2,1,0:T(8,128)S(1)} %get-tuple-element.45.taps), custom_call_target="tpu_custom_call" | custom-call | flops 4325376 | bytes 524288 | tf_op jit(solution)/shard_map/lon_back/pallas_call | solution.py:552
  36.1 5.2 %collective-permute-start.10 = (bf16[16,32,128]{2,1,0:T(8,128)(2,1)S(1)}, bf16[16,32,128]{2,1,0:T(8,128)(2,1)S(1)}, u32[]{:S(2)}, u32[]{:S(2)}) collective-permute-start(bf16[16,32,128]{2,1,0:T(8,128)(2,1)S(1)} %get-tuple-element.55), channel_id=1, source_target_pairs={{4,8},{8,4},{12,16},{16,12},{20,24},{24,20},{5,9},{9,5},{13,17},{1... | collective-permute-start | bytes 393224 | tf_op jit(solution)/shard_map/ppermute | solution.py:390
  41.3 0.1 collective-permute-start.11
  41.3 3.7 %collective-permute-done.10.far = bf16[16,32,128]{2,1,0:T(8,128)(2,1)S(1)} collective-permute-done((bf16[16,32,128]{2,1,0:T(8,128)(2,1)S(1)}, bf16[16,32,128]{2,1,0:T(8,128)(2,1)S(1)}, u32[]{:S(2)}, u32[]{:S(2)}) %collective-permute-start.10) | collective-permute-done | bytes 131104 | tf_op jit(solution)/shard_map/ppermute | solution.py:390
  45.1 1.4 %lat_back.1 = f32[16,32,128]{2,1,0:T(8,128)} custom-call(bf16[16,32,128]{2,1,0:T(8,128)(2,1)S(1)} %collective-permute-done.10.far, bf16[16,32,128]{2,1,0:T(8,128)(2,1)S(1)} %collective-permute-done.11.close, f32[16,32,128]{2,1,0:T(8,128)S(1)} %get-tuple-element.56.own, f32[16,32,128]{2,1,0:T(8,128)S(1)} %get-tuple-element.36.own.control), custom_call_target="tpu_custom_call" | custom-call | flops 4325376 | bytes 1310720 | tf_op jit(solution)/shard_map/lat_back/pallas_call | solution.py:564
  (9 shorter events, 0.1 us)
Async XLA Ops:
  1.1 8.5 %collective-permute-start = (bf16[37,16,128]{2,1,0:T(8,128)(2,1)S(1)}, bf16[37,16,128]{2,1,0:T(8,128)(2,1)S(1)}, u32[]{:S(2)}, u32[]{:S(2)}) collective-permute-start(bf16[37,16,128]{2,1,0:T(8,128)(2,1)S(1)} %get-tuple-element.31), channel_id=1, source_target_pairs={{0,8},{4,12},{8,0},{12,4},{16,24},{20,28},{24,16},{28,20},{1,9},{5... | collective-permute-start | bytes 454664 | tf_op jit(solution)/shard_map/ppermute | solution.py:449
  3.2 6.4 %collective-permute-start.1 = (bf16[16,32,128]{2,1,0:T(8,128)(2,1)S(1)}, bf16[16,32,128]{2,1,0:T(8,128)(2,1)S(1)}, u32[]{:S(2)}, u32[]{:S(2)}) collective-permute-start(bf16[16,32,128]{2,1,0:T(8,128)(2,1)S(1)} %get-tuple-element.32), channel_id=1, source_target_pairs={{4,8},{8,4},{12,16},{16,12},{20,24},{24,20},{5,9},{9,5},{13,17},{1... | collective-permute-start | bytes 393224 | tf_op jit(solution)/shard_map/ppermute | solution.py:390
  5.7 3.9 %collective-permute-start.2 = (bf16[16,32,128]{2,1,0:T(8,128)(2,1)S(1)}, bf16[16,32,128]{2,1,0:T(8,128)(2,1)S(1)}, u32[]{:S(2)}, u32[]{:S(2)}) collective-permute-start(bf16[16,32,128]{2,1,0:T(8,128)(2,1)S(1)} %get-tuple-element.32), channel_id=1, source_target_pairs={{0,4},{4,0},{8,12},{12,8},{16,20},{20,16},{24,28},{28,24},{1,5},{5... | collective-permute-start | bytes 393224 | tf_op jit(solution)/shard_map/ppermute | solution.py:390
  9.7 8.6 %collective-permute-start.3 = (bf16[74,16,128]{2,1,0:T(8,128)(2,1)S(1)}, bf16[74,16,128]{2,1,0:T(8,128)(2,1)S(1)}, u32[]{:S(2)}, u32[]{:S(2)}) collective-permute-start(bf16[74,16,128]{2,1,0:T(8,128)(2,1)S(1)} %constant_dynamic-update-slice_fusion.refs_0_), channel_id=1, source_target_pairs={{0,16},{4,20},{8,24},{12,28},{16,0},{20,4},{24,8},{28,12},{1,17},{... | collective-permute-start | bytes 909320 | tf_op jit(solution)/shard_map/ppermute | solution.py:449
  11.9 4.7 %collective-permute-start.4 = (f32[4,16,128]{2,1,0:T(8,128)S(1)}, f32[4,16,128]{2,1,0:T(8,128)S(1)}, u32[]{:S(2)}, u32[]{:S(2)}) collective-permute-start(f32[4,16,128]{2,1,0:T(8,128)S(1)} %get-tuple-element.37), channel_id=1, source_target_pairs={{1,2},{2,1},{3,0},{0,3},{5,6},{6,5},{7,4},{4,7},{9,10},{10,9},{11,... | collective-permute-start | bytes 98312 | tf_op jit(solution)/shard_map/ppermute | solution.py:390
  15.3 3.1 %collective-permute-start.5 = (f32[4,16,128]{2,1,0:T(8,128)S(1)}, f32[4,16,128]{2,1,0:T(8,128)S(1)}, u32[]{:S(2)}, u32[]{:S(2)}) collective-permute-start(f32[4,16,128]{2,1,0:T(8,128)S(1)} %get-tuple-element.38), channel_id=1, source_target_pairs={{0,1},{1,0},{2,3},{3,2},{4,5},{5,4},{6,7},{7,6},{8,9},{9,8},{10,11... | collective-permute-start | bytes 98312 | tf_op jit(solution)/shard_map/ppermute | solution.py:390
  18.3 8.4 %collective-permute-start.6 = (bf16[74,16,128]{2,1,0:T(8,128)(2,1)S(1)}, bf16[74,16,128]{2,1,0:T(8,128)(2,1)S(1)}, u32[]{:S(2)}, u32[]{:S(2)}) collective-permute-start(bf16[74,16,128]{2,1,0:T(8,128)(2,1)S(1)} %constant_dynamic-update-slice_fusion.refs_0_), channel_id=1, source_target_pairs={{0,4},{4,0},{8,12},{12,8},{16,20},{20,16},{24,28},{28,24},{1,5},{5... | collective-permute-start | bytes 909320 | tf_op jit(solution)/shard_map/ppermute | solution.py:482
  21.5 5.3 %collective-permute-start.7 = (bf16[74,16,128]{2,1,0:T(8,128)(2,1)S(1)}, bf16[74,16,128]{2,1,0:T(8,128)(2,1)S(1)}, u32[]{:S(2)}, u32[]{:S(2)}) collective-permute-start(bf16[74,16,128]{2,1,0:T(8,128)(2,1)S(1)} %collective-permute-done.3.refs_1_), channel_id=1, source_target_pairs={{0,4},{4,0},{8,12},{12,8},{16,20},{20,16},{24,28},{28,24},{1,5},{5... | collective-permute-start | bytes 909320 | tf_op jit(solution)/shard_map/ppermute | solution.py:482
  30.9 4.5 %collective-permute-start.8 = (bf16[4,16,128]{2,1,0:T(8,128)(2,1)S(1)}, bf16[4,16,128]{2,1,0:T(8,128)(2,1)S(1)}, u32[]{:S(2)}, u32[]{:S(2)}) collective-permute-start(bf16[4,16,128]{2,1,0:T(8,128)(2,1)S(1)} %get-tuple-element.52), channel_id=1, source_target_pairs={{1,2},{2,1},{3,0},{0,3},{5,6},{6,5},{7,4},{4,7},{9,10},{10,9},{11,... | collective-permute-start | bytes 49160 | tf_op jit(solution)/shard_map/ppermute | solution.py:390
  32.6 2.8 %collective-permute-start.9 = (bf16[4,16,128]{2,1,0:T(8,128)(2,1)S(1)}, bf16[4,16,128]{2,1,0:T(8,128)(2,1)S(1)}, u32[]{:S(2)}, u32[]{:S(2)}) collective-permute-start(bf16[4,16,128]{2,1,0:T(8,128)(2,1)S(1)} %get-tuple-element.53), channel_id=1, source_target_pairs={{0,1},{1,0},{2,3},{3,2},{4,5},{5,4},{6,7},{7,6},{8,9},{9,8},{10,11... | collective-permute-start | bytes 49160 | tf_op jit(solution)/shard_map/ppermute | solution.py:390
  36.1 9.0 %collective-permute-start.10 = (bf16[16,32,128]{2,1,0:T(8,128)(2,1)S(1)}, bf16[16,32,128]{2,1,0:T(8,128)(2,1)S(1)}, u32[]{:S(2)}, u32[]{:S(2)}) collective-permute-start(bf16[16,32,128]{2,1,0:T(8,128)(2,1)S(1)} %get-tuple-element.55), channel_id=1, source_target_pairs={{4,8},{8,4},{12,16},{16,12},{20,24},{24,20},{5,9},{9,5},{13,17},{1... | collective-permute-start | bytes 393224 | tf_op jit(solution)/shard_map/ppermute | solution.py:390
  41.3 3.8 %collective-permute-start.11 = (bf16[16,32,128]{2,1,0:T(8,128)(2,1)S(1)}, bf16[16,32,128]{2,1,0:T(8,128)(2,1)S(1)}, u32[]{:S(2)}, u32[]{:S(2)}) collective-permute-start(bf16[16,32,128]{2,1,0:T(8,128)(2,1)S(1)} %get-tuple-element.55), channel_id=1, source_target_pairs={{0,4},{4,0},{8,12},{12,8},{16,20},{20,16},{24,28},{28,24},{1,5},{5... | collective-permute-start | bytes 393224 | tf_op jit(solution)/shard_map/ppermute | solution.py:390

commit v4 on v3

--- a/solution.py
+++ b/solution.py
@@ -68,12 +68,17 @@
     padded[:, REACH + width :, :] = high
 
 
-def lon_conv(padded, taps, tile, width):
-    acc = taps[tile, 0:1, :] * padded[tile, pl.ds(REACH, width), :]
+def lon_conv(padded, taps, tile, start, width):
+    middle = REACH + start
+    acc = taps[tile, 0:1, :] * padded[tile, pl.ds(middle, width), :]
     for j in range(1, REACH + 1):
-        both = padded[tile, pl.ds(REACH + j, width), :] + padded[tile, pl.ds(REACH - j, width), :]
+        both = padded[tile, pl.ds(middle + j, width), :] + padded[tile, pl.ds(middle - j, width), :]
         acc = acc + taps[tile, j : j + 1, :] * both
     return acc
+
+
+def rounded(value):
+    return value.astype(jnp.bfloat16).astype(jnp.float32)
 
 
 def first_kernel(
@@ -102,16 +107,48 @@
     last.wait()
 
 
-def prepare_kernel(lon_width, background, taps, turned, widths, field, sems):
+def prepare_kernel(
+    lon_width, background, block_cells, block_owner, taps, turned, plan, widths, cells, owners, rows, field, sems
+):
     moves = [
         pltpu.make_async_copy(lon_width, widths, sems.at[0]),
-        pltpu.make_async_copy(background, field, sems.at[1]),
+        pltpu.make_async_copy(block_cells, cells, sems.at[1]),
+        pltpu.make_async_copy(block_owner, owners, sems.at[2]),
+        pltpu.make_async_copy(background, field, sems.at[3]),
     ]
     for move in moves:
         move.start()
     tiles = turned.shape[0]
     height, levels, width = background.shape
     per_tile = height // tiles
+    groups = width // BLOCK_COLS
+    rim = REACH // BLOCK_COLS
+    slot_count = cells.shape[0]
+
+    moves[1].wait()
+    moves[2].wait()
+
+    def outer(slot):
+        group = cells[slot] % groups
+        return ((group < rim) | (group >= groups - rim)) & (owners[slot] >= 0)
+
+    outer_count = lax.fori_loop(
+        0, slot_count, lambda slot, total: total + jnp.where(outer(slot), 1, 0), 0, unroll=8
+    )
+
+    def place(slot, nexts):
+        first, second = nexts
+        hit = outer(slot)
+        position = jnp.where(hit, first, second)
+        rows[0, position] = cells[slot]
+        rows[1, position] = slot
+        return first + jnp.where(hit, 1, 0), second + jnp.where(hit, 0, 1)
+
+    lax.fori_loop(0, slot_count, place, (0, outer_count), unroll=8)
+    rows[2, 0] = outer_count
+    plan_out = pltpu.make_async_copy(rows, plan, sems.at[4])
+    plan_out.start()
+
     lane_row = lax.broadcasted_iota(jnp.int32, (1, LANES), 1) // levels
     steps = lax.broadcasted_iota(jnp.int32, (taps.shape[1], LANES), 0)
     dist = steps.astype(jnp.float32)
@@ -125,10 +162,11 @@
         raw = jnp.exp(-dist * dist / (2.0 * spread * spread))
         norm = jnp.sum(weight * raw * raw, axis=0, keepdims=True)
         taps[tile] = raw / jnp.sqrt(norm)
-    moves[1].wait()
+    moves[3].wait()
     for tile in range(tiles):
-        rows = field[tile * per_tile : (tile + 1) * per_tile].reshape(per_tile * levels, width)
-        turned[tile] = jnp.transpose(rows)
+        block = field[tile * per_tile : (tile + 1) * per_tile].reshape(per_tile * levels, width)
+        turned[tile] = jnp.transpose(block)
+    plan_out.wait()
 
 
 def routing(recv_most, slot_count, tables, table):
@@ -198,13 +236,45 @@
         to_far[tile], to_close[tile] = split_sides(turned[0:REACH], turned[width - REACH : width], "lon")
 
 
-def block_place(cells, slot, groups, per_tile, width):
-    block = cells[slot]
+def block_place(plan, position, groups, per_tile, width):
+    block = plan[0, position]
     row = block // groups
     start = (row // per_tile) * width + (block % groups) * BLOCK_COLS
     return pl.multiple_of(start, BLOCK_COLS), row % per_tile
 
 
+def take_blocks(plan, profile, picked, first, count, per_tile, width):
+    groups = width // BLOCK_COLS
+    lane_row = lax.broadcasted_iota(jnp.int32, (BLOCK_COLS, LANES), 1) // (LANES // per_tile)
+    for k in range(count):
+        start, sub = block_place(plan, first + k, groups, per_tile, width)
+        block = profile[pl.ds(start, BLOCK_COLS), :]
+        picked[k * BLOCK_COLS : (k + 1) * BLOCK_COLS, :] = jnp.where(lane_row == sub, block, 0.0)
+
+
+def land_blocks(plan, field, sens, first, count, per_tile, width):
+    groups = width // BLOCK_COLS
+    lane_row = lax.broadcasted_iota(jnp.int32, (BLOCK_COLS, LANES), 1) // (LANES // per_tile)
+    for k in range(first, first + count):
+        start, sub = block_place(plan, k, groups, per_tile, width)
+        block = sens[k * BLOCK_COLS : (k + 1) * BLOCK_COLS, :]
+        field[pl.ds(start, BLOCK_COLS), :] += jnp.where(lane_row == sub, block, 0.0)
+
+
+def take_observed(plan, table, held, observed, first, count):
+    channels = observed.shape[1]
+    channel = lax.broadcasted_iota(jnp.int32, (BLOCK_COLS, LANES), 1)
+    for k in range(count):
+        slot = plan[1, first + k]
+        slab = held[table[0, slot]].astype(jnp.float32)
+        kept = table[1, slot]
+        for h in range(channels // LANES):
+            part = slab[h * BLOCK_COLS : (h + 1) * BLOCK_COLS]
+            observed[k * BLOCK_COLS : (k + 1) * BLOCK_COLS, h * LANES : (h + 1) * LANES] = jnp.where(
+                channel + h * LANES < kept, part, jnp.inf
+            )
+
+
 def dot(a, b):
     return jnp.dot(a, b, preferred_element_type=jnp.float32)
 
@@ -213,10 +283,30 @@
     return lax.dot_general(a, b, (((1,), (1,)), ((), ())), preferred_element_type=jnp.float32)
 
 
-def forward_kernel(
-    block_cells,
-    far,
-    close,
+def net_forward(picked, weights, states):
+    wide_in, weight_two, weight_out, bias_one, bias_two, bias_out = weights
+    act_one, act_two, emitted = states
+    inputs = picked[...].astype(jnp.bfloat16)
+    act_one[...] = jnp.tanh(dot(inputs, wide_in[...]) + bias_one[...]).astype(jnp.bfloat16)
+    act_two[...] = jnp.tanh(dot(act_one[...], weight_two[...]) + bias_two[...]).astype(jnp.bfloat16)
+    emitted[...] = dot(act_two[...], weight_out[...]) + bias_out[...]
+
+
+def net_backward(observed, states, weights):
+    wide_in, weight_two, weight_out = weights[:3]
+    act_one, act_two, emitted = states
+    seen = observed[...]
+    misfit = jnp.where(seen < jnp.inf, emitted[...] - seen, 0.0).astype(jnp.bfloat16)
+    two = act_two[...].astype(jnp.float32)
+    grad_two = (dot_t(misfit, weight_out[...]) * (1.0 - two * two)).astype(jnp.bfloat16)
+    one = act_one[...].astype(jnp.float32)
+    grad_one = (dot_t(grad_two, weight_two[...]) * (1.0 - one * one)).astype(jnp.bfloat16)
+    return rounded(dot_t(grad_one, wide_in[...]))
+
+
+def inner_forward_kernel(
+    outer_slots,
+    plan,
     own,
     turned,
     taps,
@@ -226,84 +316,105 @@
     mid_bias,
     out_weight,
     out_bias,
+    profile,
     act_one,
     act_two,
     emitted,
     wide_in,
     weight_two,
     weight_out,
-    cells,
-    padded,
-    profile,
-    picked,
     bias_one,
     bias_two,
     bias_out,
+    rows,
+    padded,
+    picked,
     sems,
 ):
     tiles, width, _ = own.shape
     levels = in_weight.shape[0]
     per_tile = LANES // levels
-    groups = width // BLOCK_COLS
-    slot_count = block_cells.shape[0]
-
-    cells_in = pltpu.make_async_copy(block_cells, cells, sems.at[0])
-    first_in = [
-        pltpu.make_async_copy(in_weight, wide_in.at[pl.ds(sub * levels, levels)], sems.at[1 + sub])
+    count = picked.shape[0] // BLOCK_COLS
+
+    moves = [
+        pltpu.make_async_copy(plan, rows, sems.at[0]),
+        pltpu.make_async_copy(in_bias, bias_one, sems.at[1]),
+        pltpu.make_async_copy(mid_weight, weight_two, sems.at[2]),
+        pltpu.make_async_copy(mid_bias, bias_two, sems.at[3]),
+        pltpu.make_async_copy(out_weight, weight_out, sems.at[4]),
+        pltpu.make_async_copy(out_bias, bias_out, sems.at[5]),
+    ] + [
+        pltpu.make_async_copy(in_weight, wide_in.at[pl.ds(sub * levels, levels)], sems.at[6 + sub])
         for sub in range(per_tile)
-    ] + [pltpu.make_async_copy(in_bias, bias_one, sems.at[1 + per_tile])]
-    mid_in = [
-        pltpu.make_async_copy(mid_weight, weight_two, sems.at[2 + per_tile]),
-        pltpu.make_async_copy(mid_bias, bias_two, sems.at[3 + per_tile]),
     ]
-    out_in = [
-        pltpu.make_async_copy(out_weight, weight_out, sems.at[4 + per_tile]),
-        pltpu.make_async_copy(out_bias, bias_out, sems.at[5 + per_tile]),
-    ]
-    for move in [cells_in] + first_in + mid_in + out_in:
+    for move in moves:
         move.start()
-
-    fill_padded(padded, far, own, close)
+    zeros = jnp.zeros((tiles, REACH, LANES), jnp.float32)
+    padded[:, 0:REACH, :] = zeros
+    padded[:, REACH : REACH + width, :] = own[...]
+    padded[:, REACH + width :, :] = zeros
     for tile in range(tiles):
-        total = turned[tile] + lon_conv(padded, taps, tile, width)
-        profile[tile * width : (tile + 1) * width, :] = total.astype(jnp.bfloat16).astype(jnp.float32)
-
-    lane_row = lax.broadcasted_iota(jnp.int32, (BLOCK_COLS, LANES), 1) // levels
-    cells_in.wait()
-    for slot in range(slot_count):
-        start, sub = block_place(cells, slot, groups, per_tile, width)
-        block = profile[pl.ds(start, BLOCK_COLS), :]
-        picked[slot * BLOCK_COLS : (slot + 1) * BLOCK_COLS, :] = jnp.where(lane_row == sub, block, 0.0)
-
-    for move in first_in:
+        total = turned[tile] + lon_conv(padded, taps, tile, 0, width)
+        profile[tile * width : (tile + 1) * width, :] = rounded(total)
+    for move in moves:
         move.wait()
-    inputs = picked[...].astype(jnp.bfloat16)
-    act_one[...] = jnp.tanh(dot(inputs, wide_in[...]) + bias_one[...]).astype(jnp.bfloat16)
-    for move in mid_in:
-        move.wait()
-    act_two[...] = jnp.tanh(dot(act_one[...], weight_two[...]) + bias_two[...]).astype(jnp.bfloat16)
-    for move in out_in:
-        move.wait()
-    emitted[...] = dot(act_two[...], weight_out[...]) + bias_out[...]
-
-
-def backward_kernel(
+
+    @pl.when(rows[2, 0] <= outer_slots)
+    def _():
+        take_blocks(rows, profile, picked, outer_slots, count, per_tile, width)
+        weights = (wide_in, weight_two, weight_out, bias_one, bias_two, bias_out)
+        net_forward(picked, weights, (act_one, act_two, emitted))
+
+
+def outer_forward_kernel(
     per_tile,
-    parts,
-    block_cells,
+    plan,
+    far,
+    close,
+    own,
+    turned,
+    taps,
+    inner_profile,
     *refs,
 ):
+    weights, states, late_states, (rows, padded, profile, picked, late_picked, sem) = (
+        refs[:6],
+        refs[6:9],
+        refs[9:12],
+        refs[12:],
+    )
+    tiles, width, _ = own.shape
+    outer_slots = picked.shape[0] // BLOCK_COLS
+    late_slots = late_picked.shape[0] // BLOCK_COLS
+    plan_in = pltpu.make_async_copy(plan, rows, sem)
+    plan_in.start()
+    fill_padded(padded, far, own, close)
+    profile[...] = inner_profile[...]
+    for tile in range(tiles):
+        for start in (0, width - REACH):
+            total = turned[tile, start : start + REACH, :] + lon_conv(padded, taps, tile, start, REACH)
+            profile[tile * width + start : tile * width + start + REACH, :] = rounded(total)
+    plan_in.wait()
+    take_blocks(rows, profile, picked, 0, outer_slots, per_tile, width)
+    net_forward(picked, weights, states)
+
+    @pl.when(rows[2, 0] > outer_slots)
+    def _():
+        take_blocks(rows, profile, late_picked, outer_slots, late_slots, per_tile, width)
+        net_forward(late_picked, weights, late_states)
+
+
+def outer_backward_kernel(per_tile, parts, plan, *refs):
     slabs, refs = refs[:parts], refs[parts:]
-    (act_one, act_two, emitted, wide_in, weight_two, weight_out) = refs[:6]
-    (landing, to_far, to_close) = refs[6:9]
-    (cells, tables, table_rows, table, held, observed, field, picked, sems) = refs[9:]
-    tiles, width, _ = landing.shape
+    weights, states, late_states, refs = refs[:3], refs[3:6], refs[6:9], refs[9:]
+    (held, table_rows, sens, to_far, to_close) = refs[:5]
+    (rows, tables, table, observed, late_observed, field, sems) = refs[5:]
+    tiles = to_far.shape[0]
+    width = field.shape[0] // tiles
     owners = tables.shape[0]
     per_owner = held.shape[0] // owners
-    slot_count = block_cells.shape[0]
-    channels = weight_out.shape[1]
-    groups = width // BLOCK_COLS
-    levels = LANES // per_tile
+    outer_slots = observed.shape[0] // BLOCK_COLS
+    late_slots = late_observed.shape[0] // BLOCK_COLS
 
     routes, bulk = [], []
     for part, ref in enumerate(slabs):
@@ -318,48 +429,60 @@
                 ref, held.at[pl.ds(start * per_owner, ref.shape[0])], sems.at[owners + part]
             )
         )
-    cells_in = pltpu.make_async_copy(block_cells, cells, sems.at[owners + parts])
-    for move in routes + [cells_in] + bulk:
+    plan_in = pltpu.make_async_copy(plan, rows, sems.at[owners + parts])
+    for move in routes + [plan_in] + bulk:
         move.start()
     field[...] = jnp.zeros_like(field)
     for move in routes:
         move.wait()
-    routing(per_owner - 1, slot_count, tables, table_rows)
+    routing(per_owner - 1, outer_slots + late_slots, tables, table_rows)
     table_in = pltpu.make_async_copy(table_rows, table, sems.at[owners + parts + 1])
     table_in.start()
-    for move in bulk + [table_in]:
+    for move in bulk + [plan_in, table_in]:
         move.wait()
 
-    channel = lax.broadcasted_iota(jnp.int32, (BLOCK_COLS, LANES), 1)
-    for slot in range(slot_count):
-        slab = held[table[0, slot]].astype(jnp.float32)
-        for h in range(channels // LANES):
-            part = slab[h * BLOCK_COLS : (h + 1) * BLOCK_COLS]
-            kept = channel + h * LANES < table[1, slot]
-            observed[slot * BLOCK_COLS : (slot + 1) * BLOCK_COLS, h * LANES : (h + 1) * LANES] = jnp.where(
-                kept, part, jnp.inf
-            )
-
-    seen = observed[...]
-    misfit = jnp.where(seen < jnp.inf, emitted[...] - seen, 0.0).astype(jnp.bfloat16)
-    two = act_two[...].astype(jnp.float32)
-    grad_two = (dot_t(misfit, weight_out[...]) * (1.0 - two * two)).astype(jnp.bfloat16)
-    one = act_one[...].astype(jnp.float32)
-    grad_one = (dot_t(grad_two, weight_two[...]) * (1.0 - one * one)).astype(jnp.bfloat16)
-    picked[...] = dot_t(grad_one, wide_in[...]).astype(jnp.bfloat16).astype(jnp.float32)
-
-    lane_row = lax.broadcasted_iota(jnp.int32, (BLOCK_COLS, LANES), 1) // levels
-    cells_in.wait()
-    for slot in range(slot_count):
-        start, sub = block_place(cells, slot, groups, per_tile, width)
-        block = picked[slot * BLOCK_COLS : (slot + 1) * BLOCK_COLS, :]
-        field[pl.ds(start, BLOCK_COLS), :] += jnp.where(lane_row == sub, block, 0.0)
+    take_observed(rows, table, held, observed, 0, outer_slots)
+    sens[0 : outer_slots * BLOCK_COLS, :] = net_backward(observed, states, weights)
+    land_blocks(rows, field, sens, 0, outer_slots, per_tile, width)
+
+    @pl.when(rows[2, 0] > outer_slots)
+    def _():
+        take_observed(rows, table, held, late_observed, outer_slots, late_slots)
+        sens[outer_slots * BLOCK_COLS :, :] = net_backward(late_observed, late_states, weights)
+        land_blocks(rows, field, sens, outer_slots, late_slots, per_tile, width)
+
     for tile in range(tiles):
-        landing[tile] = field[tile * width : (tile + 1) * width, :]
         low = field[tile * width : tile * width + REACH, :]
         high = field[(tile + 1) * width - REACH : (tile + 1) * width, :]
         low, high = split_sides(low, high, "lon")
         to_far[tile], to_close[tile] = low.astype(jnp.bfloat16), high.astype(jnp.bfloat16)
+
+
+def inner_backward_kernel(per_tile, outer_slots, plan, held, table_rows, sens, *refs):
+    weights, states, refs = refs[:3], refs[3:6], refs[6:]
+    landing, rows, table, observed, inner, field, sems = refs
+    tiles, width, _ = landing.shape
+    late_slots = observed.shape[0] // BLOCK_COLS
+    split = outer_slots * BLOCK_COLS
+    moves = [
+        pltpu.make_async_copy(plan, rows, sems.at[0]),
+        pltpu.make_async_copy(table_rows, table, sems.at[1]),
+    ]
+    for move in moves:
+        move.start()
+    field[...] = jnp.zeros_like(field)
+    inner[...] = sens[...]
+    for move in moves:
+        move.wait()
+
+    @pl.when(rows[2, 0] <= outer_slots)
+    def _():
+        take_observed(rows, table, held, observed, outer_slots, late_slots)
+        inner[split:, :] = net_backward(observed, states, weights)
+
+    land_blocks(rows, field, inner, 0, outer_slots + late_slots, per_tile, width)
+    for tile in range(tiles):
+        landing[tile] = field[tile * width : (tile + 1) * width, :]
 
 
 def lon_back_kernel(far, close, own, taps, back, halved, padded):
@@ -368,7 +491,7 @@
     per_tile = height // tiles
     fill_padded(padded, far, own, close)
     for tile in range(tiles):
-        rows = jnp.transpose(lon_conv(padded, taps, tile, width))
+        rows = jnp.transpose(lon_conv(padded, taps, tile, 0, width))
         rows = rows.reshape(per_tile, levels, width)
         back[tile * per_tile : (tile + 1) * per_tile] = rows
         halved[tile * per_tile : (tile + 1) * per_tile] = rows.astype(jnp.bfloat16)
@@ -442,6 +565,28 @@
         name="slabs_halves",
     )(*pinned(radiance, block_owner.reshape(1, slot_count), channel_count.reshape(1, recv_most), control))
 
+    cells = block_cells.reshape(slot_count)
+    taps, turned, plan = call(
+        prepare_kernel,
+        (
+            shape((tiles, 24, LANES), f32),
+            shape((tiles, width, LANES), f32),
+            shape((8, LANES), i32),
+        ),
+        [HBM] * 4,
+        (VMEM, VMEM, HBM),
+        0,
+        8 * field,
+        scratch=(
+            pltpu.SMEM((height,), i32),
+            pltpu.SMEM((slot_count,), i32),
+            pltpu.SMEM((slot_count,), i32),
+            pltpu.SMEM((8, LANES), i32),
+            pltpu.VMEM((height, levels, width), f32),
+            pltpu.SemaphoreType.DMA((5,)),
+        ),
+        name="taps_background",
+    )(*pinned(lon_width, background, cells, block_owner.reshape(slot_count)))
     lat_count = lax.axis_size("lat")
     near = [slabs]
     for bit in range(1, lat_count.bit_length() - 1):
@@ -449,22 +594,7 @@
         near = [held_sets, lax.ppermute(held_sets, "lat", [(i, i ^ (1 << bit)) for i in range(lat_count)])]
         if bit == 1:
             far, close = exchange(halved, halved, "lat", False)
-            near[1], far, close = lax.optimization_barrier((near[1], far, close))
-
-    taps, turned = call(
-        prepare_kernel,
-        (shape((tiles, 24, LANES), f32), shape((tiles, width, LANES), f32)),
-        [HBM, HBM],
-        (VMEM, VMEM),
-        0,
-        8 * field,
-        scratch=(
-            pltpu.SMEM((height,), i32),
-            pltpu.VMEM((height, levels, width), f32),
-            pltpu.SemaphoreType.DMA((2,)),
-        ),
-        name="taps_background",
-    )(*pinned(lon_width, background))
+            near[1], far, close, taps = lax.optimization_barrier((near[1], far, close, taps))
 
     halos = pltpu.VMEM((2, REACH, levels, width), f32)
     smoothed, to_far, to_close = call(
@@ -478,41 +608,44 @@
         name="lat_smooth",
     )(far, close, held)
     far, close = exchange(to_far, to_close, "lon", True)
-    near, far, close = lax.optimization_barrier((near, far, close))
-    across = [lax.ppermute(part, "lat", [(i, i ^ 1) for i in range(lat_count)]) for part in near]
-
+
+    outer_slots = 3 * slot_count // 8
+    late_slots = slot_count - outer_slots
     x_rows = slot_count * BLOCK_COLS
-    net_flops = 2 * x_rows * hidden * (LANES + hidden + channels)
-    cells = block_cells.reshape(slot_count)
-    states = call(
-        forward_kernel,
-        (
-            shape((x_rows, hidden), bf16),
-            shape((x_rows, hidden), bf16),
-            shape((x_rows, channels), f32),
-            shape((LANES, hidden), bf16),
-            shape((hidden, hidden), bf16),
-            shape((hidden, channels), bf16),
-        ),
-        [HBM] + [VMEM] * 5 + [HBM] * 6,
-        (VMEM,) * 6,
-        net_flops,
-        6 * 1024 * 1024,
+    outer_rows, late_rows = outer_slots * BLOCK_COLS, late_slots * BLOCK_COLS
+    row_flops = 2 * hidden * (LANES + hidden + channels)
+    weight_shapes = (
+        shape((LANES, hidden), bf16),
+        shape((hidden, hidden), bf16),
+        shape((hidden, channels), bf16),
+        shape((1, hidden), f32),
+        shape((1, hidden), f32),
+        shape((1, channels), f32),
+    )
+
+    def state_shapes(rows):
+        return (shape((rows, hidden), bf16), shape((rows, hidden), bf16), shape((rows, channels), f32))
+
+    plan_rows = pltpu.SMEM((8, LANES), i32)
+    padded = pltpu.VMEM((tiles, width + 2 * REACH, LANES), f32)
+    flat = pltpu.VMEM((tiles * width, LANES), f32)
+
+    profile, *rest = call(
+        functools.partial(inner_forward_kernel, outer_slots),
+        (shape((tiles * width, LANES), f32),) + state_shapes(late_rows) + weight_shapes,
+        [HBM] + [VMEM] * 3 + [HBM] * 6,
+        (VMEM,) * 10,
+        late_rows * row_flops,
+        4 * 1024 * 1024,
         scratch=(
-            pltpu.SMEM((slot_count,), i32),
-            pltpu.VMEM((tiles, width + 2 * REACH, LANES), f32),
-            pltpu.VMEM((tiles * width, LANES), f32),
-            pltpu.VMEM((x_rows, LANES), f32),
-            pltpu.VMEM((1, hidden), f32),
-            pltpu.VMEM((1, hidden), f32),
-            pltpu.VMEM((1, channels), f32),
+            plan_rows,
+            padded,
+            pltpu.VMEM((late_rows, LANES), f32),
             pltpu.SemaphoreType.DMA((6 + per_tile,)),
         ),
-        name="net_forward",
+        name="inner_forward",
     )(
-        *pinned(cells),
-        far,
-        close,
+        *pinned(plan),
         smoothed,
         turned,
         taps,
@@ -525,29 +658,72 @@
             out_bias.reshape(1, channels),
         ),
     )
+    inner_states, weights = rest[:3], rest[3:]
+    near, far, close, profile = lax.optimization_barrier((near, far, close, profile))
+    across = [lax.ppermute(part, "lat", [(i, i ^ 1) for i in range(lat_count)]) for part in near]
+
+    states = call(
+        functools.partial(outer_forward_kernel, per_tile),
+        state_shapes(outer_rows) + state_shapes(late_rows),
+        [HBM] + [VMEM] * 12,
+        (VMEM,) * 6,
+        outer_rows * row_flops,
+        4 * 1024 * 1024,
+        scratch=(
+            plan_rows,
+            padded,
+            flat,
+            pltpu.VMEM((outer_rows, LANES), f32),
+            pltpu.VMEM((late_rows, LANES), f32),
+            pltpu.SemaphoreType.DMA,
+        ),
+        name="outer_forward",
+    )(*pinned(plan), far, close, smoothed, turned, taps, profile, *weights)
 
     slabs = [*near, *across]
-    landing, to_far, to_close = call(
-        functools.partial(backward_kernel, per_tile, len(slabs)),
-        (shape((tiles, width, LANES), f32),) + (shape((tiles, REACH, LANES), bf16),) * 2,
-        [HBM] + [ANY] * len(slabs) + [VMEM] * 6,
-        (VMEM,) * 3,
-        net_flops,
-        6 * 1024 * 1024,
+    held_slabs, table, sens, to_far, to_close = call(
+        functools.partial(outer_backward_kernel, per_tile, len(slabs)),
+        (
+            shape((lat_count * (recv_most + 1), slab_rows, LANES), bf16),
+            shape((8, LANES), i32),
+            shape((x_rows, LANES), f32),
+            shape((tiles, REACH, LANES), bf16),
+            shape((tiles, REACH, LANES), bf16),
+        ),
+        [HBM] + [ANY] * len(slabs) + [VMEM] * 9,
+        (VMEM,) * 5,
+        outer_rows * row_flops,
+        4 * 1024 * 1024,
         scratch=(
-            pltpu.SMEM((slot_count,), i32),
+            plan_rows,
             pltpu.VMEM((lat_count, slab_rows, LANES), bf16),
-            pltpu.VMEM((8, LANES), i32),
             pltpu.SMEM((8, LANES), i32),
-            pltpu.VMEM((lat_count * (recv_most + 1), slab_rows, LANES), bf16),
-            pltpu.VMEM((x_rows, channels), f32),
-            pltpu.VMEM((tiles * width, LANES), f32),
+            pltpu.VMEM((outer_rows, channels), f32),
+            pltpu.VMEM((late_rows, channels), f32),
+            flat,
+            pltpu.SemaphoreType.DMA((lat_count + len(slabs) + 2,)),
+        ),
+        name="outer_backward",
+    )(*pinned(plan), *slabs, *weights[:3], *states)
+    far, close = exchange(to_far, to_close, "lon", True)
+
+    landing = call(
+        functools.partial(inner_backward_kernel, per_tile, outer_slots),
+        shape((tiles, width, LANES), f32),
+        [HBM, VMEM, ANY] + [VMEM] * 7,
+        VMEM,
+        late_rows * row_flops,
+        4 * 1024 * 1024,
+        scratch=(
+            plan_rows,
+            pltpu.SMEM((8, LANES), i32),
+            pltpu.VMEM((late_rows, channels), f32),
             pltpu.VMEM((x_rows, LANES), f32),
-            pltpu.SemaphoreType.DMA((lat_count + len(slabs) + 2,)),
-        ),
-        name="net_backward",
-    )(*pinned(cells), *slabs, *states)
-    far, close = exchange(to_far, to_close, "lon", True)
+            flat,
+            pltpu.SemaphoreType.DMA((2,)),
+        ),
+        name="inner_backward",
+    )(*pinned(plan), held_slabs, table, sens, *weights[:3], *inner_states)
 
     back, halved = call(
         lon_back_kernel,

time: 46.6 us -> 43.4 us (0.931)
  waiting for transfers between devices: 13.4 us -> 8.57 us
  Pallas kernels: 13.3 us -> 17.2 us
  starting transfers between devices: 19.5 us -> 17.1 us
    ppermute x4, waiting for transfers between devices: 11.7 us -> 8.28 us  [exchange(): lax.ppermute(to_far, axis, far)]
    ppermute x4, starting transfers between devices: 12.7 us -> 9.41 us  [exchange(): lax.ppermute(to_far, axis, far)]
    pallas_call x2 -> x4, Pallas kernels: 8.31 us -> 10.9 us  [the longest x1 3.5 us: shards(): call(functools.partial(inner_forward_kernel, outer_slots), (shape((tiles...]
    ppermute x4, starting transfers between devices: 0.15 us -> 2.66 us  [exchange(): lax.ppermute(to_close, axis, close)]
    ppermute x4, waiting for transfers between devices: 1.76 us -> 0.01 us  [exchange(): lax.ppermute(to_close, axis, close)]
    pallas_call x1, Pallas kernels: 1.1 us -> 2.37 us  [shards(): call(prepare_kernel, (shape((tiles, 24, LANES), f32), shape((tiles, width...]
    ppermute x2, starting transfers between devices: 3.55 us -> 2.58 us  [shards(): lax.ppermute(held_sets, 'lat', [(i, i ^ 1 << bit) for i in range(lat_coun...]
    ppermute x2, starting transfers between devices: 3.16 us -> 2.42 us  [shards(): lax.ppermute(part, 'lat', [(i, i ^ 1) for i in range(lat_count)])]
  transfers between devices with their start and end apart: 12 -> 12, of which waited for: 5 -> 3; matrix products, arithmetic and copies ran while one was open for 0% -> 0% of each run, Pallas kernels for 13% -> 26%
where the time goes in v4:
time: 43.4 us; the launch traced here: 43.1 us
  Pallas kernels  17.2 us (40%)
  starting transfers between devices  17.1 us (39%)
  waiting for transfers between devices  8.57 us (20%)
    ppermute x4, starting transfers between devices, exchange(): lax.ppermute(to_far, axis, far)  9.41 us
    ppermute x4, waiting for transfers between devices, exchange(): lax.ppermute(to_far, axis, far)  8.28 us
    pallas_call x1, Pallas kernels, shards(): call(functools.partial(inner_forward_kernel, outer_slots), (shape((tiles...  3.5 us
    pallas_call x1, Pallas kernels, shards(): call(functools.partial(inner_backward_kernel, per_tile, outer_slots), sha...  2.86 us
    pallas_call x1, Pallas kernels, shards(): call(functools.partial(outer_backward_kernel, per_tile, len(slabs)), (sha...  2.76 us
    ppermute x4, starting transfers between devices, exchange(): lax.ppermute(to_close, axis, close)  2.66 us
    ppermute x2, starting transfers between devices, shards(): lax.ppermute(held_sets, 'lat', [(i, i ^ 1 << bit) for i in range(lat_coun...  2.58 us
    ppermute x2, starting transfers between devices, shards(): lax.ppermute(part, 'lat', [(i, i ^ 1) for i in range(lat_count)])  2.42 us
  transfers between devices with their start and end apart: 12, of which 3 were waited for; matrix products, arithmetic and copies ran while one was open for 0% of the time, Pallas kernels for 26%

profile of v4, /device:TPU:1, one launch (start us, length us, event | category | flops | bytes accessed | tf_op | source)
XLA Modules:
  0.0 43.1 jit_solution(6025701397015331227)
XLA Ops:
  0.0 1.1 %slabs_halves.1 = (bf16[37,16,128]{2,1,0:T(8,128)(2,1)S(1)}, f32[16,32,128]{2,1,0:T(8,128)S(1)}, bf16[16,32,128]{2,1,0:T(8,128)(2,1)S(1)}) custom-call(bf16[36,16,128]{2,1,0:T(8,128)(2,1)} %bitcast.14, s32[1,64]{1,0:T(1,128)} %bitcast.15, s32[1,36]{1,0:T(1,128)} %bitcast.17, f32[16,32,128]{2,1,0:T(8,128)} %control.1), custom_call_target="tpu_custom_call" | custom-call | bytes 1048576 | tf_op jit(solution)/shard_map/slabs_halves/pallas_call | solution.py:547
  1.1 2.1 %collective-permute-start = (bf16[37,16,128]{2,1,0:T(8,128)(2,1)S(1)}, bf16[37,16,128]{2,1,0:T(8,128)(2,1)S(1)}, u32[]{:S(2)}, u32[]{:S(2)}) collective-permute-start(bf16[37,16,128]{2,1,0:T(8,128)(2,1)S(1)} %get-tuple-element.47), channel_id=1, source_target_pairs={{0,8},{4,12},{8,0},{12,4},{16,24},{20,28},{24,16},{28,20},{1,9},{5... | collective-permute-start | bytes 454664 | tf_op jit(solution)/shard_map/ppermute | solution.py:594
  3.2 1.0 %collective-permute-start.2 = (bf16[16,32,128]{2,1,0:T(8,128)(2,1)S(1)}, bf16[16,32,128]{2,1,0:T(8,128)(2,1)S(1)}, u32[]{:S(2)}, u32[]{:S(2)}) collective-permute-start(bf16[16,32,128]{2,1,0:T(8,128)(2,1)S(1)} %get-tuple-element.48), channel_id=1, source_target_pairs={{0,4},{4,0},{8,12},{12,8},{16,20},{20,16},{24,28},{28,24},{1,5},{5... | collective-permute-start | bytes 393224 | tf_op jit(solution)/shard_map/ppermute | solution.py:513
  4.2 1.9 %collective-permute-start.1 = (bf16[16,32,128]{2,1,0:T(8,128)(2,1)S(1)}, bf16[16,32,128]{2,1,0:T(8,128)(2,1)S(1)}, u32[]{:S(2)}, u32[]{:S(2)}) collective-permute-start(bf16[16,32,128]{2,1,0:T(8,128)(2,1)S(1)} %get-tuple-element.48), channel_id=1, source_target_pairs={{4,8},{8,4},{12,16},{16,12},{20,24},{24,20},{5,9},{9,5},{13,17},{1... | collective-permute-start | bytes 393224 | tf_op jit(solution)/shard_map/ppermute | solution.py:513
  6.1 2.4 %taps_background.1 = (f32[4,24,128]{2,1,0:T(8,128)S(1)}, f32[4,128,128]{2,1,0:T(8,128)S(1)}, s32[8,128]{1,0:T(8,128)S(1)}) custom-call(s32[16]{0:T(128)} %lon_width.1, f32[16,32,128]{2,1,0:T(8,128)} %background.1, s32[64]{0:T(128)} %bitcast.18, s32[64]{0:T(128)} %bitcast.16), custom_call_target="tpu_custom_call" | custom-call | bytes 524288 | tf_op jit(solution)/shard_map/taps_background/pallas_call | solution.py:569
  8.5 0.0 copy-start
  8.5 3.1 %collective-permute-done.1.far = bf16[16,32,128]{2,1,0:T(8,128)(2,1)S(1)} collective-permute-done((bf16[16,32,128]{2,1,0:T(8,128)(2,1)S(1)}, bf16[16,32,128]{2,1,0:T(8,128)(2,1)S(1)}, u32[]{:S(2)}, u32[]{:S(2)}) %collective-permute-start.1) | collective-permute-done | bytes 131104 | tf_op jit(solution)/shard_map/ppermute | solution.py:513
  11.6 0.5 %collective-permute-start.3 = (bf16[74,16,128]{2,1,0:T(8,128)(2,1)S(1)}, bf16[74,16,128]{2,1,0:T(8,128)(2,1)S(1)}, u32[]{:S(2)}, u32[]{:S(2)}) collective-permute-start(bf16[74,16,128]{2,1,0:T(8,128)(2,1)S(1)} %constant_dynamic-update-slice_fusion.refs_0_), channel_id=1, source_target_pairs={{0,16},{4,20},{8,24},{12,28},{16,0},{20,4},{24,8},{28,12},{1,17},{... | collective-permute-start | bytes 909320 | tf_op jit(solution)/shard_map/ppermute | solution.py:594
  12.1 0.8 %lat_smooth.1 = (f32[4,128,128]{2,1,0:T(8,128)S(1)}, f32[4,16,128]{2,1,0:T(8,128)S(1)}, f32[4,16,128]{2,1,0:T(8,128)S(1)}) custom-call(bf16[16,32,128]{2,1,0:T(8,128)(2,1)S(1)} %collective-permute-done.1.far, bf16[16,32,128]{2,1,0:T(8,128)(2,1)S(1)} %collective-permute-done.2.close, f32[16,32,128]{2,1,0:T(8,128)S(1)} %get-tuple-element.53.own.control), custom_call_target="tpu_custom_call" | custom-call | flops 4325376 | bytes 1048576 | tf_op jit(solution)/shard_map/lat_smooth/pallas_call | solution.py:600
  12.9 3.4 %collective-permute-start.4 = (f32[4,16,128]{2,1,0:T(8,128)S(1)}, f32[4,16,128]{2,1,0:T(8,128)S(1)}, u32[]{:S(2)}, u32[]{:S(2)}) collective-permute-start(f32[4,16,128]{2,1,0:T(8,128)S(1)} %get-tuple-element.54), channel_id=1, source_target_pairs={{1,2},{2,1},{3,0},{0,3},{5,6},{6,5},{7,4},{4,7},{9,10},{10,9},{11,... | collective-permute-start | bytes 98312 | tf_op jit(solution)/shard_map/ppermute | solution.py:513
  16.3 3.5 %inner_forward.1 = (f32[512,128]{1,0:T(8,128)S(1)}, bf16[320,1024]{1,0:T(8,128)(2,1)S(1)}, bf16[320,1024]{1,0:T(8,128)(2,1)S(1)}, f32[320,256]{1,0:T(8,128)S(1)}...) custom-call(s32[8,128]{1,0:T(8,128)} %copy-done, ...), custom_call_target="tpu_custom_call" | custom-call | flops 922746880 | bytes 4194304 | tf_op jit(solution)/shard_map/inner_forward/pallas_call | solution.py:633
  19.8 0.3 collective-permute-done.3.refs_1_
  20.1 2.4 %collective-permute-start.6 = (bf16[74,16,128]{2,1,0:T(8,128)(2,1)S(1)}, bf16[74,16,128]{2,1,0:T(8,128)(2,1)S(1)}, u32[]{:S(2)}, u32[]{:S(2)}) collective-permute-start(bf16[74,16,128]{2,1,0:T(8,128)(2,1)S(1)} %constant_dynamic-update-slice_fusion.refs_0_), channel_id=1, source_target_pairs={{0,4},{4,0},{8,12},{12,8},{16,20},{20,16},{24,28},{28,24},{1,5},{5... | collective-permute-start | bytes 909320 | tf_op jit(solution)/shard_map/ppermute | solution.py:663
  22.5 0.0 collective-permute-start.7
  22.5 1.8 %outer_forward.1 = (bf16[192,1024]{1,0:T(8,128)(2,1)S(1)}, bf16[192,1024]{1,0:T(8,128)(2,1)S(1)}, f32[192,256]{1,0:T(8,128)S(1)}, bf16[320,1024]{1,0:T(8,128)(2,...) custom-call(s32[8,128]{1,0:T(8,128)} %copy-done, f32[4,16,128]{2,1,0:T(8,128)S(1)} %collective-permute-done.4.far, ...), custom_call_target="tpu_custom_call" | custom-call | flops 553648128 | bytes 4194304 | tf_op jit(solution)/shard_map/outer_forward/pallas_call | solution.py:665
  24.3 2.8 %outer_backward.1 = (bf16[296,16,128]{2,1,0:T(8,128)(2,1)S(1)}, s32[8,128]{1,0:T(8,128)S(1)}, f32[512,128]{1,0:T(8,128)S(1)}, bf16[4,16,128]{2,1,0:T(8,128)(2,1)S(1)}, bf16[4,16,128]{2,1,0:T(8,128)(2,1)S(1)}) custom-call(s32[8,128]{1,0:T(8,128)} %copy-done, bf16[74,16,128]{2,1,0:T(8,128)(2,1)S(1)} %constant_dynamic-update-slice_fusion.refs_0_, ...), custom_call_target="tpu_custom_call" | custom-call | flops 553648128 | bytes 4194304 | tf_op jit(solution)/shard_map/outer_backward/pallas_call | solution.py:684
  27.1 2.2 %collective-permute-start.8 = (bf16[4,16,128]{2,1,0:T(8,128)(2,1)S(1)}, bf16[4,16,128]{2,1,0:T(8,128)(2,1)S(1)}, u32[]{:S(2)}, u32[]{:S(2)}) collective-permute-start(bf16[4,16,128]{2,1,0:T(8,128)(2,1)S(1)} %get-tuple-element.77), channel_id=1, source_target_pairs={{1,2},{2,1},{3,0},{0,3},{5,6},{6,5},{7,4},{4,7},{9,10},{10,9},{11,... | collective-permute-start | bytes 49160 | tf_op jit(solution)/shard_map/ppermute | solution.py:513
  29.3 2.9 %inner_backward.1.own = f32[4,128,128]{2,1,0:T(8,128)S(1)} custom-call(s32[8,128]{1,0:T(8,128)} %copy-done, bf16[296,16,128]{2,1,0:T(8,128)(2,1)S(1)} %get-tuple-element.79.held, s32[8,128]{1,0:T(8,128)S(1)} %get-tuple-element.80.table_rows, f32[512,128]{1,0:T(8,128)S(1)} %get-tuple-element.81.sens, bf16[128,1024]{1,0:T(8,128)(2,1)S(1)} %get-tuple-element.62.refs_0_.refs_4_, ...), custom_call_target="tpu_custom_call" | custom-call | flops 922746880 | bytes 4194304 | tf_op jit(solution)/shard_map/inner_backward/pallas_call | solution.py:710
  32.2 0.0 collective-permute-done.9.close
  32.2 0.7 %lon_back.1 = (f32[16,32,128]{2,1,0:T(8,128)S(1)}, bf16[16,32,128]{2,1,0:T(8,128)(2,1)S(1)}) custom-call(bf16[4,16,128]{2,1,0:T(8,128)(2,1)S(1)} %collective-permute-done.8.far, bf16[4,16,128]{2,1,0:T(8,128)(2,1)S(1)} %collective-permute-done.9.close, f32[4,128,128]{2,1,0:T(8,128)S(1)} %inner_backward.1.own, f32[4,24,128]{2,1,0:T(8,128)S(1)} %get-tuple-element.58.taps), custom_call_target="tpu_custom_call" | custom-call | flops 4325376 | bytes 524288 | tf_op jit(solution)/shard_map/lon_back/pallas_call | solution.py:728
  32.9 1.7 %collective-permute-start.11 = (bf16[16,32,128]{2,1,0:T(8,128)(2,1)S(1)}, bf16[16,32,128]{2,1,0:T(8,128)(2,1)S(1)}, u32[]{:S(2)}, u32[]{:S(2)}) collective-permute-start(bf16[16,32,128]{2,1,0:T(8,128)(2,1)S(1)} %get-tuple-element.85), channel_id=1, source_target_pairs={{0,4},{4,0},{8,12},{12,8},{16,20},{20,16},{24,28},{28,24},{1,5},{5... | collective-permute-start | bytes 393224 | tf_op jit(solution)/shard_map/ppermute | solution.py:513
  34.6 1.9 %collective-permute-start.10 = (bf16[16,32,128]{2,1,0:T(8,128)(2,1)S(1)}, bf16[16,32,128]{2,1,0:T(8,128)(2,1)S(1)}, u32[]{:S(2)}, u32[]{:S(2)}) collective-permute-start(bf16[16,32,128]{2,1,0:T(8,128)(2,1)S(1)} %get-tuple-element.85), channel_id=1, source_target_pairs={{4,8},{8,4},{12,16},{16,12},{20,24},{24,20},{5,9},{9,5},{13,17},{1... | collective-permute-start | bytes 393224 | tf_op jit(solution)/shard_map/ppermute | solution.py:513
  36.5 5.2 %collective-permute-done.10.far = bf16[16,32,128]{2,1,0:T(8,128)(2,1)S(1)} collective-permute-done((bf16[16,32,128]{2,1,0:T(8,128)(2,1)S(1)}, bf16[16,32,128]{2,1,0:T(8,128)(2,1)S(1)}, u32[]{:S(2)}, u32[]{:S(2)}) %collective-permute-start.10) | collective-permute-done | bytes 131104 | tf_op jit(solution)/shard_map/ppermute | solution.py:513
  41.7 1.4 %lat_back.1 = f32[16,32,128]{2,1,0:T(8,128)} custom-call(bf16[16,32,128]{2,1,0:T(8,128)(2,1)S(1)} %collective-permute-done.10.far, bf16[16,32,128]{2,1,0:T(8,128)(2,1)S(1)} %collective-permute-done.11.close, f32[16,32,128]{2,1,0:T(8,128)S(1)} %get-tuple-element.86.own, f32[16,32,128]{2,1,0:T(8,128)S(1)} %get-tuple-element.53.own.control), custom_call_target="tpu_custom_call" | custom-call | flops 4325376 | bytes 1310720 | tf_op jit(solution)/shard_map/lat_back/pallas_call | solution.py:740
  (13 shorter events, 0.1 us)
Async XLA Ops:
  1.1 10.5 %collective-permute-start = (bf16[37,16,128]{2,1,0:T(8,128)(2,1)S(1)}, bf16[37,16,128]{2,1,0:T(8,128)(2,1)S(1)}, u32[]{:S(2)}, u32[]{:S(2)}) collective-permute-start(bf16[37,16,128]{2,1,0:T(8,128)(2,1)S(1)} %get-tuple-element.47), channel_id=1, source_target_pairs={{0,8},{4,12},{8,0},{12,4},{16,24},{20,28},{24,16},{28,20},{1,9},{5... | collective-permute-start | bytes 454664 | tf_op jit(solution)/shard_map/ppermute | solution.py:594
  3.2 5.3 %collective-permute-start.2 = (bf16[16,32,128]{2,1,0:T(8,128)(2,1)S(1)}, bf16[16,32,128]{2,1,0:T(8,128)(2,1)S(1)}, u32[]{:S(2)}, u32[]{:S(2)}) collective-permute-start(bf16[16,32,128]{2,1,0:T(8,128)(2,1)S(1)} %get-tuple-element.48), channel_id=1, source_target_pairs={{0,4},{4,0},{8,12},{12,8},{16,20},{20,16},{24,28},{28,24},{1,5},{5... | collective-permute-start | bytes 393224 | tf_op jit(solution)/shard_map/ppermute | solution.py:513
  4.2 7.4 %collective-permute-start.1 = (bf16[16,32,128]{2,1,0:T(8,128)(2,1)S(1)}, bf16[16,32,128]{2,1,0:T(8,128)(2,1)S(1)}, u32[]{:S(2)}, u32[]{:S(2)}) collective-permute-start(bf16[16,32,128]{2,1,0:T(8,128)(2,1)S(1)} %get-tuple-element.48), channel_id=1, source_target_pairs={{4,8},{8,4},{12,16},{16,12},{20,24},{24,20},{5,9},{9,5},{13,17},{1... | collective-permute-start | bytes 393224 | tf_op jit(solution)/shard_map/ppermute | solution.py:513
  8.5 7.8 %copy-start = (s32[8,128]{1,0:T(8,128)}, s32[8,128]{1,0:T(8,128)S(1)}, u32[]{:S(2)}) copy-start(s32[8,128]{1,0:T(8,128)S(1)} %get-tuple-element.46.plan) | copy-start | bytes 12292
  11.6 8.4 %collective-permute-start.3 = (bf16[74,16,128]{2,1,0:T(8,128)(2,1)S(1)}, bf16[74,16,128]{2,1,0:T(8,128)(2,1)S(1)}, u32[]{:S(2)}, u32[]{:S(2)}) collective-permute-start(bf16[74,16,128]{2,1,0:T(8,128)(2,1)S(1)} %constant_dynamic-update-slice_fusion.refs_0_), channel_id=1, source_target_pairs={{0,16},{4,20},{8,24},{12,28},{16,0},{20,4},{24,8},{28,12},{1,17},{... | collective-permute-start | bytes 909320 | tf_op jit(solution)/shard_map/ppermute | solution.py:594
  12.9 6.9 %collective-permute-start.4 = (f32[4,16,128]{2,1,0:T(8,128)S(1)}, f32[4,16,128]{2,1,0:T(8,128)S(1)}, u32[]{:S(2)}, u32[]{:S(2)}) collective-permute-start(f32[4,16,128]{2,1,0:T(8,128)S(1)} %get-tuple-element.54), channel_id=1, source_target_pairs={{1,2},{2,1},{3,0},{0,3},{5,6},{6,5},{7,4},{4,7},{9,10},{10,9},{11,... | collective-permute-start | bytes 98312 | tf_op jit(solution)/shard_map/ppermute | solution.py:513
  16.2 3.5 %collective-permute-start.5 = (f32[4,16,128]{2,1,0:T(8,128)S(1)}, f32[4,16,128]{2,1,0:T(8,128)S(1)}, u32[]{:S(2)}, u32[]{:S(2)}) collective-permute-start(f32[4,16,128]{2,1,0:T(8,128)S(1)} %get-tuple-element.55), channel_id=1, source_target_pairs={{0,1},{1,0},{2,3},{3,2},{4,5},{5,4},{6,7},{7,6},{8,9},{9,8},{10,11... | collective-permute-start | bytes 98312 | tf_op jit(solution)/shard_map/ppermute | solution.py:513
  20.1 4.3 %collective-permute-start.6 = (bf16[74,16,128]{2,1,0:T(8,128)(2,1)S(1)}, bf16[74,16,128]{2,1,0:T(8,128)(2,1)S(1)}, u32[]{:S(2)}, u32[]{:S(2)}) collective-permute-start(bf16[74,16,128]{2,1,0:T(8,128)(2,1)S(1)} %constant_dynamic-update-slice_fusion.refs_0_), channel_id=1, source_target_pairs={{0,4},{4,0},{8,12},{12,8},{16,20},{20,16},{24,28},{28,24},{1,5},{5... | collective-permute-start | bytes 909320 | tf_op jit(solution)/shard_map/ppermute | solution.py:663
  22.5 1.9 %collective-permute-start.7 = (bf16[74,16,128]{2,1,0:T(8,128)(2,1)S(1)}, bf16[74,16,128]{2,1,0:T(8,128)(2,1)S(1)}, u32[]{:S(2)}, u32[]{:S(2)}) collective-permute-start(bf16[74,16,128]{2,1,0:T(8,128)(2,1)S(1)} %collective-permute-done.3.refs_1_), channel_id=1, source_target_pairs={{0,4},{4,0},{8,12},{12,8},{16,20},{20,16},{24,28},{28,24},{1,5},{5... | collective-permute-start | bytes 909320 | tf_op jit(solution)/shard_map/ppermute | solution.py:663
  27.1 5.1 %collective-permute-start.8 = (bf16[4,16,128]{2,1,0:T(8,128)(2,1)S(1)}, bf16[4,16,128]{2,1,0:T(8,128)(2,1)S(1)}, u32[]{:S(2)}, u32[]{:S(2)}) collective-permute-start(bf16[4,16,128]{2,1,0:T(8,128)(2,1)S(1)} %get-tuple-element.77), channel_id=1, source_target_pairs={{1,2},{2,1},{3,0},{0,3},{5,6},{6,5},{7,4},{4,7},{9,10},{10,9},{11,... | collective-permute-start | bytes 49160 | tf_op jit(solution)/shard_map/ppermute | solution.py:513
  29.3 2.9 %collective-permute-start.9 = (bf16[4,16,128]{2,1,0:T(8,128)(2,1)S(1)}, bf16[4,16,128]{2,1,0:T(8,128)(2,1)S(1)}, u32[]{:S(2)}, u32[]{:S(2)}) collective-permute-start(bf16[4,16,128]{2,1,0:T(8,128)(2,1)S(1)} %get-tuple-element.78), channel_id=1, source_target_pairs={{0,1},{1,0},{2,3},{3,2},{4,5},{5,4},{6,7},{7,6},{8,9},{9,8},{10,11... | collective-permute-start | bytes 49160 | tf_op jit(solution)/shard_map/ppermute | solution.py:513
  32.9 3.6 %collective-permute-start.11 = (bf16[16,32,128]{2,1,0:T(8,128)(2,1)S(1)}, bf16[16,32,128]{2,1,0:T(8,128)(2,1)S(1)}, u32[]{:S(2)}, u32[]{:S(2)}) collective-permute-start(bf16[16,32,128]{2,1,0:T(8,128)(2,1)S(1)} %get-tuple-element.85), channel_id=1, source_target_pairs={{0,4},{4,0},{8,12},{12,8},{16,20},{20,16},{24,28},{28,24},{1,5},{5... | collective-permute-start | bytes 393224 | tf_op jit(solution)/shard_map/ppermute | solution.py:513
  34.6 7.1 %collective-permute-start.10 = (bf16[16,32,128]{2,1,0:T(8,128)(2,1)S(1)}, bf16[16,32,128]{2,1,0:T(8,128)(2,1)S(1)}, u32[]{:S(2)}, u32[]{:S(2)}) collective-permute-start(bf16[16,32,128]{2,1,0:T(8,128)(2,1)S(1)} %get-tuple-element.85), channel_id=1, source_target_pairs={{4,8},{8,4},{12,16},{16,12},{20,24},{24,20},{5,9},{9,5},{13,17},{1... | collective-permute-start | bytes 393224 | tf_op jit(solution)/shard_map/ppermute | solution.py:513

commit v5 on v4

--- a/solution.py
+++ b/solution.py
@@ -43,21 +43,20 @@
     return [pltpu.with_memory_space_constraint(value, pltpu.HBM) for value in values]
 
 
-def lat_conv_row(row, low, own, high):
+def lat_sum(parts, row, first, height, start=None):
     taps = lat_taps()
-    height = own.shape[0]
-    acc = None
-    for j in range(-REACH, REACH + 1):
-        source = row + j
-        if source < 0:
-            part = low[source + REACH]
-        elif source < height:
-            part = own[source]
-        else:
-            part = high[source - height]
-        term = taps[j + REACH] * part
-        acc = term if acc is None else acc + term
+    acc = start
+    for k in range(height):
+        j = first + k - row
+        if abs(j) <= REACH:
+            term = taps[j + REACH] * parts[k]
+            acc = term if acc is None else acc + term
     return acc
+
+
+def lat_rims(row, part, halos, height):
+    low = lat_sum(halos.at[0], row, -REACH, REACH, part)
+    return lat_sum(halos.at[1], row, height, REACH, low)
 
 
 def fill_padded(padded, far, own, close):
@@ -81,15 +80,12 @@
     return value.astype(jnp.bfloat16).astype(jnp.float32)
 
 
-def first_kernel(
-    radiance, block_owner, channel_count, control, slabs, held, halved, owners, counts, rows, tables, sems
-):
+def slabs_kernel(radiance, block_owner, channel_count, slabs, owners, counts, rows, tables, sems):
     recv_most = radiance.shape[0]
     moves = [
         pltpu.make_async_copy(radiance, slabs.at[pl.ds(0, recv_most)], sems.at[0]),
         pltpu.make_async_copy(block_owner, owners, sems.at[1]),
         pltpu.make_async_copy(channel_count, counts, sems.at[2]),
-        pltpu.make_async_copy(control, held, sems.at[3]),
     ]
     for move in moves:
         move.start()
@@ -99,22 +95,35 @@
     rows[0:1, 0 : owners.shape[1]] = owners[...].astype(jnp.float32)
     rows[1:2, 0 : counts.shape[1]] = counts[...].astype(jnp.float32)
     tables[...] = rows[...].astype(jnp.bfloat16)
-    last = pltpu.make_async_copy(tables, slabs.at[recv_most], sems.at[4])
+    last = pltpu.make_async_copy(tables, slabs.at[recv_most], sems.at[3])
     last.start()
-    moves[3].wait()
-    halved[...] = held[...].astype(jnp.bfloat16)
     moves[0].wait()
     last.wait()
 
 
 def prepare_kernel(
-    lon_width, background, block_cells, block_owner, taps, turned, plan, widths, cells, owners, rows, field, sems
+    lon_width,
+    background,
+    block_cells,
+    block_owner,
+    control,
+    taps,
+    turned,
+    plan,
+    own_part,
+    widths,
+    cells,
+    owners,
+    field,
+    band,
+    sems,
 ):
     moves = [
         pltpu.make_async_copy(lon_width, widths, sems.at[0]),
         pltpu.make_async_copy(block_cells, cells, sems.at[1]),
         pltpu.make_async_copy(block_owner, owners, sems.at[2]),
         pltpu.make_async_copy(background, field, sems.at[3]),
+        pltpu.make_async_copy(control, band, sems.at[4]),
     ]
     for move in moves:
         move.start()
@@ -123,31 +132,7 @@
     per_tile = height // tiles
     groups = width // BLOCK_COLS
     rim = REACH // BLOCK_COLS
-    slot_count = cells.shape[0]
-
-    moves[1].wait()
-    moves[2].wait()
-
-    def outer(slot):
-        group = cells[slot] % groups
-        return ((group < rim) | (group >= groups - rim)) & (owners[slot] >= 0)
-
-    outer_count = lax.fori_loop(
-        0, slot_count, lambda slot, total: total + jnp.where(outer(slot), 1, 0), 0, unroll=8
-    )
-
-    def place(slot, nexts):
-        first, second = nexts
-        hit = outer(slot)
-        position = jnp.where(hit, first, second)
-        rows[0, position] = cells[slot]
-        rows[1, position] = slot
-        return first + jnp.where(hit, 1, 0), second + jnp.where(hit, 0, 1)
-
-    lax.fori_loop(0, slot_count, place, (0, outer_count), unroll=8)
-    rows[2, 0] = outer_count
-    plan_out = pltpu.make_async_copy(rows, plan, sems.at[4])
-    plan_out.start()
+    slot_count = cells.shape[1]
 
     lane_row = lax.broadcasted_iota(jnp.int32, (1, LANES), 1) // levels
     steps = lax.broadcasted_iota(jnp.int32, (taps.shape[1], LANES), 0)
@@ -162,11 +147,38 @@
         raw = jnp.exp(-dist * dist / (2.0 * spread * spread))
         norm = jnp.sum(weight * raw * raw, axis=0, keepdims=True)
         taps[tile] = raw / jnp.sqrt(norm)
+
+    moves[1].wait()
+    moves[2].wait()
+    rows = lax.broadcasted_iota(jnp.int32, (slot_count, slot_count), 0)
+    lanes = lax.broadcasted_iota(jnp.int32, (slot_count, slot_count), 1)
+    group = cells[...] % groups
+    outer = ((group < rim) | (group >= groups - rim)) & (owners[...] >= 0)
+    outer_here = jnp.where(outer, 1, 0)
+    outer_count = jnp.sum(outer_here, axis=1, keepdims=True)
+    earlier = jnp.sum(jnp.where(lanes < rows, outer_here, 0), axis=1, keepdims=True)
+    here = jnp.sum(jnp.where(lanes == rows, outer_here, 0), axis=1, keepdims=True)
+    cell = jnp.sum(jnp.where(lanes == rows, cells[...], 0), axis=1, keepdims=True)
+    position = jnp.where(here == 1, earlier, outer_count + rows[:, 0:1] - earlier)
+    at = lax.broadcasted_iota(jnp.int32, (slot_count, LANES), 1)
+    hit = position == at
+    slot = lax.broadcasted_iota(jnp.int32, (slot_count, LANES), 0)
+    plan[...] = jnp.zeros_like(plan)
+    plan[0:1, :] = jnp.sum(jnp.where(hit, cell, 0), axis=0, keepdims=True)
+    plan[1:2, :] = jnp.sum(jnp.where(hit, slot, 0), axis=0, keepdims=True)
+    plan[2:3, :] = jnp.broadcast_to(outer_count, (1, LANES))
+
     moves[3].wait()
     for tile in range(tiles):
         block = field[tile * per_tile : (tile + 1) * per_tile].reshape(per_tile * levels, width)
         turned[tile] = jnp.transpose(block)
-    plan_out.wait()
+    moves[4].wait()
+    for row in range(height):
+        own_part[row] = lat_sum(band, row, 0, height)
+
+
+def swap_bits(count):
+    return list(range(count.bit_length() - 2, 0, -1))
 
 
 def routing(recv_most, slot_count, tables, table):
@@ -178,8 +190,13 @@
     diagonal = rows == lanes
     zero = jnp.zeros((slot_count, LANES), jnp.int32)
 
+    bits = swap_bits(count)
+
     def device_of(k):
-        return here ^ jnp.where(k < half, 2 * k, 2 * (k - half) + 1)
+        apart = jnp.where(k < half, 0, 1)
+        for place, bit in enumerate(bits):
+            apart = apart + (((k >> place) & 1) << bit)
+        return here ^ apart
 
     def line(k, row):
         return tables[k].astype(jnp.float32)[row : row + 1].astype(jnp.int32)
@@ -200,8 +217,10 @@
 
     kept = jnp.sum(lax.fori_loop(0, count, counted, zero, unroll=unroll), axis=1, keepdims=True)
     apart = owner ^ here
-    place = (apart >> 1) + (apart & 1) * half
-    target = jnp.where(owner >= 0, place * (recv_most + 1) + arrival, 0)
+    entry = (apart & 1) * half
+    for place, bit in enumerate(bits):
+        entry = entry + (((apart >> bit) & 1) << place)
+    target = jnp.where(owner >= 0, entry * (recv_most + 1) + arrival, 0)
     table[...] = jnp.zeros_like(table)
     for row, column in enumerate((target, kept)):
         table[row : row + 1, :] = jnp.sum(jnp.where(diagonal, column, 0), axis=0, keepdims=True)
@@ -222,15 +241,14 @@
     return jnp.where(odd, high, low), jnp.where(odd, low, high)
 
 
-def lat_smooth_kernel(far, close, own, smoothed, to_far, to_close, halos):
+def lat_smooth_kernel(far, close, own_part, smoothed, to_far, to_close, halos):
     tiles = smoothed.shape[0]
-    height, levels, width = own.shape
+    height, levels, width = own_part.shape
     per_tile = height // tiles
     halos[0], halos[1] = sides(far[...], close[...], "lat")
     for tile in range(tiles):
-        rows = [
-            lat_conv_row(tile * per_tile + sub, halos.at[0], own, halos.at[1]) for sub in range(per_tile)
-        ]
+        rows = range(tile * per_tile, (tile + 1) * per_tile)
+        rows = [lat_rims(row, own_part[row], halos, height) for row in rows]
         turned = jnp.transpose(jnp.concatenate(rows, axis=0))
         smoothed[tile] = turned
         to_far[tile], to_close[tile] = split_sides(turned[0:REACH], turned[width - REACH : width], "lon")
@@ -497,10 +515,20 @@
         halved[tile * per_tile : (tile + 1) * per_tile] = rows.astype(jnp.bfloat16)
 
 
-def lat_back_kernel(far, close, own, control, gradient, halos):
+def own_back_kernel(back, control, own_part, held, sem):
+    control_in = pltpu.make_async_copy(control, held, sem)
+    control_in.start()
+    control_in.wait()
+    height = back.shape[0]
+    for row in range(height):
+        own_part[row] = lat_sum(back, row, 0, height, held[row])
+
+
+def lat_back_kernel(far, close, own_part, gradient, halos):
     halos[0], halos[1] = sides(far[...], close[...], "lat")
-    for row in range(own.shape[0]):
-        gradient[row] = control[row] + lat_conv_row(row, halos.at[0], own, halos.at[1])
+    height = own_part.shape[0]
+    for row in range(height):
+        gradient[row] = lat_rims(row, own_part[row], halos, height)
 
 
 def exchange(to_far, to_close, axis, periodic):
@@ -544,57 +572,67 @@
     halves = channels // LANES
     radiance = radiance.T.reshape(recv_most, BLOCK_COLS, halves, LANES)
     radiance = jnp.swapaxes(radiance, 1, 2).reshape(recv_most, slab_rows, LANES)
-    slabs, held, halved = call(
-        first_kernel,
-        (
-            shape((recv_most + 1, slab_rows, LANES), bf16),
-            shape(control.shape, f32),
-            shape(control.shape, bf16),
-        ),
-        [HBM] * 4,
-        (HBM, VMEM, VMEM),
+    slabs = call(
+        slabs_kernel,
+        shape((recv_most + 1, slab_rows, LANES), bf16),
+        [HBM] * 3,
+        HBM,
         0,
-        16 * field,
+        4 * channels * columns,
         scratch=(
             pltpu.VMEM((1, slot_count), i32),
             pltpu.VMEM((1, recv_most), i32),
             pltpu.VMEM((slab_rows, LANES), f32),
             pltpu.VMEM((slab_rows, LANES), bf16),
-            pltpu.SemaphoreType.DMA((5,)),
-        ),
-        name="slabs_halves",
-    )(*pinned(radiance, block_owner.reshape(1, slot_count), channel_count.reshape(1, recv_most), control))
-
-    cells = block_cells.reshape(slot_count)
-    taps, turned, plan = call(
+            pltpu.SemaphoreType.DMA((4,)),
+        ),
+        name="slabs",
+    )(*pinned(radiance, block_owner.reshape(1, slot_count), channel_count.reshape(1, recv_most)))
+
+    band = pltpu.VMEM((height, levels, width), f32)
+    taps, turned, plan, own_part = call(
         prepare_kernel,
         (
             shape((tiles, 24, LANES), f32),
             shape((tiles, width, LANES), f32),
             shape((8, LANES), i32),
-        ),
-        [HBM] * 4,
-        (VMEM, VMEM, HBM),
-        0,
-        8 * field,
+            shape(control.shape, f32),
+        ),
+        [HBM] * 5,
+        (VMEM,) * 4,
+        conv_flops // 2,
+        12 * field,
         scratch=(
             pltpu.SMEM((height,), i32),
-            pltpu.SMEM((slot_count,), i32),
-            pltpu.SMEM((slot_count,), i32),
-            pltpu.SMEM((8, LANES), i32),
-            pltpu.VMEM((height, levels, width), f32),
+            pltpu.VMEM((1, slot_count), i32),
+            pltpu.VMEM((1, slot_count), i32),
+            band,
+            band,
             pltpu.SemaphoreType.DMA((5,)),
         ),
         name="taps_background",
-    )(*pinned(lon_width, background, cells, block_owner.reshape(slot_count)))
+    )(
+        *pinned(
+            lon_width,
+            background,
+            block_cells.reshape(1, slot_count),
+            block_owner.reshape(1, slot_count),
+            control,
+        )
+    )
+
+    far, close = exchange(control, control, "lat", False)
     lat_count = lax.axis_size("lat")
     near = [slabs]
-    for bit in range(1, lat_count.bit_length() - 1):
-        held_sets = near[0] if len(near) == 1 else jnp.concatenate(near, axis=0)
-        near = [held_sets, lax.ppermute(held_sets, "lat", [(i, i ^ (1 << bit)) for i in range(lat_count)])]
-        if bit == 1:
-            far, close = exchange(halved, halved, "lat", False)
+    for step, bit in enumerate(swap_bits(lat_count)):
+        if len(near) > 2:
+            half = len(near) // 2
+            near = [jnp.concatenate(near[:half], axis=0), jnp.concatenate(near[half:], axis=0)]
+        if step == 1:
             near[1], far, close, taps = lax.optimization_barrier((near[1], far, close, taps))
+        pairs = [(i, i ^ (1 << bit)) for i in range(lat_count)]
+        near = near + [lax.ppermute(part, "lat", pairs) for part in near]
+    near = [jnp.concatenate(near[:-1], axis=0), near[-1]]
 
     halos = pltpu.VMEM((2, REACH, levels, width), f32)
     smoothed, to_far, to_close = call(
@@ -606,7 +644,7 @@
         16 * field,
         scratch=(halos,),
         name="lat_smooth",
-    )(far, close, held)
+    )(far, close, own_part)
     far, close = exchange(to_far, to_close, "lon", True)
 
     outer_slots = 3 * slot_count // 8
@@ -633,7 +671,7 @@
     profile, *rest = call(
         functools.partial(inner_forward_kernel, outer_slots),
         (shape((tiles * width, LANES), f32),) + state_shapes(late_rows) + weight_shapes,
-        [HBM] + [VMEM] * 3 + [HBM] * 6,
+        [ANY] + [VMEM] * 3 + [HBM] * 6,
         (VMEM,) * 10,
         late_rows * row_flops,
         4 * 1024 * 1024,
@@ -645,7 +683,7 @@
         ),
         name="inner_forward",
     )(
-        *pinned(plan),
+        plan,
         smoothed,
         turned,
         taps,
@@ -665,7 +703,7 @@
     states = call(
         functools.partial(outer_forward_kernel, per_tile),
         state_shapes(outer_rows) + state_shapes(late_rows),
-        [HBM] + [VMEM] * 12,
+        [ANY] + [VMEM] * 12,
         (VMEM,) * 6,
         outer_rows * row_flops,
         4 * 1024 * 1024,
@@ -678,7 +716,7 @@
             pltpu.SemaphoreType.DMA,
         ),
         name="outer_forward",
-    )(*pinned(plan), far, close, smoothed, turned, taps, profile, *weights)
+    )(plan, far, close, smoothed, turned, taps, profile, *weights)
 
     slabs = [*near, *across]
     held_slabs, table, sens, to_far, to_close = call(
@@ -690,7 +728,7 @@
             shape((tiles, REACH, LANES), bf16),
             shape((tiles, REACH, LANES), bf16),
         ),
-        [HBM] + [ANY] * len(slabs) + [VMEM] * 9,
+        [ANY] + [ANY] * len(slabs) + [VMEM] * 9,
         (VMEM,) * 5,
         outer_rows * row_flops,
         4 * 1024 * 1024,
@@ -704,13 +742,13 @@
             pltpu.SemaphoreType.DMA((lat_count + len(slabs) + 2,)),
         ),
         name="outer_backward",
-    )(*pinned(plan), *slabs, *weights[:3], *states)
+    )(plan, *slabs, *weights[:3], *states)
     far, close = exchange(to_far, to_close, "lon", True)
 
     landing = call(
         functools.partial(inner_backward_kernel, per_tile, outer_slots),
         shape((tiles, width, LANES), f32),
-        [HBM, VMEM, ANY] + [VMEM] * 7,
+        [ANY, VMEM, ANY] + [VMEM] * 7,
         VMEM,
         late_rows * row_flops,
         4 * 1024 * 1024,
@@ -723,7 +761,7 @@
             pltpu.SemaphoreType.DMA((2,)),
         ),
         name="inner_backward",
-    )(*pinned(plan), held_slabs, table, sens, *weights[:3], *inner_states)
+    )(plan, held_slabs, table, sens, *weights[:3], *inner_states)
 
     back, halved = call(
         lon_back_kernel,
@@ -736,17 +774,27 @@
         name="lon_back",
     )(far, close, landing, taps)
     far, close = exchange(halved, halved, "lat", False)
+    own_part = call(
+        own_back_kernel,
+        shape((height, levels, width), f32),
+        [VMEM, HBM],
+        VMEM,
+        conv_flops // 2,
+        12 * field,
+        scratch=(band, pltpu.SemaphoreType.DMA),
+        name="lat_back_own",
+    )(back, *pinned(control))
 
     return call(
         lat_back_kernel,
         shape((height, levels, width), f32),
-        [VMEM] * 4,
+        [VMEM] * 3,
         VMEM,
-        conv_flops,
-        20 * field,
+        conv_flops // 2,
+        16 * field,
         scratch=(halos,),
         name="lat_back",
-    )(far, close, back, held)
+    )(far, close, own_part)
 
 
 def solution(mesh):

time: 43.4 us -> 44.6 us (1.028)
  starting transfers between devices: 17.1 us -> 19.6 us
  waiting for transfers between devices: 8.57 us -> 6.97 us
    ppermute x4, waiting for transfers between devices: 8.28 us -> 3.19 us  [exchange(): lax.ppermute(to_far, axis, far)]
    ppermute x2 -> x3, waiting for transfers between devices: 0.28 us -> 3.77 us  [shards(): near = near + [lax.ppermute(part, 'lat', pairs) for part in near]]
    ppermute x4, starting transfers between devices: 9.41 us -> 11.5 us  [exchange(): lax.ppermute(to_far, axis, far)]
    ppermute x2 -> x3, starting transfers between devices: 2.58 us -> 3.73 us  [shards(): near = near + [lax.ppermute(part, 'lat', pairs) for part in near]]
    pallas_call x1, Pallas kernels: 2.37 us -> 1.45 us  [shards(): call(prepare_kernel, (shape((tiles, 24, LANES), f32), shape((tiles, width...]
    ppermute x2, starting transfers between devices: 2.42 us -> 1.56 us  [shards(): lax.ppermute(part, 'lat', [(i, i ^ 1) for i in range(lat_count)])]
    pallas_call x2 -> x3, Pallas kernels: 2.5 us -> 3.28 us  [the longest x1 1.26 us: shards(): call(own_back_kernel, shape((height, levels, width), f32), [VMEM, HBM], V...]
    pallas_call x1, Pallas kernels: 2.76 us -> 3.46 us  [shards(): call(functools.partial(outer_backward_kernel, per_tile, len(slabs)), (sha...]
  transfers between devices with their start and end apart: 12 -> 13, of which waited for: 3 -> 2; matrix products, arithmetic and copies ran while one was open for 0% -> 0% of each run, Pallas kernels for 26% -> 27%
where the time goes in v5:
time: 44.6 us; the launch traced here: 44.1 us
  starting transfers between devices  19.6 us (44%)
  Pallas kernels  17.3 us (39%)
  waiting for transfers between devices  6.97 us (16%)
    ppermute x4, starting transfers between devices, exchange(): lax.ppermute(to_far, axis, far)  11.5 us
    ppermute x3, waiting for transfers between devices, shards(): near = near + [lax.ppermute(part, 'lat', pairs) for part in near]  3.77 us
    ppermute x3, starting transfers between devices, shards(): near = near + [lax.ppermute(part, 'lat', pairs) for part in near]  3.73 us
    pallas_call x1, Pallas kernels, shards(): call(functools.partial(inner_forward_kernel, outer_slots), (shape((tiles...  3.51 us
    pallas_call x1, Pallas kernels, shards(): call(functools.partial(outer_backward_kernel, per_tile, len(slabs)), (sha...  3.46 us
    ppermute x4, waiting for transfers between devices, exchange(): lax.ppermute(to_far, axis, far)  3.19 us
    ppermute x4, starting transfers between devices, exchange(): lax.ppermute(to_close, axis, close)  2.81 us
    pallas_call x1, Pallas kernels, shards(): call(functools.partial(inner_backward_kernel, per_tile, outer_slots), sha...  2.78 us
  transfers between devices with their start and end apart: 13, of which 2 were waited for; matrix products, arithmetic and copies ran while one was open for 0% of the time, Pallas kernels for 27%

profile of v5, /device:TPU:1, one launch (start us, length us, event | category | flops | bytes accessed | tf_op | source)
XLA Modules:
  0.0 44.1 jit_solution(5600975336567752246)
XLA Ops:
  0.0 4.5 %collective-permute-start.1 = (f32[16,32,128]{2,1,0:T(8,128)}, f32[16,32,128]{2,1,0:T(8,128)S(1)}, u32[]{:S(2)}, u32[]{:S(2)}) collective-permute-start(f32[16,32,128]{2,1,0:T(8,128)} %control.3), channel_id=1, source_target_pairs={{4,8},{8,4},{12,16},{16,12},{20,24},{24,20},{5,9},{9,5},{13,17},{1... | collective-permute-start | bytes 786440 | tf_op jit(solution)/shard_map/ppermute | solution.py:541
  4.5 0.1 collective-permute-start.2
  4.6 0.9 %slabs.1 = bf16[37,16,128]{2,1,0:T(8,128)(2,1)S(1)} custom-call(bf16[36,16,128]{2,1,0:T(8,128)(2,1)} %bitcast.13, s32[1,64]{1,0:T(1,128)} %bitcast.14, s32[1,36]{1,0:T(1,128)} %bitcast.16), custom_call_target="tpu_custom_call" | custom-call | bytes 294912 | tf_op jit(solution)/shard_map/slabs/pallas_call | solution.py:575
  5.5 1.3 %collective-permute-start = (bf16[37,16,128]{2,1,0:T(8,128)(2,1)S(1)}, bf16[37,16,128]{2,1,0:T(8,128)(2,1)S(1)}, u32[]{:S(2)}, u32[]{:S(2)}) collective-permute-start(bf16[37,16,128]{2,1,0:T(8,128)(2,1)S(1)} %slabs.1), channel_id=1, source_target_pairs={{0,16},{4,20},{8,24},{12,28},{16,0},{20,4},{24,8},{28,12},{1,17},{... | collective-permute-start | bytes 454664 | tf_op jit(solution)/shard_map/ppermute | solution.py:634
  6.8 0.1 collective-permute-start.3
  7.0 1.5 %taps_background.1 = (f32[4,24,128]{2,1,0:T(8,128)S(1)}, f32[4,128,128]{2,1,0:T(8,128)S(1)}, s32[8,128]{1,0:T(8,128)S(1)}, f32[16,32,128]{2,1,0:T(8,128)S(1)}) custom-call(s32[16]{0:T(128)} %lon_width.1, f32[16,32,128]{2,1,0:T(8,128)} %background.1, s32[1,64]{1,0:T(1,128)} %bitcast.17, s32[1,64]{1,0:T(1,128)} %bitcast.15, f32[16,32,128]{2,1,0:T(8,128)} %control.3), custom_call_target="tpu_custom_call" | custom-call | flops 2162688 | bytes 786432 | tf_op jit(solution)/shard_map/taps_background/pallas_call | solution.py:593
  8.4 3.8 %collective-permute-done = bf16[37,16,128]{2,1,0:T(8,128)(2,1)S(1)} collective-permute-done((bf16[37,16,128]{2,1,0:T(8,128)(2,1)S(1)}, bf16[37,16,128]{2,1,0:T(8,128)(2,1)S(1)}, u32[]{:S(2)}, u32[]{:S(2)}) %collective-permute-start) | collective-permute-done | bytes 151584 | tf_op jit(solution)/shard_map/ppermute | solution.py:634
  12.2 0.4 lat_smooth.1
  12.6 3.4 %collective-permute-start.5 = (f32[4,16,128]{2,1,0:T(8,128)S(1)}, f32[4,16,128]{2,1,0:T(8,128)S(1)}, u32[]{:S(2)}, u32[]{:S(2)}) collective-permute-start(f32[4,16,128]{2,1,0:T(8,128)S(1)} %get-tuple-element.50), channel_id=1, source_target_pairs={{1,2},{2,1},{3,0},{0,3},{5,6},{6,5},{7,4},{4,7},{9,10},{10,9},{11,... | collective-permute-start | bytes 98312 | tf_op jit(solution)/shard_map/ppermute | solution.py:541
  16.0 2.3 %collective-permute-start.4 = (bf16[37,16,128]{2,1,0:T(8,128)(2,1)S(1)}, bf16[37,16,128]{2,1,0:T(8,128)(2,1)S(1)}, u32[]{:S(2)}, u32[]{:S(2)}) collective-permute-start(bf16[37,16,128]{2,1,0:T(8,128)(2,1)S(1)} %collective-permute-done), channel_id=1, source_target_pairs={{0,8},{4,12},{8,0},{12,4},{16,24},{20,28},{24,16},{28,20},{1,9},{5... | collective-permute-start | bytes 454664 | tf_op jit(solution)/shard_map/ppermute | solution.py:634
  18.4 3.5 %inner_forward.1 = (f32[512,128]{1,0:T(8,128)S(1)}, bf16[320,1024]{1,0:T(8,128)(2,1)S(1)}, bf16[320,1024]{1,0:T(8,128)(2,1)S(1)}, f32[320,256]{1,0:T(8,128)S(1)}...) custom-call(s32[8,128]{1,0:T(8,128)S(1)} %get-tuple-element.44.plan,, ...), custom_call_target="tpu_custom_call" | custom-call | flops 922746880 | bytes 4194304 | tf_op jit(solution)/shard_map/inner_forward/pallas_call | solution.py:671
  21.9 1.5 %collective-permute-start.7 = (bf16[111,16,128]{2,1,0:T(8,128)(2,1)S(1)}, bf16[111,16,128]{2,1,0:T(8,128)(2,1)S(1)}, u32[]{:S(2)}, u32[]{:S(2)}) collective-permute-start(bf16[111,16,128]{2,1,0:T(8,128)(2,1)S(1)} %pad_maximum_fusion.refs_0_), channel_id=1, source_target_pairs={{0,4},{4,0},{8,12},{12,8},{16,20},{20,16},{24,28},{28,24},{1,5},{5... | collective-permute-start | bytes 1363976 | tf_op jit(solution)/shard_map/ppermute | solution.py:701
  23.4 0.1 collective-permute-start.8
  23.5 1.7 %outer_forward.1 = (bf16[192,1024]{1,0:T(8,128)(2,1)S(1)}, bf16[192,1024]{1,0:T(8,128)(2,1)S(1)}, f32[192,256]{1,0:T(8,128)S(1)}, bf16[320,1024]{1,0:T(8,128)(2,...) custom-call(s32[8,128]{1,0:T(8,128)S(1)} %get-tuple-element.44.plan, ...), custom_call_target="tpu_custom_call" | custom-call | flops 553648128 | bytes 4194304 | tf_op jit(solution)/shard_map/outer_forward/pallas_call | solution.py:703
  25.2 3.5 %outer_backward.1 = (bf16[296,16,128]{2,1,0:T(8,128)(2,1)S(1)}, s32[8,128]{1,0:T(8,128)S(1)}, f32[512,128]{1,0:T(8,128)S(1)}, bf16[4,16,128]{2,1,0:T(8,128)(2,1)S(1)}, bf16[4,16,128]{2,1,0:T(8,128)(2,1)S(1)}) custom-call(s32[8,128]{1,0:T(8,128)S(1)} %get-tuple-element.44.plan, bf16[111,16,128]{2,1,0:T(8,128)(2,1)S(1)} %pad_maximum_fusion.refs_0_, ...), custom_call_target="tpu_custom_call" | custom-call | flops 553648128 | bytes 4194304 | tf_op jit(solution)/shard_map/outer_backward/pallas_call | solution.py:722
  28.7 0.7 %collective-permute-start.9 = (bf16[4,16,128]{2,1,0:T(8,128)(2,1)S(1)}, bf16[4,16,128]{2,1,0:T(8,128)(2,1)S(1)}, u32[]{:S(2)}, u32[]{:S(2)}) collective-permute-start(bf16[4,16,128]{2,1,0:T(8,128)(2,1)S(1)} %get-tuple-element.73), channel_id=1, source_target_pairs={{1,2},{2,1},{3,0},{0,3},{5,6},{6,5},{7,4},{4,7},{9,10},{10,9},{11,... | collective-permute-start | bytes 49160 | tf_op jit(solution)/shard_map/ppermute | solution.py:541
  29.4 1.2 %collective-permute-start.10 = (bf16[4,16,128]{2,1,0:T(8,128)(2,1)S(1)}, bf16[4,16,128]{2,1,0:T(8,128)(2,1)S(1)}, u32[]{:S(2)}, u32[]{:S(2)}) collective-permute-start(bf16[4,16,128]{2,1,0:T(8,128)(2,1)S(1)} %get-tuple-element.74), channel_id=1, source_target_pairs={{0,1},{1,0},{2,3},{3,2},{4,5},{5,4},{6,7},{7,6},{8,9},{9,8},{10,11... | collective-permute-start | bytes 49160 | tf_op jit(solution)/shard_map/ppermute | solution.py:541
  30.6 2.8 %inner_backward.1.own = f32[4,128,128]{2,1,0:T(8,128)S(1)} custom-call(s32[8,128]{1,0:T(8,128)S(1)} %get-tuple-element.44.plan, bf16[296,16,128]{2,1,0:T(8,128)(2,1)S(1)} %get-tuple-element.75.held, s32[8,128]{1,0:T(8,128)S(1)} %get-tuple-element.76.table_rows, f32[512,128]{1,0:T(8,128)S(1)} %get-tuple-element.77.sens, ...), custom_call_target="tpu_custom_call" | custom-call | flops 922746880 | bytes 4194304 | tf_op jit(solution)/shard_map/inner_backward/pallas_call | solution.py:748
  33.4 0.7 %lon_back.1 = (f32[16,32,128]{2,1,0:T(8,128)S(1)}, bf16[16,32,128]{2,1,0:T(8,128)(2,1)S(1)}) custom-call(bf16[4,16,128]{2,1,0:T(8,128)(2,1)S(1)} %collective-permute-done.9.far, bf16[4,16,128]{2,1,0:T(8,128)(2,1)S(1)} %collective-permute-done.10.close, f32[4,128,128]{2,1,0:T(8,128)S(1)} %inner_backward.1.own, f32[4,24,128]{2,1,0:T(8,128)S(1)} %get-tuple-element.54.taps), custom_call_target="tpu_custom_call" | custom-call | flops 4325376 | bytes 524288 | tf_op jit(solution)/shard_map/lon_back/pallas_call | solution.py:766
  34.1 1.5 %collective-permute-start.12 = (bf16[16,32,128]{2,1,0:T(8,128)(2,1)S(1)}, bf16[16,32,128]{2,1,0:T(8,128)(2,1)S(1)}, u32[]{:S(2)}, u32[]{:S(2)}) collective-permute-start(bf16[16,32,128]{2,1,0:T(8,128)(2,1)S(1)} %get-tuple-element.81), channel_id=1, source_target_pairs={{0,4},{4,0},{8,12},{12,8},{16,20},{20,16},{24,28},{28,24},{1,5},{5... | collective-permute-start | bytes 393224 | tf_op jit(solution)/shard_map/ppermute | solution.py:541
  35.6 3.0 %collective-permute-start.11 = (bf16[16,32,128]{2,1,0:T(8,128)(2,1)S(1)}, bf16[16,32,128]{2,1,0:T(8,128)(2,1)S(1)}, u32[]{:S(2)}, u32[]{:S(2)}) collective-permute-start(bf16[16,32,128]{2,1,0:T(8,128)(2,1)S(1)} %get-tuple-element.81), channel_id=1, source_target_pairs={{4,8},{8,4},{12,16},{16,12},{20,24},{24,20},{5,9},{9,5},{13,17},{1... | collective-permute-start | bytes 393224 | tf_op jit(solution)/shard_map/ppermute | solution.py:541
  38.6 1.3 %lat_back_own.1.own_part = f32[16,32,128]{2,1,0:T(8,128)S(1)} custom-call(f32[16,32,128]{2,1,0:T(8,128)S(1)} %get-tuple-element.82.back, f32[16,32,128]{2,1,0:T(8,128)} %control.3), custom_call_target="tpu_custom_call" | custom-call | flops 2162688 | bytes 786432 | tf_op jit(solution)/shard_map/lat_back_own/pallas_call | solution.py:777
  39.9 3.2 %collective-permute-done.11.far = bf16[16,32,128]{2,1,0:T(8,128)(2,1)S(1)} collective-permute-done((bf16[16,32,128]{2,1,0:T(8,128)(2,1)S(1)}, bf16[16,32,128]{2,1,0:T(8,128)(2,1)S(1)}, u32[]{:S(2)}, u32[]{:S(2)}) %collective-permute-start.11) | collective-permute-done | bytes 131104 | tf_op jit(solution)/shard_map/ppermute | solution.py:541
  43.0 1.1 %lat_back.1 = f32[16,32,128]{2,1,0:T(8,128)} custom-call(bf16[16,32,128]{2,1,0:T(8,128)(2,1)S(1)} %collective-permute-done.11.far, bf16[16,32,128]{2,1,0:T(8,128)(2,1)S(1)} %collective-permute-done.12.close, f32[16,32,128]{2,1,0:T(8,128)S(1)} %lat_back_own.1.own_part), custom_call_target="tpu_custom_call" | custom-call | flops 2162688 | bytes 1048576 | tf_op jit(solution)/shard_map/lat_back/pallas_call | solution.py:788
  (13 shorter events, 0.1 us)
Async XLA Ops:
  0.0 12.2 %collective-permute-start.1 = (f32[16,32,128]{2,1,0:T(8,128)}, f32[16,32,128]{2,1,0:T(8,128)S(1)}, u32[]{:S(2)}, u32[]{:S(2)}) collective-permute-start(f32[16,32,128]{2,1,0:T(8,128)} %control.3), channel_id=1, source_target_pairs={{4,8},{8,4},{12,16},{16,12},{20,24},{24,20},{5,9},{9,5},{13,17},{1... | collective-permute-start | bytes 786440 | tf_op jit(solution)/shard_map/ppermute | solution.py:541
  4.5 7.7 %collective-permute-start.2 = (f32[16,32,128]{2,1,0:T(8,128)}, f32[16,32,128]{2,1,0:T(8,128)S(1)}, u32[]{:S(2)}, u32[]{:S(2)}) collective-permute-start(f32[16,32,128]{2,1,0:T(8,128)} %control.3), channel_id=1, source_target_pairs={{0,4},{4,0},{8,12},{12,8},{16,20},{20,16},{24,28},{28,24},{1,5},{5... | collective-permute-start | bytes 786440 | tf_op jit(solution)/shard_map/ppermute | solution.py:541
  5.5 6.6 %collective-permute-start = (bf16[37,16,128]{2,1,0:T(8,128)(2,1)S(1)}, bf16[37,16,128]{2,1,0:T(8,128)(2,1)S(1)}, u32[]{:S(2)}, u32[]{:S(2)}) collective-permute-start(bf16[37,16,128]{2,1,0:T(8,128)(2,1)S(1)} %slabs.1), channel_id=1, source_target_pairs={{0,16},{4,20},{8,24},{12,28},{16,0},{20,4},{24,8},{28,12},{1,17},{... | collective-permute-start | bytes 454664 | tf_op jit(solution)/shard_map/ppermute | solution.py:634
  6.8 11.5 %collective-permute-start.3 = (bf16[37,16,128]{2,1,0:T(8,128)(2,1)S(1)}, bf16[37,16,128]{2,1,0:T(8,128)(2,1)S(1)}, u32[]{:S(2)}, u32[]{:S(2)}) collective-permute-start(bf16[37,16,128]{2,1,0:T(8,128)(2,1)S(1)} %slabs.1), channel_id=1, source_target_pairs={{0,8},{4,12},{8,0},{12,4},{16,24},{20,28},{24,16},{28,20},{1,9},{5... | collective-permute-start | bytes 454664 | tf_op jit(solution)/shard_map/ppermute | solution.py:634
  12.6 9.3 %collective-permute-start.5 = (f32[4,16,128]{2,1,0:T(8,128)S(1)}, f32[4,16,128]{2,1,0:T(8,128)S(1)}, u32[]{:S(2)}, u32[]{:S(2)}) collective-permute-start(f32[4,16,128]{2,1,0:T(8,128)S(1)} %get-tuple-element.50), channel_id=1, source_target_pairs={{1,2},{2,1},{3,0},{0,3},{5,6},{6,5},{7,4},{4,7},{9,10},{10,9},{11,... | collective-permute-start | bytes 98312 | tf_op jit(solution)/shard_map/ppermute | solution.py:541
  16.0 5.9 %collective-permute-start.6 = (f32[4,16,128]{2,1,0:T(8,128)S(1)}, f32[4,16,128]{2,1,0:T(8,128)S(1)}, u32[]{:S(2)}, u32[]{:S(2)}) collective-permute-start(f32[4,16,128]{2,1,0:T(8,128)S(1)} %get-tuple-element.51), channel_id=1, source_target_pairs={{0,1},{1,0},{2,3},{3,2},{4,5},{5,4},{6,7},{7,6},{8,9},{9,8},{10,11... | collective-permute-start | bytes 98312 | tf_op jit(solution)/shard_map/ppermute | solution.py:541
  16.0 5.9 %collective-permute-start.4 = (bf16[37,16,128]{2,1,0:T(8,128)(2,1)S(1)}, bf16[37,16,128]{2,1,0:T(8,128)(2,1)S(1)}, u32[]{:S(2)}, u32[]{:S(2)}) collective-permute-start(bf16[37,16,128]{2,1,0:T(8,128)(2,1)S(1)} %collective-permute-done), channel_id=1, source_target_pairs={{0,8},{4,12},{8,0},{12,4},{16,24},{20,28},{24,16},{28,20},{1,9},{5... | collective-permute-start | bytes 454664 | tf_op jit(solution)/shard_map/ppermute | solution.py:634
  21.9 3.3 %collective-permute-start.7 = (bf16[111,16,128]{2,1,0:T(8,128)(2,1)S(1)}, bf16[111,16,128]{2,1,0:T(8,128)(2,1)S(1)}, u32[]{:S(2)}, u32[]{:S(2)}) collective-permute-start(bf16[111,16,128]{2,1,0:T(8,128)(2,1)S(1)} %pad_maximum_fusion.refs_0_), channel_id=1, source_target_pairs={{0,4},{4,0},{8,12},{12,8},{16,20},{20,16},{24,28},{28,24},{1,5},{5... | collective-permute-start | bytes 1363976 | tf_op jit(solution)/shard_map/ppermute | solution.py:701
  23.4 1.8 %collective-permute-start.8 = (bf16[37,16,128]{2,1,0:T(8,128)(2,1)S(1)}, bf16[37,16,128]{2,1,0:T(8,128)(2,1)S(1)}, u32[]{:S(2)}, u32[]{:S(2)}) collective-permute-start(bf16[37,16,128]{2,1,0:T(8,128)(2,1)S(1)} %collective-permute-done.4.refs_1_), channel_id=1, source_target_pairs={{0,4},{4,0},{8,12},{12,8},{16,20},{20,16},{24,28},{28,24},{1,5},{5... | collective-permute-start | bytes 454664 | tf_op jit(solution)/shard_map/ppermute | solution.py:701
  28.7 4.7 %collective-permute-start.9 = (bf16[4,16,128]{2,1,0:T(8,128)(2,1)S(1)}, bf16[4,16,128]{2,1,0:T(8,128)(2,1)S(1)}, u32[]{:S(2)}, u32[]{:S(2)}) collective-permute-start(bf16[4,16,128]{2,1,0:T(8,128)(2,1)S(1)} %get-tuple-element.73), channel_id=1, source_target_pairs={{1,2},{2,1},{3,0},{0,3},{5,6},{6,5},{7,4},{4,7},{9,10},{10,9},{11,... | collective-permute-start | bytes 49160 | tf_op jit(solution)/shard_map/ppermute | solution.py:541
  29.4 4.0 %collective-permute-start.10 = (bf16[4,16,128]{2,1,0:T(8,128)(2,1)S(1)}, bf16[4,16,128]{2,1,0:T(8,128)(2,1)S(1)}, u32[]{:S(2)}, u32[]{:S(2)}) collective-permute-start(bf16[4,16,128]{2,1,0:T(8,128)(2,1)S(1)} %get-tuple-element.74), channel_id=1, source_target_pairs={{0,1},{1,0},{2,3},{3,2},{4,5},{5,4},{6,7},{7,6},{8,9},{9,8},{10,11... | collective-permute-start | bytes 49160 | tf_op jit(solution)/shard_map/ppermute | solution.py:541
  34.1 5.8 %collective-permute-start.12 = (bf16[16,32,128]{2,1,0:T(8,128)(2,1)S(1)}, bf16[16,32,128]{2,1,0:T(8,128)(2,1)S(1)}, u32[]{:S(2)}, u32[]{:S(2)}) collective-permute-start(bf16[16,32,128]{2,1,0:T(8,128)(2,1)S(1)} %get-tuple-element.81), channel_id=1, source_target_pairs={{0,4},{4,0},{8,12},{12,8},{16,20},{20,16},{24,28},{28,24},{1,5},{5... | collective-permute-start | bytes 393224 | tf_op jit(solution)/shard_map/ppermute | solution.py:541
  35.6 7.4 %collective-permute-start.11 = (bf16[16,32,128]{2,1,0:T(8,128)(2,1)S(1)}, bf16[16,32,128]{2,1,0:T(8,128)(2,1)S(1)}, u32[]{:S(2)}, u32[]{:S(2)}) collective-permute-start(bf16[16,32,128]{2,1,0:T(8,128)(2,1)S(1)} %get-tuple-element.81), channel_id=1, source_target_pairs={{4,8},{8,4},{12,16},{16,12},{20,24},{24,20},{5,9},{9,5},{13,17},{1... | collective-permute-start | bytes 393224 | tf_op jit(solution)/shard_map/ppermute | solution.py:541

commit v6 on v5

--- a/solution.py
+++ b/solution.py
@@ -12,6 +12,7 @@
 BLOCK_COLS = 8
 LANES = 128
 LAT_SIGMA = 8.0
+WEIGHT_PIECES = 4
 VMEM_BYTES = 40 * 1024 * 1024
 
 VMEM = pl.BlockSpec(memory_space=pltpu.VMEM)
@@ -107,10 +108,22 @@
     block_cells,
     block_owner,
     control,
+    in_weight,
+    in_bias,
+    mid_weight,
+    mid_bias,
+    out_weight,
+    out_bias,
     taps,
     turned,
     plan,
     own_part,
+    wide_in,
+    weight_two,
+    weight_out,
+    bias_one,
+    bias_two,
+    bias_out,
     widths,
     cells,
     owners,
@@ -125,11 +138,20 @@
         pltpu.make_async_copy(background, field, sems.at[3]),
         pltpu.make_async_copy(control, band, sems.at[4]),
     ]
-    for move in moves:
-        move.start()
     tiles = turned.shape[0]
     height, levels, width = background.shape
     per_tile = height // tiles
+    weights = [(in_bias, bias_one), (mid_bias, bias_two), (out_weight, weight_out), (out_bias, bias_out)]
+    weights += [(in_weight, wide_in.at[pl.ds(sub * levels, levels)]) for sub in range(per_tile)]
+    piece = mid_weight.shape[0] // WEIGHT_PIECES
+    for k in range(WEIGHT_PIECES):
+        rows = pl.ds(k * piece, piece)
+        weights.append((mid_weight.at[rows], weight_two.at[rows]))
+    loads = [
+        pltpu.make_async_copy(source, target, sems.at[5 + k]) for k, (source, target) in enumerate(weights)
+    ]
+    for move in moves + loads:
+        move.start()
     groups = width // BLOCK_COLS
     rim = REACH // BLOCK_COLS
     slot_count = cells.shape[1]
@@ -175,14 +197,20 @@
     moves[4].wait()
     for row in range(height):
         own_part[row] = lat_sum(band, row, 0, height)
+    for move in loads:
+        move.wait()
 
 
 def swap_bits(count):
     return list(range(count.bit_length() - 2, 0, -1))
 
 
-def routing(recv_most, slot_count, tables, table):
-    count = tables.shape[0]
+def routing(recv_most, slot_count, slabs, table):
+    per_owner = recv_most + 1
+    spans, count = [], 0
+    for ref in slabs:
+        spans.append((ref, count))
+        count += ref.shape[0] // per_owner
     half = count // 2
     here = lax.axis_index("lat")
     rows = lax.broadcasted_iota(jnp.int32, (slot_count, LANES), 0)
@@ -198,29 +226,36 @@
             apart = apart + (((k >> place) & 1) << bit)
         return here ^ apart
 
-    def line(k, row):
-        return tables[k].astype(jnp.float32)[row : row + 1].astype(jnp.int32)
-
-    owner = jnp.sum(jnp.where(diagonal, line(0, 0), 0), axis=1, keepdims=True)
-
-    def rank(k, acc):
-        device = device_of(k)
+    def over_sets(step):
+        acc = zero
+        for ref, first in spans:
+
+            def add(k, acc, ref=ref, first=first):
+                lines = ref[k * per_owner + recv_most].astype(jnp.float32)
+                owners, counts = lines[0:1].astype(jnp.int32), lines[1:2].astype(jnp.int32)
+                return acc + step(device_of(first + k), owners, counts)
+
+            acc = lax.fori_loop(0, ref.shape[0] // per_owner, add, acc, unroll=count <= 8)
+        return jnp.sum(acc, axis=1, keepdims=True)
+
+    mine = slabs[0][recv_most].astype(jnp.float32)[0:1].astype(jnp.int32)
+    owner = jnp.sum(jnp.where(diagonal, mine, 0), axis=1, keepdims=True)
+
+    def rank(device, owners, counts):
         before = (device < here) | ((device == here) & (lanes < rows))
-        return acc + jnp.where((line(k, 0) == owner) & before, 1, 0)
-
-    unroll = count <= 8
-    arrival = jnp.sum(lax.fori_loop(0, count, rank, zero, unroll=unroll), axis=1, keepdims=True)
-
-    def counted(k, acc):
-        hit = (owner == device_of(k)) & (lanes == arrival)
-        return acc + jnp.where(hit, line(k, 1), 0)
-
-    kept = jnp.sum(lax.fori_loop(0, count, counted, zero, unroll=unroll), axis=1, keepdims=True)
+        return jnp.where((owners == owner) & before, 1, 0)
+
+    arrival = over_sets(rank)
+
+    def counted(device, owners, counts):
+        return jnp.where((owner == device) & (lanes == arrival), counts, 0)
+
+    kept = over_sets(counted)
     apart = owner ^ here
     entry = (apart & 1) * half
     for place, bit in enumerate(bits):
         entry = entry + (((apart >> bit) & 1) << place)
-    target = jnp.where(owner >= 0, entry * (recv_most + 1) + arrival, 0)
+    target = jnp.where(owner >= 0, entry * per_owner + arrival, 0)
     table[...] = jnp.zeros_like(table)
     for row, column in enumerate((target, kept)):
         table[row : row + 1, :] = jnp.sum(jnp.where(diagonal, column, 0), axis=0, keepdims=True)
@@ -279,18 +314,25 @@
         field[pl.ds(start, BLOCK_COLS), :] += jnp.where(lane_row == sub, block, 0.0)
 
 
-def take_observed(plan, table, held, observed, first, count):
+def take_observed(plan, table, slabs, observed, first, count):
     channels = observed.shape[1]
     channel = lax.broadcasted_iota(jnp.int32, (BLOCK_COLS, LANES), 1)
     for k in range(count):
         slot = plan[1, first + k]
-        slab = held[table[0, slot]].astype(jnp.float32)
-        kept = table[1, slot]
-        for h in range(channels // LANES):
-            part = slab[h * BLOCK_COLS : (h + 1) * BLOCK_COLS]
-            observed[k * BLOCK_COLS : (k + 1) * BLOCK_COLS, h * LANES : (h + 1) * LANES] = jnp.where(
-                channel + h * LANES < kept, part, jnp.inf
-            )
+        at, kept = table[0, slot], table[1, slot]
+        start = 0
+        for ref in slabs:
+            size = ref.shape[0]
+
+            @pl.when((at >= start) & (at < start + size))
+            def _(ref=ref, start=start):
+                slab = ref[at - start].astype(jnp.float32)
+                for h in range(channels // LANES):
+                    part = slab[h * BLOCK_COLS : (h + 1) * BLOCK_COLS]
+                    part = jnp.where(channel + h * LANES < kept, part, jnp.inf)
+                    observed[k * BLOCK_COLS : (k + 1) * BLOCK_COLS, h * LANES : (h + 1) * LANES] = part
+
+            start += size
 
 
 def dot(a, b):
@@ -322,51 +364,12 @@
     return rounded(dot_t(grad_one, wide_in[...]))
 
 
-def inner_forward_kernel(
-    outer_slots,
-    plan,
-    own,
-    turned,
-    taps,
-    in_weight,
-    in_bias,
-    mid_weight,
-    mid_bias,
-    out_weight,
-    out_bias,
-    profile,
-    act_one,
-    act_two,
-    emitted,
-    wide_in,
-    weight_two,
-    weight_out,
-    bias_one,
-    bias_two,
-    bias_out,
-    rows,
-    padded,
-    picked,
-    sems,
-):
+def inner_forward_kernel(per_tile, outer_slots, plan, own, turned, taps, *refs):
+    weights, profile, states, (rows, padded, picked, sem) = refs[:6], refs[6], refs[7:10], refs[10:]
     tiles, width, _ = own.shape
-    levels = in_weight.shape[0]
-    per_tile = LANES // levels
     count = picked.shape[0] // BLOCK_COLS
-
-    moves = [
-        pltpu.make_async_copy(plan, rows, sems.at[0]),
-        pltpu.make_async_copy(in_bias, bias_one, sems.at[1]),
-        pltpu.make_async_copy(mid_weight, weight_two, sems.at[2]),
-        pltpu.make_async_copy(mid_bias, bias_two, sems.at[3]),
-        pltpu.make_async_copy(out_weight, weight_out, sems.at[4]),
-        pltpu.make_async_copy(out_bias, bias_out, sems.at[5]),
-    ] + [
-        pltpu.make_async_copy(in_weight, wide_in.at[pl.ds(sub * levels, levels)], sems.at[6 + sub])
-        for sub in range(per_tile)
-    ]
-    for move in moves:
-        move.start()
+    plan_in = pltpu.make_async_copy(plan, rows, sem)
+    plan_in.start()
     zeros = jnp.zeros((tiles, REACH, LANES), jnp.float32)
     padded[:, 0:REACH, :] = zeros
     padded[:, REACH : REACH + width, :] = own[...]
@@ -374,14 +377,12 @@
     for tile in range(tiles):
         total = turned[tile] + lon_conv(padded, taps, tile, 0, width)
         profile[tile * width : (tile + 1) * width, :] = rounded(total)
-    for move in moves:
-        move.wait()
+    plan_in.wait()
 
     @pl.when(rows[2, 0] <= outer_slots)
     def _():
         take_blocks(rows, profile, picked, outer_slots, count, per_tile, width)
-        weights = (wide_in, weight_two, weight_out, bias_one, bias_two, bias_out)
-        net_forward(picked, weights, (act_one, act_two, emitted))
+        net_forward(picked, weights, states)
 
 
 def outer_forward_kernel(
@@ -422,50 +423,32 @@
         net_forward(late_picked, weights, late_states)
 
 
-def outer_backward_kernel(per_tile, parts, plan, *refs):
+def outer_backward_kernel(per_tile, parts, recv_most, plan, *refs):
     slabs, refs = refs[:parts], refs[parts:]
     weights, states, late_states, refs = refs[:3], refs[3:6], refs[6:9], refs[9:]
-    (held, table_rows, sens, to_far, to_close) = refs[:5]
-    (rows, tables, table, observed, late_observed, field, sems) = refs[5:]
+    (table_rows, sens, to_far, to_close) = refs[:4]
+    (rows, table, observed, late_observed, field, sems) = refs[4:]
     tiles = to_far.shape[0]
     width = field.shape[0] // tiles
-    owners = tables.shape[0]
-    per_owner = held.shape[0] // owners
     outer_slots = observed.shape[0] // BLOCK_COLS
     late_slots = late_observed.shape[0] // BLOCK_COLS
 
-    routes, bulk = [], []
-    for part, ref in enumerate(slabs):
-        sets = ref.shape[0] // per_owner
-        for k in range(sets):
-            entry = len(routes)
-            source = ref.at[k * per_owner + per_owner - 1]
-            routes.append(pltpu.make_async_copy(source, tables.at[entry], sems.at[entry]))
-        start = len(routes) - sets
-        bulk.append(
-            pltpu.make_async_copy(
-                ref, held.at[pl.ds(start * per_owner, ref.shape[0])], sems.at[owners + part]
-            )
-        )
-    plan_in = pltpu.make_async_copy(plan, rows, sems.at[owners + parts])
-    for move in routes + [plan_in] + bulk:
-        move.start()
+    plan_in = pltpu.make_async_copy(plan, rows, sems.at[0])
+    plan_in.start()
+    routing(recv_most, outer_slots + late_slots, slabs, table_rows)
+    table_in = pltpu.make_async_copy(table_rows, table, sems.at[1])
+    table_in.start()
     field[...] = jnp.zeros_like(field)
-    for move in routes:
-        move.wait()
-    routing(per_owner - 1, outer_slots + late_slots, tables, table_rows)
-    table_in = pltpu.make_async_copy(table_rows, table, sems.at[owners + parts + 1])
-    table_in.start()
-    for move in bulk + [plan_in, table_in]:
-        move.wait()
-
-    take_observed(rows, table, held, observed, 0, outer_slots)
+    plan_in.wait()
+    table_in.wait()
+
+    take_observed(rows, table, slabs, observed, 0, outer_slots)
     sens[0 : outer_slots * BLOCK_COLS, :] = net_backward(observed, states, weights)
     land_blocks(rows, field, sens, 0, outer_slots, per_tile, width)
 
     @pl.when(rows[2, 0] > outer_slots)
     def _():
-        take_observed(rows, table, held, late_observed, outer_slots, late_slots)
+        take_observed(rows, table, slabs, late_observed, outer_slots, late_slots)
         sens[outer_slots * BLOCK_COLS :, :] = net_backward(late_observed, late_states, weights)
         land_blocks(rows, field, sens, outer_slots, late_slots, per_tile, width)
 
@@ -476,7 +459,8 @@
         to_far[tile], to_close[tile] = low.astype(jnp.bfloat16), high.astype(jnp.bfloat16)
 
 
-def inner_backward_kernel(per_tile, outer_slots, plan, held, table_rows, sens, *refs):
+def inner_backward_kernel(per_tile, parts, outer_slots, plan, table_rows, sens, *refs):
+    slabs, refs = refs[:parts], refs[parts:]
     weights, states, refs = refs[:3], refs[3:6], refs[6:]
     landing, rows, table, observed, inner, field, sems = refs
     tiles, width, _ = landing.shape
@@ -495,7 +479,7 @@
 
     @pl.when(rows[2, 0] <= outer_slots)
     def _():
-        take_observed(rows, table, held, observed, outer_slots, late_slots)
+        take_observed(rows, table, slabs, observed, outer_slots, late_slots)
         inner[split:, :] = net_backward(observed, states, weights)
 
     land_blocks(rows, field, inner, 0, outer_slots + late_slots, per_tile, width)
@@ -538,6 +522,8 @@
         if odd + 1 < count or periodic:
             far += [(odd, (odd + 1) % count), ((odd + 1) % count, odd)]
     close = [(i, i ^ 1) for i in range(count)]
+    if to_far is not to_close:
+        to_close, _ = lax.optimization_barrier((to_close, to_far))
     return lax.ppermute(to_far, axis, far), lax.ppermute(to_close, axis, close)
 
 
@@ -590,25 +576,31 @@
     )(*pinned(radiance, block_owner.reshape(1, slot_count), channel_count.reshape(1, recv_most)))
 
     band = pltpu.VMEM((height, levels, width), f32)
-    taps, turned, plan, own_part = call(
+    taps, turned, plan, own_part, *weights = call(
         prepare_kernel,
         (
             shape((tiles, 24, LANES), f32),
             shape((tiles, width, LANES), f32),
             shape((8, LANES), i32),
             shape(control.shape, f32),
+            shape((LANES, hidden), bf16),
+            shape((hidden, hidden), bf16),
+            shape((hidden, channels), bf16),
+            shape((1, hidden), f32),
+            shape((1, hidden), f32),
+            shape((1, channels), f32),
         ),
-        [HBM] * 5,
-        (VMEM,) * 4,
+        [HBM] * 11,
+        (VMEM,) * 10,
         conv_flops // 2,
-        12 * field,
+        12 * field + 6 * hidden * hidden,
         scratch=(
             pltpu.SMEM((height,), i32),
             pltpu.VMEM((1, slot_count), i32),
             pltpu.VMEM((1, slot_count), i32),
             band,
             band,
-            pltpu.SemaphoreType.DMA((5,)),
+            pltpu.SemaphoreType.DMA((9 + per_tile + WEIGHT_PIECES,)),
         ),
         name="taps_background",
     )(
@@ -618,21 +610,25 @@
             block_cells.reshape(1, slot_count),
             block_owner.reshape(1, slot_count),
             control,
+            in_weight,
+            in_bias.reshape(1, hidden),
+            mid_weight,
+            mid_bias.reshape(1, hidden),
+            out_weight,
+            out_bias.reshape(1, channels),
         )
     )
 
     far, close = exchange(control, control, "lat", False)
+
     lat_count = lax.axis_size("lat")
-    near = [slabs]
-    for step, bit in enumerate(swap_bits(lat_count)):
-        if len(near) > 2:
-            half = len(near) // 2
-            near = [jnp.concatenate(near[:half], axis=0), jnp.concatenate(near[half:], axis=0)]
-        if step == 1:
-            near[1], far, close, taps = lax.optimization_barrier((near[1], far, close, taps))
-        pairs = [(i, i ^ (1 << bit)) for i in range(lat_count)]
-        near = near + [lax.ppermute(part, "lat", pairs) for part in near]
-    near = [jnp.concatenate(near[:-1], axis=0), near[-1]]
+    one, two, *others = swap_bits(lat_count)
+
+    def swapped(part, bit, odd_bit):
+        pairs = [(i, i ^ (1 << (odd_bit if i % 2 else bit))) for i in range(lat_count)]
+        return lax.ppermute(part, "lat", pairs)
+
+    first, second = swapped(slabs, one, one), swapped(slabs, two, two)
 
     halos = pltpu.VMEM((2, REACH, levels, width), f32)
     smoothed, to_far, to_close = call(
@@ -646,21 +642,19 @@
         name="lat_smooth",
     )(far, close, own_part)
     far, close = exchange(to_far, to_close, "lon", True)
+    first, second, *_ = lax.optimization_barrier((first, second, to_far, to_close))
+    passed = jnp.where(odd_index("lat"), first, second)
+    near = [slabs, first, second, swapped(passed, one, two)]
+    for bit in others:
+        near = [jnp.concatenate(near, axis=0)]
+        near.append(swapped(near[0], bit, bit))
+    near = [jnp.concatenate(near[:-1], axis=0), near[-1]]
 
     outer_slots = 3 * slot_count // 8
     late_slots = slot_count - outer_slots
     x_rows = slot_count * BLOCK_COLS
     outer_rows, late_rows = outer_slots * BLOCK_COLS, late_slots * BLOCK_COLS
     row_flops = 2 * hidden * (LANES + hidden + channels)
-    weight_shapes = (
-        shape((LANES, hidden), bf16),
-        shape((hidden, hidden), bf16),
-        shape((hidden, channels), bf16),
-        shape((1, hidden), f32),
-        shape((1, hidden), f32),
-        shape((1, channels), f32),
-    )
-
     def state_shapes(rows):
         return (shape((rows, hidden), bf16), shape((rows, hidden), bf16), shape((rows, channels), f32))
 
@@ -668,35 +662,16 @@
     padded = pltpu.VMEM((tiles, width + 2 * REACH, LANES), f32)
     flat = pltpu.VMEM((tiles * width, LANES), f32)
 
-    profile, *rest = call(
-        functools.partial(inner_forward_kernel, outer_slots),
-        (shape((tiles * width, LANES), f32),) + state_shapes(late_rows) + weight_shapes,
-        [ANY] + [VMEM] * 3 + [HBM] * 6,
-        (VMEM,) * 10,
+    profile, *inner_states = call(
+        functools.partial(inner_forward_kernel, per_tile, outer_slots),
+        (shape((tiles * width, LANES), f32),) + state_shapes(late_rows),
+        [ANY] + [VMEM] * 9,
+        (VMEM,) * 4,
         late_rows * row_flops,
         4 * 1024 * 1024,
-        scratch=(
-            plan_rows,
-            padded,
-            pltpu.VMEM((late_rows, LANES), f32),
-            pltpu.SemaphoreType.DMA((6 + per_tile,)),
-        ),
+        scratch=(plan_rows, padded, pltpu.VMEM((late_rows, LANES), f32), pltpu.SemaphoreType.DMA),
         name="inner_forward",
-    )(
-        plan,
-        smoothed,
-        turned,
-        taps,
-        *pinned(
-            in_weight,
-            in_bias.reshape(1, hidden),
-            mid_weight,
-            mid_bias.reshape(1, hidden),
-            out_weight,
-            out_bias.reshape(1, channels),
-        ),
-    )
-    inner_states, weights = rest[:3], rest[3:]
+    )(plan, smoothed, turned, taps, *weights)
     near, far, close, profile = lax.optimization_barrier((near, far, close, profile))
     across = [lax.ppermute(part, "lat", [(i, i ^ 1) for i in range(lat_count)]) for part in near]
 
@@ -719,36 +694,34 @@
     )(plan, far, close, smoothed, turned, taps, profile, *weights)
 
     slabs = [*near, *across]
-    held_slabs, table, sens, to_far, to_close = call(
-        functools.partial(outer_backward_kernel, per_tile, len(slabs)),
+    table, sens, to_far, to_close = call(
+        functools.partial(outer_backward_kernel, per_tile, len(slabs), recv_most),
         (
-            shape((lat_count * (recv_most + 1), slab_rows, LANES), bf16),
             shape((8, LANES), i32),
             shape((x_rows, LANES), f32),
             shape((tiles, REACH, LANES), bf16),
             shape((tiles, REACH, LANES), bf16),
         ),
-        [ANY] + [ANY] * len(slabs) + [VMEM] * 9,
-        (VMEM,) * 5,
+        [ANY] + [VMEM] * (len(slabs) + 9),
+        (VMEM,) * 4,
         outer_rows * row_flops,
         4 * 1024 * 1024,
         scratch=(
             plan_rows,
-            pltpu.VMEM((lat_count, slab_rows, LANES), bf16),
             pltpu.SMEM((8, LANES), i32),
             pltpu.VMEM((outer_rows, channels), f32),
             pltpu.VMEM((late_rows, channels), f32),
             flat,
-            pltpu.SemaphoreType.DMA((lat_count + len(slabs) + 2,)),
+            pltpu.SemaphoreType.DMA((2,)),
         ),
         name="outer_backward",
     )(plan, *slabs, *weights[:3], *states)
     far, close = exchange(to_far, to_close, "lon", True)
 
     landing = call(
-        functools.partial(inner_backward_kernel, per_tile, outer_slots),
+        functools.partial(inner_backward_kernel, per_tile, len(slabs), outer_slots),
         shape((tiles, width, LANES), f32),
-        [ANY, VMEM, ANY] + [VMEM] * 7,
+        [ANY, ANY] + [VMEM] * (len(slabs) + 7),
         VMEM,
         late_rows * row_flops,
         4 * 1024 * 1024,
@@ -761,7 +734,7 @@
             pltpu.SemaphoreType.DMA((2,)),
         ),
         name="inner_backward",
-    )(plan, held_slabs, table, sens, *weights[:3], *inner_states)
+    )(plan, table, sens, *slabs, *weights[:3], *inner_states)
 
     back, halved = call(
         lon_back_kernel,
@@ -784,6 +757,7 @@
         scratch=(band, pltpu.SemaphoreType.DMA),
         name="lat_back_own",
     )(back, *pinned(control))
+    far, own_part = lax.optimization_barrier((far, own_part))
 
     return call(
         lat_back_kernel,

time: 44.6 us -> 42.9 us (0.962)
  waiting for transfers between devices: 6.97 us -> 5.27 us
    ppermute x3, waiting for transfers between devices: 3.77 us -> 0.32 us  [swapped(): return lax.ppermute(part, 'lat', pairs)]
    ppermute x4, starting transfers between devices: 2.81 us -> 0.15 us  [exchange(): lax.ppermute(to_close, axis, close)]
    ppermute x4, starting transfers between devices: 11.5 us -> 13.2 us  [exchange(): lax.ppermute(to_far, axis, far)]
    ppermute x4, waiting for transfers between devices: 3.19 us -> 4.23 us  [exchange(): lax.ppermute(to_far, axis, far)]
    ppermute x4, waiting for transfers between devices: 0.01 us -> 0.72 us  [exchange(): lax.ppermute(to_close, axis, close)]
    pallas_call x1, Pallas kernels: 1.45 us -> 2.14 us  [shards(): call(prepare_kernel, (shape((tiles, 24, LANES), f32), shape((tiles, width...]
    ppermute x2, starting transfers between devices: 1.56 us -> 2.21 us  [shards(): lax.ppermute(part, 'lat', [(i, i ^ 1) for i in range(lat_count)])]
    pallas_call x3, Pallas kernels: 9.75 us -> 9.23 us  [the longest x1 3.96 us: shards(): call(functools.partial(inner_backward_kernel, per_tile, len(slabs), outer...]
  transfers between devices with their start and end apart: 13 -> 13, of which waited for: 2 -> 4; matrix products, arithmetic and copies ran while one was open for 0% -> 0% of each run, Pallas kernels for 27% -> 30%
where the time goes in v6:
time: 42.9 us; the launch traced here: 42.3 us
  starting transfers between devices  19.3 us (45%)
  Pallas kernels  17.5 us (41%)
  waiting for transfers between devices  5.27 us (12%)
    ppermute x4, starting transfers between devices, exchange(): lax.ppermute(to_far, axis, far)  13.2 us
    ppermute x4, waiting for transfers between devices, exchange(): lax.ppermute(to_far, axis, far)  4.23 us
    pallas_call x1, Pallas kernels, shards(): call(functools.partial(inner_backward_kernel, per_tile, len(slabs), outer...  3.96 us
    ppermute x3, starting transfers between devices, swapped(): return lax.ppermute(part, 'lat', pairs)  3.8 us
    pallas_call x1, Pallas kernels, shards(): call(functools.partial(outer_backward_kernel, per_tile, len(slabs), recv_...  2.98 us
    pallas_call x1, Pallas kernels, shards(): call(functools.partial(inner_forward_kernel, per_tile, outer_slots), (sha...  2.29 us
    ppermute x2, starting transfers between devices, shards(): lax.ppermute(part, 'lat', [(i, i ^ 1) for i in range(lat_count)])  2.21 us
    pallas_call x1, Pallas kernels, shards(): call(prepare_kernel, (shape((tiles, 24, LANES), f32), shape((tiles, width...  2.14 us
  transfers between devices with their start and end apart: 13, of which 4 were waited for; matrix products, arithmetic and copies ran while one was open for 0% of the time, Pallas kernels for 30%

profile of v6, /device:TPU:1, one launch (start us, length us, event | category | flops | bytes accessed | tf_op | source)
XLA Modules:
  0.0 42.3 jit_solution(17998582157830759200)
XLA Ops:
  0.0 4.5 %collective-permute-start.2 = (f32[16,32,128]{2,1,0:T(8,128)}, f32[16,32,128]{2,1,0:T(8,128)S(1)}, u32[]{:S(2)}, u32[]{:S(2)}) collective-permute-start(f32[16,32,128]{2,1,0:T(8,128)} %control.3), channel_id=1, source_target_pairs={{4,8},{8,4},{12,16},{16,12},{20,24},{24,20},{5,9},{9,5},{13,17},{1... | collective-permute-start | bytes 786440 | tf_op jit(solution)/shard_map/ppermute | solution.py:527
  4.5 0.1 collective-permute-start.3
  4.6 0.9 %slabs.1 = bf16[37,16,128]{2,1,0:T(8,128)(2,1)S(1)} custom-call(bf16[36,16,128]{2,1,0:T(8,128)(2,1)} %bitcast.13, s32[1,64]{1,0:T(1,128)} %bitcast.16, s32[1,36]{1,0:T(1,128)} %bitcast.19), custom_call_target="tpu_custom_call" | custom-call | bytes 294912 | tf_op jit(solution)/shard_map/slabs/pallas_call | solution.py:561
  5.5 1.3 %collective-permute-start = (bf16[37,16,128]{2,1,0:T(8,128)(2,1)S(1)}, bf16[37,16,128]{2,1,0:T(8,128)(2,1)S(1)}, u32[]{:S(2)}, u32[]{:S(2)}) collective-permute-start(bf16[37,16,128]{2,1,0:T(8,128)(2,1)S(1)} %slabs.1), channel_id=1, source_target_pairs={{0,16},{4,20},{8,24},{12,28},{16,0},{20,4},{24,8},{28,12},{1,17},{... | collective-permute-start | bytes 454664 | tf_op jit(solution)/shard_map/ppermute | solution.py:629
  6.8 0.1 collective-permute-start.1
  7.0 2.1 %taps_background.1 = (f32[4,24,128]{2,1,0:T(8,128)S(1)}, f32[4,128,128]{2,1,0:T(8,128)S(1)}, s32[8,128]{1,0:T(8,128)S(1)}, f32[16,32,128]{2,1,0:T(8,128)S(1)}, b...) custom-call(s32[16]{0:T(128)} %lon_width.1, ...), custom_call_target="tpu_custom_call" | custom-call | flops 2162688 | bytes 7077888 | tf_op jit(solution)/shard_map/taps_background/pallas_call | solution.py:579
  9.1 1.9 %collective-permute-done.2.far = f32[16,32,128]{2,1,0:T(8,128)S(1)} collective-permute-done((f32[16,32,128]{2,1,0:T(8,128)}, f32[16,32,128]{2,1,0:T(8,128)S(1)}, u32[]{:S(2)}, u32[]{:S(2)}) %collective-permute-start.2) | collective-permute-done | bytes 262176 | tf_op jit(solution)/shard_map/ppermute | solution.py:527
  11.0 0.4 %lat_smooth.1 = (f32[4,128,128]{2,1,0:T(8,128)S(1)}, f32[4,16,128]{2,1,0:T(8,128)S(1)}, f32[4,16,128]{2,1,0:T(8,128)S(1)}) custom-call(f32[16,32,128]{2,1,0:T(8,128)S(1)} %collective-permute-done.2.far, f32[16,32,128]{2,1,0:T(8,128)S(1)} %collective-permute-done.3.close, f32[16,32,128]{2,1,0:T(8,128)S(1)} %get-tuple-element.46.own_part), custom_call_target="tpu_custom_call" | custom-call | flops 4325376 | bytes 1048576 | tf_op jit(solution)/shard_map/lat_smooth/pallas_call | solution.py:634
  11.4 3.4 %collective-permute-start.5 = (f32[4,16,128]{2,1,0:T(8,128)S(1)}, f32[4,16,128]{2,1,0:T(8,128)S(1)}, u32[]{:S(2)}, u32[]{:S(2)}) collective-permute-start(f32[4,16,128]{2,1,0:T(8,128)S(1)} %get-tuple-element.47), channel_id=1, source_target_pairs={{1,2},{2,1},{3,0},{0,3},{5,6},{6,5},{7,4},{4,7},{9,10},{10,9},{11,... | collective-permute-start | bytes 98312 | tf_op jit(solution)/shard_map/ppermute | solution.py:527
  14.8 0.3 collective-permute-done.1
  15.1 2.4 %collective-permute-start.4 = (bf16[37,16,128]{2,1,0:T(8,128)(2,1)S(1)}, bf16[37,16,128]{2,1,0:T(8,128)(2,1)S(1)}, u32[]{:S(2)}, u32[]{:S(2)}) collective-permute-start(bf16[37,16,128]{2,1,0:T(8,128)(2,1)S(1)} %broadcast_select_fusion), channel_id=1, source_target_pairs={{0,16},{4,12},{8,24},{12,4},{16,0},{20,28},{24,8},{28,20},{1,17},{... | collective-permute-start | bytes 454664 | tf_op jit(solution)/shard_map/ppermute | solution.py:629
  17.6 2.3 %inner_forward.1 = (f32[512,128]{1,0:T(8,128)S(1)}, bf16[320,1024]{1,0:T(8,128)(2,1)S(1)}, bf16[320,1024]{1,0:T(8,128)(2,1)S(1)}, f32[320,256]{1,0:T(8,128)S(1)}) custom-call(s32[8,128]{1,0:T(8,128)S(1)} %get-tuple-element.45.plan, f32[4,128,128]{2,1,0:T(8,128)S(1)} %get-tuple-element.52.own, f32[4,128,128]{2,1,0:T(8,128)S(1)} %get-tuple-element.53.turned, ...), custom_call_target="tpu_custom_call" | custom-call | flops 922746880 | bytes 4194304 | tf_op jit(solution)/shard_map/inner_forward/pallas_call | solution.py:665
  19.9 0.7 %collective-permute-done.6.close = f32[4,16,128]{2,1,0:T(8,128)S(1)} collective-permute-done((f32[4,16,128]{2,1,0:T(8,128)S(1)}, f32[4,16,128]{2,1,0:T(8,128)S(1)}, u32[]{:S(2)}, u32[]{:S(2)}) %collective-permute-start.6) | collective-permute-done | bytes 32800 | tf_op jit(solution)/shard_map/ppermute | solution.py:527
  20.6 2.1 %collective-permute-start.7 = (bf16[111,16,128]{2,1,0:T(8,128)(2,1)S(1)}, bf16[111,16,128]{2,1,0:T(8,128)(2,1)S(1)}, u32[]{:S(2)}, u32[]{:S(2)}) collective-permute-start(bf16[111,16,128]{2,1,0:T(8,128)(2,1)S(1)} %pad_maximum_fusion.refs_0_), channel_id=1, source_target_pairs={{0,4},{4,0},{8,12},{12,8},{16,20},{20,16},{24,28},{28,24},{1,5},{5... | collective-permute-start | bytes 1363976 | tf_op jit(solution)/shard_map/ppermute | solution.py:676
  22.7 0.1 collective-permute-start.8
  22.8 1.7 %outer_forward.1 = (bf16[192,1024]{1,0:T(8,128)(2,1)S(1)}, bf16[192,1024]{1,0:T(8,128)(2,1)S(1)}, f32[192,256]{1,0:T(8,128)S(1)}, bf16[320,1024]{1,0:T(8,128)(2,...) custom-call(s32[8,128]{1,0:T(8,128)S(1)} %get-tuple-element.45.plan, ...), custom_call_target="tpu_custom_call" | custom-call | flops 553648128 | bytes 4194304 | tf_op jit(solution)/shard_map/outer_forward/pallas_call | solution.py:678
  24.5 3.0 %outer_backward.1 = (s32[8,128]{1,0:T(8,128)S(1)}, f32[512,128]{1,0:T(8,128)S(1)}, bf16[4,16,128]{2,1,0:T(8,128)(2,1)S(1)}, bf16[4,16,128]{2,1,0:T(8,128)(2,1)S(1)}) custom-call(s32[8,128]{1,0:T(8,128)S(1)} %get-tuple-element.45.plan, bf16[111,16,128]{2,1,0:T(8,128)(2,1)S(1)} %pad_maximum_fusion.refs_0_, ...), custom_call_target="tpu_custom_call" | custom-call | flops 553648128 | bytes 4194304 | tf_op jit(solution)/shard_map/outer_backward/pallas_call | solution.py:697
  27.5 0.6 %collective-permute-start.9 = (bf16[4,16,128]{2,1,0:T(8,128)(2,1)S(1)}, bf16[4,16,128]{2,1,0:T(8,128)(2,1)S(1)}, u32[]{:S(2)}, u32[]{:S(2)}) collective-permute-start(bf16[4,16,128]{2,1,0:T(8,128)(2,1)S(1)} %get-tuple-element.73), channel_id=1, source_target_pairs={{1,2},{2,1},{3,0},{0,3},{5,6},{6,5},{7,4},{4,7},{9,10},{10,9},{11,... | collective-permute-start | bytes 49160 | tf_op jit(solution)/shard_map/ppermute | solution.py:527
  28.1 4.0 %inner_backward.1.own = f32[4,128,128]{2,1,0:T(8,128)S(1)} custom-call(s32[8,128]{1,0:T(8,128)S(1)} %get-tuple-element.45.plan, s32[8,128]{1,0:T(8,128)S(1)} %get-tuple-element.76.table_rows, f32[512,128]{1,0:T(8,128)S(1)} %get-tuple-element.77.sens, bf16[111,16,128]{2,1,0:T(8,128)(2,1)S(1)} %pad_maximum_fusion.refs_0_, ...), custom_call_target="tpu_custom_call" | custom-call | flops 922746880 | bytes 4194304 | tf_op jit(solution)/shard_map/inner_backward/pallas_call | solution.py:721
  32.1 0.7 %lon_back.1 = (f32[16,32,128]{2,1,0:T(8,128)S(1)}, bf16[16,32,128]{2,1,0:T(8,128)(2,1)S(1)}) custom-call(bf16[4,16,128]{2,1,0:T(8,128)(2,1)S(1)} %collective-permute-done.9.far, bf16[4,16,128]{2,1,0:T(8,128)(2,1)S(1)} %collective-permute-done.10.close, f32[4,128,128]{2,1,0:T(8,128)S(1)} %inner_backward.1.own, f32[4,24,128]{2,1,0:T(8,128)S(1)} %get-tuple-element.54.taps), custom_call_target="tpu_custom_call" | custom-call | flops 4325376 | bytes 524288 | tf_op jit(solution)/shard_map/lon_back/pallas_call | solution.py:739
  32.8 4.7 %collective-permute-start.11 = (bf16[16,32,128]{2,1,0:T(8,128)(2,1)S(1)}, bf16[16,32,128]{2,1,0:T(8,128)(2,1)S(1)}, u32[]{:S(2)}, u32[]{:S(2)}) collective-permute-start(bf16[16,32,128]{2,1,0:T(8,128)(2,1)S(1)} %get-tuple-element.81), channel_id=1, source_target_pairs={{4,8},{8,4},{12,16},{16,12},{20,24},{24,20},{5,9},{9,5},{13,17},{1... | collective-permute-start | bytes 393224 | tf_op jit(solution)/shard_map/ppermute | solution.py:527
  37.6 1.3 %lat_back_own.1.own_part = f32[16,32,128]{2,1,0:T(8,128)S(1)} custom-call(f32[16,32,128]{2,1,0:T(8,128)S(1)} %get-tuple-element.82.back, f32[16,32,128]{2,1,0:T(8,128)} %control.3), custom_call_target="tpu_custom_call" | custom-call | flops 2162688 | bytes 786432 | tf_op jit(solution)/shard_map/lat_back_own/pallas_call | solution.py:750
  38.9 2.4 %collective-permute-done.11.far = bf16[16,32,128]{2,1,0:T(8,128)(2,1)S(1)} collective-permute-done((bf16[16,32,128]{2,1,0:T(8,128)(2,1)S(1)}, bf16[16,32,128]{2,1,0:T(8,128)(2,1)S(1)}, u32[]{:S(2)}, u32[]{:S(2)}) %collective-permute-start.11) | collective-permute-done | bytes 131104 | tf_op jit(solution)/shard_map/ppermute | solution.py:527
  41.2 1.1 %lat_back.1 = f32[16,32,128]{2,1,0:T(8,128)} custom-call(bf16[16,32,128]{2,1,0:T(8,128)(2,1)S(1)} %collective-permute-done.11.far, bf16[16,32,128]{2,1,0:T(8,128)(2,1)S(1)} %collective-permute-done.12.close, f32[16,32,128]{2,1,0:T(8,128)S(1)} %lat_back_own.1.own_part), custom_call_target="tpu_custom_call" | custom-call | flops 2162688 | bytes 1048576 | tf_op jit(solution)/shard_map/lat_back/pallas_call | solution.py:762
  (14 shorter events, 0.2 us)
Async XLA Ops:
  0.0 11.0 %collective-permute-start.2 = (f32[16,32,128]{2,1,0:T(8,128)}, f32[16,32,128]{2,1,0:T(8,128)S(1)}, u32[]{:S(2)}, u32[]{:S(2)}) collective-permute-start(f32[16,32,128]{2,1,0:T(8,128)} %control.3), channel_id=1, source_target_pairs={{4,8},{8,4},{12,16},{16,12},{20,24},{24,20},{5,9},{9,5},{13,17},{1... | collective-permute-start | bytes 786440 | tf_op jit(solution)/shard_map/ppermute | solution.py:527
  4.5 6.5 %collective-permute-start.3 = (f32[16,32,128]{2,1,0:T(8,128)}, f32[16,32,128]{2,1,0:T(8,128)S(1)}, u32[]{:S(2)}, u32[]{:S(2)}) collective-permute-start(f32[16,32,128]{2,1,0:T(8,128)} %control.3), channel_id=1, source_target_pairs={{0,4},{4,0},{8,12},{12,8},{16,20},{20,16},{24,28},{28,24},{1,5},{5... | collective-permute-start | bytes 786440 | tf_op jit(solution)/shard_map/ppermute | solution.py:527
  5.5 9.3 %collective-permute-start = (bf16[37,16,128]{2,1,0:T(8,128)(2,1)S(1)}, bf16[37,16,128]{2,1,0:T(8,128)(2,1)S(1)}, u32[]{:S(2)}, u32[]{:S(2)}) collective-permute-start(bf16[37,16,128]{2,1,0:T(8,128)(2,1)S(1)} %slabs.1), channel_id=1, source_target_pairs={{0,16},{4,20},{8,24},{12,28},{16,0},{20,4},{24,8},{28,12},{1,17},{... | collective-permute-start | bytes 454664 | tf_op jit(solution)/shard_map/ppermute | solution.py:629
  6.8 8.3 %collective-permute-start.1 = (bf16[37,16,128]{2,1,0:T(8,128)(2,1)S(1)}, bf16[37,16,128]{2,1,0:T(8,128)(2,1)S(1)}, u32[]{:S(2)}, u32[]{:S(2)}) collective-permute-start(bf16[37,16,128]{2,1,0:T(8,128)(2,1)S(1)} %slabs.1), channel_id=1, source_target_pairs={{0,8},{4,12},{8,0},{12,4},{16,24},{20,28},{24,16},{28,20},{1,9},{5... | collective-permute-start | bytes 454664 | tf_op jit(solution)/shard_map/ppermute | solution.py:629
  11.4 9.2 %collective-permute-start.5 = (f32[4,16,128]{2,1,0:T(8,128)S(1)}, f32[4,16,128]{2,1,0:T(8,128)S(1)}, u32[]{:S(2)}, u32[]{:S(2)}) collective-permute-start(f32[4,16,128]{2,1,0:T(8,128)S(1)} %get-tuple-element.47), channel_id=1, source_target_pairs={{1,2},{2,1},{3,0},{0,3},{5,6},{6,5},{7,4},{4,7},{9,10},{10,9},{11,... | collective-permute-start | bytes 98312 | tf_op jit(solution)/shard_map/ppermute | solution.py:527
  15.1 5.4 %collective-permute-start.4 = (bf16[37,16,128]{2,1,0:T(8,128)(2,1)S(1)}, bf16[37,16,128]{2,1,0:T(8,128)(2,1)S(1)}, u32[]{:S(2)}, u32[]{:S(2)}) collective-permute-start(bf16[37,16,128]{2,1,0:T(8,128)(2,1)S(1)} %broadcast_select_fusion), channel_id=1, source_target_pairs={{0,16},{4,12},{8,24},{12,4},{16,0},{20,28},{24,8},{28,20},{1,17},{... | collective-permute-start | bytes 454664 | tf_op jit(solution)/shard_map/ppermute | solution.py:629
  17.5 3.1 %collective-permute-start.6 = (f32[4,16,128]{2,1,0:T(8,128)S(1)}, f32[4,16,128]{2,1,0:T(8,128)S(1)}, u32[]{:S(2)}, u32[]{:S(2)}) collective-permute-start(f32[4,16,128]{2,1,0:T(8,128)S(1)} %get-tuple-element.51), channel_id=1, source_target_pairs={{0,1},{1,0},{2,3},{3,2},{4,5},{5,4},{6,7},{7,6},{8,9},{9,8},{10,11... | collective-permute-start | bytes 98312 | tf_op jit(solution)/shard_map/ppermute | solution.py:527
  20.6 4.0 %collective-permute-start.7 = (bf16[111,16,128]{2,1,0:T(8,128)(2,1)S(1)}, bf16[111,16,128]{2,1,0:T(8,128)(2,1)S(1)}, u32[]{:S(2)}, u32[]{:S(2)}) collective-permute-start(bf16[111,16,128]{2,1,0:T(8,128)(2,1)S(1)} %pad_maximum_fusion.refs_0_), channel_id=1, source_target_pairs={{0,4},{4,0},{8,12},{12,8},{16,20},{20,16},{24,28},{28,24},{1,5},{5... | collective-permute-start | bytes 1363976 | tf_op jit(solution)/shard_map/ppermute | solution.py:676
  22.7 1.8 %collective-permute-start.8 = (bf16[37,16,128]{2,1,0:T(8,128)(2,1)S(1)}, bf16[37,16,128]{2,1,0:T(8,128)(2,1)S(1)}, u32[]{:S(2)}, u32[]{:S(2)}) collective-permute-start(bf16[37,16,128]{2,1,0:T(8,128)(2,1)S(1)} %collective-permute-done.4.refs_1_), channel_id=1, source_target_pairs={{0,4},{4,0},{8,12},{12,8},{16,20},{20,16},{24,28},{28,24},{1,5},{5... | collective-permute-start | bytes 454664 | tf_op jit(solution)/shard_map/ppermute | solution.py:676
  27.5 4.6 %collective-permute-start.9 = (bf16[4,16,128]{2,1,0:T(8,128)(2,1)S(1)}, bf16[4,16,128]{2,1,0:T(8,128)(2,1)S(1)}, u32[]{:S(2)}, u32[]{:S(2)}) collective-permute-start(bf16[4,16,128]{2,1,0:T(8,128)(2,1)S(1)} %get-tuple-element.73), channel_id=1, source_target_pairs={{1,2},{2,1},{3,0},{0,3},{5,6},{6,5},{7,4},{4,7},{9,10},{10,9},{11,... | collective-permute-start | bytes 49160 | tf_op jit(solution)/shard_map/ppermute | solution.py:527
  28.1 4.0 %collective-permute-start.10 = (bf16[4,16,128]{2,1,0:T(8,128)(2,1)S(1)}, bf16[4,16,128]{2,1,0:T(8,128)(2,1)S(1)}, u32[]{:S(2)}, u32[]{:S(2)}) collective-permute-start(bf16[4,16,128]{2,1,0:T(8,128)(2,1)S(1)} %get-tuple-element.75), channel_id=1, source_target_pairs={{0,1},{1,0},{2,3},{3,2},{4,5},{5,4},{6,7},{7,6},{8,9},{9,8},{10,11... | collective-permute-start | bytes 49160 | tf_op jit(solution)/shard_map/ppermute | solution.py:527
  32.8 8.4 %collective-permute-start.11 = (bf16[16,32,128]{2,1,0:T(8,128)(2,1)S(1)}, bf16[16,32,128]{2,1,0:T(8,128)(2,1)S(1)}, u32[]{:S(2)}, u32[]{:S(2)}) collective-permute-start(bf16[16,32,128]{2,1,0:T(8,128)(2,1)S(1)} %get-tuple-element.81), channel_id=1, source_target_pairs={{4,8},{8,4},{12,16},{16,12},{20,24},{24,20},{5,9},{9,5},{13,17},{1... | collective-permute-start | bytes 393224 | tf_op jit(solution)/shard_map/ppermute | solution.py:527
  37.5 3.7 %collective-permute-start.12 = (bf16[16,32,128]{2,1,0:T(8,128)(2,1)S(1)}, bf16[16,32,128]{2,1,0:T(8,128)(2,1)S(1)}, u32[]{:S(2)}, u32[]{:S(2)}) collective-permute-start(bf16[16,32,128]{2,1,0:T(8,128)(2,1)S(1)} %get-tuple-element.81), channel_id=1, source_target_pairs={{0,4},{4,0},{8,12},{12,8},{16,20},{20,16},{24,28},{28,24},{1,5},{5... | collective-permute-start | bytes 393224 | tf_op jit(solution)/shard_map/ppermute | solution.py:527

commit v7 on v6

--- a/solution.py
+++ b/solution.py
@@ -81,12 +81,33 @@
     return value.astype(jnp.bfloat16).astype(jnp.float32)
 
 
-def slabs_kernel(radiance, block_owner, channel_count, slabs, owners, counts, rows, tables, sems):
+def halved_rows(rows, order):
+    halves, carry = {}, None
+    for row in order:
+        value = rows[row] if carry is None else rows[row] + carry
+        halves[row] = value.astype(jnp.bfloat16)
+        carry = value - halves[row].astype(jnp.float32)
+    return [halves[row] for row in sorted(halves)]
+
+
+def halve_for_sides(rows, height, to_far, to_close):
+    odd = odd_index("lat")
+    upward = halved_rows(rows, range(height - 1, -1, -1))
+    downward = halved_rows(rows, range(height))
+    for row in range(height):
+        to_far[row] = jnp.where(odd, upward[row], downward[row])
+        to_close[row] = jnp.where(odd, downward[row], upward[row])
+
+
+def first_kernel(
+    radiance, block_owner, channel_count, control, slabs, to_far, to_close, owners, counts, rows, tables, held, sems
+):
     recv_most = radiance.shape[0]
     moves = [
         pltpu.make_async_copy(radiance, slabs.at[pl.ds(0, recv_most)], sems.at[0]),
         pltpu.make_async_copy(block_owner, owners, sems.at[1]),
         pltpu.make_async_copy(channel_count, counts, sems.at[2]),
+        pltpu.make_async_copy(control, held, sems.at[3]),
     ]
     for move in moves:
         move.start()
@@ -96,8 +117,10 @@
     rows[0:1, 0 : owners.shape[1]] = owners[...].astype(jnp.float32)
     rows[1:2, 0 : counts.shape[1]] = counts[...].astype(jnp.float32)
     tables[...] = rows[...].astype(jnp.bfloat16)
-    last = pltpu.make_async_copy(tables, slabs.at[recv_most], sems.at[3])
+    last = pltpu.make_async_copy(tables, slabs.at[recv_most], sems.at[4])
     last.start()
+    moves[3].wait()
+    halve_for_sides(held, held.shape[0], to_far, to_close)
     moves[0].wait()
     last.wait()
 
@@ -108,22 +131,10 @@
     block_cells,
     block_owner,
     control,
-    in_weight,
-    in_bias,
-    mid_weight,
-    mid_bias,
-    out_weight,
-    out_bias,
     taps,
     turned,
     plan,
     own_part,
-    wide_in,
-    weight_two,
-    weight_out,
-    bias_one,
-    bias_two,
-    bias_out,
     widths,
     cells,
     owners,
@@ -141,16 +152,7 @@
     tiles = turned.shape[0]
     height, levels, width = background.shape
     per_tile = height // tiles
-    weights = [(in_bias, bias_one), (mid_bias, bias_two), (out_weight, weight_out), (out_bias, bias_out)]
-    weights += [(in_weight, wide_in.at[pl.ds(sub * levels, levels)]) for sub in range(per_tile)]
-    piece = mid_weight.shape[0] // WEIGHT_PIECES
-    for k in range(WEIGHT_PIECES):
-        rows = pl.ds(k * piece, piece)
-        weights.append((mid_weight.at[rows], weight_two.at[rows]))
-    loads = [
-        pltpu.make_async_copy(source, target, sems.at[5 + k]) for k, (source, target) in enumerate(weights)
-    ]
-    for move in moves + loads:
+    for move in moves:
         move.start()
     groups = width // BLOCK_COLS
     rim = REACH // BLOCK_COLS
@@ -197,8 +199,6 @@
     moves[4].wait()
     for row in range(height):
         own_part[row] = lat_sum(band, row, 0, height)
-    for move in loads:
-        move.wait()
 
 
 def swap_bits(count):
@@ -320,19 +320,16 @@
     for k in range(count):
         slot = plan[1, first + k]
         at, kept = table[0, slot], table[1, slot]
-        start = 0
+        slab, start = None, 0
         for ref in slabs:
             size = ref.shape[0]
-
-            @pl.when((at >= start) & (at < start + size))
-            def _(ref=ref, start=start):
-                slab = ref[at - start].astype(jnp.float32)
-                for h in range(channels // LANES):
-                    part = slab[h * BLOCK_COLS : (h + 1) * BLOCK_COLS]
-                    part = jnp.where(channel + h * LANES < kept, part, jnp.inf)
-                    observed[k * BLOCK_COLS : (k + 1) * BLOCK_COLS, h * LANES : (h + 1) * LANES] = part
-
+            found = ref[jnp.clip(at - start, 0, size - 1)].astype(jnp.float32)
+            slab = found if slab is None else jnp.where(at >= start, found, slab)
             start += size
+        for h in range(channels // LANES):
+            part = slab[h * BLOCK_COLS : (h + 1) * BLOCK_COLS]
+            part = jnp.where(channel + h * LANES < kept, part, jnp.inf)
+            observed[k * BLOCK_COLS : (k + 1) * BLOCK_COLS, h * LANES : (h + 1) * LANES] = part
 
 
 def dot(a, b):
@@ -343,13 +340,21 @@
     return lax.dot_general(a, b, (((1,), (1,)), ((), ())), preferred_element_type=jnp.float32)
 
 
-def net_forward(picked, weights, states):
-    wide_in, weight_two, weight_out, bias_one, bias_two, bias_out = weights
+def net_first(picked, weights, act_one):
+    inputs = picked[...].astype(jnp.bfloat16)
+    act_one[...] = jnp.tanh(dot(inputs, weights[0][...]) + weights[3][...]).astype(jnp.bfloat16)
+
+
+def net_rest(weights, states):
+    _, weight_two, weight_out, _, bias_two, bias_out = weights
     act_one, act_two, emitted = states
-    inputs = picked[...].astype(jnp.bfloat16)
-    act_one[...] = jnp.tanh(dot(inputs, wide_in[...]) + bias_one[...]).astype(jnp.bfloat16)
     act_two[...] = jnp.tanh(dot(act_one[...], weight_two[...]) + bias_two[...]).astype(jnp.bfloat16)
     emitted[...] = dot(act_two[...], weight_out[...]) + bias_out[...]
+
+
+def net_forward(picked, weights, states):
+    net_first(picked, weights, states[0])
+    net_rest(weights, states)
 
 
 def net_backward(observed, states, weights):
@@ -365,11 +370,24 @@
 
 
 def inner_forward_kernel(per_tile, outer_slots, plan, own, turned, taps, *refs):
-    weights, profile, states, (rows, padded, picked, sem) = refs[:6], refs[6], refs[7:10], refs[10:]
+    (in_weight, in_bias, mid_weight, mid_bias, out_weight, out_bias), refs = refs[:6], refs[6:]
+    profile, states, weights, (rows, padded, picked, sems) = refs[0], refs[1:4], refs[4:10], refs[10:]
+    wide_in, weight_two, weight_out, bias_one, bias_two, bias_out = weights
     tiles, width, _ = own.shape
+    levels = in_weight.shape[0]
     count = picked.shape[0] // BLOCK_COLS
-    plan_in = pltpu.make_async_copy(plan, rows, sem)
-    plan_in.start()
+    piece = mid_weight.shape[0] // WEIGHT_PIECES
+    pieces = [pl.ds(k * piece, piece) for k in range(WEIGHT_PIECES)]
+    loads = [(plan, rows), (in_bias, bias_one)]
+    loads += [(in_weight, wide_in.at[pl.ds(sub * levels, levels)]) for sub in range(per_tile)]
+    early = len(loads)
+    loads += [(mid_weight.at[part], weight_two.at[part]) for part in pieces] + [(mid_bias, bias_two)]
+    loads += [(out_weight, weight_out), (out_bias, bias_out)]
+    loads = [
+        pltpu.make_async_copy(source, target, sems.at[k]) for k, (source, target) in enumerate(loads)
+    ]
+    for move in loads:
+        move.start()
     zeros = jnp.zeros((tiles, REACH, LANES), jnp.float32)
     padded[:, 0:REACH, :] = zeros
     padded[:, REACH : REACH + width, :] = own[...]
@@ -377,12 +395,17 @@
     for tile in range(tiles):
         total = turned[tile] + lon_conv(padded, taps, tile, 0, width)
         profile[tile * width : (tile + 1) * width, :] = rounded(total)
-    plan_in.wait()
+    for move in loads[:early]:
+        move.wait()
+    take_blocks(rows, profile, picked, outer_slots, count, per_tile, width)
+    act_one, act_two, emitted = states
+    net_first(picked, weights, act_one)
+    for move in loads[early:]:
+        move.wait()
 
     @pl.when(rows[2, 0] <= outer_slots)
     def _():
-        take_blocks(rows, profile, picked, outer_slots, count, per_tile, width)
-        net_forward(picked, weights, states)
+        net_rest(weights, states)
 
 
 def outer_forward_kernel(
@@ -487,7 +510,7 @@
         landing[tile] = field[tile * width : (tile + 1) * width, :]
 
 
-def lon_back_kernel(far, close, own, taps, back, halved, padded):
+def lon_back_kernel(far, close, own, taps, back, to_far, to_close, padded):
     tiles, width, _ = own.shape
     height, levels, _ = back.shape
     per_tile = height // tiles
@@ -496,7 +519,7 @@
         rows = jnp.transpose(lon_conv(padded, taps, tile, 0, width))
         rows = rows.reshape(per_tile, levels, width)
         back[tile * per_tile : (tile + 1) * per_tile] = rows
-        halved[tile * per_tile : (tile + 1) * per_tile] = rows.astype(jnp.bfloat16)
+    halve_for_sides(back, height, to_far, to_close)
 
 
 def own_back_kernel(back, control, own_part, held, sem):
@@ -522,9 +545,11 @@
         if odd + 1 < count or periodic:
             far += [(odd, (odd + 1) % count), ((odd + 1) % count, odd)]
     close = [(i, i ^ 1) for i in range(count)]
-    if to_far is not to_close:
-        to_close, _ = lax.optimization_barrier((to_close, to_far))
-    return lax.ppermute(to_far, axis, far), lax.ppermute(to_close, axis, close)
+    to_close, _ = lax.optimization_barrier((to_close, to_far))
+    from_far, from_close = lax.ppermute(to_far, axis, far), lax.ppermute(to_close, axis, close)
+    from_far = lax.optimization_barrier(from_far)
+    from_close, _ = lax.optimization_barrier((from_close, from_far))
+    return from_far, from_close, to_close
 
 
 def shards(
@@ -558,49 +583,46 @@
     halves = channels // LANES
     radiance = radiance.T.reshape(recv_most, BLOCK_COLS, halves, LANES)
     radiance = jnp.swapaxes(radiance, 1, 2).reshape(recv_most, slab_rows, LANES)
-    slabs = call(
-        slabs_kernel,
-        shape((recv_most + 1, slab_rows, LANES), bf16),
-        [HBM] * 3,
-        HBM,
+    half_field = shape(control.shape, bf16)
+    slabs, to_far, to_close = call(
+        first_kernel,
+        (shape((recv_most + 1, slab_rows, LANES), bf16), half_field, half_field),
+        [HBM] * 4,
+        (HBM, VMEM, VMEM),
         0,
-        4 * channels * columns,
+        16 * field,
         scratch=(
             pltpu.VMEM((1, slot_count), i32),
             pltpu.VMEM((1, recv_most), i32),
             pltpu.VMEM((slab_rows, LANES), f32),
             pltpu.VMEM((slab_rows, LANES), bf16),
-            pltpu.SemaphoreType.DMA((4,)),
-        ),
-        name="slabs",
-    )(*pinned(radiance, block_owner.reshape(1, slot_count), channel_count.reshape(1, recv_most)))
+            pltpu.VMEM(control.shape, f32),
+            pltpu.SemaphoreType.DMA((5,)),
+        ),
+        name="slabs_halves",
+    )(*pinned(radiance, block_owner.reshape(1, slot_count), channel_count.reshape(1, recv_most), control))
+    far, close, sent = exchange(to_far, to_close, "lat", False)
 
     band = pltpu.VMEM((height, levels, width), f32)
-    taps, turned, plan, own_part, *weights = call(
+    taps, turned, plan, own_part = call(
         prepare_kernel,
         (
             shape((tiles, 24, LANES), f32),
             shape((tiles, width, LANES), f32),
             shape((8, LANES), i32),
             shape(control.shape, f32),
-            shape((LANES, hidden), bf16),
-            shape((hidden, hidden), bf16),
-            shape((hidden, channels), bf16),
-            shape((1, hidden), f32),
-            shape((1, hidden), f32),
-            shape((1, channels), f32),
-        ),
-        [HBM] * 11,
-        (VMEM,) * 10,
+        ),
+        [HBM] * 5,
+        (VMEM,) * 4,
         conv_flops // 2,
-        12 * field + 6 * hidden * hidden,
+        12 * field,
         scratch=(
             pltpu.SMEM((height,), i32),
             pltpu.VMEM((1, slot_count), i32),
             pltpu.VMEM((1, slot_count), i32),
             band,
             band,
-            pltpu.SemaphoreType.DMA((9 + per_tile + WEIGHT_PIECES,)),
+            pltpu.SemaphoreType.DMA((5,)),
         ),
         name="taps_background",
     )(
@@ -610,25 +632,17 @@
             block_cells.reshape(1, slot_count),
             block_owner.reshape(1, slot_count),
             control,
-            in_weight,
-            in_bias.reshape(1, hidden),
-            mid_weight,
-            mid_bias.reshape(1, hidden),
-            out_weight,
-            out_bias.reshape(1, channels),
         )
     )
 
-    far, close = exchange(control, control, "lat", False)
-
     lat_count = lax.axis_size("lat")
     one, two, *others = swap_bits(lat_count)
 
-    def swapped(part, bit, odd_bit):
-        pairs = [(i, i ^ (1 << (odd_bit if i % 2 else bit))) for i in range(lat_count)]
-        return lax.ppermute(part, "lat", pairs)
-
-    first, second = swapped(slabs, one, one), swapped(slabs, two, two)
+    def swapped(part, apart):
+        return lax.ppermute(part, "lat", [(i, i ^ apart) for i in range(lat_count)])
+
+    slabs, _ = lax.optimization_barrier((slabs, sent))
+    near = [slabs] + [swapped(slabs, apart) for apart in (1 << one, 1 << two, (1 << one) + (1 << two))]
 
     halos = pltpu.VMEM((2, REACH, levels, width), f32)
     smoothed, to_far, to_close = call(
@@ -641,15 +655,7 @@
         scratch=(halos,),
         name="lat_smooth",
     )(far, close, own_part)
-    far, close = exchange(to_far, to_close, "lon", True)
-    first, second, *_ = lax.optimization_barrier((first, second, to_far, to_close))
-    passed = jnp.where(odd_index("lat"), first, second)
-    near = [slabs, first, second, swapped(passed, one, two)]
-    for bit in others:
-        near = [jnp.concatenate(near, axis=0)]
-        near.append(swapped(near[0], bit, bit))
-    near = [jnp.concatenate(near[:-1], axis=0), near[-1]]
-
+    far, close, sent = exchange(to_far, to_close, "lon", True)
     outer_slots = 3 * slot_count // 8
     late_slots = slot_count - outer_slots
     x_rows = slot_count * BLOCK_COLS
@@ -662,18 +668,50 @@
     padded = pltpu.VMEM((tiles, width + 2 * REACH, LANES), f32)
     flat = pltpu.VMEM((tiles * width, LANES), f32)
 
-    profile, *inner_states = call(
+    profile, *rest = call(
         functools.partial(inner_forward_kernel, per_tile, outer_slots),
-        (shape((tiles * width, LANES), f32),) + state_shapes(late_rows),
-        [ANY] + [VMEM] * 9,
-        (VMEM,) * 4,
+        (shape((tiles * width, LANES), f32),)
+        + state_shapes(late_rows)
+        + (
+            shape((LANES, hidden), bf16),
+            shape((hidden, hidden), bf16),
+            shape((hidden, channels), bf16),
+            shape((1, hidden), f32),
+            shape((1, hidden), f32),
+            shape((1, channels), f32),
+        ),
+        [ANY] + [VMEM] * 3 + [HBM] * 6,
+        (VMEM,) * 10,
         late_rows * row_flops,
         4 * 1024 * 1024,
-        scratch=(plan_rows, padded, pltpu.VMEM((late_rows, LANES), f32), pltpu.SemaphoreType.DMA),
+        scratch=(
+            plan_rows,
+            padded,
+            pltpu.VMEM((late_rows, LANES), f32),
+            pltpu.SemaphoreType.DMA((5 + per_tile + WEIGHT_PIECES,)),
+        ),
         name="inner_forward",
-    )(plan, smoothed, turned, taps, *weights)
-    near, far, close, profile = lax.optimization_barrier((near, far, close, profile))
-    across = [lax.ppermute(part, "lat", [(i, i ^ 1) for i in range(lat_count)]) for part in near]
+    )(
+        plan,
+        smoothed,
+        turned,
+        taps,
+        *pinned(
+            in_weight,
+            in_bias.reshape(1, hidden),
+            mid_weight,
+            mid_bias.reshape(1, hidden),
+            out_weight,
+            out_bias.reshape(1, channels),
+        ),
+    )
+    inner_states, weights = rest[:3], rest[3:]
+    *near, far, close, profile = lax.optimization_barrier((*near, far, close, profile))
+    for bit in others:
+        near = [jnp.concatenate(near, axis=0)]
+        near.append(swapped(near[0], 1 << bit))
+    near = [jnp.concatenate(near[:-1], axis=0), near[-1]]
+    across = [swapped(part, 1) for part in near]
 
     states = call(
         functools.partial(outer_forward_kernel, per_tile),
@@ -716,7 +754,7 @@
         ),
         name="outer_backward",
     )(plan, *slabs, *weights[:3], *states)
-    far, close = exchange(to_far, to_close, "lon", True)
+    far, close, sent = exchange(to_far, to_close, "lon", True)
 
     landing = call(
         functools.partial(inner_backward_kernel, per_tile, len(slabs), outer_slots),
@@ -736,17 +774,17 @@
         name="inner_backward",
     )(plan, table, sens, *slabs, *weights[:3], *inner_states)
 
-    back, halved = call(
+    back, to_far, to_close = call(
         lon_back_kernel,
-        (shape((height, levels, width), f32), shape((height, levels, width), bf16)),
+        (shape((height, levels, width), f32), half_field, half_field),
         [VMEM] * 4,
-        (VMEM, VMEM),
+        (VMEM,) * 3,
         conv_flops,
         8 * field,
         scratch=(pltpu.VMEM((tiles, width + 2 * REACH, LANES), f32),),
         name="lon_back",
     )(far, close, landing, taps)
-    far, close = exchange(halved, halved, "lat", False)
+    far, close, sent = exchange(to_far, to_close, "lat", False)
     own_part = call(
         own_back_kernel,
         shape((height, levels, width), f32),
@@ -757,7 +795,6 @@
         scratch=(band, pltpu.SemaphoreType.DMA),
         name="lat_back_own",
     )(back, *pinned(control))
-    far, own_part = lax.optimization_barrier((far, own_part))
 
     return call(
         lat_back_kernel,

time: 42.9 us -> 38.5 us (0.90)
  waiting for transfers between devices: 5.27 us -> 2.11 us
  Pallas kernels: 17.5 us -> 16.8 us
    ppermute x4, waiting for transfers between devices: 4.23 us -> 1.96 us  [exchange(): lax.ppermute(to_far, axis, far)]
    ppermute x5, starting transfers between devices: 6.01 us -> 5.06 us  [swapped(): return lax.ppermute(part, 'lat', [(i, i ^ apart) for i in range(lat_count)])]
    pallas_call x1, Pallas kernels: 2.29 us -> 3.12 us  [shards(): call(functools.partial(inner_forward_kernel, per_tile, outer_slots), (sha...]
    ppermute x4, starting transfers between devices: 13.2 us -> 13.9 us  [exchange(): lax.ppermute(to_far, axis, far)]
    pallas_call x1, Pallas kernels: 2.14 us -> 1.45 us  [shards(): call(prepare_kernel, (shape((tiles, 24, LANES), f32), shape((tiles, width...]
    pallas_call x1, Pallas kernels: 3.96 us -> 3.34 us  [shards(): call(functools.partial(inner_backward_kernel, per_tile, len(slabs), outer...]
    ppermute x4, waiting for transfers between devices: 0.72 us -> 0.13 us  [exchange(): lax.ppermute(to_close, axis, close)]
    pallas_call x1, Pallas kernels: 2.98 us -> 2.43 us  [shards(): call(functools.partial(outer_backward_kernel, per_tile, len(slabs), recv_...]
  transfers between devices with their start and end apart: 13 -> 13, of which waited for: 4 -> 2; matrix products, arithmetic and copies ran while one was open for 0% -> 0% of each run, Pallas kernels for 30% -> 30%
where the time goes in v7:
time: 38.5 us; the launch traced here: 38.2 us
  starting transfers between devices  19.1 us (50%)
  Pallas kernels  16.8 us (44%)
  waiting for transfers between devices  2.11 us (5%)
    ppermute x4, starting transfers between devices, exchange(): lax.ppermute(to_far, axis, far)  13.9 us
    ppermute x5, starting transfers between devices, swapped(): return lax.ppermute(part, 'lat', [(i, i ^ apart) for i in range(lat_count)])  5.06 us
    pallas_call x1, Pallas kernels, shards(): call(functools.partial(inner_backward_kernel, per_tile, len(slabs), outer...  3.34 us
    pallas_call x1, Pallas kernels, shards(): call(functools.partial(inner_forward_kernel, per_tile, outer_slots), (sha...  3.12 us
    pallas_call x1, Pallas kernels, shards(): call(functools.partial(outer_backward_kernel, per_tile, len(slabs), recv_...  2.43 us
    ppermute x4, waiting for transfers between devices, exchange(): lax.ppermute(to_far, axis, far)  1.96 us
    pallas_call x1, Pallas kernels, shards(): call(functools.partial(outer_forward_kernel, per_tile), state_shapes(oute...  1.72 us
    pallas_call x1, Pallas kernels, shards(): call(prepare_kernel, (shape((tiles, 24, LANES), f32), shape((tiles, width...  1.45 us
  transfers between devices with their start and end apart: 13, of which 2 were waited for; matrix products, arithmetic and copies ran while one was open for 0% of the time, Pallas kernels for 30%

profile of v7, /device:TPU:1, one launch (start us, length us, event | category | flops | bytes accessed | tf_op | source)
XLA Modules:
  0.0 38.2 jit_solution(1170270595425161902)
XLA Ops:
  0.0 1.2 %slabs_halves.1 = (bf16[37,16,128]{2,1,0:T(8,128)(2,1)S(1)}, bf16[16,32,128]{2,1,0:T(8,128)(2,1)S(1)}, bf16[16,32,128]{2,1,0:T(8,128)(2,1)S(1)}) custom-call(bf16[36,16,128]{2,1,0:T(8,128)(2,1)} %bitcast.13, s32[1,64]{1,0:T(1,128)} %bitcast.14, s32[1,36]{1,0:T(1,128)} %bitcast.16, f32[16,32,128]{2,1,0:T(8,128)} %control.5), custom_call_target="tpu_custom_call" | custom-call | bytes 1048576 | tf_op jit(solution)/shard_map/slabs_halves/pallas_call | solution.py:587
  1.2 4.5 %collective-permute-start.3 = (bf16[16,32,128]{2,1,0:T(8,128)(2,1)S(1)}, bf16[16,32,128]{2,1,0:T(8,128)(2,1)S(1)}, u32[]{:S(2)}, u32[]{:S(2)}) collective-permute-start(bf16[16,32,128]{2,1,0:T(8,128)(2,1)S(1)} %get-tuple-element.57), channel_id=1, source_target_pairs={{4,8},{8,4},{12,16},{16,12},{20,24},{24,20},{5,9},{9,5},{13,17},{1... | collective-permute-start | bytes 393224 | tf_op jit(solution)/shard_map/ppermute | solution.py:549
  5.7 0.1 collective-permute-start.4
  5.8 1.3 %collective-permute-start = (bf16[37,16,128]{2,1,0:T(8,128)(2,1)S(1)}, bf16[37,16,128]{2,1,0:T(8,128)(2,1)S(1)}, u32[]{:S(2)}, u32[]{:S(2)}) collective-permute-start(bf16[37,16,128]{2,1,0:T(8,128)(2,1)S(1)} %get-tuple-element.70), channel_id=1, source_target_pairs={{0,16},{4,20},{8,24},{12,28},{16,0},{20,4},{24,8},{28,12},{1,17},{... | collective-permute-start | bytes 454664 | tf_op jit(solution)/shard_map/ppermute | solution.py:642
  7.1 0.1 collective-permute-start.1
  7.2 1.3 %collective-permute-start.2 = (bf16[37,16,128]{2,1,0:T(8,128)(2,1)S(1)}, bf16[37,16,128]{2,1,0:T(8,128)(2,1)S(1)}, u32[]{:S(2)}, u32[]{:S(2)}) collective-permute-start(bf16[37,16,128]{2,1,0:T(8,128)(2,1)S(1)} %get-tuple-element.70), channel_id=1, source_target_pairs={{0,24},{4,28},{8,16},{12,20},{16,8},{20,12},{24,0},{28,4},{1,25},{... | collective-permute-start | bytes 454664 | tf_op jit(solution)/shard_map/ppermute | solution.py:642
  8.5 1.5 %taps_background.1 = (f32[4,24,128]{2,1,0:T(8,128)S(1)}, f32[4,128,128]{2,1,0:T(8,128)S(1)}, s32[8,128]{1,0:T(8,128)S(1)}, f32[16,32,128]{2,1,0:T(8,128)S(1)}) custom-call(s32[16]{0:T(128)} %lon_width.1, f32[16,32,128]{2,1,0:T(8,128)} %background.1, s32[1,64]{1,0:T(1,128)} %bitcast.17, s32[1,64]{1,0:T(1,128)} %bitcast.15, f32[16,32,128]{2,1,0:T(8,128)} %control.5), custom_call_target="tpu_custom_call" | custom-call | flops 2162688 | bytes 786432 | tf_op jit(solution)/shard_map/taps_background/pallas_call | solution.py:607
  10.0 0.0 collective-permute-done.4.close
  10.0 0.4 %lat_smooth.1 = (f32[4,128,128]{2,1,0:T(8,128)S(1)}, f32[4,16,128]{2,1,0:T(8,128)S(1)}, f32[4,16,128]{2,1,0:T(8,128)S(1)}) custom-call(bf16[16,32,128]{2,1,0:T(8,128)(2,1)S(1)} %collective-permute-done.3.far, bf16[16,32,128]{2,1,0:T(8,128)(2,1)S(1)} %collective-permute-done.4.close, f32[16,32,128]{2,1,0:T(8,128)S(1)} %get-tuple-element.61.own_part), custom_call_target="tpu_custom_call" | custom-call | flops 4325376 | bytes 1048576 | tf_op jit(solution)/shard_map/lat_smooth/pallas_call | solution.py:648
  10.4 3.4 %collective-permute-start.5 = (f32[4,16,128]{2,1,0:T(8,128)S(1)}, f32[4,16,128]{2,1,0:T(8,128)S(1)}, u32[]{:S(2)}, u32[]{:S(2)}) collective-permute-start(f32[4,16,128]{2,1,0:T(8,128)S(1)} %get-tuple-element.62), channel_id=1, source_target_pairs={{1,2},{2,1},{3,0},{0,3},{5,6},{6,5},{7,4},{4,7},{9,10},{10,9},{11,... | collective-permute-start | bytes 98312 | tf_op jit(solution)/shard_map/ppermute | solution.py:549
  13.8 3.1 %inner_forward.1 = (f32[512,128]{1,0:T(8,128)S(1)}, bf16[320,1024]{1,0:T(8,128)(2,1)S(1)}, bf16[320,1024]{1,0:T(8,128)(2,1)S(1)}, f32[320,256]{1,0:T(8,128)S(1)}...) custom-call(s32[8,128]{1,0:T(8,128)S(1)} %get-tuple-element.54.plan,, ...), custom_call_target="tpu_custom_call" | custom-call | flops 922746880 | bytes 4194304 | tf_op jit(solution)/shard_map/inner_forward/pallas_call | solution.py:671
  17.0 0.1 collective-permute-done.6.close
  17.2 2.3 %collective-permute-start.7 = (bf16[111,16,128]{2,1,0:T(8,128)(2,1)S(1)}, bf16[111,16,128]{2,1,0:T(8,128)(2,1)S(1)}, u32[]{:S(2)}, u32[]{:S(2)}) collective-permute-start(bf16[111,16,128]{2,1,0:T(8,128)(2,1)S(1)} %constant_dynamic-update-slice_fusion.refs_0_), channel_id=1, source_target_pairs={{0,4},{4,0},{8,12},{12,8},{16,20},{20,16},{24,28},{28,24},{1,5},{5... | collective-permute-start | bytes 1363976 | tf_op jit(solution)/shard_map/ppermute | solution.py:642
  19.5 0.1 collective-permute-start.8
  19.5 1.7 %outer_forward.1 = (bf16[192,1024]{1,0:T(8,128)(2,1)S(1)}, bf16[192,1024]{1,0:T(8,128)(2,1)S(1)}, f32[192,256]{1,0:T(8,128)S(1)}, bf16[320,1024]{1,0:T(8,128)(2,...) custom-call(s32[8,128]{1,0:T(8,128)S(1)} %get-tuple-element.54.plan, ...), custom_call_target="tpu_custom_call" | custom-call | flops 553648128 | bytes 4194304 | tf_op jit(solution)/shard_map/outer_forward/pallas_call | solution.py:716
  21.3 2.4 %outer_backward.1 = (s32[8,128]{1,0:T(8,128)S(1)}, f32[512,128]{1,0:T(8,128)S(1)}, bf16[4,16,128]{2,1,0:T(8,128)(2,1)S(1)}, bf16[4,16,128]{2,1,0:T(8,128)(2,1)S(1)}) custom-call(s32[8,128]{1,0:T(8,128)S(1)} %get-tuple-element.54.plan, bf16[111,16,128]{2,1,0:T(8,128)(2,1)S(1)} %constant_dynamic-update-slice_fusion.refs_0_, ...), custom_call_target="tpu_custom_call" | custom-call | flops 553648128 | bytes 4194304 | tf_op jit(solution)/shard_map/outer_backward/pallas_call | solution.py:735
  23.7 1.6 %collective-permute-start.9 = (bf16[4,16,128]{2,1,0:T(8,128)(2,1)S(1)}, bf16[4,16,128]{2,1,0:T(8,128)(2,1)S(1)}, u32[]{:S(2)}, u32[]{:S(2)}) collective-permute-start(bf16[4,16,128]{2,1,0:T(8,128)(2,1)S(1)} %get-tuple-element.89), channel_id=1, source_target_pairs={{1,2},{2,1},{3,0},{0,3},{5,6},{6,5},{7,4},{4,7},{9,10},{10,9},{11,... | collective-permute-start | bytes 49160 | tf_op jit(solution)/shard_map/ppermute | solution.py:549
  25.3 3.3 %inner_backward.1.own = f32[4,128,128]{2,1,0:T(8,128)S(1)} custom-call(s32[8,128]{1,0:T(8,128)S(1)} %get-tuple-element.54.plan, s32[8,128]{1,0:T(8,128)S(1)} %get-tuple-element.93.table_rows, f32[512,128]{1,0:T(8,128)S(1)} %get-tuple-element.94.sens, bf16[111,16,128]{2,1,0:T(8,128)(2,1)S(1)} %constant_dynamic-update-slice_fusion.refs_0_, ...), custom_call_target="tpu_custom_call" | custom-call | flops 922746880 | bytes 4194304 | tf_op jit(solution)/shard_map/inner_backward/pallas_call | solution.py:759
  28.7 0.8 %lon_back.1 = (f32[16,32,128]{2,1,0:T(8,128)S(1)}, bf16[16,32,128]{2,1,0:T(8,128)(2,1)S(1)}, bf16[16,32,128]{2,1,0:T(8,128)(2,1)S(1)}) custom-call(bf16[4,16,128]{2,1,0:T(8,128)(2,1)S(1)} %collective-permute-done.9.far, bf16[4,16,128]{2,1,0:T(8,128)(2,1)S(1)} %collective-permute-done.10.close, f32[4,128,128]{2,1,0:T(8,128)S(1)} %inner_backward.1.own, ...), custom_call_target="tpu_custom_call" | custom-call | flops 4325376 | bytes 524288 | tf_op jit(solution)/shard_map/lon_back/pallas_call | solution.py:777
  29.5 4.4 %collective-permute-start.11 = (bf16[16,32,128]{2,1,0:T(8,128)(2,1)S(1)}, bf16[16,32,128]{2,1,0:T(8,128)(2,1)S(1)}, u32[]{:S(2)}, u32[]{:S(2)}) collective-permute-start(bf16[16,32,128]{2,1,0:T(8,128)(2,1)S(1)} %get-tuple-element.98), channel_id=1, source_target_pairs={{4,8},{8,4},{12,16},{16,12},{20,24},{24,20},{5,9},{9,5},{13,17},{1... | collective-permute-start | bytes 393224 | tf_op jit(solution)/shard_map/ppermute | solution.py:549
  33.9 0.1 collective-permute-start.12
  33.9 1.3 %lat_back_own.1.own_part = f32[16,32,128]{2,1,0:T(8,128)S(1)} custom-call(f32[16,32,128]{2,1,0:T(8,128)S(1)} %get-tuple-element.102.back, f32[16,32,128]{2,1,0:T(8,128)} %control.5), custom_call_target="tpu_custom_call" | custom-call | flops 2162688 | bytes 786432 | tf_op jit(solution)/shard_map/lat_back_own/pallas_call | solution.py:788
  35.2 2.0 %collective-permute-done.11.far = bf16[16,32,128]{2,1,0:T(8,128)(2,1)S(1)} collective-permute-done((bf16[16,32,128]{2,1,0:T(8,128)(2,1)S(1)}, bf16[16,32,128]{2,1,0:T(8,128)(2,1)S(1)}, u32[]{:S(2)}, u32[]{:S(2)}) %collective-permute-start.11) | collective-permute-done | bytes 131104 | tf_op jit(solution)/shard_map/ppermute | solution.py:549
  37.2 1.1 %lat_back.1 = f32[16,32,128]{2,1,0:T(8,128)} custom-call(bf16[16,32,128]{2,1,0:T(8,128)(2,1)S(1)} %collective-permute-done.11.far, bf16[16,32,128]{2,1,0:T(8,128)(2,1)S(1)} %collective-permute-done.12.close, f32[16,32,128]{2,1,0:T(8,128)S(1)} %lat_back_own.1.own_part), custom_call_target="tpu_custom_call" | custom-call | flops 2162688 | bytes 1048576 | tf_op jit(solution)/shard_map/lat_back/pallas_call | solution.py:799
  (15 shorter events, 0.1 us)
Async XLA Ops:
  1.2 8.8 %collective-permute-start.3 = (bf16[16,32,128]{2,1,0:T(8,128)(2,1)S(1)}, bf16[16,32,128]{2,1,0:T(8,128)(2,1)S(1)}, u32[]{:S(2)}, u32[]{:S(2)}) collective-permute-start(bf16[16,32,128]{2,1,0:T(8,128)(2,1)S(1)} %get-tuple-element.57), channel_id=1, source_target_pairs={{4,8},{8,4},{12,16},{16,12},{20,24},{24,20},{5,9},{9,5},{13,17},{1... | collective-permute-start | bytes 393224 | tf_op jit(solution)/shard_map/ppermute | solution.py:549
  5.7 4.3 %collective-permute-start.4 = (bf16[16,32,128]{2,1,0:T(8,128)(2,1)S(1)}, bf16[16,32,128]{2,1,0:T(8,128)(2,1)S(1)}, u32[]{:S(2)}, u32[]{:S(2)}) collective-permute-start(bf16[16,32,128]{2,1,0:T(8,128)(2,1)S(1)} %get-tuple-element.58), channel_id=1, source_target_pairs={{0,4},{4,0},{8,12},{12,8},{16,20},{20,16},{24,28},{28,24},{1,5},{5... | collective-permute-start | bytes 393224 | tf_op jit(solution)/shard_map/ppermute | solution.py:549
  5.8 11.3 %collective-permute-start = (bf16[37,16,128]{2,1,0:T(8,128)(2,1)S(1)}, bf16[37,16,128]{2,1,0:T(8,128)(2,1)S(1)}, u32[]{:S(2)}, u32[]{:S(2)}) collective-permute-start(bf16[37,16,128]{2,1,0:T(8,128)(2,1)S(1)} %get-tuple-element.70), channel_id=1, source_target_pairs={{0,16},{4,20},{8,24},{12,28},{16,0},{20,4},{24,8},{28,12},{1,17},{... | collective-permute-start | bytes 454664 | tf_op jit(solution)/shard_map/ppermute | solution.py:642
  7.1 10.0 %collective-permute-start.1 = (bf16[37,16,128]{2,1,0:T(8,128)(2,1)S(1)}, bf16[37,16,128]{2,1,0:T(8,128)(2,1)S(1)}, u32[]{:S(2)}, u32[]{:S(2)}) collective-permute-start(bf16[37,16,128]{2,1,0:T(8,128)(2,1)S(1)} %get-tuple-element.70), channel_id=1, source_target_pairs={{0,8},{4,12},{8,0},{12,4},{16,24},{20,28},{24,16},{28,20},{1,9},{5... | collective-permute-start | bytes 454664 | tf_op jit(solution)/shard_map/ppermute | solution.py:642
  7.2 9.9 %collective-permute-start.2 = (bf16[37,16,128]{2,1,0:T(8,128)(2,1)S(1)}, bf16[37,16,128]{2,1,0:T(8,128)(2,1)S(1)}, u32[]{:S(2)}, u32[]{:S(2)}) collective-permute-start(bf16[37,16,128]{2,1,0:T(8,128)(2,1)S(1)} %get-tuple-element.70), channel_id=1, source_target_pairs={{0,24},{4,28},{8,16},{12,20},{16,8},{20,12},{24,0},{28,4},{1,25},{... | collective-permute-start | bytes 454664 | tf_op jit(solution)/shard_map/ppermute | solution.py:642
  10.4 6.5 %collective-permute-start.5 = (f32[4,16,128]{2,1,0:T(8,128)S(1)}, f32[4,16,128]{2,1,0:T(8,128)S(1)}, u32[]{:S(2)}, u32[]{:S(2)}) collective-permute-start(f32[4,16,128]{2,1,0:T(8,128)S(1)} %get-tuple-element.62), channel_id=1, source_target_pairs={{1,2},{2,1},{3,0},{0,3},{5,6},{6,5},{7,4},{4,7},{9,10},{10,9},{11,... | collective-permute-start | bytes 98312 | tf_op jit(solution)/shard_map/ppermute | solution.py:549
  13.8 3.3 %collective-permute-start.6 = (f32[4,16,128]{2,1,0:T(8,128)S(1)}, f32[4,16,128]{2,1,0:T(8,128)S(1)}, u32[]{:S(2)}, u32[]{:S(2)}) collective-permute-start(f32[4,16,128]{2,1,0:T(8,128)S(1)} %get-tuple-element.64), channel_id=1, source_target_pairs={{0,1},{1,0},{2,3},{3,2},{4,5},{5,4},{6,7},{7,6},{8,9},{9,8},{10,11... | collective-permute-start | bytes 98312 | tf_op jit(solution)/shard_map/ppermute | solution.py:549
  17.2 4.1 %collective-permute-start.7 = (bf16[111,16,128]{2,1,0:T(8,128)(2,1)S(1)}, bf16[111,16,128]{2,1,0:T(8,128)(2,1)S(1)}, u32[]{:S(2)}, u32[]{:S(2)}) collective-permute-start(bf16[111,16,128]{2,1,0:T(8,128)(2,1)S(1)} %constant_dynamic-update-slice_fusion.refs_0_), channel_id=1, source_target_pairs={{0,4},{4,0},{8,12},{12,8},{16,20},{20,16},{24,28},{28,24},{1,5},{5... | collective-permute-start | bytes 1363976 | tf_op jit(solution)/shard_map/ppermute | solution.py:642
  19.5 1.8 %collective-permute-start.8 = (bf16[37,16,128]{2,1,0:T(8,128)(2,1)S(1)}, bf16[37,16,128]{2,1,0:T(8,128)(2,1)S(1)}, u32[]{:S(2)}, u32[]{:S(2)}) collective-permute-start(bf16[37,16,128]{2,1,0:T(8,128)(2,1)S(1)} %collective-permute-done.2.refs_1_), channel_id=1, source_target_pairs={{0,4},{4,0},{8,12},{12,8},{16,20},{20,16},{24,28},{28,24},{1,5},{5... | collective-permute-start | bytes 454664 | tf_op jit(solution)/shard_map/ppermute | solution.py:642
  23.7 5.0 %collective-permute-start.9 = (bf16[4,16,128]{2,1,0:T(8,128)(2,1)S(1)}, bf16[4,16,128]{2,1,0:T(8,128)(2,1)S(1)}, u32[]{:S(2)}, u32[]{:S(2)}) collective-permute-start(bf16[4,16,128]{2,1,0:T(8,128)(2,1)S(1)} %get-tuple-element.89), channel_id=1, source_target_pairs={{1,2},{2,1},{3,0},{0,3},{5,6},{6,5},{7,4},{4,7},{9,10},{10,9},{11,... | collective-permute-start | bytes 49160 | tf_op jit(solution)/shard_map/ppermute | solution.py:549
  25.3 3.4 %collective-permute-start.10 = (bf16[4,16,128]{2,1,0:T(8,128)(2,1)S(1)}, bf16[4,16,128]{2,1,0:T(8,128)(2,1)S(1)}, u32[]{:S(2)}, u32[]{:S(2)}) collective-permute-start(bf16[4,16,128]{2,1,0:T(8,128)(2,1)S(1)} %get-tuple-element.91), channel_id=1, source_target_pairs={{0,1},{1,0},{2,3},{3,2},{4,5},{5,4},{6,7},{7,6},{8,9},{9,8},{10,11... | collective-permute-start | bytes 49160 | tf_op jit(solution)/shard_map/ppermute | solution.py:549
  29.5 7.7 %collective-permute-start.11 = (bf16[16,32,128]{2,1,0:T(8,128)(2,1)S(1)}, bf16[16,32,128]{2,1,0:T(8,128)(2,1)S(1)}, u32[]{:S(2)}, u32[]{:S(2)}) collective-permute-start(bf16[16,32,128]{2,1,0:T(8,128)(2,1)S(1)} %get-tuple-element.98), channel_id=1, source_target_pairs={{4,8},{8,4},{12,16},{16,12},{20,24},{24,20},{5,9},{9,5},{13,17},{1... | collective-permute-start | bytes 393224 | tf_op jit(solution)/shard_map/ppermute | solution.py:549
  33.9 3.3 %collective-permute-start.12 = (bf16[16,32,128]{2,1,0:T(8,128)(2,1)S(1)}, bf16[16,32,128]{2,1,0:T(8,128)(2,1)S(1)}, u32[]{:S(2)}, u32[]{:S(2)}) collective-permute-start(bf16[16,32,128]{2,1,0:T(8,128)(2,1)S(1)} %get-tuple-element.100), channel_id=1, source_target_pairs={{0,4},{4,0},{8,12},{12,8},{16,20},{20,16},{24,28},{28,24},{1,5},{5... | collective-permute-start | bytes 393224 | tf_op jit(solution)/shard_map/ppermute | solution.py:549

commit v8 on v7

--- a/solution.py
+++ b/solution.py
@@ -13,6 +13,8 @@
 LANES = 128
 LAT_SIGMA = 8.0
 WEIGHT_PIECES = 4
+BAND_PIECES = 4
+SWAP_COVER = 10
 VMEM_BYTES = 40 * 1024 * 1024
 
 VMEM = pl.BlockSpec(memory_space=pltpu.VMEM)
@@ -107,9 +109,12 @@
         pltpu.make_async_copy(radiance, slabs.at[pl.ds(0, recv_most)], sems.at[0]),
         pltpu.make_async_copy(block_owner, owners, sems.at[1]),
         pltpu.make_async_copy(channel_count, counts, sems.at[2]),
-        pltpu.make_async_copy(control, held, sems.at[3]),
     ]
-    for move in moves:
+    piece = control.shape[0] // BAND_PIECES
+    for k in range(BAND_PIECES):
+        part = pl.ds(k * piece, piece)
+        moves.append(pltpu.make_async_copy(control.at[part], held.at[part], sems.at[4 + k]))
+    for move in moves[3:] + moves[:3]:
         move.start()
     rows[...] = jnp.full(rows.shape, -1.0, jnp.float32)
     moves[1].wait()
@@ -117,9 +122,10 @@
     rows[0:1, 0 : owners.shape[1]] = owners[...].astype(jnp.float32)
     rows[1:2, 0 : counts.shape[1]] = counts[...].astype(jnp.float32)
     tables[...] = rows[...].astype(jnp.bfloat16)
-    last = pltpu.make_async_copy(tables, slabs.at[recv_most], sems.at[4])
+    last = pltpu.make_async_copy(tables, slabs.at[recv_most], sems.at[3])
     last.start()
-    moves[3].wait()
+    for move in moves[3:]:
+        move.wait()
     halve_for_sides(held, held.shape[0], to_far, to_close)
     moves[0].wait()
     last.wait()
@@ -357,15 +363,18 @@
     net_rest(weights, states)
 
 
-def net_backward(observed, states, weights):
+def slopes(states, slope_one, slope_two):
+    for act, slope in zip(states, (slope_one, slope_two)):
+        value = act[...].astype(jnp.float32)
+        slope[...] = 1.0 - value * value
+
+
+def net_backward(observed, emitted, slope_one, slope_two, weights):
     wide_in, weight_two, weight_out = weights[:3]
-    act_one, act_two, emitted = states
     seen = observed[...]
     misfit = jnp.where(seen < jnp.inf, emitted[...] - seen, 0.0).astype(jnp.bfloat16)
-    two = act_two[...].astype(jnp.float32)
-    grad_two = (dot_t(misfit, weight_out[...]) * (1.0 - two * two)).astype(jnp.bfloat16)
-    one = act_one[...].astype(jnp.float32)
-    grad_one = (dot_t(grad_two, weight_two[...]) * (1.0 - one * one)).astype(jnp.bfloat16)
+    grad_two = (dot_t(misfit, weight_out[...]) * slope_two[...]).astype(jnp.bfloat16)
+    grad_one = (dot_t(grad_two, weight_two[...]) * slope_one[...]).astype(jnp.bfloat16)
     return rounded(dot_t(grad_one, wide_in[...]))
 
 
@@ -450,7 +459,7 @@
     slabs, refs = refs[:parts], refs[parts:]
     weights, states, late_states, refs = refs[:3], refs[3:6], refs[6:9], refs[9:]
     (table_rows, sens, to_far, to_close) = refs[:4]
-    (rows, table, observed, late_observed, field, sems) = refs[4:]
+    (rows, table, observed, late_observed, field, *slope, sems) = refs[4:]
     tiles = to_far.shape[0]
     width = field.shape[0] // tiles
     outer_slots = observed.shape[0] // BLOCK_COLS
@@ -462,17 +471,21 @@
     table_in = pltpu.make_async_copy(table_rows, table, sems.at[1])
     table_in.start()
     field[...] = jnp.zeros_like(field)
+    slopes(states, *slope[:2])
     plan_in.wait()
     table_in.wait()
 
     take_observed(rows, table, slabs, observed, 0, outer_slots)
-    sens[0 : outer_slots * BLOCK_COLS, :] = net_backward(observed, states, weights)
+    sens[0 : outer_slots * BLOCK_COLS, :] = net_backward(observed, states[2], *slope[:2], weights)
     land_blocks(rows, field, sens, 0, outer_slots, per_tile, width)
 
     @pl.when(rows[2, 0] > outer_slots)
     def _():
         take_observed(rows, table, slabs, late_observed, outer_slots, late_slots)
-        sens[outer_slots * BLOCK_COLS :, :] = net_backward(late_observed, late_states, weights)
+        slopes(late_states, *slope[2:])
+        sens[outer_slots * BLOCK_COLS :, :] = net_backward(
+            late_observed, late_states[2], *slope[2:], weights
+        )
         land_blocks(rows, field, sens, outer_slots, late_slots, per_tile, width)
 
     for tile in range(tiles):
@@ -485,7 +498,7 @@
 def inner_backward_kernel(per_tile, parts, outer_slots, plan, table_rows, sens, *refs):
     slabs, refs = refs[:parts], refs[parts:]
     weights, states, refs = refs[:3], refs[3:6], refs[6:]
-    landing, rows, table, observed, inner, field, sems = refs
+    landing, rows, table, observed, inner, field, *slope, sems = refs
     tiles, width, _ = landing.shape
     late_slots = observed.shape[0] // BLOCK_COLS
     split = outer_slots * BLOCK_COLS
@@ -497,13 +510,14 @@
         move.start()
     field[...] = jnp.zeros_like(field)
     inner[...] = sens[...]
+    slopes(states, *slope)
     for move in moves:
         move.wait()
 
     @pl.when(rows[2, 0] <= outer_slots)
     def _():
         take_observed(rows, table, slabs, observed, outer_slots, late_slots)
-        inner[split:, :] = net_backward(observed, states, weights)
+        inner[split:, :] = net_backward(observed, states[2], *slope, weights)
 
     land_blocks(rows, field, inner, 0, outer_slots + late_slots, per_tile, width)
     for tile in range(tiles):
@@ -531,11 +545,19 @@
         own_part[row] = lat_sum(back, row, 0, height, held[row])
 
 
-def lat_back_kernel(far, close, own_part, gradient, halos):
+def lat_back_kernel(far, close, own_part, gradient, halos, done, sems):
     halos[0], halos[1] = sides(far[...], close[...], "lat")
     height = own_part.shape[0]
-    for row in range(height):
-        gradient[row] = lat_rims(row, own_part[row], halos, height)
+    piece = height // BAND_PIECES
+    moves = []
+    for k in range(BAND_PIECES):
+        part = pl.ds(k * piece, piece)
+        for row in range(k * piece, (k + 1) * piece):
+            done[row] = lat_rims(row, own_part[row], halos, height)
+        moves.append(pltpu.make_async_copy(done.at[part], gradient.at[part], sems.at[k]))
+        moves[-1].start()
+    for move in moves:
+        move.wait()
 
 
 def exchange(to_far, to_close, axis, periodic):
@@ -597,7 +619,7 @@
             pltpu.VMEM((slab_rows, LANES), f32),
             pltpu.VMEM((slab_rows, LANES), bf16),
             pltpu.VMEM(control.shape, f32),
-            pltpu.SemaphoreType.DMA((5,)),
+            pltpu.SemaphoreType.DMA((4 + BAND_PIECES,)),
         ),
         name="slabs_halves",
     )(*pinned(radiance, block_owner.reshape(1, slot_count), channel_count.reshape(1, recv_most), control))
@@ -706,7 +728,7 @@
         ),
     )
     inner_states, weights = rest[:3], rest[3:]
-    *near, far, close, profile = lax.optimization_barrier((*near, far, close, profile))
+    *near, _ = lax.optimization_barrier((*near, profile))
     for bit in others:
         near = [jnp.concatenate(near, axis=0)]
         near.append(swapped(near[0], 1 << bit))
@@ -718,8 +740,8 @@
         state_shapes(outer_rows) + state_shapes(late_rows),
         [ANY] + [VMEM] * 12,
         (VMEM,) * 6,
-        outer_rows * row_flops,
-        4 * 1024 * 1024,
+        SWAP_COVER * outer_rows * row_flops,
+        SWAP_COVER * 4 * 1024 * 1024,
         scratch=(
             plan_rows,
             padded,
@@ -750,6 +772,10 @@
             pltpu.VMEM((outer_rows, channels), f32),
             pltpu.VMEM((late_rows, channels), f32),
             flat,
+            pltpu.VMEM((outer_rows, hidden), f32),
+            pltpu.VMEM((outer_rows, hidden), f32),
+            pltpu.VMEM((late_rows, hidden), f32),
+            pltpu.VMEM((late_rows, hidden), f32),
             pltpu.SemaphoreType.DMA((2,)),
         ),
         name="outer_backward",
@@ -769,6 +795,8 @@
             pltpu.VMEM((late_rows, channels), f32),
             pltpu.VMEM((x_rows, LANES), f32),
             flat,
+            pltpu.VMEM((late_rows, hidden), f32),
+            pltpu.VMEM((late_rows, hidden), f32),
             pltpu.SemaphoreType.DMA((2,)),
         ),
         name="inner_backward",
@@ -800,10 +828,10 @@
         lat_back_kernel,
         shape((height, levels, width), f32),
         [VMEM] * 3,
-        VMEM,
+        HBM,
         conv_flops // 2,
         16 * field,
-        scratch=(halos,),
+        scratch=(halos, band, pltpu.SemaphoreType.DMA((BAND_PIECES,))),
         name="lat_back",
     )(far, close, own_part)
 

time: 38.5 us -> 39.2 us (1.018)
  waiting for transfers between devices: 2.11 us -> 2.61 us
    ppermute x5, starting transfers between devices: 5.06 us -> 4.41 us  [swapped(): return lax.ppermute(part, 'lat', [(i, i ^ apart) for i in range(lat_count)])]
    ppermute x4, waiting for transfers between devices: 1.96 us -> 2.58 us  [exchange(): lax.ppermute(to_far, axis, far)]
  transfers between devices with their start and end apart: 13 -> 13, of which waited for: 2 -> 1; matrix products, arithmetic and copies ran while one was open for 0% -> 0% of each run, Pallas kernels for 30% -> 29%
where the time goes in v8:
time: 39.2 us; the launch traced here: 38.9 us
  starting transfers between devices  19.2 us (49%)
  Pallas kernels  16.7 us (43%)
  waiting for transfers between devices  2.61 us (7%)
    ppermute x4, starting transfers between devices, exchange(): lax.ppermute(to_far, axis, far)  14.2 us
    ppermute x5, starting transfers between devices, swapped(): return lax.ppermute(part, 'lat', [(i, i ^ apart) for i in range(lat_count)])  4.41 us
    pallas_call x1, Pallas kernels, shards(): call(functools.partial(inner_backward_kernel, per_tile, len(slabs), outer...  3.36 us
    pallas_call x1, Pallas kernels, shards(): call(functools.partial(inner_forward_kernel, per_tile, outer_slots), (sha...  3.11 us
    ppermute x4, waiting for transfers between devices, exchange(): lax.ppermute(to_far, axis, far)  2.58 us
    pallas_call x1, Pallas kernels, shards(): call(functools.partial(outer_backward_kernel, per_tile, len(slabs), recv_...  2.46 us
    pallas_call x1, Pallas kernels, shards(): call(functools.partial(outer_forward_kernel, per_tile), state_shapes(oute...  1.72 us
    pallas_call x1, Pallas kernels, shards(): call(prepare_kernel, (shape((tiles, 24, LANES), f32), shape((tiles, width...  1.45 us
  transfers between devices with their start and end apart: 13, of which 1 were waited for; matrix products, arithmetic and copies ran while one was open for 0% of the time, Pallas kernels for 29%

profile of v8, /device:TPU:1, one launch (start us, length us, event | category | flops | bytes accessed | tf_op | source)
XLA Modules:
  0.0 38.9 jit_solution(16036648243524911091)
XLA Ops:
  0.0 1.1 %slabs_halves.1 = (bf16[37,16,128]{2,1,0:T(8,128)(2,1)S(1)}, bf16[16,32,128]{2,1,0:T(8,128)(2,1)S(1)}, bf16[16,32,128]{2,1,0:T(8,128)(2,1)S(1)}) custom-call(bf16[36,16,128]{2,1,0:T(8,128)(2,1)} %bitcast.13, s32[1,64]{1,0:T(1,128)} %bitcast.14, s32[1,36]{1,0:T(1,128)} %bitcast.16, f32[16,32,128]{2,1,0:T(8,128)} %control.5), custom_call_target="tpu_custom_call" | custom-call | bytes 1048576 | tf_op jit(solution)/shard_map/slabs_halves/pallas_call | solution.py:609
  1.1 4.5 %collective-permute-start.3 = (bf16[16,32,128]{2,1,0:T(8,128)(2,1)S(1)}, bf16[16,32,128]{2,1,0:T(8,128)(2,1)S(1)}, u32[]{:S(2)}, u32[]{:S(2)}) collective-permute-start(bf16[16,32,128]{2,1,0:T(8,128)(2,1)S(1)} %get-tuple-element.54), channel_id=1, source_target_pairs={{4,8},{8,4},{12,16},{16,12},{20,24},{24,20},{5,9},{9,5},{13,17},{1... | collective-permute-start | bytes 393224 | tf_op jit(solution)/shard_map/ppermute | solution.py:571
  5.6 0.1 collective-permute-start.4
  5.7 1.3 %collective-permute-start = (bf16[37,16,128]{2,1,0:T(8,128)(2,1)S(1)}, bf16[37,16,128]{2,1,0:T(8,128)(2,1)S(1)}, u32[]{:S(2)}, u32[]{:S(2)}) collective-permute-start(bf16[37,16,128]{2,1,0:T(8,128)(2,1)S(1)} %get-tuple-element.63), channel_id=1, source_target_pairs={{0,16},{4,20},{8,24},{12,28},{16,0},{20,4},{24,8},{28,12},{1,17},{... | collective-permute-start | bytes 454664 | tf_op jit(solution)/shard_map/ppermute | solution.py:664
  7.0 0.1 collective-permute-start.1
  7.1 1.3 %collective-permute-start.2 = (bf16[37,16,128]{2,1,0:T(8,128)(2,1)S(1)}, bf16[37,16,128]{2,1,0:T(8,128)(2,1)S(1)}, u32[]{:S(2)}, u32[]{:S(2)}) collective-permute-start(bf16[37,16,128]{2,1,0:T(8,128)(2,1)S(1)} %get-tuple-element.63), channel_id=1, source_target_pairs={{0,24},{4,28},{8,16},{12,20},{16,8},{20,12},{24,0},{28,4},{1,25},{... | collective-permute-start | bytes 454664 | tf_op jit(solution)/shard_map/ppermute | solution.py:664
  8.4 1.5 %taps_background.1 = (f32[4,24,128]{2,1,0:T(8,128)S(1)}, f32[4,128,128]{2,1,0:T(8,128)S(1)}, s32[8,128]{1,0:T(8,128)S(1)}, f32[16,32,128]{2,1,0:T(8,128)S(1)}) custom-call(s32[16]{0:T(128)} %lon_width.1, f32[16,32,128]{2,1,0:T(8,128)} %background.1, s32[1,64]{1,0:T(1,128)} %bitcast.17, s32[1,64]{1,0:T(1,128)} %bitcast.15, f32[16,32,128]{2,1,0:T(8,128)} %control.5), custom_call_target="tpu_custom_call" | custom-call | flops 2162688 | bytes 786432 | tf_op jit(solution)/shard_map/taps_background/pallas_call | solution.py:629
  9.9 0.4 %lat_smooth.1 = (f32[4,128,128]{2,1,0:T(8,128)S(1)}, f32[4,16,128]{2,1,0:T(8,128)S(1)}, f32[4,16,128]{2,1,0:T(8,128)S(1)}) custom-call(bf16[16,32,128]{2,1,0:T(8,128)(2,1)S(1)} %collective-permute-done.3.far, bf16[16,32,128]{2,1,0:T(8,128)(2,1)S(1)} %collective-permute-done.4.close, f32[16,32,128]{2,1,0:T(8,128)S(1)} %get-tuple-element.58.own_part), custom_call_target="tpu_custom_call" | custom-call | flops 4325376 | bytes 1048576 | tf_op jit(solution)/shard_map/lat_smooth/pallas_call | solution.py:670
  10.3 3.4 %collective-permute-start.7 = (f32[4,16,128]{2,1,0:T(8,128)S(1)}, f32[4,16,128]{2,1,0:T(8,128)S(1)}, u32[]{:S(2)}, u32[]{:S(2)}) collective-permute-start(f32[4,16,128]{2,1,0:T(8,128)S(1)} %get-tuple-element.70), channel_id=1, source_target_pairs={{1,2},{2,1},{3,0},{0,3},{5,6},{6,5},{7,4},{4,7},{9,10},{10,9},{11,... | collective-permute-start | bytes 98312 | tf_op jit(solution)/shard_map/ppermute | solution.py:571
  13.7 0.0 collective-permute-start.8
  13.7 3.1 %inner_forward.1 = (f32[512,128]{1,0:T(8,128)S(1)}, bf16[320,1024]{1,0:T(8,128)(2,1)S(1)}, bf16[320,1024]{1,0:T(8,128)(2,1)S(1)}, f32[320,256]{1,0:T(8,128)S(1)}...) custom-call(s32[8,128]{1,0:T(8,128)S(1)} %get-tuple-element.51.plan,, ...), custom_call_target="tpu_custom_call" | custom-call | flops 922746880 | bytes 4194304 | tf_op jit(solution)/shard_map/inner_forward/pallas_call | solution.py:693
  17.0 1.6 %collective-permute-start.5 = (bf16[111,16,128]{2,1,0:T(8,128)(2,1)S(1)}, bf16[111,16,128]{2,1,0:T(8,128)(2,1)S(1)}, u32[]{:S(2)}, u32[]{:S(2)}) collective-permute-start(bf16[111,16,128]{2,1,0:T(8,128)(2,1)S(1)} %constant_dynamic-update-slice_fusion.refs_0_), channel_id=1, source_target_pairs={{0,4},{4,0},{8,12},{12,8},{16,20},{20,16},{24,28},{28,24},{1,5},{5... | collective-permute-start | bytes 1363976 | tf_op jit(solution)/shard_map/ppermute | solution.py:664
  18.6 0.1 collective-permute-start.6
  18.7 1.7 %outer_forward.1 = (bf16[192,1024]{1,0:T(8,128)(2,1)S(1)}, bf16[192,1024]{1,0:T(8,128)(2,1)S(1)}, f32[192,256]{1,0:T(8,128)S(1)}, bf16[320,1024]{1,0:T(8,128)(2,...) custom-call(s32[8,128]{1,0:T(8,128)S(1)} %get-tuple-element.51.plan, ...), custom_call_target="tpu_custom_call" | custom-call | flops 5536481280 | bytes 41943040 | tf_op jit(solution)/shard_map/outer_forward/pallas_call | solution.py:738
  20.4 2.5 %outer_backward.1 = (s32[8,128]{1,0:T(8,128)S(1)}, f32[512,128]{1,0:T(8,128)S(1)}, bf16[4,16,128]{2,1,0:T(8,128)(2,1)S(1)}, bf16[4,16,128]{2,1,0:T(8,128)(2,1)S(1)}) custom-call(s32[8,128]{1,0:T(8,128)S(1)} %get-tuple-element.51.plan, bf16[111,16,128]{2,1,0:T(8,128)(2,1)S(1)} %constant_dynamic-update-slice_fusion.refs_0_, ...), custom_call_target="tpu_custom_call" | custom-call | flops 553648128 | bytes 4194304 | tf_op jit(solution)/shard_map/outer_backward/pallas_call | solution.py:757
  22.9 1.5 %collective-permute-start.9 = (bf16[4,16,128]{2,1,0:T(8,128)(2,1)S(1)}, bf16[4,16,128]{2,1,0:T(8,128)(2,1)S(1)}, u32[]{:S(2)}, u32[]{:S(2)}) collective-permute-start(bf16[4,16,128]{2,1,0:T(8,128)(2,1)S(1)} %get-tuple-element.83), channel_id=1, source_target_pairs={{1,2},{2,1},{3,0},{0,3},{5,6},{6,5},{7,4},{4,7},{9,10},{10,9},{11,... | collective-permute-start | bytes 49160 | tf_op jit(solution)/shard_map/ppermute | solution.py:571
  24.4 0.4 collective-permute-start.10
  24.8 3.4 %inner_backward.1.own = f32[4,128,128]{2,1,0:T(8,128)S(1)} custom-call(s32[8,128]{1,0:T(8,128)S(1)} %get-tuple-element.51.plan, s32[8,128]{1,0:T(8,128)S(1)} %get-tuple-element.87.table_rows, f32[512,128]{1,0:T(8,128)S(1)} %get-tuple-element.88.sens, bf16[111,16,128]{2,1,0:T(8,128)(2,1)S(1)} %constant_dynamic-update-slice_fusion.refs_0_, ...), custom_call_target="tpu_custom_call" | custom-call | flops 922746880 | bytes 4194304 | tf_op jit(solution)/shard_map/inner_backward/pallas_call | solution.py:785
  28.2 0.8 %lon_back.1 = (f32[16,32,128]{2,1,0:T(8,128)S(1)}, bf16[16,32,128]{2,1,0:T(8,128)(2,1)S(1)}, bf16[16,32,128]{2,1,0:T(8,128)(2,1)S(1)}) custom-call(bf16[4,16,128]{2,1,0:T(8,128)(2,1)S(1)} %collective-permute-done.9.far, bf16[4,16,128]{2,1,0:T(8,128)(2,1)S(1)} %collective-permute-done.10.close, f32[4,128,128]{2,1,0:T(8,128)S(1)} %inner_backward.1.own, ...), custom_call_target="tpu_custom_call" | custom-call | flops 4325376 | bytes 524288 | tf_op jit(solution)/shard_map/lon_back/pallas_call | solution.py:805
  29.0 4.8 %collective-permute-start.11 = (bf16[16,32,128]{2,1,0:T(8,128)(2,1)S(1)}, bf16[16,32,128]{2,1,0:T(8,128)(2,1)S(1)}, u32[]{:S(2)}, u32[]{:S(2)}) collective-permute-start(bf16[16,32,128]{2,1,0:T(8,128)(2,1)S(1)} %get-tuple-element.92), channel_id=1, source_target_pairs={{4,8},{8,4},{12,16},{16,12},{20,24},{24,20},{5,9},{9,5},{13,17},{1... | collective-permute-start | bytes 393224 | tf_op jit(solution)/shard_map/ppermute | solution.py:571
  33.8 0.1 collective-permute-start.12
  33.9 1.3 %lat_back_own.1.own_part = f32[16,32,128]{2,1,0:T(8,128)S(1)} custom-call(f32[16,32,128]{2,1,0:T(8,128)S(1)} %get-tuple-element.96.back, f32[16,32,128]{2,1,0:T(8,128)} %control.5), custom_call_target="tpu_custom_call" | custom-call | flops 2162688 | bytes 786432 | tf_op jit(solution)/shard_map/lat_back_own/pallas_call | solution.py:816
  35.2 2.6 %collective-permute-done.11.far = bf16[16,32,128]{2,1,0:T(8,128)(2,1)S(1)} collective-permute-done((bf16[16,32,128]{2,1,0:T(8,128)(2,1)S(1)}, bf16[16,32,128]{2,1,0:T(8,128)(2,1)S(1)}, u32[]{:S(2)}, u32[]{:S(2)}) %collective-permute-start.11) | collective-permute-done | bytes 131104 | tf_op jit(solution)/shard_map/ppermute | solution.py:571
  37.7 1.0 %lat_back.1 = f32[16,32,128]{2,1,0:T(8,128)} custom-call(bf16[16,32,128]{2,1,0:T(8,128)(2,1)S(1)} %collective-permute-done.11.far, bf16[16,32,128]{2,1,0:T(8,128)(2,1)S(1)} %collective-permute-done.12.close, f32[16,32,128]{2,1,0:T(8,128)S(1)} %lat_back_own.1.own_part), custom_call_target="tpu_custom_call" | custom-call | flops 2162688 | bytes 1048576 | tf_op jit(solution)/shard_map/lat_back/pallas_call | solution.py:827
  (15 shorter events, 0.1 us)
Async XLA Ops:
  1.1 8.8 %collective-permute-start.3 = (bf16[16,32,128]{2,1,0:T(8,128)(2,1)S(1)}, bf16[16,32,128]{2,1,0:T(8,128)(2,1)S(1)}, u32[]{:S(2)}, u32[]{:S(2)}) collective-permute-start(bf16[16,32,128]{2,1,0:T(8,128)(2,1)S(1)} %get-tuple-element.54), channel_id=1, source_target_pairs={{4,8},{8,4},{12,16},{16,12},{20,24},{24,20},{5,9},{9,5},{13,17},{1... | collective-permute-start | bytes 393224 | tf_op jit(solution)/shard_map/ppermute | solution.py:571
  5.6 4.3 %collective-permute-start.4 = (bf16[16,32,128]{2,1,0:T(8,128)(2,1)S(1)}, bf16[16,32,128]{2,1,0:T(8,128)(2,1)S(1)}, u32[]{:S(2)}, u32[]{:S(2)}) collective-permute-start(bf16[16,32,128]{2,1,0:T(8,128)(2,1)S(1)} %get-tuple-element.55), channel_id=1, source_target_pairs={{0,4},{4,0},{8,12},{12,8},{16,20},{20,16},{24,28},{28,24},{1,5},{5... | collective-permute-start | bytes 393224 | tf_op jit(solution)/shard_map/ppermute | solution.py:571
  5.7 11.1 %collective-permute-start = (bf16[37,16,128]{2,1,0:T(8,128)(2,1)S(1)}, bf16[37,16,128]{2,1,0:T(8,128)(2,1)S(1)}, u32[]{:S(2)}, u32[]{:S(2)}) collective-permute-start(bf16[37,16,128]{2,1,0:T(8,128)(2,1)S(1)} %get-tuple-element.63), channel_id=1, source_target_pairs={{0,16},{4,20},{8,24},{12,28},{16,0},{20,4},{24,8},{28,12},{1,17},{... | collective-permute-start | bytes 454664 | tf_op jit(solution)/shard_map/ppermute | solution.py:664
  7.0 9.8 %collective-permute-start.1 = (bf16[37,16,128]{2,1,0:T(8,128)(2,1)S(1)}, bf16[37,16,128]{2,1,0:T(8,128)(2,1)S(1)}, u32[]{:S(2)}, u32[]{:S(2)}) collective-permute-start(bf16[37,16,128]{2,1,0:T(8,128)(2,1)S(1)} %get-tuple-element.63), channel_id=1, source_target_pairs={{0,8},{4,12},{8,0},{12,4},{16,24},{20,28},{24,16},{28,20},{1,9},{5... | collective-permute-start | bytes 454664 | tf_op jit(solution)/shard_map/ppermute | solution.py:664
  7.1 9.8 %collective-permute-start.2 = (bf16[37,16,128]{2,1,0:T(8,128)(2,1)S(1)}, bf16[37,16,128]{2,1,0:T(8,128)(2,1)S(1)}, u32[]{:S(2)}, u32[]{:S(2)}) collective-permute-start(bf16[37,16,128]{2,1,0:T(8,128)(2,1)S(1)} %get-tuple-element.63), channel_id=1, source_target_pairs={{0,24},{4,28},{8,16},{12,20},{16,8},{20,12},{24,0},{28,4},{1,25},{... | collective-permute-start | bytes 454664 | tf_op jit(solution)/shard_map/ppermute | solution.py:664
  10.3 8.3 %collective-permute-start.7 = (f32[4,16,128]{2,1,0:T(8,128)S(1)}, f32[4,16,128]{2,1,0:T(8,128)S(1)}, u32[]{:S(2)}, u32[]{:S(2)}) collective-permute-start(f32[4,16,128]{2,1,0:T(8,128)S(1)} %get-tuple-element.70), channel_id=1, source_target_pairs={{1,2},{2,1},{3,0},{0,3},{5,6},{6,5},{7,4},{4,7},{9,10},{10,9},{11,... | collective-permute-start | bytes 98312 | tf_op jit(solution)/shard_map/ppermute | solution.py:571
  13.7 4.9 %collective-permute-start.8 = (f32[4,16,128]{2,1,0:T(8,128)S(1)}, f32[4,16,128]{2,1,0:T(8,128)S(1)}, u32[]{:S(2)}, u32[]{:S(2)}) collective-permute-start(f32[4,16,128]{2,1,0:T(8,128)S(1)} %get-tuple-element.72), channel_id=1, source_target_pairs={{0,1},{1,0},{2,3},{3,2},{4,5},{5,4},{6,7},{7,6},{8,9},{9,8},{10,11... | collective-permute-start | bytes 98312 | tf_op jit(solution)/shard_map/ppermute | solution.py:571
  17.0 3.4 %collective-permute-start.5 = (bf16[111,16,128]{2,1,0:T(8,128)(2,1)S(1)}, bf16[111,16,128]{2,1,0:T(8,128)(2,1)S(1)}, u32[]{:S(2)}, u32[]{:S(2)}) collective-permute-start(bf16[111,16,128]{2,1,0:T(8,128)(2,1)S(1)} %constant_dynamic-update-slice_fusion.refs_0_), channel_id=1, source_target_pairs={{0,4},{4,0},{8,12},{12,8},{16,20},{20,16},{24,28},{28,24},{1,5},{5... | collective-permute-start | bytes 1363976 | tf_op jit(solution)/shard_map/ppermute | solution.py:664
  18.6 1.8 %collective-permute-start.6 = (bf16[37,16,128]{2,1,0:T(8,128)(2,1)S(1)}, bf16[37,16,128]{2,1,0:T(8,128)(2,1)S(1)}, u32[]{:S(2)}, u32[]{:S(2)}) collective-permute-start(bf16[37,16,128]{2,1,0:T(8,128)(2,1)S(1)} %collective-permute-done.2.refs_1_), channel_id=1, source_target_pairs={{0,4},{4,0},{8,12},{12,8},{16,20},{20,16},{24,28},{28,24},{1,5},{5... | collective-permute-start | bytes 454664 | tf_op jit(solution)/shard_map/ppermute | solution.py:664
  22.9 5.3 %collective-permute-start.9 = (bf16[4,16,128]{2,1,0:T(8,128)(2,1)S(1)}, bf16[4,16,128]{2,1,0:T(8,128)(2,1)S(1)}, u32[]{:S(2)}, u32[]{:S(2)}) collective-permute-start(bf16[4,16,128]{2,1,0:T(8,128)(2,1)S(1)} %get-tuple-element.83), channel_id=1, source_target_pairs={{1,2},{2,1},{3,0},{0,3},{5,6},{6,5},{7,4},{4,7},{9,10},{10,9},{11,... | collective-permute-start | bytes 49160 | tf_op jit(solution)/shard_map/ppermute | solution.py:571
  24.4 3.8 %collective-permute-start.10 = (bf16[4,16,128]{2,1,0:T(8,128)(2,1)S(1)}, bf16[4,16,128]{2,1,0:T(8,128)(2,1)S(1)}, u32[]{:S(2)}, u32[]{:S(2)}) collective-permute-start(bf16[4,16,128]{2,1,0:T(8,128)(2,1)S(1)} %get-tuple-element.85), channel_id=1, source_target_pairs={{0,1},{1,0},{2,3},{3,2},{4,5},{5,4},{6,7},{7,6},{8,9},{9,8},{10,11... | collective-permute-start | bytes 49160 | tf_op jit(solution)/shard_map/ppermute | solution.py:571
  29.0 8.8 %collective-permute-start.11 = (bf16[16,32,128]{2,1,0:T(8,128)(2,1)S(1)}, bf16[16,32,128]{2,1,0:T(8,128)(2,1)S(1)}, u32[]{:S(2)}, u32[]{:S(2)}) collective-permute-start(bf16[16,32,128]{2,1,0:T(8,128)(2,1)S(1)} %get-tuple-element.92), channel_id=1, source_target_pairs={{4,8},{8,4},{12,16},{16,12},{20,24},{24,20},{5,9},{9,5},{13,17},{1... | collective-permute-start | bytes 393224 | tf_op jit(solution)/shard_map/ppermute | solution.py:571
  33.8 3.9 %collective-permute-start.12 = (bf16[16,32,128]{2,1,0:T(8,128)(2,1)S(1)}, bf16[16,32,128]{2,1,0:T(8,128)(2,1)S(1)}, u32[]{:S(2)}, u32[]{:S(2)}) collective-permute-start(bf16[16,32,128]{2,1,0:T(8,128)(2,1)S(1)} %get-tuple-element.94), channel_id=1, source_target_pairs={{0,4},{4,0},{8,12},{12,8},{16,20},{20,16},{24,28},{28,24},{1,5},{5... | collective-permute-start | bytes 393224 | tf_op jit(solution)/shard_map/ppermute | solution.py:571

commit v9 on v8

--- a/solution.py
+++ b/solution.py
@@ -102,7 +102,21 @@
 
 
 def first_kernel(
-    radiance, block_owner, channel_count, control, slabs, to_far, to_close, owners, counts, rows, tables, held, sems
+    radiance,
+    block_owner,
+    channel_count,
+    control,
+    background,
+    slabs,
+    to_far,
+    to_close,
+    held,
+    field,
+    owners,
+    counts,
+    rows,
+    tables,
+    sems,
 ):
     recv_most = radiance.shape[0]
     moves = [
@@ -113,8 +127,9 @@
     piece = control.shape[0] // BAND_PIECES
     for k in range(BAND_PIECES):
         part = pl.ds(k * piece, piece)
-        moves.append(pltpu.make_async_copy(control.at[part], held.at[part], sems.at[4 + k]))
-    for move in moves[3:] + moves[:3]:
+        moves.append(pltpu.make_async_copy(control.at[part], held.at[part], sems.at[5 + k]))
+    field_in = pltpu.make_async_copy(background, field, sems.at[4])
+    for move in moves[3:] + moves[:3] + [field_in]:
         move.start()
     rows[...] = jnp.full(rows.shape, -1.0, jnp.float32)
     moves[1].wait()
@@ -128,15 +143,16 @@
         move.wait()
     halve_for_sides(held, held.shape[0], to_far, to_close)
     moves[0].wait()
+    field_in.wait()
     last.wait()
 
 
 def prepare_kernel(
     lon_width,
-    background,
     block_cells,
     block_owner,
-    control,
+    field,
+    band,
     taps,
     turned,
     plan,
@@ -144,25 +160,27 @@
     widths,
     cells,
     owners,
-    field,
-    band,
     sems,
 ):
     moves = [
         pltpu.make_async_copy(lon_width, widths, sems.at[0]),
         pltpu.make_async_copy(block_cells, cells, sems.at[1]),
         pltpu.make_async_copy(block_owner, owners, sems.at[2]),
-        pltpu.make_async_copy(background, field, sems.at[3]),
-        pltpu.make_async_copy(control, band, sems.at[4]),
     ]
     tiles = turned.shape[0]
-    height, levels, width = background.shape
+    height, levels, width = field.shape
     per_tile = height // tiles
     for move in moves:
         move.start()
     groups = width // BLOCK_COLS
     rim = REACH // BLOCK_COLS
     slot_count = cells.shape[1]
+
+    for row in range(height):
+        own_part[row] = lat_sum(band, row, 0, height)
+    for tile in range(tiles):
+        block = field[tile * per_tile : (tile + 1) * per_tile].reshape(per_tile * levels, width)
+        turned[tile] = jnp.transpose(block)
 
     lane_row = lax.broadcasted_iota(jnp.int32, (1, LANES), 1) // levels
     steps = lax.broadcasted_iota(jnp.int32, (taps.shape[1], LANES), 0)
@@ -198,14 +216,6 @@
     plan[1:2, :] = jnp.sum(jnp.where(hit, slot, 0), axis=0, keepdims=True)
     plan[2:3, :] = jnp.broadcast_to(outer_count, (1, LANES))
 
-    moves[3].wait()
-    for tile in range(tiles):
-        block = field[tile * per_tile : (tile + 1) * per_tile].reshape(per_tile * levels, width)
-        turned[tile] = jnp.transpose(block)
-    moves[4].wait()
-    for row in range(height):
-        own_part[row] = lat_sum(band, row, 0, height)
-
 
 def swap_bits(count):
     return list(range(count.bit_length() - 2, 0, -1))
@@ -363,18 +373,15 @@
     net_rest(weights, states)
 
 
-def slopes(states, slope_one, slope_two):
-    for act, slope in zip(states, (slope_one, slope_two)):
-        value = act[...].astype(jnp.float32)
-        slope[...] = 1.0 - value * value
-
-
-def net_backward(observed, emitted, slope_one, slope_two, weights):
+def net_backward(observed, states, weights):
     wide_in, weight_two, weight_out = weights[:3]
+    act_one, act_two, emitted = states
     seen = observed[...]
     misfit = jnp.where(seen < jnp.inf, emitted[...] - seen, 0.0).astype(jnp.bfloat16)
-    grad_two = (dot_t(misfit, weight_out[...]) * slope_two[...]).astype(jnp.bfloat16)
-    grad_one = (dot_t(grad_two, weight_two[...]) * slope_one[...]).astype(jnp.bfloat16)
+    two = act_two[...].astype(jnp.float32)
+    grad_two = (dot_t(misfit, weight_out[...]) * (1.0 - two * two)).astype(jnp.bfloat16)
+    one = act_one[...].astype(jnp.float32)
+    grad_one = (dot_t(grad_two, weight_two[...]) * (1.0 - one * one)).astype(jnp.bfloat16)
     return rounded(dot_t(grad_one, wide_in[...]))
 
 
@@ -459,7 +466,7 @@
     slabs, refs = refs[:parts], refs[parts:]
     weights, states, late_states, refs = refs[:3], refs[3:6], refs[6:9], refs[9:]
     (table_rows, sens, to_far, to_close) = refs[:4]
-    (rows, table, observed, late_observed, field, *slope, sems) = refs[4:]
+    (rows, table, observed, late_observed, field, sems) = refs[4:]
     tiles = to_far.shape[0]
     width = field.shape[0] // tiles
     outer_slots = observed.shape[0] // BLOCK_COLS
@@ -471,21 +478,17 @@
     table_in = pltpu.make_async_copy(table_rows, table, sems.at[1])
     table_in.start()
     field[...] = jnp.zeros_like(field)
-    slopes(states, *slope[:2])
     plan_in.wait()
     table_in.wait()
 
     take_observed(rows, table, slabs, observed, 0, outer_slots)
-    sens[0 : outer_slots * BLOCK_COLS, :] = net_backward(observed, states[2], *slope[:2], weights)
+    sens[0 : outer_slots * BLOCK_COLS, :] = net_backward(observed, states, weights)
     land_blocks(rows, field, sens, 0, outer_slots, per_tile, width)
 
     @pl.when(rows[2, 0] > outer_slots)
     def _():
         take_observed(rows, table, slabs, late_observed, outer_slots, late_slots)
-        slopes(late_states, *slope[2:])
-        sens[outer_slots * BLOCK_COLS :, :] = net_backward(
-            late_observed, late_states[2], *slope[2:], weights
-        )
+        sens[outer_slots * BLOCK_COLS :, :] = net_backward(late_observed, late_states, weights)
         land_blocks(rows, field, sens, outer_slots, late_slots, per_tile, width)
 
     for tile in range(tiles):
@@ -498,7 +501,7 @@
 def inner_backward_kernel(per_tile, parts, outer_slots, plan, table_rows, sens, *refs):
     slabs, refs = refs[:parts], refs[parts:]
     weights, states, refs = refs[:3], refs[3:6], refs[6:]
-    landing, rows, table, observed, inner, field, *slope, sems = refs
+    landing, rows, table, observed, inner, field, sems = refs
     tiles, width, _ = landing.shape
     late_slots = observed.shape[0] // BLOCK_COLS
     split = outer_slots * BLOCK_COLS
@@ -510,14 +513,13 @@
         move.start()
     field[...] = jnp.zeros_like(field)
     inner[...] = sens[...]
-    slopes(states, *slope)
     for move in moves:
         move.wait()
 
     @pl.when(rows[2, 0] <= outer_slots)
     def _():
         take_observed(rows, table, slabs, observed, outer_slots, late_slots)
-        inner[split:, :] = net_backward(observed, states[2], *slope, weights)
+        inner[split:, :] = net_backward(observed, states, weights)
 
     land_blocks(rows, field, inner, 0, outer_slots + late_slots, per_tile, width)
     for tile in range(tiles):
@@ -536,13 +538,10 @@
     halve_for_sides(back, height, to_far, to_close)
 
 
-def own_back_kernel(back, control, own_part, held, sem):
-    control_in = pltpu.make_async_copy(control, held, sem)
-    control_in.start()
-    control_in.wait()
+def own_back_kernel(back, control, own_part):
     height = back.shape[0]
     for row in range(height):
-        own_part[row] = lat_sum(back, row, 0, height, held[row])
+        own_part[row] = lat_sum(back, row, 0, height, control[row])
 
 
 def lat_back_kernel(far, close, own_part, gradient, halos, done, sems):
@@ -606,23 +605,36 @@
     radiance = radiance.T.reshape(recv_most, BLOCK_COLS, halves, LANES)
     radiance = jnp.swapaxes(radiance, 1, 2).reshape(recv_most, slab_rows, LANES)
     half_field = shape(control.shape, bf16)
-    slabs, to_far, to_close = call(
+    slabs, to_far, to_close, held, ground = call(
         first_kernel,
-        (shape((recv_most + 1, slab_rows, LANES), bf16), half_field, half_field),
-        [HBM] * 4,
-        (HBM, VMEM, VMEM),
+        (
+            shape((recv_most + 1, slab_rows, LANES), bf16),
+            half_field,
+            half_field,
+            shape(control.shape, f32),
+            shape(control.shape, f32),
+        ),
+        [HBM] * 5,
+        (HBM,) + (VMEM,) * 4,
         0,
-        16 * field,
+        24 * field,
         scratch=(
             pltpu.VMEM((1, slot_count), i32),
             pltpu.VMEM((1, recv_most), i32),
             pltpu.VMEM((slab_rows, LANES), f32),
             pltpu.VMEM((slab_rows, LANES), bf16),
-            pltpu.VMEM(control.shape, f32),
-            pltpu.SemaphoreType.DMA((4 + BAND_PIECES,)),
+            pltpu.SemaphoreType.DMA((5 + BAND_PIECES,)),
         ),
         name="slabs_halves",
-    )(*pinned(radiance, block_owner.reshape(1, slot_count), channel_count.reshape(1, recv_most), control))
+    )(
+        *pinned(
+            radiance,
+            block_owner.reshape(1, slot_count),
+            channel_count.reshape(1, recv_most),
+            control,
+            background,
+        )
+    )
     far, close, sent = exchange(to_far, to_close, "lat", False)
 
     band = pltpu.VMEM((height, levels, width), f32)
@@ -634,7 +646,7 @@
             shape((8, LANES), i32),
             shape(control.shape, f32),
         ),
-        [HBM] * 5,
+        [HBM] * 3 + [VMEM] * 2,
         (VMEM,) * 4,
         conv_flops // 2,
         12 * field,
@@ -642,19 +654,13 @@
             pltpu.SMEM((height,), i32),
             pltpu.VMEM((1, slot_count), i32),
             pltpu.VMEM((1, slot_count), i32),
-            band,
-            band,
-            pltpu.SemaphoreType.DMA((5,)),
+            pltpu.SemaphoreType.DMA((3,)),
         ),
         name="taps_background",
     )(
-        *pinned(
-            lon_width,
-            background,
-            block_cells.reshape(1, slot_count),
-            block_owner.reshape(1, slot_count),
-            control,
-        )
+        *pinned(lon_width, block_cells.reshape(1, slot_count), block_owner.reshape(1, slot_count)),
+        ground,
+        held,
     )
 
     lat_count = lax.axis_size("lat")
@@ -772,10 +778,6 @@
             pltpu.VMEM((outer_rows, channels), f32),
             pltpu.VMEM((late_rows, channels), f32),
             flat,
-            pltpu.VMEM((outer_rows, hidden), f32),
-            pltpu.VMEM((outer_rows, hidden), f32),
-            pltpu.VMEM((late_rows, hidden), f32),
-            pltpu.VMEM((late_rows, hidden), f32),
             pltpu.SemaphoreType.DMA((2,)),
         ),
         name="outer_backward",
@@ -795,8 +797,6 @@
             pltpu.VMEM((late_rows, channels), f32),
             pltpu.VMEM((x_rows, LANES), f32),
             flat,
-            pltpu.VMEM((late_rows, hidden), f32),
-            pltpu.VMEM((late_rows, hidden), f32),
             pltpu.SemaphoreType.DMA((2,)),
         ),
         name="inner_backward",
@@ -812,17 +812,18 @@
         scratch=(pltpu.VMEM((tiles, width + 2 * REACH, LANES), f32),),
         name="lon_back",
     )(far, close, landing, taps)
-    far, close, sent = exchange(to_far, to_close, "lat", False)
+    back, _ = lax.optimization_barrier((back, to_far))
     own_part = call(
         own_back_kernel,
         shape((height, levels, width), f32),
-        [VMEM, HBM],
+        [VMEM, VMEM],
         VMEM,
         conv_flops // 2,
         12 * field,
-        scratch=(band, pltpu.SemaphoreType.DMA),
         name="lat_back_own",
-    )(back, *pinned(control))
+    )(back, held)
+    to_close, _ = lax.optimization_barrier((to_close, own_part))
+    far, close, _ = exchange(to_far, to_close, "lat", False)
 
     return call(
         lat_back_kernel,

time: 39.2 us -> 39.4 us (level)
  Pallas kernels: 16.7 us -> 15.3 us
  waiting for transfers between devices: 2.61 us -> 3.66 us
  starting transfers between devices: 19.2 us -> 19.8 us
    ppermute x4, waiting for transfers between devices: 2.58 us -> 3.63 us  [exchange(): lax.ppermute(to_far, axis, far)]
    ppermute x4, starting transfers between devices: 14.2 us -> 15.2 us  [exchange(): lax.ppermute(to_far, axis, far)]
    pallas_call x1, Pallas kernels: 1.26 us -> 0.32 us  [shards(): call(own_back_kernel, shape((height, levels, width), f32), [VMEM, VMEM],...]
    pallas_call x1, Pallas kernels: 1.45 us -> 0.9 us  [shards(): call(prepare_kernel, (shape((tiles, 24, LANES), f32), shape((tiles, width...]
  transfers between devices with their start and end apart: 13 -> 13, of which waited for: 1 -> 1; matrix products, arithmetic and copies ran while one was open for 0% -> 0% of each run, Pallas kernels for 29% -> 25%
where the time goes in v9:
time: 39.4 us; the launch traced here: 39.2 us
  starting transfers between devices  19.8 us (50%)
  Pallas kernels  15.3 us (39%)
  waiting for transfers between devices  3.66 us (9%)
    ppermute x4, starting transfers between devices, exchange(): lax.ppermute(to_far, axis, far)  15.2 us
    ppermute x5, starting transfers between devices, swapped(): return lax.ppermute(part, 'lat', [(i, i ^ apart) for i in range(lat_count)])  4.41 us
    ppermute x4, waiting for transfers between devices, exchange(): lax.ppermute(to_far, axis, far)  3.63 us
    pallas_call x1, Pallas kernels, shards(): call(functools.partial(inner_backward_kernel, per_tile, len(slabs), outer...  3.35 us
    pallas_call x1, Pallas kernels, shards(): call(functools.partial(inner_forward_kernel, per_tile, outer_slots), (sha...  3.11 us
    pallas_call x1, Pallas kernels, shards(): call(functools.partial(outer_backward_kernel, per_tile, len(slabs), recv_...  2.43 us
    pallas_call x1, Pallas kernels, shards(): call(functools.partial(outer_forward_kernel, per_tile), state_shapes(oute...  1.72 us
    pallas_call x1, Pallas kernels, shards(): call(first_kernel, (shape((recv_most + 1, slab_rows, LANES), bf16), half_...  1.27 us
  transfers between devices with their start and end apart: 13, of which 1 were waited for; matrix products, arithmetic and copies ran while one was open for 0% of the time, Pallas kernels for 25%

profile of v9, /device:TPU:1, one launch (start us, length us, event | category | flops | bytes accessed | tf_op | source)
XLA Modules:
  0.0 39.2 jit_solution(16081367669542225136)
XLA Ops:
  0.0 1.3 %slabs_halves.1 = (bf16[37,16,128]{2,1,0:T(8,128)(2,1)S(1)}, bf16[16,32,128]{2,1,0:T(8,128)(2,1)S(1)}, bf16[16,32,128]{2,1,0:T(8,128)(2,1)S(1)}, f32[16,32,128]{2,1,0:T(8,128)S(1)}, f32[16,32,128]{2,1,0:T(8,128)S(1)}) custom-call(bf16[36,16,128]{2,1,0:T(8,128)(2,1)} %bitcast.13, s32[1,64]{1,0:T(1,128)} %bitcast.14, s32[1,36]{1,0:T(1,128)} %bitcast.17, ...), custom_call_target="tpu_custom_call" | custom-call | bytes 1572864 | tf_op jit(solution)/shard_map/slabs_halves/pallas_call | solution.py:608
  1.3 4.5 %collective-permute-start.3 = (bf16[16,32,128]{2,1,0:T(8,128)(2,1)S(1)}, bf16[16,32,128]{2,1,0:T(8,128)(2,1)S(1)}, u32[]{:S(2)}, u32[]{:S(2)}) collective-permute-start(bf16[16,32,128]{2,1,0:T(8,128)(2,1)S(1)} %get-tuple-element.60), channel_id=1, source_target_pairs={{4,8},{8,4},{12,16},{16,12},{20,24},{24,20},{5,9},{9,5},{13,17},{1... | collective-permute-start | bytes 393224 | tf_op jit(solution)/shard_map/ppermute | solution.py:570
  5.8 0.1 collective-permute-start.4
  5.9 1.3 %collective-permute-start = (bf16[37,16,128]{2,1,0:T(8,128)(2,1)S(1)}, bf16[37,16,128]{2,1,0:T(8,128)(2,1)S(1)}, u32[]{:S(2)}, u32[]{:S(2)}) collective-permute-start(bf16[37,16,128]{2,1,0:T(8,128)(2,1)S(1)} %get-tuple-element.69), channel_id=1, source_target_pairs={{0,16},{4,20},{8,24},{12,28},{16,0},{20,4},{24,8},{28,12},{1,17},{... | collective-permute-start | bytes 454664 | tf_op jit(solution)/shard_map/ppermute | solution.py:670
  7.2 0.1 collective-permute-start.1
  7.2 1.3 %collective-permute-start.2 = (bf16[37,16,128]{2,1,0:T(8,128)(2,1)S(1)}, bf16[37,16,128]{2,1,0:T(8,128)(2,1)S(1)}, u32[]{:S(2)}, u32[]{:S(2)}) collective-permute-start(bf16[37,16,128]{2,1,0:T(8,128)(2,1)S(1)} %get-tuple-element.69), channel_id=1, source_target_pairs={{0,24},{4,28},{8,16},{12,20},{16,8},{20,12},{24,0},{28,4},{1,25},{... | collective-permute-start | bytes 454664 | tf_op jit(solution)/shard_map/ppermute | solution.py:670
  8.6 0.9 %taps_background.1 = (f32[4,24,128]{2,1,0:T(8,128)S(1)}, f32[4,128,128]{2,1,0:T(8,128)S(1)}, s32[8,128]{1,0:T(8,128)S(1)}, f32[16,32,128]{2,1,0:T(8,128)S(1)}) custom-call(s32[16]{0:T(128)} %lon_width.1, s32[1,64]{1,0:T(1,128)} %bitcast.16, s32[1,64]{1,0:T(1,128)} %bitcast.15, f32[16,32,128]{2,1,0:T(8,128)S(1)} %get-tuple-element.55.field, ...), custom_call_target="tpu_custom_call" | custom-call | flops 2162688 | bytes 786432 | tf_op jit(solution)/shard_map/taps_background/pallas_call | solution.py:641
  9.5 0.0 collective-permute-done.3.far
  9.5 0.0 collective-permute-done.4.close
  9.5 0.4 %lat_smooth.1 = (f32[4,128,128]{2,1,0:T(8,128)S(1)}, f32[4,16,128]{2,1,0:T(8,128)S(1)}, f32[4,16,128]{2,1,0:T(8,128)S(1)}) custom-call(bf16[16,32,128]{2,1,0:T(8,128)(2,1)S(1)} %collective-permute-done.3.far, bf16[16,32,128]{2,1,0:T(8,128)(2,1)S(1)} %collective-permute-done.4.close, f32[16,32,128]{2,1,0:T(8,128)S(1)} %get-tuple-element.64.own_part), custom_call_target="tpu_custom_call" | custom-call | flops 4325376 | bytes 1048576 | tf_op jit(solution)/shard_map/lat_smooth/pallas_call | solution.py:676
  10.0 3.4 %collective-permute-start.7 = (f32[4,16,128]{2,1,0:T(8,128)S(1)}, f32[4,16,128]{2,1,0:T(8,128)S(1)}, u32[]{:S(2)}, u32[]{:S(2)}) collective-permute-start(f32[4,16,128]{2,1,0:T(8,128)S(1)} %get-tuple-element.76), channel_id=1, source_target_pairs={{1,2},{2,1},{3,0},{0,3},{5,6},{6,5},{7,4},{4,7},{9,10},{10,9},{11,... | collective-permute-start | bytes 98312 | tf_op jit(solution)/shard_map/ppermute | solution.py:570
  13.3 3.1 %inner_forward.1 = (f32[512,128]{1,0:T(8,128)S(1)}, bf16[320,1024]{1,0:T(8,128)(2,1)S(1)}, bf16[320,1024]{1,0:T(8,128)(2,1)S(1)}, f32[320,256]{1,0:T(8,128)S(1)}...) custom-call(s32[8,128]{1,0:T(8,128)S(1)} %get-tuple-element.57.plan,, ...), custom_call_target="tpu_custom_call" | custom-call | flops 922746880 | bytes 4194304 | tf_op jit(solution)/shard_map/inner_forward/pallas_call | solution.py:699
  16.6 1.6 %collective-permute-start.5 = (bf16[111,16,128]{2,1,0:T(8,128)(2,1)S(1)}, bf16[111,16,128]{2,1,0:T(8,128)(2,1)S(1)}, u32[]{:S(2)}, u32[]{:S(2)}) collective-permute-start(bf16[111,16,128]{2,1,0:T(8,128)(2,1)S(1)} %constant_dynamic-update-slice_fusion.refs_0_), channel_id=1, source_target_pairs={{0,4},{4,0},{8,12},{12,8},{16,20},{20,16},{24,28},{28,24},{1,5},{5... | collective-permute-start | bytes 1363976 | tf_op jit(solution)/shard_map/ppermute | solution.py:670
  18.2 0.1 collective-permute-start.6
  18.3 1.7 %outer_forward.1 = (bf16[192,1024]{1,0:T(8,128)(2,1)S(1)}, bf16[192,1024]{1,0:T(8,128)(2,1)S(1)}, f32[192,256]{1,0:T(8,128)S(1)}, bf16[320,1024]{1,0:T(8,128)(2,...) custom-call(s32[8,128]{1,0:T(8,128)S(1)} %get-tuple-element.57.plan, ...), custom_call_target="tpu_custom_call" | custom-call | flops 5536481280 | bytes 41943040 | tf_op jit(solution)/shard_map/outer_forward/pallas_call | solution.py:744
  20.0 2.4 %outer_backward.1 = (s32[8,128]{1,0:T(8,128)S(1)}, f32[512,128]{1,0:T(8,128)S(1)}, bf16[4,16,128]{2,1,0:T(8,128)(2,1)S(1)}, bf16[4,16,128]{2,1,0:T(8,128)(2,1)S(1)}) custom-call(s32[8,128]{1,0:T(8,128)S(1)} %get-tuple-element.57.plan, bf16[111,16,128]{2,1,0:T(8,128)(2,1)S(1)} %constant_dynamic-update-slice_fusion.refs_0_, ...), custom_call_target="tpu_custom_call" | custom-call | flops 553648128 | bytes 4194304 | tf_op jit(solution)/shard_map/outer_backward/pallas_call | solution.py:763
  22.5 2.1 %collective-permute-start.9 = (bf16[4,16,128]{2,1,0:T(8,128)(2,1)S(1)}, bf16[4,16,128]{2,1,0:T(8,128)(2,1)S(1)}, u32[]{:S(2)}, u32[]{:S(2)}) collective-permute-start(bf16[4,16,128]{2,1,0:T(8,128)(2,1)S(1)} %get-tuple-element.89), channel_id=1, source_target_pairs={{1,2},{2,1},{3,0},{0,3},{5,6},{6,5},{7,4},{4,7},{9,10},{10,9},{11,... | collective-permute-start | bytes 49160 | tf_op jit(solution)/shard_map/ppermute | solution.py:570
  24.5 3.3 %inner_backward.1.own = f32[4,128,128]{2,1,0:T(8,128)S(1)} custom-call(s32[8,128]{1,0:T(8,128)S(1)} %get-tuple-element.57.plan, s32[8,128]{1,0:T(8,128)S(1)} %get-tuple-element.93.table_rows, f32[512,128]{1,0:T(8,128)S(1)} %get-tuple-element.94.sens, bf16[111,16,128]{2,1,0:T(8,128)(2,1)S(1)} %constant_dynamic-update-slice_fusion.refs_0_, ...), custom_call_target="tpu_custom_call" | custom-call | flops 922746880 | bytes 4194304 | tf_op jit(solution)/shard_map/inner_backward/pallas_call | solution.py:787
  27.9 0.8 %lon_back.1 = (f32[16,32,128]{2,1,0:T(8,128)S(1)}, bf16[16,32,128]{2,1,0:T(8,128)(2,1)S(1)}, bf16[16,32,128]{2,1,0:T(8,128)(2,1)S(1)}) custom-call(bf16[4,16,128]{2,1,0:T(8,128)(2,1)S(1)} %collective-permute-done.9.far, bf16[4,16,128]{2,1,0:T(8,128)(2,1)S(1)} %collective-permute-done.10.close, f32[4,128,128]{2,1,0:T(8,128)S(1)} %inner_backward.1.own, ...), custom_call_target="tpu_custom_call" | custom-call | flops 4325376 | bytes 524288 | tf_op jit(solution)/shard_map/lon_back/pallas_call | solution.py:805
  28.7 5.2 %collective-permute-start.11 = (bf16[16,32,128]{2,1,0:T(8,128)(2,1)S(1)}, bf16[16,32,128]{2,1,0:T(8,128)(2,1)S(1)}, u32[]{:S(2)}, u32[]{:S(2)}) collective-permute-start(bf16[16,32,128]{2,1,0:T(8,128)(2,1)S(1)} %get-tuple-element.98), channel_id=1, source_target_pairs={{4,8},{8,4},{12,16},{16,12},{20,24},{24,20},{5,9},{9,5},{13,17},{1... | collective-permute-start | bytes 393224 | tf_op jit(solution)/shard_map/ppermute | solution.py:570
  33.9 0.3 lat_back_own.1.own_part
  34.3 0.1 collective-permute-start.12
  34.3 3.6 %collective-permute-done.11.far = bf16[16,32,128]{2,1,0:T(8,128)(2,1)S(1)} collective-permute-done((bf16[16,32,128]{2,1,0:T(8,128)(2,1)S(1)}, bf16[16,32,128]{2,1,0:T(8,128)(2,1)S(1)}, u32[]{:S(2)}, u32[]{:S(2)}) %collective-permute-start.11) | collective-permute-done | bytes 131104 | tf_op jit(solution)/shard_map/ppermute | solution.py:570
  38.0 1.0 %lat_back.1 = f32[16,32,128]{2,1,0:T(8,128)} custom-call(bf16[16,32,128]{2,1,0:T(8,128)(2,1)S(1)} %collective-permute-done.11.far, bf16[16,32,128]{2,1,0:T(8,128)(2,1)S(1)} %collective-permute-done.12.close, f32[16,32,128]{2,1,0:T(8,128)S(1)} %lat_back_own.1.own_part), custom_call_target="tpu_custom_call" | custom-call | flops 2162688 | bytes 1048576 | tf_op jit(solution)/shard_map/lat_back/pallas_call | solution.py:828
  (15 shorter events, 0.1 us)
Async XLA Ops:
  1.3 8.2 %collective-permute-start.3 = (bf16[16,32,128]{2,1,0:T(8,128)(2,1)S(1)}, bf16[16,32,128]{2,1,0:T(8,128)(2,1)S(1)}, u32[]{:S(2)}, u32[]{:S(2)}) collective-permute-start(bf16[16,32,128]{2,1,0:T(8,128)(2,1)S(1)} %get-tuple-element.60), channel_id=1, source_target_pairs={{4,8},{8,4},{12,16},{16,12},{20,24},{24,20},{5,9},{9,5},{13,17},{1... | collective-permute-start | bytes 393224 | tf_op jit(solution)/shard_map/ppermute | solution.py:570
  5.8 3.7 %collective-permute-start.4 = (bf16[16,32,128]{2,1,0:T(8,128)(2,1)S(1)}, bf16[16,32,128]{2,1,0:T(8,128)(2,1)S(1)}, u32[]{:S(2)}, u32[]{:S(2)}) collective-permute-start(bf16[16,32,128]{2,1,0:T(8,128)(2,1)S(1)} %get-tuple-element.61), channel_id=1, source_target_pairs={{0,4},{4,0},{8,12},{12,8},{16,20},{20,16},{24,28},{28,24},{1,5},{5... | collective-permute-start | bytes 393224 | tf_op jit(solution)/shard_map/ppermute | solution.py:570
  5.9 10.6 %collective-permute-start = (bf16[37,16,128]{2,1,0:T(8,128)(2,1)S(1)}, bf16[37,16,128]{2,1,0:T(8,128)(2,1)S(1)}, u32[]{:S(2)}, u32[]{:S(2)}) collective-permute-start(bf16[37,16,128]{2,1,0:T(8,128)(2,1)S(1)} %get-tuple-element.69), channel_id=1, source_target_pairs={{0,16},{4,20},{8,24},{12,28},{16,0},{20,4},{24,8},{28,12},{1,17},{... | collective-permute-start | bytes 454664 | tf_op jit(solution)/shard_map/ppermute | solution.py:670
  7.2 9.3 %collective-permute-start.1 = (bf16[37,16,128]{2,1,0:T(8,128)(2,1)S(1)}, bf16[37,16,128]{2,1,0:T(8,128)(2,1)S(1)}, u32[]{:S(2)}, u32[]{:S(2)}) collective-permute-start(bf16[37,16,128]{2,1,0:T(8,128)(2,1)S(1)} %get-tuple-element.69), channel_id=1, source_target_pairs={{0,8},{4,12},{8,0},{12,4},{16,24},{20,28},{24,16},{28,20},{1,9},{5... | collective-permute-start | bytes 454664 | tf_op jit(solution)/shard_map/ppermute | solution.py:670
  7.2 9.2 %collective-permute-start.2 = (bf16[37,16,128]{2,1,0:T(8,128)(2,1)S(1)}, bf16[37,16,128]{2,1,0:T(8,128)(2,1)S(1)}, u32[]{:S(2)}, u32[]{:S(2)}) collective-permute-start(bf16[37,16,128]{2,1,0:T(8,128)(2,1)S(1)} %get-tuple-element.69), channel_id=1, source_target_pairs={{0,24},{4,28},{8,16},{12,20},{16,8},{20,12},{24,0},{28,4},{1,25},{... | collective-permute-start | bytes 454664 | tf_op jit(solution)/shard_map/ppermute | solution.py:670
  10.0 8.3 %collective-permute-start.7 = (f32[4,16,128]{2,1,0:T(8,128)S(1)}, f32[4,16,128]{2,1,0:T(8,128)S(1)}, u32[]{:S(2)}, u32[]{:S(2)}) collective-permute-start(f32[4,16,128]{2,1,0:T(8,128)S(1)} %get-tuple-element.76), channel_id=1, source_target_pairs={{1,2},{2,1},{3,0},{0,3},{5,6},{6,5},{7,4},{4,7},{9,10},{10,9},{11,... | collective-permute-start | bytes 98312 | tf_op jit(solution)/shard_map/ppermute | solution.py:570
  13.3 4.9 %collective-permute-start.8 = (f32[4,16,128]{2,1,0:T(8,128)S(1)}, f32[4,16,128]{2,1,0:T(8,128)S(1)}, u32[]{:S(2)}, u32[]{:S(2)}) collective-permute-start(f32[4,16,128]{2,1,0:T(8,128)S(1)} %get-tuple-element.78), channel_id=1, source_target_pairs={{0,1},{1,0},{2,3},{3,2},{4,5},{5,4},{6,7},{7,6},{8,9},{9,8},{10,11... | collective-permute-start | bytes 98312 | tf_op jit(solution)/shard_map/ppermute | solution.py:570
  16.6 3.4 %collective-permute-start.5 = (bf16[111,16,128]{2,1,0:T(8,128)(2,1)S(1)}, bf16[111,16,128]{2,1,0:T(8,128)(2,1)S(1)}, u32[]{:S(2)}, u32[]{:S(2)}) collective-permute-start(bf16[111,16,128]{2,1,0:T(8,128)(2,1)S(1)} %constant_dynamic-update-slice_fusion.refs_0_), channel_id=1, source_target_pairs={{0,4},{4,0},{8,12},{12,8},{16,20},{20,16},{24,28},{28,24},{1,5},{5... | collective-permute-start | bytes 1363976 | tf_op jit(solution)/shard_map/ppermute | solution.py:670
  18.2 1.8 %collective-permute-start.6 = (bf16[37,16,128]{2,1,0:T(8,128)(2,1)S(1)}, bf16[37,16,128]{2,1,0:T(8,128)(2,1)S(1)}, u32[]{:S(2)}, u32[]{:S(2)}) collective-permute-start(bf16[37,16,128]{2,1,0:T(8,128)(2,1)S(1)} %collective-permute-done.2.refs_1_), channel_id=1, source_target_pairs={{0,4},{4,0},{8,12},{12,8},{16,20},{20,16},{24,28},{28,24},{1,5},{5... | collective-permute-start | bytes 454664 | tf_op jit(solution)/shard_map/ppermute | solution.py:670
  22.5 5.4 %collective-permute-start.9 = (bf16[4,16,128]{2,1,0:T(8,128)(2,1)S(1)}, bf16[4,16,128]{2,1,0:T(8,128)(2,1)S(1)}, u32[]{:S(2)}, u32[]{:S(2)}) collective-permute-start(bf16[4,16,128]{2,1,0:T(8,128)(2,1)S(1)} %get-tuple-element.89), channel_id=1, source_target_pairs={{1,2},{2,1},{3,0},{0,3},{5,6},{6,5},{7,4},{4,7},{9,10},{10,9},{11,... | collective-permute-start | bytes 49160 | tf_op jit(solution)/shard_map/ppermute | solution.py:570
  24.5 3.4 %collective-permute-start.10 = (bf16[4,16,128]{2,1,0:T(8,128)(2,1)S(1)}, bf16[4,16,128]{2,1,0:T(8,128)(2,1)S(1)}, u32[]{:S(2)}, u32[]{:S(2)}) collective-permute-start(bf16[4,16,128]{2,1,0:T(8,128)(2,1)S(1)} %get-tuple-element.91), channel_id=1, source_target_pairs={{0,1},{1,0},{2,3},{3,2},{4,5},{5,4},{6,7},{7,6},{8,9},{9,8},{10,11... | collective-permute-start | bytes 49160 | tf_op jit(solution)/shard_map/ppermute | solution.py:570
  28.7 9.3 %collective-permute-start.11 = (bf16[16,32,128]{2,1,0:T(8,128)(2,1)S(1)}, bf16[16,32,128]{2,1,0:T(8,128)(2,1)S(1)}, u32[]{:S(2)}, u32[]{:S(2)}) collective-permute-start(bf16[16,32,128]{2,1,0:T(8,128)(2,1)S(1)} %get-tuple-element.98), channel_id=1, source_target_pairs={{4,8},{8,4},{12,16},{16,12},{20,24},{24,20},{5,9},{9,5},{13,17},{1... | collective-permute-start | bytes 393224 | tf_op jit(solution)/shard_map/ppermute | solution.py:570
  34.3 3.7 %collective-permute-start.12 = (bf16[16,32,128]{2,1,0:T(8,128)(2,1)S(1)}, bf16[16,32,128]{2,1,0:T(8,128)(2,1)S(1)}, u32[]{:S(2)}, u32[]{:S(2)}) collective-permute-start(bf16[16,32,128]{2,1,0:T(8,128)(2,1)S(1)} %get-tuple-element.103), channel_id=1, source_target_pairs={{0,4},{4,0},{8,12},{12,8},{16,20},{20,16},{24,28},{28,24},{1,5},{5... | collective-permute-start | bytes 393224 | tf_op jit(solution)/shard_map/ppermute | solution.py:570

commit v10 on v9

--- a/solution.py
+++ b/solution.py
@@ -12,8 +12,10 @@
 BLOCK_COLS = 8
 LANES = 128
 LAT_SIGMA = 8.0
-WEIGHT_PIECES = 4
+WEIGHT_PIECES = 8
 BAND_PIECES = 4
+LAT_COVER = 64
+LON_COVER = 10
 SWAP_COVER = 10
 VMEM_BYTES = 40 * 1024 * 1024
 
@@ -153,10 +155,22 @@
     block_owner,
     field,
     band,
+    in_weight,
+    in_bias,
+    mid_weight,
+    mid_bias,
+    out_weight,
+    out_bias,
     taps,
     turned,
     plan,
     own_part,
+    wide_in,
+    weight_two,
+    weight_out,
+    bias_one,
+    bias_two,
+    bias_out,
     widths,
     cells,
     owners,
@@ -170,7 +184,15 @@
     tiles = turned.shape[0]
     height, levels, width = field.shape
     per_tile = height // tiles
-    for move in moves:
+    piece = mid_weight.shape[0] // WEIGHT_PIECES
+    pieces = [pl.ds(k * piece, piece) for k in range(WEIGHT_PIECES)]
+    loads = [(in_bias, bias_one), (mid_bias, bias_two), (out_bias, bias_out), (out_weight, weight_out)]
+    loads += [(in_weight, wide_in.at[pl.ds(sub * levels, levels)]) for sub in range(per_tile)]
+    loads += [(mid_weight.at[part], weight_two.at[part]) for part in pieces]
+    loads = [
+        pltpu.make_async_copy(source, target, sems.at[3 + k]) for k, (source, target) in enumerate(loads)
+    ]
+    for move in moves + loads:
         move.start()
     groups = width // BLOCK_COLS
     rim = REACH // BLOCK_COLS
@@ -215,6 +237,8 @@
     plan[0:1, :] = jnp.sum(jnp.where(hit, cell, 0), axis=0, keepdims=True)
     plan[1:2, :] = jnp.sum(jnp.where(hit, slot, 0), axis=0, keepdims=True)
     plan[2:3, :] = jnp.broadcast_to(outer_count, (1, LANES))
+    for move in loads:
+        move.wait()
 
 
 def swap_bits(count):
@@ -386,24 +410,11 @@
 
 
 def inner_forward_kernel(per_tile, outer_slots, plan, own, turned, taps, *refs):
-    (in_weight, in_bias, mid_weight, mid_bias, out_weight, out_bias), refs = refs[:6], refs[6:]
-    profile, states, weights, (rows, padded, picked, sems) = refs[0], refs[1:4], refs[4:10], refs[10:]
-    wide_in, weight_two, weight_out, bias_one, bias_two, bias_out = weights
+    weights, profile, states, (rows, padded, picked, sem) = refs[:6], refs[6], refs[7:10], refs[10:]
     tiles, width, _ = own.shape
-    levels = in_weight.shape[0]
     count = picked.shape[0] // BLOCK_COLS
-    piece = mid_weight.shape[0] // WEIGHT_PIECES
-    pieces = [pl.ds(k * piece, piece) for k in range(WEIGHT_PIECES)]
-    loads = [(plan, rows), (in_bias, bias_one)]
-    loads += [(in_weight, wide_in.at[pl.ds(sub * levels, levels)]) for sub in range(per_tile)]
-    early = len(loads)
-    loads += [(mid_weight.at[part], weight_two.at[part]) for part in pieces] + [(mid_bias, bias_two)]
-    loads += [(out_weight, weight_out), (out_bias, bias_out)]
-    loads = [
-        pltpu.make_async_copy(source, target, sems.at[k]) for k, (source, target) in enumerate(loads)
-    ]
-    for move in loads:
-        move.start()
+    plan_in = pltpu.make_async_copy(plan, rows, sem)
+    plan_in.start()
     zeros = jnp.zeros((tiles, REACH, LANES), jnp.float32)
     padded[:, 0:REACH, :] = zeros
     padded[:, REACH : REACH + width, :] = own[...]
@@ -411,17 +422,12 @@
     for tile in range(tiles):
         total = turned[tile] + lon_conv(padded, taps, tile, 0, width)
         profile[tile * width : (tile + 1) * width, :] = rounded(total)
-    for move in loads[:early]:
-        move.wait()
-    take_blocks(rows, profile, picked, outer_slots, count, per_tile, width)
-    act_one, act_two, emitted = states
-    net_first(picked, weights, act_one)
-    for move in loads[early:]:
-        move.wait()
+    plan_in.wait()
 
     @pl.when(rows[2, 0] <= outer_slots)
     def _():
-        net_rest(weights, states)
+        take_blocks(rows, profile, picked, outer_slots, count, per_tile, width)
+        net_forward(picked, weights, states)
 
 
 def outer_forward_kernel(
@@ -638,39 +644,54 @@
     far, close, sent = exchange(to_far, to_close, "lat", False)
 
     band = pltpu.VMEM((height, levels, width), f32)
-    taps, turned, plan, own_part = call(
+    taps, turned, plan, own_part, *weights = call(
         prepare_kernel,
         (
             shape((tiles, 24, LANES), f32),
             shape((tiles, width, LANES), f32),
             shape((8, LANES), i32),
             shape(control.shape, f32),
-        ),
-        [HBM] * 3 + [VMEM] * 2,
-        (VMEM,) * 4,
+            shape((LANES, hidden), bf16),
+            shape((hidden, hidden), bf16),
+            shape((hidden, channels), bf16),
+            shape((1, hidden), f32),
+            shape((1, hidden), f32),
+            shape((1, channels), f32),
+        ),
+        [HBM] * 3 + [VMEM] * 2 + [HBM] * 6,
+        (VMEM,) * 10,
         conv_flops // 2,
         12 * field,
         scratch=(
             pltpu.SMEM((height,), i32),
             pltpu.VMEM((1, slot_count), i32),
             pltpu.VMEM((1, slot_count), i32),
-            pltpu.SemaphoreType.DMA((3,)),
+            pltpu.SemaphoreType.DMA((7 + per_tile + WEIGHT_PIECES,)),
         ),
         name="taps_background",
     )(
         *pinned(lon_width, block_cells.reshape(1, slot_count), block_owner.reshape(1, slot_count)),
         ground,
         held,
+        *pinned(
+            in_weight,
+            in_bias.reshape(1, hidden),
+            mid_weight,
+            mid_bias.reshape(1, hidden),
+            out_weight,
+            out_bias.reshape(1, channels),
+        ),
     )
 
     lat_count = lax.axis_size("lat")
     one, two, *others = swap_bits(lat_count)
 
-    def swapped(part, apart):
-        return lax.ppermute(part, "lat", [(i, i ^ apart) for i in range(lat_count)])
+    def swapped(part, apart, odd_apart=None):
+        pairs = [(i, i ^ (odd_apart if odd_apart and i % 2 else apart)) for i in range(lat_count)]
+        return lax.ppermute(part, "lat", pairs)
 
     slabs, _ = lax.optimization_barrier((slabs, sent))
-    near = [slabs] + [swapped(slabs, apart) for apart in (1 << one, 1 << two, (1 << one) + (1 << two))]
+    first, second = swapped(slabs, 1 << one), swapped(slabs, 1 << two)
 
     halos = pltpu.VMEM((2, REACH, levels, width), f32)
     smoothed, to_far, to_close = call(
@@ -678,12 +699,16 @@
         (shape((tiles, width, LANES), f32),) + (shape((tiles, REACH, LANES), f32),) * 2,
         [VMEM] * 3,
         (VMEM,) * 3,
-        conv_flops,
-        16 * field,
+        LAT_COVER * conv_flops,
+        LAT_COVER * 16 * field,
         scratch=(halos,),
         name="lat_smooth",
     )(far, close, own_part)
-    far, close, sent = exchange(to_far, to_close, "lon", True)
+    far, close, _ = exchange(to_far, to_close, "lon", True)
+    first, second, *_ = lax.optimization_barrier((first, second, to_far, to_close))
+    passed = jnp.where(odd_index("lat"), first, second)
+    near = [slabs, first, second, swapped(passed, 1 << one, 1 << two)]
+
     outer_slots = 3 * slot_count // 8
     late_slots = slot_count - outer_slots
     x_rows = slot_count * BLOCK_COLS
@@ -696,44 +721,16 @@
     padded = pltpu.VMEM((tiles, width + 2 * REACH, LANES), f32)
     flat = pltpu.VMEM((tiles * width, LANES), f32)
 
-    profile, *rest = call(
+    profile, *inner_states = call(
         functools.partial(inner_forward_kernel, per_tile, outer_slots),
-        (shape((tiles * width, LANES), f32),)
-        + state_shapes(late_rows)
-        + (
-            shape((LANES, hidden), bf16),
-            shape((hidden, hidden), bf16),
-            shape((hidden, channels), bf16),
-            shape((1, hidden), f32),
-            shape((1, hidden), f32),
-            shape((1, channels), f32),
-        ),
-        [ANY] + [VMEM] * 3 + [HBM] * 6,
-        (VMEM,) * 10,
-        late_rows * row_flops,
-        4 * 1024 * 1024,
-        scratch=(
-            plan_rows,
-            padded,
-            pltpu.VMEM((late_rows, LANES), f32),
-            pltpu.SemaphoreType.DMA((5 + per_tile + WEIGHT_PIECES,)),
-        ),
+        (shape((tiles * width, LANES), f32),) + state_shapes(late_rows),
+        [ANY] + [VMEM] * 9,
+        (VMEM,) * 4,
+        LON_COVER * late_rows * row_flops,
+        LON_COVER * 4 * 1024 * 1024,
+        scratch=(plan_rows, padded, pltpu.VMEM((late_rows, LANES), f32), pltpu.SemaphoreType.DMA),
         name="inner_forward",
-    )(
-        plan,
-        smoothed,
-        turned,
-        taps,
-        *pinned(
-            in_weight,
-            in_bias.reshape(1, hidden),
-            mid_weight,
-            mid_bias.reshape(1, hidden),
-            out_weight,
-            out_bias.reshape(1, channels),
-        ),
-    )
-    inner_states, weights = rest[:3], rest[3:]
+    )(plan, smoothed, turned, taps, *weights)
     *near, _ = lax.optimization_barrier((*near, profile))
     for bit in others:
         near = [jnp.concatenate(near, axis=0)]
@@ -812,7 +809,7 @@
         scratch=(pltpu.VMEM((tiles, width + 2 * REACH, LANES), f32),),
         name="lon_back",
     )(far, close, landing, taps)
-    back, _ = lax.optimization_barrier((back, to_far))
+    far, close, _ = exchange(to_far, to_close, "lat", False)
     own_part = call(
         own_back_kernel,
         shape((height, levels, width), f32),
@@ -822,9 +819,6 @@
         12 * field,
         name="lat_back_own",
     )(back, held)
-    to_close, _ = lax.optimization_barrier((to_close, own_part))
-    far, close, _ = exchange(to_far, to_close, "lat", False)
-
     return call(
         lat_back_kernel,
         shape((height, levels, width), f32),

time: 39.4 us -> 39.4 us (level)
    pallas_call x1, Pallas kernels: 0.9 us -> 1.98 us  [shards(): call(prepare_kernel, (shape((tiles, 24, LANES), f32), shape((tiles, width...]
    ppermute x4, waiting for transfers between devices: 3.63 us -> 2.77 us  [exchange(): lax.ppermute(to_far, axis, far)]
    pallas_call x1, Pallas kernels: 3.11 us -> 2.28 us  [shards(): call(functools.partial(inner_forward_kernel, per_tile, outer_slots), (sha...]
    ppermute x4, starting transfers between devices: 15.2 us -> 14.6 us  [exchange(): lax.ppermute(to_far, axis, far)]
    ppermute x5, starting transfers between devices: 4.41 us -> 4.99 us  [swapped(): return lax.ppermute(part, 'lat', pairs)]
    ppermute x5, waiting for transfers between devices: 0.01 us -> 0.57 us  [swapped(): return lax.ppermute(part, 'lat', pairs)]
  transfers between devices with their start and end apart: 13 -> 13, of which waited for: 1 -> 2; matrix products, arithmetic and copies ran while one was open for 0% -> 0% of each run, Pallas kernels for 25% -> 26%
where the time goes in v10:
time: 39.4 us; the launch traced here: 39.1 us
  starting transfers between devices  19.8 us (50%)
  Pallas kernels  15.5 us (39%)
  waiting for transfers between devices  3.35 us (9%)
    ppermute x4, starting transfers between devices, exchange(): lax.ppermute(to_far, axis, far)  14.6 us
    ppermute x5, starting transfers between devices, swapped(): return lax.ppermute(part, 'lat', pairs)  4.99 us
    pallas_call x1, Pallas kernels, shards(): call(functools.partial(inner_backward_kernel, per_tile, len(slabs), outer...  3.35 us
    ppermute x4, waiting for transfers between devices, exchange(): lax.ppermute(to_far, axis, far)  2.77 us
    pallas_call x1, Pallas kernels, shards(): call(functools.partial(outer_backward_kernel, per_tile, len(slabs), recv_...  2.43 us
    pallas_call x1, Pallas kernels, shards(): call(functools.partial(inner_forward_kernel, per_tile, outer_slots), (sha...  2.28 us
    pallas_call x1, Pallas kernels, shards(): call(prepare_kernel, (shape((tiles, 24, LANES), f32), shape((tiles, width...  1.98 us
    pallas_call x1, Pallas kernels, shards(): call(functools.partial(outer_forward_kernel, per_tile), state_shapes(oute...  1.72 us
  transfers between devices with their start and end apart: 13, of which 2 were waited for; matrix products, arithmetic and copies ran while one was open for 0% of the time, Pallas kernels for 26%

profile of v10, /device:TPU:1, one launch (start us, length us, event | category | flops | bytes accessed | tf_op | source)
XLA Modules:
  0.0 39.1 jit_solution(8766592764843711621)
XLA Ops:
  0.0 1.3 %slabs_halves.1 = (bf16[37,16,128]{2,1,0:T(8,128)(2,1)S(1)}, bf16[16,32,128]{2,1,0:T(8,128)(2,1)S(1)}, bf16[16,32,128]{2,1,0:T(8,128)(2,1)S(1)}, f32[16,32,128]{2,1,0:T(8,128)S(1)}, f32[16,32,128]{2,1,0:T(8,128)S(1)}) custom-call(bf16[36,16,128]{2,1,0:T(8,128)(2,1)} %bitcast.13, s32[1,64]{1,0:T(1,128)} %bitcast.16, s32[1,36]{1,0:T(1,128)} %bitcast.20, ...), custom_call_target="tpu_custom_call" | custom-call | bytes 1572864 | tf_op jit(solution)/shard_map/slabs_halves/pallas_call | solution.py:614
  1.3 4.5 %collective-permute-start.2 = (bf16[16,32,128]{2,1,0:T(8,128)(2,1)S(1)}, bf16[16,32,128]{2,1,0:T(8,128)(2,1)S(1)}, u32[]{:S(2)}, u32[]{:S(2)}) collective-permute-start(bf16[16,32,128]{2,1,0:T(8,128)(2,1)S(1)} %get-tuple-element.60), channel_id=1, source_target_pairs={{4,8},{8,4},{12,16},{16,12},{20,24},{24,20},{5,9},{9,5},{13,17},{1... | collective-permute-start | bytes 393224 | tf_op jit(solution)/shard_map/ppermute | solution.py:576
  5.8 0.1 collective-permute-start.3
  5.9 1.3 %collective-permute-start = (bf16[37,16,128]{2,1,0:T(8,128)(2,1)S(1)}, bf16[37,16,128]{2,1,0:T(8,128)(2,1)S(1)}, u32[]{:S(2)}, u32[]{:S(2)}) collective-permute-start(bf16[37,16,128]{2,1,0:T(8,128)(2,1)S(1)} %get-tuple-element.79), channel_id=1, source_target_pairs={{0,16},{4,20},{8,24},{12,28},{16,0},{20,4},{24,8},{28,12},{1,17},{... | collective-permute-start | bytes 454664 | tf_op jit(solution)/shard_map/ppermute | solution.py:691
  7.2 0.1 collective-permute-start.1
  7.2 2.0 %taps_background.1 = (f32[4,24,128]{2,1,0:T(8,128)S(1)}, f32[4,128,128]{2,1,0:T(8,128)S(1)}, s32[8,128]{1,0:T(8,128)S(1)}, f32[16,32,128]{2,1,0:T(8,128)S(1)}, b...) custom-call(s32[16]{0:T(128)} %lon_width.1, ...), custom_call_target="tpu_custom_call" | custom-call | flops 2162688 | bytes 786432 | tf_op jit(solution)/shard_map/taps_background/pallas_call | solution.py:647
  9.2 0.0 collective-permute-done.3.close
  9.3 0.4 %lat_smooth.1 = (f32[4,128,128]{2,1,0:T(8,128)S(1)}, f32[4,16,128]{2,1,0:T(8,128)S(1)}, f32[4,16,128]{2,1,0:T(8,128)S(1)}) custom-call(bf16[16,32,128]{2,1,0:T(8,128)(2,1)S(1)} %collective-permute-done.2.far, bf16[16,32,128]{2,1,0:T(8,128)(2,1)S(1)} %collective-permute-done.3.close, f32[16,32,128]{2,1,0:T(8,128)S(1)} %get-tuple-element.64.own_part), custom_call_target="tpu_custom_call" | custom-call | flops 276824064 | bytes 67108864 | tf_op jit(solution)/shard_map/lat_smooth/pallas_call | solution.py:697
  9.7 3.4 %collective-permute-start.7 = (f32[4,16,128]{2,1,0:T(8,128)S(1)}, f32[4,16,128]{2,1,0:T(8,128)S(1)}, u32[]{:S(2)}, u32[]{:S(2)}) collective-permute-start(f32[4,16,128]{2,1,0:T(8,128)S(1)} %get-tuple-element.65), channel_id=1, source_target_pairs={{1,2},{2,1},{3,0},{0,3},{5,6},{6,5},{7,4},{4,7},{9,10},{10,9},{11,... | collective-permute-start | bytes 98312 | tf_op jit(solution)/shard_map/ppermute | solution.py:576
  13.1 2.7 %collective-permute-start.4 = (bf16[37,16,128]{2,1,0:T(8,128)(2,1)S(1)}, bf16[37,16,128]{2,1,0:T(8,128)(2,1)S(1)}, u32[]{:S(2)}, u32[]{:S(2)}) collective-permute-start(bf16[37,16,128]{2,1,0:T(8,128)(2,1)S(1)} %broadcast_select_fusion), channel_id=1, source_target_pairs={{0,16},{4,12},{8,24},{12,4},{16,0},{20,28},{24,8},{28,20},{1,17},{... | collective-permute-start | bytes 454664 | tf_op jit(solution)/shard_map/ppermute | solution.py:691
  15.8 2.3 %inner_forward.1 = (f32[512,128]{1,0:T(8,128)S(1)}, bf16[320,1024]{1,0:T(8,128)(2,1)S(1)}, bf16[320,1024]{1,0:T(8,128)(2,1)S(1)}, f32[320,256]{1,0:T(8,128)S(1)}) custom-call(s32[8,128]{1,0:T(8,128)S(1)} %get-tuple-element.57.plan, f32[4,128,128]{2,1,0:T(8,128)S(1)} %get-tuple-element.69.own, f32[4,128,128]{2,1,0:T(8,128)S(1)} %get-tuple-element.70.turned, ...), custom_call_target="tpu_custom_call" | custom-call | flops 9227468800 | bytes 41943040 | tf_op jit(solution)/shard_map/inner_forward/pallas_call | solution.py:724
  18.1 0.6 %collective-permute-done.4.refs_1_ = bf16[37,16,128]{2,1,0:T(8,128)(2,1)S(1)} collective-permute-done((bf16[37,16,128]{2,1,0:T(8,128)(2,1)S(1)}, bf16[37,16,128]{2,1,0:T(8,128)(2,1)S(1)}, u32[]{:S(2)}, u32[]{:S(2)}) %collective-permute-start.4) | collective-permute-done | bytes 151584 | tf_op jit(solution)/shard_map/ppermute | solution.py:691
  18.7 0.9 %collective-permute-start.5 = (bf16[111,16,128]{2,1,0:T(8,128)(2,1)S(1)}, bf16[111,16,128]{2,1,0:T(8,128)(2,1)S(1)}, u32[]{:S(2)}, u32[]{:S(2)}) collective-permute-start(bf16[111,16,128]{2,1,0:T(8,128)(2,1)S(1)} %constant_dynamic-update-slice_fusion.refs_0_), channel_id=1, source_target_pairs={{0,4},{4,0},{8,12},{12,8},{16,20},{20,16},{24,28},{28,24},{1,5},{5... | collective-permute-start | bytes 1363976 | tf_op jit(solution)/shard_map/ppermute | solution.py:691
  19.6 0.1 collective-permute-start.6
  19.7 1.7 %outer_forward.1 = (bf16[192,1024]{1,0:T(8,128)(2,1)S(1)}, bf16[192,1024]{1,0:T(8,128)(2,1)S(1)}, f32[192,256]{1,0:T(8,128)S(1)}, bf16[320,1024]{1,0:T(8,128)(2,...) custom-call(s32[8,128]{1,0:T(8,128)S(1)} %get-tuple-element.57.plan, ...), custom_call_target="tpu_custom_call" | custom-call | flops 5536481280 | bytes 41943040 | tf_op jit(solution)/shard_map/outer_forward/pallas_call | solution.py:741
  21.4 2.4 %outer_backward.1 = (s32[8,128]{1,0:T(8,128)S(1)}, f32[512,128]{1,0:T(8,128)S(1)}, bf16[4,16,128]{2,1,0:T(8,128)(2,1)S(1)}, bf16[4,16,128]{2,1,0:T(8,128)(2,1)S(1)}) custom-call(s32[8,128]{1,0:T(8,128)S(1)} %get-tuple-element.57.plan, bf16[111,16,128]{2,1,0:T(8,128)(2,1)S(1)} %constant_dynamic-update-slice_fusion.refs_0_, ...), custom_call_target="tpu_custom_call" | custom-call | flops 553648128 | bytes 4194304 | tf_op jit(solution)/shard_map/outer_backward/pallas_call | solution.py:760
  23.9 3.0 %collective-permute-start.9 = (bf16[4,16,128]{2,1,0:T(8,128)(2,1)S(1)}, bf16[4,16,128]{2,1,0:T(8,128)(2,1)S(1)}, u32[]{:S(2)}, u32[]{:S(2)}) collective-permute-start(bf16[4,16,128]{2,1,0:T(8,128)(2,1)S(1)} %get-tuple-element.91), channel_id=1, source_target_pairs={{1,2},{2,1},{3,0},{0,3},{5,6},{6,5},{7,4},{4,7},{9,10},{10,9},{11,... | collective-permute-start | bytes 49160 | tf_op jit(solution)/shard_map/ppermute | solution.py:576
  26.9 3.3 %inner_backward.1.own = f32[4,128,128]{2,1,0:T(8,128)S(1)} custom-call(s32[8,128]{1,0:T(8,128)S(1)} %get-tuple-element.57.plan, s32[8,128]{1,0:T(8,128)S(1)} %get-tuple-element.95.table_rows, f32[512,128]{1,0:T(8,128)S(1)} %get-tuple-element.96.sens, bf16[111,16,128]{2,1,0:T(8,128)(2,1)S(1)} %constant_dynamic-update-slice_fusion.refs_0_, ...), custom_call_target="tpu_custom_call" | custom-call | flops 922746880 | bytes 4194304 | tf_op jit(solution)/shard_map/inner_backward/pallas_call | solution.py:784
  30.2 0.7 %lon_back.1 = (f32[16,32,128]{2,1,0:T(8,128)S(1)}, bf16[16,32,128]{2,1,0:T(8,128)(2,1)S(1)}, bf16[16,32,128]{2,1,0:T(8,128)(2,1)S(1)}) custom-call(bf16[4,16,128]{2,1,0:T(8,128)(2,1)S(1)} %collective-permute-done.9.far, bf16[4,16,128]{2,1,0:T(8,128)(2,1)S(1)} %collective-permute-done.10.close, f32[4,128,128]{2,1,0:T(8,128)S(1)} %inner_backward.1.own, ...), custom_call_target="tpu_custom_call" | custom-call | flops 4325376 | bytes 524288 | tf_op jit(solution)/shard_map/lon_back/pallas_call | solution.py:802
  31.0 3.7 %collective-permute-start.11 = (bf16[16,32,128]{2,1,0:T(8,128)(2,1)S(1)}, bf16[16,32,128]{2,1,0:T(8,128)(2,1)S(1)}, u32[]{:S(2)}, u32[]{:S(2)}) collective-permute-start(bf16[16,32,128]{2,1,0:T(8,128)(2,1)S(1)} %get-tuple-element.100), channel_id=1, source_target_pairs={{4,8},{8,4},{12,16},{16,12},{20,24},{24,20},{5,9},{9,5},{13,17},{1... | collective-permute-start | bytes 393224 | tf_op jit(solution)/shard_map/ppermute | solution.py:576
  34.7 0.1 collective-permute-start.12
  34.8 0.3 lat_back_own.1.own_part
  35.1 2.8 %collective-permute-done.11.far = bf16[16,32,128]{2,1,0:T(8,128)(2,1)S(1)} collective-permute-done((bf16[16,32,128]{2,1,0:T(8,128)(2,1)S(1)}, bf16[16,32,128]{2,1,0:T(8,128)(2,1)S(1)}, u32[]{:S(2)}, u32[]{:S(2)}) %collective-permute-start.11) | collective-permute-done | bytes 131104 | tf_op jit(solution)/shard_map/ppermute | solution.py:576
  37.9 1.0 %lat_back.1 = f32[16,32,128]{2,1,0:T(8,128)} custom-call(bf16[16,32,128]{2,1,0:T(8,128)(2,1)S(1)} %collective-permute-done.11.far, bf16[16,32,128]{2,1,0:T(8,128)(2,1)S(1)} %collective-permute-done.12.close, f32[16,32,128]{2,1,0:T(8,128)S(1)} %lat_back_own.1.own_part), custom_call_target="tpu_custom_call" | custom-call | flops 2162688 | bytes 1048576 | tf_op jit(solution)/shard_map/lat_back/pallas_call | solution.py:822
  (16 shorter events, 0.1 us)
Async XLA Ops:
  1.3 8.0 %collective-permute-start.2 = (bf16[16,32,128]{2,1,0:T(8,128)(2,1)S(1)}, bf16[16,32,128]{2,1,0:T(8,128)(2,1)S(1)}, u32[]{:S(2)}, u32[]{:S(2)}) collective-permute-start(bf16[16,32,128]{2,1,0:T(8,128)(2,1)S(1)} %get-tuple-element.60), channel_id=1, source_target_pairs={{4,8},{8,4},{12,16},{16,12},{20,24},{24,20},{5,9},{9,5},{13,17},{1... | collective-permute-start | bytes 393224 | tf_op jit(solution)/shard_map/ppermute | solution.py:576
  5.8 3.5 %collective-permute-start.3 = (bf16[16,32,128]{2,1,0:T(8,128)(2,1)S(1)}, bf16[16,32,128]{2,1,0:T(8,128)(2,1)S(1)}, u32[]{:S(2)}, u32[]{:S(2)}) collective-permute-start(bf16[16,32,128]{2,1,0:T(8,128)(2,1)S(1)} %get-tuple-element.61), channel_id=1, source_target_pairs={{0,4},{4,0},{8,12},{12,8},{16,20},{20,16},{24,28},{28,24},{1,5},{5... | collective-permute-start | bytes 393224 | tf_op jit(solution)/shard_map/ppermute | solution.py:576
  5.9 7.2 %collective-permute-start = (bf16[37,16,128]{2,1,0:T(8,128)(2,1)S(1)}, bf16[37,16,128]{2,1,0:T(8,128)(2,1)S(1)}, u32[]{:S(2)}, u32[]{:S(2)}) collective-permute-start(bf16[37,16,128]{2,1,0:T(8,128)(2,1)S(1)} %get-tuple-element.79), channel_id=1, source_target_pairs={{0,16},{4,20},{8,24},{12,28},{16,0},{20,4},{24,8},{28,12},{1,17},{... | collective-permute-start | bytes 454664 | tf_op jit(solution)/shard_map/ppermute | solution.py:691
  7.2 5.9 %collective-permute-start.1 = (bf16[37,16,128]{2,1,0:T(8,128)(2,1)S(1)}, bf16[37,16,128]{2,1,0:T(8,128)(2,1)S(1)}, u32[]{:S(2)}, u32[]{:S(2)}) collective-permute-start(bf16[37,16,128]{2,1,0:T(8,128)(2,1)S(1)} %get-tuple-element.79), channel_id=1, source_target_pairs={{0,8},{4,12},{8,0},{12,4},{16,24},{20,28},{24,16},{28,20},{1,9},{5... | collective-permute-start | bytes 454664 | tf_op jit(solution)/shard_map/ppermute | solution.py:691
  9.7 8.4 %collective-permute-start.7 = (f32[4,16,128]{2,1,0:T(8,128)S(1)}, f32[4,16,128]{2,1,0:T(8,128)S(1)}, u32[]{:S(2)}, u32[]{:S(2)}) collective-permute-start(f32[4,16,128]{2,1,0:T(8,128)S(1)} %get-tuple-element.65), channel_id=1, source_target_pairs={{1,2},{2,1},{3,0},{0,3},{5,6},{6,5},{7,4},{4,7},{9,10},{10,9},{11,... | collective-permute-start | bytes 98312 | tf_op jit(solution)/shard_map/ppermute | solution.py:576
  13.1 5.0 %collective-permute-start.8 = (f32[4,16,128]{2,1,0:T(8,128)S(1)}, f32[4,16,128]{2,1,0:T(8,128)S(1)}, u32[]{:S(2)}, u32[]{:S(2)}) collective-permute-start(f32[4,16,128]{2,1,0:T(8,128)S(1)} %get-tuple-element.83), channel_id=1, source_target_pairs={{0,1},{1,0},{2,3},{3,2},{4,5},{5,4},{6,7},{7,6},{8,9},{9,8},{10,11... | collective-permute-start | bytes 98312 | tf_op jit(solution)/shard_map/ppermute | solution.py:576
  13.1 5.6 %collective-permute-start.4 = (bf16[37,16,128]{2,1,0:T(8,128)(2,1)S(1)}, bf16[37,16,128]{2,1,0:T(8,128)(2,1)S(1)}, u32[]{:S(2)}, u32[]{:S(2)}) collective-permute-start(bf16[37,16,128]{2,1,0:T(8,128)(2,1)S(1)} %broadcast_select_fusion), channel_id=1, source_target_pairs={{0,16},{4,12},{8,24},{12,4},{16,0},{20,28},{24,8},{28,20},{1,17},{... | collective-permute-start | bytes 454664 | tf_op jit(solution)/shard_map/ppermute | solution.py:691
  18.7 2.7 %collective-permute-start.5 = (bf16[111,16,128]{2,1,0:T(8,128)(2,1)S(1)}, bf16[111,16,128]{2,1,0:T(8,128)(2,1)S(1)}, u32[]{:S(2)}, u32[]{:S(2)}) collective-permute-start(bf16[111,16,128]{2,1,0:T(8,128)(2,1)S(1)} %constant_dynamic-update-slice_fusion.refs_0_), channel_id=1, source_target_pairs={{0,4},{4,0},{8,12},{12,8},{16,20},{20,16},{24,28},{28,24},{1,5},{5... | collective-permute-start | bytes 1363976 | tf_op jit(solution)/shard_map/ppermute | solution.py:691
  19.6 1.8 %collective-permute-start.6 = (bf16[37,16,128]{2,1,0:T(8,128)(2,1)S(1)}, bf16[37,16,128]{2,1,0:T(8,128)(2,1)S(1)}, u32[]{:S(2)}, u32[]{:S(2)}) collective-permute-start(bf16[37,16,128]{2,1,0:T(8,128)(2,1)S(1)} %collective-permute-done.4.refs_1_), channel_id=1, source_target_pairs={{0,4},{4,0},{8,12},{12,8},{16,20},{20,16},{24,28},{28,24},{1,5},{5... | collective-permute-start | bytes 454664 | tf_op jit(solution)/shard_map/ppermute | solution.py:691
  23.9 6.3 %collective-permute-start.9 = (bf16[4,16,128]{2,1,0:T(8,128)(2,1)S(1)}, bf16[4,16,128]{2,1,0:T(8,128)(2,1)S(1)}, u32[]{:S(2)}, u32[]{:S(2)}) collective-permute-start(bf16[4,16,128]{2,1,0:T(8,128)(2,1)S(1)} %get-tuple-element.91), channel_id=1, source_target_pairs={{1,2},{2,1},{3,0},{0,3},{5,6},{6,5},{7,4},{4,7},{9,10},{10,9},{11,... | collective-permute-start | bytes 49160 | tf_op jit(solution)/shard_map/ppermute | solution.py:576
  26.8 3.4 %collective-permute-start.10 = (bf16[4,16,128]{2,1,0:T(8,128)(2,1)S(1)}, bf16[4,16,128]{2,1,0:T(8,128)(2,1)S(1)}, u32[]{:S(2)}, u32[]{:S(2)}) collective-permute-start(bf16[4,16,128]{2,1,0:T(8,128)(2,1)S(1)} %get-tuple-element.93), channel_id=1, source_target_pairs={{0,1},{1,0},{2,3},{3,2},{4,5},{5,4},{6,7},{7,6},{8,9},{9,8},{10,11... | collective-permute-start | bytes 49160 | tf_op jit(solution)/shard_map/ppermute | solution.py:576
  31.0 6.9 %collective-permute-start.11 = (bf16[16,32,128]{2,1,0:T(8,128)(2,1)S(1)}, bf16[16,32,128]{2,1,0:T(8,128)(2,1)S(1)}, u32[]{:S(2)}, u32[]{:S(2)}) collective-permute-start(bf16[16,32,128]{2,1,0:T(8,128)(2,1)S(1)} %get-tuple-element.100), channel_id=1, source_target_pairs={{4,8},{8,4},{12,16},{16,12},{20,24},{24,20},{5,9},{9,5},{13,17},{1... | collective-permute-start | bytes 393224 | tf_op jit(solution)/shard_map/ppermute | solution.py:576
  34.7 3.1 %collective-permute-start.12 = (bf16[16,32,128]{2,1,0:T(8,128)(2,1)S(1)}, bf16[16,32,128]{2,1,0:T(8,128)(2,1)S(1)}, u32[]{:S(2)}, u32[]{:S(2)}) collective-permute-start(bf16[16,32,128]{2,1,0:T(8,128)(2,1)S(1)} %get-tuple-element.102), channel_id=1, source_target_pairs={{0,4},{4,0},{8,12},{12,8},{16,20},{20,16},{24,28},{28,24},{1,5},{5... | collective-permute-start | bytes 393224 | tf_op jit(solution)/shard_map/ppermute | solution.py:576

commit v11 on v10

--- a/solution.py
+++ b/solution.py
@@ -14,6 +14,7 @@
 LAT_SIGMA = 8.0
 WEIGHT_PIECES = 8
 BAND_PIECES = 4
+FEW_SLOTS = 8
 LAT_COVER = 64
 LON_COVER = 10
 SWAP_COVER = 10
@@ -237,6 +238,8 @@
     plan[0:1, :] = jnp.sum(jnp.where(hit, cell, 0), axis=0, keepdims=True)
     plan[1:2, :] = jnp.sum(jnp.where(hit, slot, 0), axis=0, keepdims=True)
     plan[2:3, :] = jnp.broadcast_to(outer_count, (1, LANES))
+    live_count = jnp.sum(jnp.where(owners[...] >= 0, 1, 0), axis=1, keepdims=True)
+    plan[3:4, :] = jnp.broadcast_to(live_count, (1, LANES))
     for move in loads:
         move.wait()
 
@@ -409,6 +412,10 @@
     return rounded(dot_t(grad_one, wide_in[...]))
 
 
+def few_of(ref):
+    return ref.at[pl.ds(0, FEW_SLOTS * BLOCK_COLS)]
+
+
 def inner_forward_kernel(per_tile, outer_slots, plan, own, turned, taps, *refs):
     weights, profile, states, (rows, padded, picked, sem) = refs[:6], refs[6], refs[7:10], refs[10:]
     tiles, width, _ = own.shape
@@ -424,10 +431,17 @@
         profile[tile * width : (tile + 1) * width, :] = rounded(total)
     plan_in.wait()
 
-    @pl.when(rows[2, 0] <= outer_slots)
+    in_time, many = rows[2, 0] <= outer_slots, rows[3, 0] > outer_slots + FEW_SLOTS
+
+    @pl.when(in_time & many)
     def _():
         take_blocks(rows, profile, picked, outer_slots, count, per_tile, width)
         net_forward(picked, weights, states)
+
+    @pl.when(in_time & ~many)
+    def _():
+        take_blocks(rows, profile, picked, outer_slots, FEW_SLOTS, per_tile, width)
+        net_forward(few_of(picked), weights, [few_of(state) for state in states])
 
 
 def outer_forward_kernel(
@@ -522,12 +536,27 @@
     for move in moves:
         move.wait()
 
-    @pl.when(rows[2, 0] <= outer_slots)
+    in_time, many = rows[2, 0] <= outer_slots, rows[3, 0] > outer_slots + FEW_SLOTS
+    first = outer_slots + FEW_SLOTS
+
+    @pl.when(in_time & many)
     def _():
         take_observed(rows, table, slabs, observed, outer_slots, late_slots)
         inner[split:, :] = net_backward(observed, states, weights)
 
-    land_blocks(rows, field, inner, 0, outer_slots + late_slots, per_tile, width)
+    @pl.when(in_time & ~many)
+    def _():
+        take_observed(rows, table, slabs, observed, outer_slots, FEW_SLOTS)
+        inner[split : split + FEW_SLOTS * BLOCK_COLS, :] = net_backward(
+            few_of(observed), [few_of(state) for state in states], weights
+        )
+
+    land_blocks(rows, field, inner, 0, first, per_tile, width)
+
+    @pl.when(many)
+    def _():
+        land_blocks(rows, field, inner, first, outer_slots + late_slots - first, per_tile, width)
+
     for tile in range(tiles):
         landing[tile] = field[tile * width : (tile + 1) * width, :]
 
@@ -686,12 +715,11 @@
     lat_count = lax.axis_size("lat")
     one, two, *others = swap_bits(lat_count)
 
-    def swapped(part, apart, odd_apart=None):
-        pairs = [(i, i ^ (odd_apart if odd_apart and i % 2 else apart)) for i in range(lat_count)]
-        return lax.ppermute(part, "lat", pairs)
-
-    slabs, _ = lax.optimization_barrier((slabs, sent))
-    first, second = swapped(slabs, 1 << one), swapped(slabs, 1 << two)
+    def swapped(part, apart):
+        return lax.ppermute(part, "lat", [(i, i ^ apart) for i in range(lat_count)])
+
+    later, _ = lax.optimization_barrier((slabs, sent))
+    near = [slabs, swapped(later, 1 << one), swapped(later, 1 << two), swapped(slabs, (1 << one) + (1 << two))]
 
     halos = pltpu.VMEM((2, REACH, levels, width), f32)
     smoothed, to_far, to_close = call(
@@ -705,9 +733,6 @@
         name="lat_smooth",
     )(far, close, own_part)
     far, close, _ = exchange(to_far, to_close, "lon", True)
-    first, second, *_ = lax.optimization_barrier((first, second, to_far, to_close))
-    passed = jnp.where(odd_index("lat"), first, second)
-    near = [slabs, first, second, swapped(passed, 1 << one, 1 << two)]
 
     outer_slots = 3 * slot_count // 8
     late_slots = slot_count - outer_slots

time: 39.4 us -> 38.7 us (0.982)
  Pallas kernels: 15.5 us -> 13.6 us
  starting transfers between devices: 19.8 us -> 20.9 us
    pallas_call x1, Pallas kernels: 3.35 us -> 2.28 us  [shards(): call(functools.partial(inner_backward_kernel, per_tile, len(slabs), outer...]
    ppermute x4, starting transfers between devices: 14.6 us -> 15.5 us  [exchange(): lax.ppermute(to_far, axis, far)]
    pallas_call x1, Pallas kernels: 2.28 us -> 1.46 us  [shards(): call(functools.partial(inner_forward_kernel, per_tile, outer_slots), (sha...]
    ppermute x4, waiting for transfers between devices: 2.77 us -> 3.57 us  [exchange(): lax.ppermute(to_far, axis, far)]
    ppermute x5, waiting for transfers between devices: 0.57 us -> 0.01 us  [swapped(): return lax.ppermute(part, 'lat', [(i, i ^ apart) for i in range(lat_count)])]
  transfers between devices with their start and end apart: 13 -> 13, of which waited for: 2 -> 2; matrix products, arithmetic and copies ran while one was open for 0% -> 0% of each run, Pallas kernels for 26% -> 21%
where the time goes in v11:
time: 38.7 us; the launch traced here: 38.5 us
  starting transfers between devices  20.9 us (54%)
  Pallas kernels  13.6 us (35%)
  waiting for transfers between devices  3.59 us (9%)
    ppermute x4, starting transfers between devices, exchange(): lax.ppermute(to_far, axis, far)  15.5 us
    ppermute x5, starting transfers between devices, swapped(): return lax.ppermute(part, 'lat', [(i, i ^ apart) for i in range(lat_count)])  5.25 us
    ppermute x4, waiting for transfers between devices, exchange(): lax.ppermute(to_far, axis, far)  3.57 us
    pallas_call x1, Pallas kernels, shards(): call(functools.partial(outer_backward_kernel, per_tile, len(slabs), recv_...  2.43 us
    pallas_call x1, Pallas kernels, shards(): call(functools.partial(inner_backward_kernel, per_tile, len(slabs), outer...  2.28 us
    pallas_call x1, Pallas kernels, shards(): call(prepare_kernel, (shape((tiles, 24, LANES), f32), shape((tiles, width...  1.98 us
    pallas_call x1, Pallas kernels, shards(): call(functools.partial(outer_forward_kernel, per_tile), state_shapes(oute...  1.72 us
    pallas_call x1, Pallas kernels, shards(): call(functools.partial(inner_forward_kernel, per_tile, outer_slots), (sha...  1.46 us
  transfers between devices with their start and end apart: 13, of which 2 were waited for; matrix products, arithmetic and copies ran while one was open for 0% of the time, Pallas kernels for 21%

profile of v11, /device:TPU:1, one launch (start us, length us, event | category | flops | bytes accessed | tf_op | source)
XLA Modules:
  0.0 38.5 jit_solution(5658238701170950768)
XLA Ops:
  0.0 1.3 %slabs_halves.1 = (bf16[37,16,128]{2,1,0:T(8,128)(2,1)S(1)}, bf16[16,32,128]{2,1,0:T(8,128)(2,1)S(1)}, bf16[16,32,128]{2,1,0:T(8,128)(2,1)S(1)}, f32[16,32,128]{2,1,0:T(8,128)S(1)}, f32[16,32,128]{2,1,0:T(8,128)S(1)}) custom-call(bf16[36,16,128]{2,1,0:T(8,128)(2,1)} %bitcast.13, s32[1,64]{1,0:T(1,128)} %bitcast.16, s32[1,36]{1,0:T(1,128)} %bitcast.20, ...), custom_call_target="tpu_custom_call" | custom-call | bytes 1572864 | tf_op jit(solution)/shard_map/slabs_halves/pallas_call | solution.py:643
  1.3 4.5 %collective-permute-start.3 = (bf16[16,32,128]{2,1,0:T(8,128)(2,1)S(1)}, bf16[16,32,128]{2,1,0:T(8,128)(2,1)S(1)}, u32[]{:S(2)}, u32[]{:S(2)}) collective-permute-start(bf16[16,32,128]{2,1,0:T(8,128)(2,1)S(1)} %get-tuple-element.58), channel_id=1, source_target_pairs={{4,8},{8,4},{12,16},{16,12},{20,24},{24,20},{5,9},{9,5},{13,17},{1... | collective-permute-start | bytes 393224 | tf_op jit(solution)/shard_map/ppermute | solution.py:605
  5.8 0.1 collective-permute-start.4
  5.9 1.3 %collective-permute-start = (bf16[37,16,128]{2,1,0:T(8,128)(2,1)S(1)}, bf16[37,16,128]{2,1,0:T(8,128)(2,1)S(1)}, u32[]{:S(2)}, u32[]{:S(2)}) collective-permute-start(bf16[37,16,128]{2,1,0:T(8,128)(2,1)S(1)} %get-tuple-element.73), channel_id=1, source_target_pairs={{0,16},{4,20},{8,24},{12,28},{16,0},{20,4},{24,8},{28,12},{1,17},{... | collective-permute-start | bytes 454664 | tf_op jit(solution)/shard_map/ppermute | solution.py:719
  7.2 0.1 collective-permute-start.1
  7.2 1.3 %collective-permute-start.2 = (bf16[37,16,128]{2,1,0:T(8,128)(2,1)S(1)}, bf16[37,16,128]{2,1,0:T(8,128)(2,1)S(1)}, u32[]{:S(2)}, u32[]{:S(2)}) collective-permute-start(bf16[37,16,128]{2,1,0:T(8,128)(2,1)S(1)} %get-tuple-element.73), channel_id=1, source_target_pairs={{0,24},{4,28},{8,16},{12,20},{16,8},{20,12},{24,0},{28,4},{1,25},{... | collective-permute-start | bytes 454664 | tf_op jit(solution)/shard_map/ppermute | solution.py:719
  8.6 2.0 %taps_background.1 = (f32[4,24,128]{2,1,0:T(8,128)S(1)}, f32[4,128,128]{2,1,0:T(8,128)S(1)}, s32[8,128]{1,0:T(8,128)S(1)}, f32[16,32,128]{2,1,0:T(8,128)S(1)}, b...) custom-call(s32[16]{0:T(128)} %lon_width.1, ...), custom_call_target="tpu_custom_call" | custom-call | flops 2162688 | bytes 786432 | tf_op jit(solution)/shard_map/taps_background/pallas_call | solution.py:676
  10.6 0.0 collective-permute-done.3.far
  10.6 0.4 %lat_smooth.1 = (f32[4,128,128]{2,1,0:T(8,128)S(1)}, f32[4,16,128]{2,1,0:T(8,128)S(1)}, f32[4,16,128]{2,1,0:T(8,128)S(1)}) custom-call(bf16[16,32,128]{2,1,0:T(8,128)(2,1)S(1)} %collective-permute-done.3.far, bf16[16,32,128]{2,1,0:T(8,128)(2,1)S(1)} %collective-permute-done.4.close, f32[16,32,128]{2,1,0:T(8,128)S(1)} %get-tuple-element.62.own_part), custom_call_target="tpu_custom_call" | custom-call | flops 276824064 | bytes 67108864 | tf_op jit(solution)/shard_map/lat_smooth/pallas_call | solution.py:725
  11.0 3.4 %collective-permute-start.7 = (f32[4,16,128]{2,1,0:T(8,128)S(1)}, f32[4,16,128]{2,1,0:T(8,128)S(1)}, u32[]{:S(2)}, u32[]{:S(2)}) collective-permute-start(f32[4,16,128]{2,1,0:T(8,128)S(1)} %get-tuple-element.77), channel_id=1, source_target_pairs={{1,2},{2,1},{3,0},{0,3},{5,6},{6,5},{7,4},{4,7},{9,10},{10,9},{11,... | collective-permute-start | bytes 98312 | tf_op jit(solution)/shard_map/ppermute | solution.py:605
  14.4 1.5 %inner_forward.1 = (f32[512,128]{1,0:T(8,128)S(1)}, bf16[320,1024]{1,0:T(8,128)(2,1)S(1)}, bf16[320,1024]{1,0:T(8,128)(2,1)S(1)}, f32[320,256]{1,0:T(8,128)S(1)}) custom-call(s32[8,128]{1,0:T(8,128)S(1)} %get-tuple-element.55.plan, f32[4,128,128]{2,1,0:T(8,128)S(1)} %get-tuple-element.63.own, f32[4,128,128]{2,1,0:T(8,128)S(1)} %get-tuple-element.64.turned, ...), custom_call_target="tpu_custom_call" | custom-call | flops 9227468800 | bytes 41943040 | tf_op jit(solution)/shard_map/inner_forward/pallas_call | solution.py:749
  16.0 2.5 %collective-permute-start.5 = (bf16[111,16,128]{2,1,0:T(8,128)(2,1)S(1)}, bf16[111,16,128]{2,1,0:T(8,128)(2,1)S(1)}, u32[]{:S(2)}, u32[]{:S(2)}) collective-permute-start(bf16[111,16,128]{2,1,0:T(8,128)(2,1)S(1)} %constant_dynamic-update-slice_fusion.refs_0_), channel_id=1, source_target_pairs={{0,4},{4,0},{8,12},{12,8},{16,20},{20,16},{24,28},{28,24},{1,5},{5... | collective-permute-start | bytes 1363976 | tf_op jit(solution)/shard_map/ppermute | solution.py:719
  18.5 0.1 collective-permute-start.6
  18.5 1.7 %outer_forward.1 = (bf16[192,1024]{1,0:T(8,128)(2,1)S(1)}, bf16[192,1024]{1,0:T(8,128)(2,1)S(1)}, f32[192,256]{1,0:T(8,128)S(1)}, bf16[320,1024]{1,0:T(8,128)(2,...) custom-call(s32[8,128]{1,0:T(8,128)S(1)} %get-tuple-element.55.plan, ...), custom_call_target="tpu_custom_call" | custom-call | flops 5536481280 | bytes 41943040 | tf_op jit(solution)/shard_map/outer_forward/pallas_call | solution.py:766
  20.3 2.4 %outer_backward.1 = (s32[8,128]{1,0:T(8,128)S(1)}, f32[512,128]{1,0:T(8,128)S(1)}, bf16[4,16,128]{2,1,0:T(8,128)(2,1)S(1)}, bf16[4,16,128]{2,1,0:T(8,128)(2,1)S(1)}) custom-call(s32[8,128]{1,0:T(8,128)S(1)} %get-tuple-element.55.plan, bf16[111,16,128]{2,1,0:T(8,128)(2,1)S(1)} %constant_dynamic-update-slice_fusion.refs_0_, ...), custom_call_target="tpu_custom_call" | custom-call | flops 553648128 | bytes 4194304 | tf_op jit(solution)/shard_map/outer_backward/pallas_call | solution.py:785
  22.7 1.8 %collective-permute-start.9 = (bf16[4,16,128]{2,1,0:T(8,128)(2,1)S(1)}, bf16[4,16,128]{2,1,0:T(8,128)(2,1)S(1)}, u32[]{:S(2)}, u32[]{:S(2)}) collective-permute-start(bf16[4,16,128]{2,1,0:T(8,128)(2,1)S(1)} %get-tuple-element.87), channel_id=1, source_target_pairs={{1,2},{2,1},{3,0},{0,3},{5,6},{6,5},{7,4},{4,7},{9,10},{10,9},{11,... | collective-permute-start | bytes 49160 | tf_op jit(solution)/shard_map/ppermute | solution.py:605
  24.5 2.3 %inner_backward.1.own = f32[4,128,128]{2,1,0:T(8,128)S(1)} custom-call(s32[8,128]{1,0:T(8,128)S(1)} %get-tuple-element.55.plan, s32[8,128]{1,0:T(8,128)S(1)} %get-tuple-element.91.table_rows, f32[512,128]{1,0:T(8,128)S(1)} %get-tuple-element.92.sens, bf16[111,16,128]{2,1,0:T(8,128)(2,1)S(1)} %constant_dynamic-update-slice_fusion.refs_0_, ...), custom_call_target="tpu_custom_call" | custom-call | flops 922746880 | bytes 4194304 | tf_op jit(solution)/shard_map/inner_backward/pallas_call | solution.py:809
  26.8 0.5 %collective-permute-done.9.far = bf16[4,16,128]{2,1,0:T(8,128)(2,1)S(1)} collective-permute-done((bf16[4,16,128]{2,1,0:T(8,128)(2,1)S(1)}, bf16[4,16,128]{2,1,0:T(8,128)(2,1)S(1)}, u32[]{:S(2)}, u32[]{:S(2)}) %collective-permute-start.9) | collective-permute-done | bytes 16416 | tf_op jit(solution)/shard_map/ppermute | solution.py:605
  27.3 0.7 %lon_back.1 = (f32[16,32,128]{2,1,0:T(8,128)S(1)}, bf16[16,32,128]{2,1,0:T(8,128)(2,1)S(1)}, bf16[16,32,128]{2,1,0:T(8,128)(2,1)S(1)}) custom-call(bf16[4,16,128]{2,1,0:T(8,128)(2,1)S(1)} %collective-permute-done.9.far, bf16[4,16,128]{2,1,0:T(8,128)(2,1)S(1)} %collective-permute-done.10.close, f32[4,128,128]{2,1,0:T(8,128)S(1)} %inner_backward.1.own, ...), custom_call_target="tpu_custom_call" | custom-call | flops 4325376 | bytes 524288 | tf_op jit(solution)/shard_map/lon_back/pallas_call | solution.py:827
  28.0 5.8 %collective-permute-start.11 = (bf16[16,32,128]{2,1,0:T(8,128)(2,1)S(1)}, bf16[16,32,128]{2,1,0:T(8,128)(2,1)S(1)}, u32[]{:S(2)}, u32[]{:S(2)}) collective-permute-start(bf16[16,32,128]{2,1,0:T(8,128)(2,1)S(1)} %get-tuple-element.96), channel_id=1, source_target_pairs={{4,8},{8,4},{12,16},{16,12},{20,24},{24,20},{5,9},{9,5},{13,17},{1... | collective-permute-start | bytes 393224 | tf_op jit(solution)/shard_map/ppermute | solution.py:605
  33.9 0.1 collective-permute-start.12
  34.0 0.3 lat_back_own.1.own_part
  34.3 3.1 %collective-permute-done.11.far = bf16[16,32,128]{2,1,0:T(8,128)(2,1)S(1)} collective-permute-done((bf16[16,32,128]{2,1,0:T(8,128)(2,1)S(1)}, bf16[16,32,128]{2,1,0:T(8,128)(2,1)S(1)}, u32[]{:S(2)}, u32[]{:S(2)}) %collective-permute-start.11) | collective-permute-done | bytes 131104 | tf_op jit(solution)/shard_map/ppermute | solution.py:605
  37.4 1.0 %lat_back.1 = f32[16,32,128]{2,1,0:T(8,128)} custom-call(bf16[16,32,128]{2,1,0:T(8,128)(2,1)S(1)} %collective-permute-done.11.far, bf16[16,32,128]{2,1,0:T(8,128)(2,1)S(1)} %collective-permute-done.12.close, f32[16,32,128]{2,1,0:T(8,128)S(1)} %lat_back_own.1.own_part), custom_call_target="tpu_custom_call" | custom-call | flops 2162688 | bytes 1048576 | tf_op jit(solution)/shard_map/lat_back/pallas_call | solution.py:847
  (15 shorter events, 0.1 us)
Async XLA Ops:
  1.3 9.3 %collective-permute-start.3 = (bf16[16,32,128]{2,1,0:T(8,128)(2,1)S(1)}, bf16[16,32,128]{2,1,0:T(8,128)(2,1)S(1)}, u32[]{:S(2)}, u32[]{:S(2)}) collective-permute-start(bf16[16,32,128]{2,1,0:T(8,128)(2,1)S(1)} %get-tuple-element.58), channel_id=1, source_target_pairs={{4,8},{8,4},{12,16},{16,12},{20,24},{24,20},{5,9},{9,5},{13,17},{1... | collective-permute-start | bytes 393224 | tf_op jit(solution)/shard_map/ppermute | solution.py:605
  5.8 4.8 %collective-permute-start.4 = (bf16[16,32,128]{2,1,0:T(8,128)(2,1)S(1)}, bf16[16,32,128]{2,1,0:T(8,128)(2,1)S(1)}, u32[]{:S(2)}, u32[]{:S(2)}) collective-permute-start(bf16[16,32,128]{2,1,0:T(8,128)(2,1)S(1)} %get-tuple-element.59), channel_id=1, source_target_pairs={{0,4},{4,0},{8,12},{12,8},{16,20},{20,16},{24,28},{28,24},{1,5},{5... | collective-permute-start | bytes 393224 | tf_op jit(solution)/shard_map/ppermute | solution.py:605
  5.9 10.0 %collective-permute-start = (bf16[37,16,128]{2,1,0:T(8,128)(2,1)S(1)}, bf16[37,16,128]{2,1,0:T(8,128)(2,1)S(1)}, u32[]{:S(2)}, u32[]{:S(2)}) collective-permute-start(bf16[37,16,128]{2,1,0:T(8,128)(2,1)S(1)} %get-tuple-element.73), channel_id=1, source_target_pairs={{0,16},{4,20},{8,24},{12,28},{16,0},{20,4},{24,8},{28,12},{1,17},{... | collective-permute-start | bytes 454664 | tf_op jit(solution)/shard_map/ppermute | solution.py:719
  7.2 8.7 %collective-permute-start.1 = (bf16[37,16,128]{2,1,0:T(8,128)(2,1)S(1)}, bf16[37,16,128]{2,1,0:T(8,128)(2,1)S(1)}, u32[]{:S(2)}, u32[]{:S(2)}) collective-permute-start(bf16[37,16,128]{2,1,0:T(8,128)(2,1)S(1)} %get-tuple-element.73), channel_id=1, source_target_pairs={{0,8},{4,12},{8,0},{12,4},{16,24},{20,28},{24,16},{28,20},{1,9},{5... | collective-permute-start | bytes 454664 | tf_op jit(solution)/shard_map/ppermute | solution.py:719
  7.2 8.7 %collective-permute-start.2 = (bf16[37,16,128]{2,1,0:T(8,128)(2,1)S(1)}, bf16[37,16,128]{2,1,0:T(8,128)(2,1)S(1)}, u32[]{:S(2)}, u32[]{:S(2)}) collective-permute-start(bf16[37,16,128]{2,1,0:T(8,128)(2,1)S(1)} %get-tuple-element.73), channel_id=1, source_target_pairs={{0,24},{4,28},{8,16},{12,20},{16,8},{20,12},{24,0},{28,4},{1,25},{... | collective-permute-start | bytes 454664 | tf_op jit(solution)/shard_map/ppermute | solution.py:719
  11.0 7.5 %collective-permute-start.7 = (f32[4,16,128]{2,1,0:T(8,128)S(1)}, f32[4,16,128]{2,1,0:T(8,128)S(1)}, u32[]{:S(2)}, u32[]{:S(2)}) collective-permute-start(f32[4,16,128]{2,1,0:T(8,128)S(1)} %get-tuple-element.77), channel_id=1, source_target_pairs={{1,2},{2,1},{3,0},{0,3},{5,6},{6,5},{7,4},{4,7},{9,10},{10,9},{11,... | collective-permute-start | bytes 98312 | tf_op jit(solution)/shard_map/ppermute | solution.py:605
  14.4 4.1 %collective-permute-start.8 = (f32[4,16,128]{2,1,0:T(8,128)S(1)}, f32[4,16,128]{2,1,0:T(8,128)S(1)}, u32[]{:S(2)}, u32[]{:S(2)}) collective-permute-start(f32[4,16,128]{2,1,0:T(8,128)S(1)} %get-tuple-element.79), channel_id=1, source_target_pairs={{0,1},{1,0},{2,3},{3,2},{4,5},{5,4},{6,7},{7,6},{8,9},{9,8},{10,11... | collective-permute-start | bytes 98312 | tf_op jit(solution)/shard_map/ppermute | solution.py:605
  16.0 4.3 %collective-permute-start.5 = (bf16[111,16,128]{2,1,0:T(8,128)(2,1)S(1)}, bf16[111,16,128]{2,1,0:T(8,128)(2,1)S(1)}, u32[]{:S(2)}, u32[]{:S(2)}) collective-permute-start(bf16[111,16,128]{2,1,0:T(8,128)(2,1)S(1)} %constant_dynamic-update-slice_fusion.refs_0_), channel_id=1, source_target_pairs={{0,4},{4,0},{8,12},{12,8},{16,20},{20,16},{24,28},{28,24},{1,5},{5... | collective-permute-start | bytes 1363976 | tf_op jit(solution)/shard_map/ppermute | solution.py:719
  18.5 1.8 %collective-permute-start.6 = (bf16[37,16,128]{2,1,0:T(8,128)(2,1)S(1)}, bf16[37,16,128]{2,1,0:T(8,128)(2,1)S(1)}, u32[]{:S(2)}, u32[]{:S(2)}) collective-permute-start(bf16[37,16,128]{2,1,0:T(8,128)(2,1)S(1)} %collective-permute-done.2.refs_1_), channel_id=1, source_target_pairs={{0,4},{4,0},{8,12},{12,8},{16,20},{20,16},{24,28},{28,24},{1,5},{5... | collective-permute-start | bytes 454664 | tf_op jit(solution)/shard_map/ppermute | solution.py:719
  22.7 4.6 %collective-permute-start.9 = (bf16[4,16,128]{2,1,0:T(8,128)(2,1)S(1)}, bf16[4,16,128]{2,1,0:T(8,128)(2,1)S(1)}, u32[]{:S(2)}, u32[]{:S(2)}) collective-permute-start(bf16[4,16,128]{2,1,0:T(8,128)(2,1)S(1)} %get-tuple-element.87), channel_id=1, source_target_pairs={{1,2},{2,1},{3,0},{0,3},{5,6},{6,5},{7,4},{4,7},{9,10},{10,9},{11,... | collective-permute-start | bytes 49160 | tf_op jit(solution)/shard_map/ppermute | solution.py:605
  24.5 2.8 %collective-permute-start.10 = (bf16[4,16,128]{2,1,0:T(8,128)(2,1)S(1)}, bf16[4,16,128]{2,1,0:T(8,128)(2,1)S(1)}, u32[]{:S(2)}, u32[]{:S(2)}) collective-permute-start(bf16[4,16,128]{2,1,0:T(8,128)(2,1)S(1)} %get-tuple-element.89), channel_id=1, source_target_pairs={{0,1},{1,0},{2,3},{3,2},{4,5},{5,4},{6,7},{7,6},{8,9},{9,8},{10,11... | collective-permute-start | bytes 49160 | tf_op jit(solution)/shard_map/ppermute | solution.py:605
  28.0 9.3 %collective-permute-start.11 = (bf16[16,32,128]{2,1,0:T(8,128)(2,1)S(1)}, bf16[16,32,128]{2,1,0:T(8,128)(2,1)S(1)}, u32[]{:S(2)}, u32[]{:S(2)}) collective-permute-start(bf16[16,32,128]{2,1,0:T(8,128)(2,1)S(1)} %get-tuple-element.96), channel_id=1, source_target_pairs={{4,8},{8,4},{12,16},{16,12},{20,24},{24,20},{5,9},{9,5},{13,17},{1... | collective-permute-start | bytes 393224 | tf_op jit(solution)/shard_map/ppermute | solution.py:605
  33.9 3.5 %collective-permute-start.12 = (bf16[16,32,128]{2,1,0:T(8,128)(2,1)S(1)}, bf16[16,32,128]{2,1,0:T(8,128)(2,1)S(1)}, u32[]{:S(2)}, u32[]{:S(2)}) collective-permute-start(bf16[16,32,128]{2,1,0:T(8,128)(2,1)S(1)} %get-tuple-element.98), channel_id=1, source_target_pairs={{0,4},{4,0},{8,12},{12,8},{16,20},{20,16},{24,28},{28,24},{1,5},{5... | collective-permute-start | bytes 393224 | tf_op jit(solution)/shard_map/ppermute | solution.py:605

commit v12 on v9

--- a/solution.py
+++ b/solution.py
@@ -14,6 +14,9 @@
 LAT_SIGMA = 8.0
 WEIGHT_PIECES = 4
 BAND_PIECES = 4
+FEW_SLOTS = 8
+LAT_COVER = 64
+LON_COVER = 10
 SWAP_COVER = 10
 VMEM_BYTES = 40 * 1024 * 1024
 
@@ -215,6 +218,8 @@
     plan[0:1, :] = jnp.sum(jnp.where(hit, cell, 0), axis=0, keepdims=True)
     plan[1:2, :] = jnp.sum(jnp.where(hit, slot, 0), axis=0, keepdims=True)
     plan[2:3, :] = jnp.broadcast_to(outer_count, (1, LANES))
+    live_count = jnp.sum(jnp.where(owners[...] >= 0, 1, 0), axis=1, keepdims=True)
+    plan[3:4, :] = jnp.broadcast_to(live_count, (1, LANES))
 
 
 def swap_bits(count):
@@ -383,6 +388,10 @@
     one = act_one[...].astype(jnp.float32)
     grad_one = (dot_t(grad_two, weight_two[...]) * (1.0 - one * one)).astype(jnp.bfloat16)
     return rounded(dot_t(grad_one, wide_in[...]))
+
+
+def few_of(ref):
+    return ref.at[pl.ds(0, FEW_SLOTS * BLOCK_COLS)]
 
 
 def inner_forward_kernel(per_tile, outer_slots, plan, own, turned, taps, *refs):
@@ -413,15 +422,28 @@
         profile[tile * width : (tile + 1) * width, :] = rounded(total)
     for move in loads[:early]:
         move.wait()
-    take_blocks(rows, profile, picked, outer_slots, count, per_tile, width)
-    act_one, act_two, emitted = states
-    net_first(picked, weights, act_one)
+    in_time, many = rows[2, 0] <= outer_slots, rows[3, 0] > outer_slots + FEW_SLOTS
+
+    @pl.when(in_time & many)
+    def _():
+        take_blocks(rows, profile, picked, outer_slots, count, per_tile, width)
+        net_first(picked, weights, states[0])
+
+    @pl.when(in_time & ~many)
+    def _():
+        take_blocks(rows, profile, picked, outer_slots, FEW_SLOTS, per_tile, width)
+        net_first(few_of(picked), weights, few_of(states[0]))
+
     for move in loads[early:]:
         move.wait()
 
-    @pl.when(rows[2, 0] <= outer_slots)
+    @pl.when(in_time & many)
     def _():
         net_rest(weights, states)
+
+    @pl.when(in_time & ~many)
+    def _():
+        net_rest(weights, [few_of(state) for state in states])
 
 
 def outer_forward_kernel(
@@ -516,12 +538,27 @@
     for move in moves:
         move.wait()
 
-    @pl.when(rows[2, 0] <= outer_slots)
+    in_time, many = rows[2, 0] <= outer_slots, rows[3, 0] > outer_slots + FEW_SLOTS
+    first = outer_slots + FEW_SLOTS
+
+    @pl.when(in_time & many)
     def _():
         take_observed(rows, table, slabs, observed, outer_slots, late_slots)
         inner[split:, :] = net_backward(observed, states, weights)
 
-    land_blocks(rows, field, inner, 0, outer_slots + late_slots, per_tile, width)
+    @pl.when(in_time & ~many)
+    def _():
+        take_observed(rows, table, slabs, observed, outer_slots, FEW_SLOTS)
+        inner[split : split + FEW_SLOTS * BLOCK_COLS, :] = net_backward(
+            few_of(observed), [few_of(state) for state in states], weights
+        )
+
+    land_blocks(rows, field, inner, 0, first, per_tile, width)
+
+    @pl.when(many)
+    def _():
+        land_blocks(rows, field, inner, first, outer_slots + late_slots - first, per_tile, width)
+
     for tile in range(tiles):
         landing[tile] = field[tile * width : (tile + 1) * width, :]
 
@@ -669,8 +706,8 @@
     def swapped(part, apart):
         return lax.ppermute(part, "lat", [(i, i ^ apart) for i in range(lat_count)])
 
-    slabs, _ = lax.optimization_barrier((slabs, sent))
-    near = [slabs] + [swapped(slabs, apart) for apart in (1 << one, 1 << two, (1 << one) + (1 << two))]
+    later, _ = lax.optimization_barrier((slabs, sent))
+    near = [slabs, swapped(later, 1 << one), swapped(later, 1 << two), swapped(slabs, (1 << one) + (1 << two))]
 
     halos = pltpu.VMEM((2, REACH, levels, width), f32)
     smoothed, to_far, to_close = call(
@@ -678,12 +715,13 @@
         (shape((tiles, width, LANES), f32),) + (shape((tiles, REACH, LANES), f32),) * 2,
         [VMEM] * 3,
         (VMEM,) * 3,
-        conv_flops,
-        16 * field,
+        LAT_COVER * conv_flops,
+        LAT_COVER * 16 * field,
         scratch=(halos,),
         name="lat_smooth",
     )(far, close, own_part)
-    far, close, sent = exchange(to_far, to_close, "lon", True)
+    far, close, _ = exchange(to_far, to_close, "lon", True)
+
     outer_slots = 3 * slot_count // 8
     late_slots = slot_count - outer_slots
     x_rows = slot_count * BLOCK_COLS
@@ -710,8 +748,8 @@
         ),
         [ANY] + [VMEM] * 3 + [HBM] * 6,
         (VMEM,) * 10,
-        late_rows * row_flops,
-        4 * 1024 * 1024,
+        LON_COVER * late_rows * row_flops,
+        LON_COVER * 4 * 1024 * 1024,
         scratch=(
             plan_rows,
             padded,
@@ -812,7 +850,7 @@
         scratch=(pltpu.VMEM((tiles, width + 2 * REACH, LANES), f32),),
         name="lon_back",
     )(far, close, landing, taps)
-    back, _ = lax.optimization_barrier((back, to_far))
+    far, close, _ = exchange(to_far, to_close, "lat", False)
     own_part = call(
         own_back_kernel,
         shape((height, levels, width), f32),
@@ -822,9 +860,6 @@
         12 * field,
         name="lat_back_own",
     )(back, held)
-    to_close, _ = lax.optimization_barrier((to_close, own_part))
-    far, close, _ = exchange(to_far, to_close, "lat", False)
-
     return call(
         lat_back_kernel,
         shape((height, levels, width), f32),

time: 39.4 us -> 39.4 us (level)
  Pallas kernels: 15.3 us -> 13.8 us
  starting transfers between devices: 19.8 us -> 20.7 us
  waiting for transfers between devices: 3.66 us -> 4.23 us
    pallas_call x1, Pallas kernels: 3.35 us -> 2.28 us  [shards(): call(functools.partial(inner_backward_kernel, per_tile, len(slabs), outer...]
    ppermute x4, starting transfers between devices: 15.2 us -> 16.2 us  [exchange(): lax.ppermute(to_far, axis, far)]
    ppermute x4, waiting for transfers between devices: 0.01 us -> 0.59 us  [exchange(): lax.ppermute(to_close, axis, close)]
    pallas_call x1, Pallas kernels: 3.11 us -> 2.63 us  [shards(): call(functools.partial(inner_forward_kernel, per_tile, outer_slots), (sha...]
  transfers between devices with their start and end apart: 13 -> 13, of which waited for: 1 -> 2; matrix products, arithmetic and copies ran while one was open for 0% -> 0% of each run, Pallas kernels for 25% -> 21%
where the time goes in v12:
time: 39.4 us; the launch traced here: 39.2 us
  starting transfers between devices  20.7 us (53%)
  Pallas kernels  13.8 us (35%)
  waiting for transfers between devices  4.23 us (11%)
    ppermute x4, starting transfers between devices, exchange(): lax.ppermute(to_far, axis, far)  16.2 us
    ppermute x5, starting transfers between devices, swapped(): return lax.ppermute(part, 'lat', [(i, i ^ apart) for i in range(lat_count)])  4.41 us
    ppermute x4, waiting for transfers between devices, exchange(): lax.ppermute(to_far, axis, far)  3.63 us
    pallas_call x1, Pallas kernels, shards(): call(functools.partial(inner_forward_kernel, per_tile, outer_slots), (sha...  2.63 us
    pallas_call x1, Pallas kernels, shards(): call(functools.partial(outer_backward_kernel, per_tile, len(slabs), recv_...  2.43 us
    pallas_call x1, Pallas kernels, shards(): call(functools.partial(inner_backward_kernel, per_tile, len(slabs), outer...  2.28 us
    pallas_call x1, Pallas kernels, shards(): call(functools.partial(outer_forward_kernel, per_tile), state_shapes(oute...  1.72 us
    pallas_call x1, Pallas kernels, shards(): call(first_kernel, (shape((recv_most + 1, slab_rows, LANES), bf16), half_...  1.27 us
  transfers between devices with their start and end apart: 13, of which 2 were waited for; matrix products, arithmetic and copies ran while one was open for 0% of the time, Pallas kernels for 21%

profile of v12, /device:TPU:1, one launch (start us, length us, event | category | flops | bytes accessed | tf_op | source)
XLA Modules:
  0.0 39.2 jit_solution(4225514561969543440)
XLA Ops:
  0.0 1.3 %slabs_halves.1 = (bf16[37,16,128]{2,1,0:T(8,128)(2,1)S(1)}, bf16[16,32,128]{2,1,0:T(8,128)(2,1)S(1)}, bf16[16,32,128]{2,1,0:T(8,128)(2,1)S(1)}, f32[16,32,128]{2,1,0:T(8,128)S(1)}, f32[16,32,128]{2,1,0:T(8,128)S(1)}) custom-call(bf16[36,16,128]{2,1,0:T(8,128)(2,1)} %bitcast.13, s32[1,64]{1,0:T(1,128)} %bitcast.14, s32[1,36]{1,0:T(1,128)} %bitcast.17, ...), custom_call_target="tpu_custom_call" | custom-call | bytes 1572864 | tf_op jit(solution)/shard_map/slabs_halves/pallas_call | solution.py:645
  1.3 4.5 %collective-permute-start.3 = (bf16[16,32,128]{2,1,0:T(8,128)(2,1)S(1)}, bf16[16,32,128]{2,1,0:T(8,128)(2,1)S(1)}, u32[]{:S(2)}, u32[]{:S(2)}) collective-permute-start(bf16[16,32,128]{2,1,0:T(8,128)(2,1)S(1)} %get-tuple-element.58), channel_id=1, source_target_pairs={{4,8},{8,4},{12,16},{16,12},{20,24},{24,20},{5,9},{9,5},{13,17},{1... | collective-permute-start | bytes 393224 | tf_op jit(solution)/shard_map/ppermute | solution.py:607
  5.8 0.1 collective-permute-start.4
  5.9 1.3 %collective-permute-start = (bf16[37,16,128]{2,1,0:T(8,128)(2,1)S(1)}, bf16[37,16,128]{2,1,0:T(8,128)(2,1)S(1)}, u32[]{:S(2)}, u32[]{:S(2)}) collective-permute-start(bf16[37,16,128]{2,1,0:T(8,128)(2,1)S(1)} %get-tuple-element.67), channel_id=1, source_target_pairs={{0,16},{4,20},{8,24},{12,28},{16,0},{20,4},{24,8},{28,12},{1,17},{... | collective-permute-start | bytes 454664 | tf_op jit(solution)/shard_map/ppermute | solution.py:707
  7.2 0.1 collective-permute-start.1
  7.2 1.3 %collective-permute-start.2 = (bf16[37,16,128]{2,1,0:T(8,128)(2,1)S(1)}, bf16[37,16,128]{2,1,0:T(8,128)(2,1)S(1)}, u32[]{:S(2)}, u32[]{:S(2)}) collective-permute-start(bf16[37,16,128]{2,1,0:T(8,128)(2,1)S(1)} %get-tuple-element.67), channel_id=1, source_target_pairs={{0,24},{4,28},{8,16},{12,20},{16,8},{20,12},{24,0},{28,4},{1,25},{... | collective-permute-start | bytes 454664 | tf_op jit(solution)/shard_map/ppermute | solution.py:707
  8.6 0.9 %taps_background.1 = (f32[4,24,128]{2,1,0:T(8,128)S(1)}, f32[4,128,128]{2,1,0:T(8,128)S(1)}, s32[8,128]{1,0:T(8,128)S(1)}, f32[16,32,128]{2,1,0:T(8,128)S(1)}) custom-call(s32[16]{0:T(128)} %lon_width.1, s32[1,64]{1,0:T(1,128)} %bitcast.16, s32[1,64]{1,0:T(1,128)} %bitcast.15, f32[16,32,128]{2,1,0:T(8,128)S(1)} %get-tuple-element.53.field, ...), custom_call_target="tpu_custom_call" | custom-call | flops 2162688 | bytes 786432 | tf_op jit(solution)/shard_map/taps_background/pallas_call | solution.py:678
  9.5 0.4 %lat_smooth.1 = (f32[4,128,128]{2,1,0:T(8,128)S(1)}, f32[4,16,128]{2,1,0:T(8,128)S(1)}, f32[4,16,128]{2,1,0:T(8,128)S(1)}) custom-call(bf16[16,32,128]{2,1,0:T(8,128)(2,1)S(1)} %collective-permute-done.3.far, bf16[16,32,128]{2,1,0:T(8,128)(2,1)S(1)} %collective-permute-done.4.close, f32[16,32,128]{2,1,0:T(8,128)S(1)} %get-tuple-element.62.own_part), custom_call_target="tpu_custom_call" | custom-call | flops 276824064 | bytes 67108864 | tf_op jit(solution)/shard_map/lat_smooth/pallas_call | solution.py:713
  10.0 3.4 %collective-permute-start.7 = (f32[4,16,128]{2,1,0:T(8,128)S(1)}, f32[4,16,128]{2,1,0:T(8,128)S(1)}, u32[]{:S(2)}, u32[]{:S(2)}) collective-permute-start(f32[4,16,128]{2,1,0:T(8,128)S(1)} %get-tuple-element.74), channel_id=1, source_target_pairs={{1,2},{2,1},{3,0},{0,3},{5,6},{6,5},{7,4},{4,7},{9,10},{10,9},{11,... | collective-permute-start | bytes 98312 | tf_op jit(solution)/shard_map/ppermute | solution.py:607
  13.3 2.6 %inner_forward.1 = (f32[512,128]{1,0:T(8,128)S(1)}, bf16[320,1024]{1,0:T(8,128)(2,1)S(1)}, bf16[320,1024]{1,0:T(8,128)(2,1)S(1)}, f32[320,256]{1,0:T(8,128)S(1)}...) custom-call(s32[8,128]{1,0:T(8,128)S(1)} %get-tuple-element.55.plan,, ...), custom_call_target="tpu_custom_call" | custom-call | flops 9227468800 | bytes 41943040 | tf_op jit(solution)/shard_map/inner_forward/pallas_call | solution.py:737
  16.0 0.0 collective-permute-done
  16.1 1.6 %collective-permute-start.5 = (bf16[111,16,128]{2,1,0:T(8,128)(2,1)S(1)}, bf16[111,16,128]{2,1,0:T(8,128)(2,1)S(1)}, u32[]{:S(2)}, u32[]{:S(2)}) collective-permute-start(bf16[111,16,128]{2,1,0:T(8,128)(2,1)S(1)} %constant_dynamic-update-slice_fusion.refs_0_), channel_id=1, source_target_pairs={{0,4},{4,0},{8,12},{12,8},{16,20},{20,16},{24,28},{28,24},{1,5},{5... | collective-permute-start | bytes 1363976 | tf_op jit(solution)/shard_map/ppermute | solution.py:707
  17.7 0.1 collective-permute-start.6
  17.8 1.7 %outer_forward.1 = (bf16[192,1024]{1,0:T(8,128)(2,1)S(1)}, bf16[192,1024]{1,0:T(8,128)(2,1)S(1)}, f32[192,256]{1,0:T(8,128)S(1)}, bf16[320,1024]{1,0:T(8,128)(2,...) custom-call(s32[8,128]{1,0:T(8,128)S(1)} %get-tuple-element.55.plan, ...), custom_call_target="tpu_custom_call" | custom-call | flops 5536481280 | bytes 41943040 | tf_op jit(solution)/shard_map/outer_forward/pallas_call | solution.py:782
  19.5 2.4 %outer_backward.1 = (s32[8,128]{1,0:T(8,128)S(1)}, f32[512,128]{1,0:T(8,128)S(1)}, bf16[4,16,128]{2,1,0:T(8,128)(2,1)S(1)}, bf16[4,16,128]{2,1,0:T(8,128)(2,1)S(1)}) custom-call(s32[8,128]{1,0:T(8,128)S(1)} %get-tuple-element.55.plan, bf16[111,16,128]{2,1,0:T(8,128)(2,1)S(1)} %constant_dynamic-update-slice_fusion.refs_0_, ...), custom_call_target="tpu_custom_call" | custom-call | flops 553648128 | bytes 4194304 | tf_op jit(solution)/shard_map/outer_backward/pallas_call | solution.py:801
  22.0 2.5 %collective-permute-start.9 = (bf16[4,16,128]{2,1,0:T(8,128)(2,1)S(1)}, bf16[4,16,128]{2,1,0:T(8,128)(2,1)S(1)}, u32[]{:S(2)}, u32[]{:S(2)}) collective-permute-start(bf16[4,16,128]{2,1,0:T(8,128)(2,1)S(1)} %get-tuple-element.87), channel_id=1, source_target_pairs={{1,2},{2,1},{3,0},{0,3},{5,6},{6,5},{7,4},{4,7},{9,10},{10,9},{11,... | collective-permute-start | bytes 49160 | tf_op jit(solution)/shard_map/ppermute | solution.py:607
  24.5 2.3 %inner_backward.1.own = f32[4,128,128]{2,1,0:T(8,128)S(1)} custom-call(s32[8,128]{1,0:T(8,128)S(1)} %get-tuple-element.55.plan, s32[8,128]{1,0:T(8,128)S(1)} %get-tuple-element.91.table_rows, f32[512,128]{1,0:T(8,128)S(1)} %get-tuple-element.92.sens, bf16[111,16,128]{2,1,0:T(8,128)(2,1)S(1)} %constant_dynamic-update-slice_fusion.refs_0_, ...), custom_call_target="tpu_custom_call" | custom-call | flops 922746880 | bytes 4194304 | tf_op jit(solution)/shard_map/inner_backward/pallas_call | solution.py:825
  26.8 0.6 %collective-permute-done.10.close = bf16[4,16,128]{2,1,0:T(8,128)(2,1)S(1)} collective-permute-done((bf16[4,16,128]{2,1,0:T(8,128)(2,1)S(1)}, bf16[4,16,128]{2,1,0:T(8,128)(2,1)S(1)}, u32[]{:S(2)}, u32[]{:S(2)}) %collective-permute-start.10) | collective-permute-done | bytes 16416 | tf_op jit(solution)/shard_map/ppermute | solution.py:607
  27.4 0.8 %lon_back.1 = (f32[16,32,128]{2,1,0:T(8,128)S(1)}, bf16[16,32,128]{2,1,0:T(8,128)(2,1)S(1)}, bf16[16,32,128]{2,1,0:T(8,128)(2,1)S(1)}) custom-call(bf16[4,16,128]{2,1,0:T(8,128)(2,1)S(1)} %collective-permute-done.9.far, bf16[4,16,128]{2,1,0:T(8,128)(2,1)S(1)} %collective-permute-done.10.close, f32[4,128,128]{2,1,0:T(8,128)S(1)} %inner_backward.1.own, ...), custom_call_target="tpu_custom_call" | custom-call | flops 4325376 | bytes 524288 | tf_op jit(solution)/shard_map/lon_back/pallas_call | solution.py:843
  28.2 5.7 %collective-permute-start.11 = (bf16[16,32,128]{2,1,0:T(8,128)(2,1)S(1)}, bf16[16,32,128]{2,1,0:T(8,128)(2,1)S(1)}, u32[]{:S(2)}, u32[]{:S(2)}) collective-permute-start(bf16[16,32,128]{2,1,0:T(8,128)(2,1)S(1)} %get-tuple-element.96), channel_id=1, source_target_pairs={{4,8},{8,4},{12,16},{16,12},{20,24},{24,20},{5,9},{9,5},{13,17},{1... | collective-permute-start | bytes 393224 | tf_op jit(solution)/shard_map/ppermute | solution.py:607
  33.9 0.1 collective-permute-start.12
  34.0 0.3 lat_back_own.1.own_part
  34.3 3.6 %collective-permute-done.11.far = bf16[16,32,128]{2,1,0:T(8,128)(2,1)S(1)} collective-permute-done((bf16[16,32,128]{2,1,0:T(8,128)(2,1)S(1)}, bf16[16,32,128]{2,1,0:T(8,128)(2,1)S(1)}, u32[]{:S(2)}, u32[]{:S(2)}) %collective-permute-start.11) | collective-permute-done | bytes 131104 | tf_op jit(solution)/shard_map/ppermute | solution.py:607
  38.0 1.0 %lat_back.1 = f32[16,32,128]{2,1,0:T(8,128)} custom-call(bf16[16,32,128]{2,1,0:T(8,128)(2,1)S(1)} %collective-permute-done.11.far, bf16[16,32,128]{2,1,0:T(8,128)(2,1)S(1)} %collective-permute-done.12.close, f32[16,32,128]{2,1,0:T(8,128)S(1)} %lat_back_own.1.own_part), custom_call_target="tpu_custom_call" | custom-call | flops 2162688 | bytes 1048576 | tf_op jit(solution)/shard_map/lat_back/pallas_call | solution.py:863
  (15 shorter events, 0.1 us)
Async XLA Ops:
  1.3 8.2 %collective-permute-start.3 = (bf16[16,32,128]{2,1,0:T(8,128)(2,1)S(1)}, bf16[16,32,128]{2,1,0:T(8,128)(2,1)S(1)}, u32[]{:S(2)}, u32[]{:S(2)}) collective-permute-start(bf16[16,32,128]{2,1,0:T(8,128)(2,1)S(1)} %get-tuple-element.58), channel_id=1, source_target_pairs={{4,8},{8,4},{12,16},{16,12},{20,24},{24,20},{5,9},{9,5},{13,17},{1... | collective-permute-start | bytes 393224 | tf_op jit(solution)/shard_map/ppermute | solution.py:607
  5.8 3.7 %collective-permute-start.4 = (bf16[16,32,128]{2,1,0:T(8,128)(2,1)S(1)}, bf16[16,32,128]{2,1,0:T(8,128)(2,1)S(1)}, u32[]{:S(2)}, u32[]{:S(2)}) collective-permute-start(bf16[16,32,128]{2,1,0:T(8,128)(2,1)S(1)} %get-tuple-element.59), channel_id=1, source_target_pairs={{0,4},{4,0},{8,12},{12,8},{16,20},{20,16},{24,28},{28,24},{1,5},{5... | collective-permute-start | bytes 393224 | tf_op jit(solution)/shard_map/ppermute | solution.py:607
  5.9 10.1 %collective-permute-start = (bf16[37,16,128]{2,1,0:T(8,128)(2,1)S(1)}, bf16[37,16,128]{2,1,0:T(8,128)(2,1)S(1)}, u32[]{:S(2)}, u32[]{:S(2)}) collective-permute-start(bf16[37,16,128]{2,1,0:T(8,128)(2,1)S(1)} %get-tuple-element.67), channel_id=1, source_target_pairs={{0,16},{4,20},{8,24},{12,28},{16,0},{20,4},{24,8},{28,12},{1,17},{... | collective-permute-start | bytes 454664 | tf_op jit(solution)/shard_map/ppermute | solution.py:707
  7.2 8.8 %collective-permute-start.1 = (bf16[37,16,128]{2,1,0:T(8,128)(2,1)S(1)}, bf16[37,16,128]{2,1,0:T(8,128)(2,1)S(1)}, u32[]{:S(2)}, u32[]{:S(2)}) collective-permute-start(bf16[37,16,128]{2,1,0:T(8,128)(2,1)S(1)} %get-tuple-element.67), channel_id=1, source_target_pairs={{0,8},{4,12},{8,0},{12,4},{16,24},{20,28},{24,16},{28,20},{1,9},{5... | collective-permute-start | bytes 454664 | tf_op jit(solution)/shard_map/ppermute | solution.py:707
  7.2 8.8 %collective-permute-start.2 = (bf16[37,16,128]{2,1,0:T(8,128)(2,1)S(1)}, bf16[37,16,128]{2,1,0:T(8,128)(2,1)S(1)}, u32[]{:S(2)}, u32[]{:S(2)}) collective-permute-start(bf16[37,16,128]{2,1,0:T(8,128)(2,1)S(1)} %get-tuple-element.67), channel_id=1, source_target_pairs={{0,24},{4,28},{8,16},{12,20},{16,8},{20,12},{24,0},{28,4},{1,25},{... | collective-permute-start | bytes 454664 | tf_op jit(solution)/shard_map/ppermute | solution.py:707
  10.0 7.8 %collective-permute-start.7 = (f32[4,16,128]{2,1,0:T(8,128)S(1)}, f32[4,16,128]{2,1,0:T(8,128)S(1)}, u32[]{:S(2)}, u32[]{:S(2)}) collective-permute-start(f32[4,16,128]{2,1,0:T(8,128)S(1)} %get-tuple-element.74), channel_id=1, source_target_pairs={{1,2},{2,1},{3,0},{0,3},{5,6},{6,5},{7,4},{4,7},{9,10},{10,9},{11,... | collective-permute-start | bytes 98312 | tf_op jit(solution)/shard_map/ppermute | solution.py:607
  13.3 4.5 %collective-permute-start.8 = (f32[4,16,128]{2,1,0:T(8,128)S(1)}, f32[4,16,128]{2,1,0:T(8,128)S(1)}, u32[]{:S(2)}, u32[]{:S(2)}) collective-permute-start(f32[4,16,128]{2,1,0:T(8,128)S(1)} %get-tuple-element.76), channel_id=1, source_target_pairs={{0,1},{1,0},{2,3},{3,2},{4,5},{5,4},{6,7},{7,6},{8,9},{9,8},{10,11... | collective-permute-start | bytes 98312 | tf_op jit(solution)/shard_map/ppermute | solution.py:607
  16.1 3.4 %collective-permute-start.5 = (bf16[111,16,128]{2,1,0:T(8,128)(2,1)S(1)}, bf16[111,16,128]{2,1,0:T(8,128)(2,1)S(1)}, u32[]{:S(2)}, u32[]{:S(2)}) collective-permute-start(bf16[111,16,128]{2,1,0:T(8,128)(2,1)S(1)} %constant_dynamic-update-slice_fusion.refs_0_), channel_id=1, source_target_pairs={{0,4},{4,0},{8,12},{12,8},{16,20},{20,16},{24,28},{28,24},{1,5},{5... | collective-permute-start | bytes 1363976 | tf_op jit(solution)/shard_map/ppermute | solution.py:707
  17.7 1.8 %collective-permute-start.6 = (bf16[37,16,128]{2,1,0:T(8,128)(2,1)S(1)}, bf16[37,16,128]{2,1,0:T(8,128)(2,1)S(1)}, u32[]{:S(2)}, u32[]{:S(2)}) collective-permute-start(bf16[37,16,128]{2,1,0:T(8,128)(2,1)S(1)} %collective-permute-done.2.refs_1_), channel_id=1, source_target_pairs={{0,4},{4,0},{8,12},{12,8},{16,20},{20,16},{24,28},{28,24},{1,5},{5... | collective-permute-start | bytes 454664 | tf_op jit(solution)/shard_map/ppermute | solution.py:707
  22.0 4.8 %collective-permute-start.9 = (bf16[4,16,128]{2,1,0:T(8,128)(2,1)S(1)}, bf16[4,16,128]{2,1,0:T(8,128)(2,1)S(1)}, u32[]{:S(2)}, u32[]{:S(2)}) collective-permute-start(bf16[4,16,128]{2,1,0:T(8,128)(2,1)S(1)} %get-tuple-element.87), channel_id=1, source_target_pairs={{1,2},{2,1},{3,0},{0,3},{5,6},{6,5},{7,4},{4,7},{9,10},{10,9},{11,... | collective-permute-start | bytes 49160 | tf_op jit(solution)/shard_map/ppermute | solution.py:607
  24.5 2.9 %collective-permute-start.10 = (bf16[4,16,128]{2,1,0:T(8,128)(2,1)S(1)}, bf16[4,16,128]{2,1,0:T(8,128)(2,1)S(1)}, u32[]{:S(2)}, u32[]{:S(2)}) collective-permute-start(bf16[4,16,128]{2,1,0:T(8,128)(2,1)S(1)} %get-tuple-element.89), channel_id=1, source_target_pairs={{0,1},{1,0},{2,3},{3,2},{4,5},{5,4},{6,7},{7,6},{8,9},{9,8},{10,11... | collective-permute-start | bytes 49160 | tf_op jit(solution)/shard_map/ppermute | solution.py:607
  28.2 9.8 %collective-permute-start.11 = (bf16[16,32,128]{2,1,0:T(8,128)(2,1)S(1)}, bf16[16,32,128]{2,1,0:T(8,128)(2,1)S(1)}, u32[]{:S(2)}, u32[]{:S(2)}) collective-permute-start(bf16[16,32,128]{2,1,0:T(8,128)(2,1)S(1)} %get-tuple-element.96), channel_id=1, source_target_pairs={{4,8},{8,4},{12,16},{16,12},{20,24},{24,20},{5,9},{9,5},{13,17},{1... | collective-permute-start | bytes 393224 | tf_op jit(solution)/shard_map/ppermute | solution.py:607
  33.9 4.0 %collective-permute-start.12 = (bf16[16,32,128]{2,1,0:T(8,128)(2,1)S(1)}, bf16[16,32,128]{2,1,0:T(8,128)(2,1)S(1)}, u32[]{:S(2)}, u32[]{:S(2)}) collective-permute-start(bf16[16,32,128]{2,1,0:T(8,128)(2,1)S(1)} %get-tuple-element.98), channel_id=1, source_target_pairs={{0,4},{4,0},{8,12},{12,8},{16,20},{20,16},{24,28},{28,24},{1,5},{5... | collective-permute-start | bytes 393224 | tf_op jit(solution)/shard_map/ppermute | solution.py:607

commit v13 on v12

--- a/solution.py
+++ b/solution.py
@@ -109,12 +109,10 @@
     block_owner,
     channel_count,
     control,
-    background,
     slabs,
     to_far,
     to_close,
     held,
-    field,
     owners,
     counts,
     rows,
@@ -130,9 +128,8 @@
     piece = control.shape[0] // BAND_PIECES
     for k in range(BAND_PIECES):
         part = pl.ds(k * piece, piece)
-        moves.append(pltpu.make_async_copy(control.at[part], held.at[part], sems.at[5 + k]))
-    field_in = pltpu.make_async_copy(background, field, sems.at[4])
-    for move in moves[3:] + moves[:3] + [field_in]:
+        moves.append(pltpu.make_async_copy(control.at[part], held.at[part], sems.at[4 + k]))
+    for move in moves[3:] + moves[:3]:
         move.start()
     rows[...] = jnp.full(rows.shape, -1.0, jnp.float32)
     moves[1].wait()
@@ -146,7 +143,6 @@
         move.wait()
     halve_for_sides(held, held.shape[0], to_far, to_close)
     moves[0].wait()
-    field_in.wait()
     last.wait()
 
 
@@ -154,7 +150,7 @@
     lon_width,
     block_cells,
     block_owner,
-    field,
+    background,
     band,
     taps,
     turned,
@@ -163,6 +159,7 @@
     widths,
     cells,
     owners,
+    field,
     sems,
 ):
     moves = [
@@ -170,6 +167,10 @@
         pltpu.make_async_copy(block_cells, cells, sems.at[1]),
         pltpu.make_async_copy(block_owner, owners, sems.at[2]),
     ]
+    piece = background.shape[0] // BAND_PIECES
+    for k in range(BAND_PIECES):
+        part = pl.ds(k * piece, piece)
+        moves.append(pltpu.make_async_copy(background.at[part], field.at[part], sems.at[3 + k]))
     tiles = turned.shape[0]
     height, levels, width = field.shape
     per_tile = height // tiles
@@ -181,9 +182,6 @@
 
     for row in range(height):
         own_part[row] = lat_sum(band, row, 0, height)
-    for tile in range(tiles):
-        block = field[tile * per_tile : (tile + 1) * per_tile].reshape(per_tile * levels, width)
-        turned[tile] = jnp.transpose(block)
 
     lane_row = lax.broadcasted_iota(jnp.int32, (1, LANES), 1) // levels
     steps = lax.broadcasted_iota(jnp.int32, (taps.shape[1], LANES), 0)
@@ -220,6 +218,11 @@
     plan[2:3, :] = jnp.broadcast_to(outer_count, (1, LANES))
     live_count = jnp.sum(jnp.where(owners[...] >= 0, 1, 0), axis=1, keepdims=True)
     plan[3:4, :] = jnp.broadcast_to(live_count, (1, LANES))
+    for move in moves[3:]:
+        move.wait()
+    for tile in range(tiles):
+        block = field[tile * per_tile : (tile + 1) * per_tile].reshape(per_tile * levels, width)
+        turned[tile] = jnp.transpose(block)
 
 
 def swap_bits(count):
@@ -563,7 +566,7 @@
         landing[tile] = field[tile * width : (tile + 1) * width, :]
 
 
-def lon_back_kernel(far, close, own, taps, back, to_far, to_close, padded):
+def lon_back_kernel(far, close, own, taps, back, halved, padded):
     tiles, width, _ = own.shape
     height, levels, _ = back.shape
     per_tile = height // tiles
@@ -572,7 +575,7 @@
         rows = jnp.transpose(lon_conv(padded, taps, tile, 0, width))
         rows = rows.reshape(per_tile, levels, width)
         back[tile * per_tile : (tile + 1) * per_tile] = rows
-    halve_for_sides(back, height, to_far, to_close)
+        halved[tile * per_tile : (tile + 1) * per_tile] = rows.astype(jnp.bfloat16)
 
 
 def own_back_kernel(back, control, own_part):
@@ -642,25 +645,24 @@
     radiance = radiance.T.reshape(recv_most, BLOCK_COLS, halves, LANES)
     radiance = jnp.swapaxes(radiance, 1, 2).reshape(recv_most, slab_rows, LANES)
     half_field = shape(control.shape, bf16)
-    slabs, to_far, to_close, held, ground = call(
+    slabs, to_far, to_close, held = call(
         first_kernel,
         (
             shape((recv_most + 1, slab_rows, LANES), bf16),
             half_field,
             half_field,
             shape(control.shape, f32),
-            shape(control.shape, f32),
-        ),
-        [HBM] * 5,
-        (HBM,) + (VMEM,) * 4,
+        ),
+        [HBM] * 4,
+        (HBM,) + (VMEM,) * 3,
         0,
-        24 * field,
+        20 * field,
         scratch=(
             pltpu.VMEM((1, slot_count), i32),
             pltpu.VMEM((1, recv_most), i32),
             pltpu.VMEM((slab_rows, LANES), f32),
             pltpu.VMEM((slab_rows, LANES), bf16),
-            pltpu.SemaphoreType.DMA((5 + BAND_PIECES,)),
+            pltpu.SemaphoreType.DMA((4 + BAND_PIECES,)),
         ),
         name="slabs_halves",
     )(
@@ -669,7 +671,6 @@
             block_owner.reshape(1, slot_count),
             channel_count.reshape(1, recv_most),
             control,
-            background,
         )
     )
     far, close, sent = exchange(to_far, to_close, "lat", False)
@@ -683,7 +684,7 @@
             shape((8, LANES), i32),
             shape(control.shape, f32),
         ),
-        [HBM] * 3 + [VMEM] * 2,
+        [HBM] * 4 + [VMEM],
         (VMEM,) * 4,
         conv_flops // 2,
         12 * field,
@@ -691,12 +692,14 @@
             pltpu.SMEM((height,), i32),
             pltpu.VMEM((1, slot_count), i32),
             pltpu.VMEM((1, slot_count), i32),
-            pltpu.SemaphoreType.DMA((3,)),
+            band,
+            pltpu.SemaphoreType.DMA((3 + BAND_PIECES,)),
         ),
         name="taps_background",
     )(
-        *pinned(lon_width, block_cells.reshape(1, slot_count), block_owner.reshape(1, slot_count)),
-        ground,
+        *pinned(
+            lon_width, block_cells.reshape(1, slot_count), block_owner.reshape(1, slot_count), background
+        ),
         held,
     )
 
@@ -840,17 +843,17 @@
         name="inner_backward",
     )(plan, table, sens, *slabs, *weights[:3], *inner_states)
 
-    back, to_far, to_close = call(
+    back, halved = call(
         lon_back_kernel,
-        (shape((height, levels, width), f32), half_field, half_field),
+        (shape((height, levels, width), f32), half_field),
         [VMEM] * 4,
-        (VMEM,) * 3,
+        (VMEM,) * 2,
         conv_flops,
         8 * field,
         scratch=(pltpu.VMEM((tiles, width + 2 * REACH, LANES), f32),),
         name="lon_back",
     )(far, close, landing, taps)
-    far, close, _ = exchange(to_far, to_close, "lat", False)
+    far, close, _ = exchange(halved, halved, "lat", False)
     own_part = call(
         own_back_kernel,
         shape((height, levels, width), f32),

time: 39.4 us -> 39.2 us (level)
  transfers between devices with their start and end apart: 13 -> 13, of which waited for: 2 -> 2; matrix products, arithmetic and copies ran while one was open for 0% -> 0% of each run, Pallas kernels for 21% -> 22%
where the time goes in v13:
time: 39.2 us; the launch traced here: 38.9 us
  starting transfers between devices  20.8 us (53%)
  Pallas kernels  13.8 us (35%)
  waiting for transfers between devices  3.95 us (10%)
    ppermute x4, starting transfers between devices, exchange(): lax.ppermute(to_far, axis, far)  16.2 us
    ppermute x5, starting transfers between devices, swapped(): return lax.ppermute(part, 'lat', [(i, i ^ apart) for i in range(lat_count)])  4.41 us
    ppermute x4, waiting for transfers between devices, exchange(): lax.ppermute(to_far, axis, far)  3.64 us
    pallas_call x1, Pallas kernels, shards(): call(functools.partial(inner_forward_kernel, per_tile, outer_slots), (sha...  2.63 us
    pallas_call x1, Pallas kernels, shards(): call(functools.partial(outer_backward_kernel, per_tile, len(slabs), recv_...  2.43 us
    pallas_call x1, Pallas kernels, shards(): call(functools.partial(inner_backward_kernel, per_tile, len(slabs), outer...  2.28 us
    pallas_call x1, Pallas kernels, shards(): call(functools.partial(outer_forward_kernel, per_tile), state_shapes(oute...  1.72 us
    pallas_call x1, Pallas kernels, shards(): call(prepare_kernel, (shape((tiles, 24, LANES), f32), shape((tiles, width...  1.16 us
  transfers between devices with their start and end apart: 13, of which 2 were waited for; matrix products, arithmetic and copies ran while one was open for 0% of the time, Pallas kernels for 22%

profile of v13, /device:TPU:1, one launch (start us, length us, event | category | flops | bytes accessed | tf_op | source)
XLA Modules:
  0.0 38.9 jit_solution(17006552183060290958)
XLA Ops:
  0.0 1.1 %slabs_halves.1 = (bf16[37,16,128]{2,1,0:T(8,128)(2,1)S(1)}, bf16[16,32,128]{2,1,0:T(8,128)(2,1)S(1)}, bf16[16,32,128]{2,1,0:T(8,128)(2,1)S(1)}, f32[16,32,128]{2,1,0:T(8,128)S(1)}) custom-call(bf16[36,16,128]{2,1,0:T(8,128)(2,1)} %bitcast.13, s32[1,64]{1,0:T(1,128)} %bitcast.14, s32[1,36]{1,0:T(1,128)} %bitcast.16, f32[16,32,128]{2,1,0:T(8,128)} %control.1), custom_call_target="tpu_custom_call" | custom-call | bytes 1310720 | tf_op jit(solution)/shard_map/slabs_halves/pallas_call | solution.py:648
  1.1 4.5 %collective-permute-start.3 = (bf16[16,32,128]{2,1,0:T(8,128)(2,1)S(1)}, bf16[16,32,128]{2,1,0:T(8,128)(2,1)S(1)}, u32[]{:S(2)}, u32[]{:S(2)}) collective-permute-start(bf16[16,32,128]{2,1,0:T(8,128)(2,1)S(1)} %get-tuple-element.55), channel_id=1, source_target_pairs={{4,8},{8,4},{12,16},{16,12},{20,24},{24,20},{5,9},{9,5},{13,17},{1... | collective-permute-start | bytes 393224 | tf_op jit(solution)/shard_map/ppermute | solution.py:610
  5.6 0.1 collective-permute-start.4
  5.7 1.3 %collective-permute-start = (bf16[37,16,128]{2,1,0:T(8,128)(2,1)S(1)}, bf16[37,16,128]{2,1,0:T(8,128)(2,1)S(1)}, u32[]{:S(2)}, u32[]{:S(2)}) collective-permute-start(bf16[37,16,128]{2,1,0:T(8,128)(2,1)S(1)} %get-tuple-element.64), channel_id=1, source_target_pairs={{0,16},{4,20},{8,24},{12,28},{16,0},{20,4},{24,8},{28,12},{1,17},{... | collective-permute-start | bytes 454664 | tf_op jit(solution)/shard_map/ppermute | solution.py:710
  7.0 0.1 collective-permute-start.1
  7.1 1.3 %collective-permute-start.2 = (bf16[37,16,128]{2,1,0:T(8,128)(2,1)S(1)}, bf16[37,16,128]{2,1,0:T(8,128)(2,1)S(1)}, u32[]{:S(2)}, u32[]{:S(2)}) collective-permute-start(bf16[37,16,128]{2,1,0:T(8,128)(2,1)S(1)} %get-tuple-element.64), channel_id=1, source_target_pairs={{0,24},{4,28},{8,16},{12,20},{16,8},{20,12},{24,0},{28,4},{1,25},{... | collective-permute-start | bytes 454664 | tf_op jit(solution)/shard_map/ppermute | solution.py:710
  8.4 1.2 %taps_background.1 = (f32[4,24,128]{2,1,0:T(8,128)S(1)}, f32[4,128,128]{2,1,0:T(8,128)S(1)}, s32[8,128]{1,0:T(8,128)S(1)}, f32[16,32,128]{2,1,0:T(8,128)S(1)}) custom-call(s32[16]{0:T(128)} %lon_width.1, s32[1,64]{1,0:T(1,128)} %bitcast.17, s32[1,64]{1,0:T(1,128)} %bitcast.15, f32[16,32,128]{2,1,0:T(8,128)} %background.1, ...), custom_call_target="tpu_custom_call" | custom-call | flops 2162688 | bytes 786432 | tf_op jit(solution)/shard_map/taps_background/pallas_call | solution.py:679
  9.6 0.0 collective-permute-done.4.close
  9.6 0.4 %lat_smooth.1 = (f32[4,128,128]{2,1,0:T(8,128)S(1)}, f32[4,16,128]{2,1,0:T(8,128)S(1)}, f32[4,16,128]{2,1,0:T(8,128)S(1)}) custom-call(bf16[16,32,128]{2,1,0:T(8,128)(2,1)S(1)} %collective-permute-done.3.far, bf16[16,32,128]{2,1,0:T(8,128)(2,1)S(1)} %collective-permute-done.4.close, f32[16,32,128]{2,1,0:T(8,128)S(1)} %get-tuple-element.59.own_part), custom_call_target="tpu_custom_call" | custom-call | flops 276824064 | bytes 67108864 | tf_op jit(solution)/shard_map/lat_smooth/pallas_call | solution.py:716
  10.1 3.4 %collective-permute-start.7 = (f32[4,16,128]{2,1,0:T(8,128)S(1)}, f32[4,16,128]{2,1,0:T(8,128)S(1)}, u32[]{:S(2)}, u32[]{:S(2)}) collective-permute-start(f32[4,16,128]{2,1,0:T(8,128)S(1)} %get-tuple-element.71), channel_id=1, source_target_pairs={{1,2},{2,1},{3,0},{0,3},{5,6},{6,5},{7,4},{4,7},{9,10},{10,9},{11,... | collective-permute-start | bytes 98312 | tf_op jit(solution)/shard_map/ppermute | solution.py:610
  13.4 2.6 %inner_forward.1 = (f32[512,128]{1,0:T(8,128)S(1)}, bf16[320,1024]{1,0:T(8,128)(2,1)S(1)}, bf16[320,1024]{1,0:T(8,128)(2,1)S(1)}, f32[320,256]{1,0:T(8,128)S(1)}...) custom-call(s32[8,128]{1,0:T(8,128)S(1)} %get-tuple-element.52.plan,, ...), custom_call_target="tpu_custom_call" | custom-call | flops 9227468800 | bytes 41943040 | tf_op jit(solution)/shard_map/inner_forward/pallas_call | solution.py:740
  16.2 1.6 %collective-permute-start.5 = (bf16[111,16,128]{2,1,0:T(8,128)(2,1)S(1)}, bf16[111,16,128]{2,1,0:T(8,128)(2,1)S(1)}, u32[]{:S(2)}, u32[]{:S(2)}) collective-permute-start(bf16[111,16,128]{2,1,0:T(8,128)(2,1)S(1)} %constant_dynamic-update-slice_fusion.refs_0_), channel_id=1, source_target_pairs={{0,4},{4,0},{8,12},{12,8},{16,20},{20,16},{24,28},{28,24},{1,5},{5... | collective-permute-start | bytes 1363976 | tf_op jit(solution)/shard_map/ppermute | solution.py:710
  17.8 0.1 collective-permute-start.6
  17.9 1.7 %outer_forward.1 = (bf16[192,1024]{1,0:T(8,128)(2,1)S(1)}, bf16[192,1024]{1,0:T(8,128)(2,1)S(1)}, f32[192,256]{1,0:T(8,128)S(1)}, bf16[320,1024]{1,0:T(8,128)(2,...) custom-call(s32[8,128]{1,0:T(8,128)S(1)} %get-tuple-element.52.plan, ...), custom_call_target="tpu_custom_call" | custom-call | flops 5536481280 | bytes 41943040 | tf_op jit(solution)/shard_map/outer_forward/pallas_call | solution.py:785
  19.7 2.4 %outer_backward.1 = (s32[8,128]{1,0:T(8,128)S(1)}, f32[512,128]{1,0:T(8,128)S(1)}, bf16[4,16,128]{2,1,0:T(8,128)(2,1)S(1)}, bf16[4,16,128]{2,1,0:T(8,128)(2,1)S(1)}) custom-call(s32[8,128]{1,0:T(8,128)S(1)} %get-tuple-element.52.plan, bf16[111,16,128]{2,1,0:T(8,128)(2,1)S(1)} %constant_dynamic-update-slice_fusion.refs_0_, ...), custom_call_target="tpu_custom_call" | custom-call | flops 553648128 | bytes 4194304 | tf_op jit(solution)/shard_map/outer_backward/pallas_call | solution.py:804
  22.1 2.3 %collective-permute-start.9 = (bf16[4,16,128]{2,1,0:T(8,128)(2,1)S(1)}, bf16[4,16,128]{2,1,0:T(8,128)(2,1)S(1)}, u32[]{:S(2)}, u32[]{:S(2)}) collective-permute-start(bf16[4,16,128]{2,1,0:T(8,128)(2,1)S(1)} %get-tuple-element.84), channel_id=1, source_target_pairs={{1,2},{2,1},{3,0},{0,3},{5,6},{6,5},{7,4},{4,7},{9,10},{10,9},{11,... | collective-permute-start | bytes 49160 | tf_op jit(solution)/shard_map/ppermute | solution.py:610
  24.4 2.3 %inner_backward.1.own = f32[4,128,128]{2,1,0:T(8,128)S(1)} custom-call(s32[8,128]{1,0:T(8,128)S(1)} %get-tuple-element.52.plan, s32[8,128]{1,0:T(8,128)S(1)} %get-tuple-element.88.table_rows, f32[512,128]{1,0:T(8,128)S(1)} %get-tuple-element.89.sens, bf16[111,16,128]{2,1,0:T(8,128)(2,1)S(1)} %constant_dynamic-update-slice_fusion.refs_0_, ...), custom_call_target="tpu_custom_call" | custom-call | flops 922746880 | bytes 4194304 | tf_op jit(solution)/shard_map/inner_backward/pallas_call | solution.py:828
  26.7 0.3 collective-permute-done.10.close
  27.0 0.7 %lon_back.1 = (f32[16,32,128]{2,1,0:T(8,128)S(1)}, bf16[16,32,128]{2,1,0:T(8,128)(2,1)S(1)}) custom-call(bf16[4,16,128]{2,1,0:T(8,128)(2,1)S(1)} %collective-permute-done.9.far, bf16[4,16,128]{2,1,0:T(8,128)(2,1)S(1)} %collective-permute-done.10.close, f32[4,128,128]{2,1,0:T(8,128)S(1)} %inner_backward.1.own, f32[4,24,128]{2,1,0:T(8,128)S(1)} %get-tuple-element.62.taps), custom_call_target="tpu_custom_call" | custom-call | flops 4325376 | bytes 524288 | tf_op jit(solution)/shard_map/lon_back/pallas_call | solution.py:846
  27.7 6.0 %collective-permute-start.11 = (bf16[16,32,128]{2,1,0:T(8,128)(2,1)S(1)}, bf16[16,32,128]{2,1,0:T(8,128)(2,1)S(1)}, u32[]{:S(2)}, u32[]{:S(2)}) collective-permute-start(bf16[16,32,128]{2,1,0:T(8,128)(2,1)S(1)} %get-tuple-element.94), channel_id=1, source_target_pairs={{4,8},{8,4},{12,16},{16,12},{20,24},{24,20},{5,9},{9,5},{13,17},{1... | collective-permute-start | bytes 393224 | tf_op jit(solution)/shard_map/ppermute | solution.py:610
  33.7 0.1 collective-permute-start.12
  33.8 0.3 lat_back_own.1.own_part
  34.1 3.6 %collective-permute-done.11.far = bf16[16,32,128]{2,1,0:T(8,128)(2,1)S(1)} collective-permute-done((bf16[16,32,128]{2,1,0:T(8,128)(2,1)S(1)}, bf16[16,32,128]{2,1,0:T(8,128)(2,1)S(1)}, u32[]{:S(2)}, u32[]{:S(2)}) %collective-permute-start.11) | collective-permute-done | bytes 131104 | tf_op jit(solution)/shard_map/ppermute | solution.py:610
  37.7 1.0 %lat_back.1 = f32[16,32,128]{2,1,0:T(8,128)} custom-call(bf16[16,32,128]{2,1,0:T(8,128)(2,1)S(1)} %collective-permute-done.11.far, bf16[16,32,128]{2,1,0:T(8,128)(2,1)S(1)} %collective-permute-done.12.close, f32[16,32,128]{2,1,0:T(8,128)S(1)} %lat_back_own.1.own_part), custom_call_target="tpu_custom_call" | custom-call | flops 2162688 | bytes 1048576 | tf_op jit(solution)/shard_map/lat_back/pallas_call | solution.py:866
  (15 shorter events, 0.1 us)
Async XLA Ops:
  1.1 8.5 %collective-permute-start.3 = (bf16[16,32,128]{2,1,0:T(8,128)(2,1)S(1)}, bf16[16,32,128]{2,1,0:T(8,128)(2,1)S(1)}, u32[]{:S(2)}, u32[]{:S(2)}) collective-permute-start(bf16[16,32,128]{2,1,0:T(8,128)(2,1)S(1)} %get-tuple-element.55), channel_id=1, source_target_pairs={{4,8},{8,4},{12,16},{16,12},{20,24},{24,20},{5,9},{9,5},{13,17},{1... | collective-permute-start | bytes 393224 | tf_op jit(solution)/shard_map/ppermute | solution.py:610
  5.6 4.0 %collective-permute-start.4 = (bf16[16,32,128]{2,1,0:T(8,128)(2,1)S(1)}, bf16[16,32,128]{2,1,0:T(8,128)(2,1)S(1)}, u32[]{:S(2)}, u32[]{:S(2)}) collective-permute-start(bf16[16,32,128]{2,1,0:T(8,128)(2,1)S(1)} %get-tuple-element.56), channel_id=1, source_target_pairs={{0,4},{4,0},{8,12},{12,8},{16,20},{20,16},{24,28},{28,24},{1,5},{5... | collective-permute-start | bytes 393224 | tf_op jit(solution)/shard_map/ppermute | solution.py:610
  5.7 10.4 %collective-permute-start = (bf16[37,16,128]{2,1,0:T(8,128)(2,1)S(1)}, bf16[37,16,128]{2,1,0:T(8,128)(2,1)S(1)}, u32[]{:S(2)}, u32[]{:S(2)}) collective-permute-start(bf16[37,16,128]{2,1,0:T(8,128)(2,1)S(1)} %get-tuple-element.64), channel_id=1, source_target_pairs={{0,16},{4,20},{8,24},{12,28},{16,0},{20,4},{24,8},{28,12},{1,17},{... | collective-permute-start | bytes 454664 | tf_op jit(solution)/shard_map/ppermute | solution.py:710
  7.0 9.1 %collective-permute-start.1 = (bf16[37,16,128]{2,1,0:T(8,128)(2,1)S(1)}, bf16[37,16,128]{2,1,0:T(8,128)(2,1)S(1)}, u32[]{:S(2)}, u32[]{:S(2)}) collective-permute-start(bf16[37,16,128]{2,1,0:T(8,128)(2,1)S(1)} %get-tuple-element.64), channel_id=1, source_target_pairs={{0,8},{4,12},{8,0},{12,4},{16,24},{20,28},{24,16},{28,20},{1,9},{5... | collective-permute-start | bytes 454664 | tf_op jit(solution)/shard_map/ppermute | solution.py:710
  7.1 9.0 %collective-permute-start.2 = (bf16[37,16,128]{2,1,0:T(8,128)(2,1)S(1)}, bf16[37,16,128]{2,1,0:T(8,128)(2,1)S(1)}, u32[]{:S(2)}, u32[]{:S(2)}) collective-permute-start(bf16[37,16,128]{2,1,0:T(8,128)(2,1)S(1)} %get-tuple-element.64), channel_id=1, source_target_pairs={{0,24},{4,28},{8,16},{12,20},{16,8},{20,12},{24,0},{28,4},{1,25},{... | collective-permute-start | bytes 454664 | tf_op jit(solution)/shard_map/ppermute | solution.py:710
  10.1 7.8 %collective-permute-start.7 = (f32[4,16,128]{2,1,0:T(8,128)S(1)}, f32[4,16,128]{2,1,0:T(8,128)S(1)}, u32[]{:S(2)}, u32[]{:S(2)}) collective-permute-start(f32[4,16,128]{2,1,0:T(8,128)S(1)} %get-tuple-element.71), channel_id=1, source_target_pairs={{1,2},{2,1},{3,0},{0,3},{5,6},{6,5},{7,4},{4,7},{9,10},{10,9},{11,... | collective-permute-start | bytes 98312 | tf_op jit(solution)/shard_map/ppermute | solution.py:610
  13.4 4.5 %collective-permute-start.8 = (f32[4,16,128]{2,1,0:T(8,128)S(1)}, f32[4,16,128]{2,1,0:T(8,128)S(1)}, u32[]{:S(2)}, u32[]{:S(2)}) collective-permute-start(f32[4,16,128]{2,1,0:T(8,128)S(1)} %get-tuple-element.73), channel_id=1, source_target_pairs={{0,1},{1,0},{2,3},{3,2},{4,5},{5,4},{6,7},{7,6},{8,9},{9,8},{10,11... | collective-permute-start | bytes 98312 | tf_op jit(solution)/shard_map/ppermute | solution.py:610
  16.2 3.4 %collective-permute-start.5 = (bf16[111,16,128]{2,1,0:T(8,128)(2,1)S(1)}, bf16[111,16,128]{2,1,0:T(8,128)(2,1)S(1)}, u32[]{:S(2)}, u32[]{:S(2)}) collective-permute-start(bf16[111,16,128]{2,1,0:T(8,128)(2,1)S(1)} %constant_dynamic-update-slice_fusion.refs_0_), channel_id=1, source_target_pairs={{0,4},{4,0},{8,12},{12,8},{16,20},{20,16},{24,28},{28,24},{1,5},{5... | collective-permute-start | bytes 1363976 | tf_op jit(solution)/shard_map/ppermute | solution.py:710
  17.8 1.8 %collective-permute-start.6 = (bf16[37,16,128]{2,1,0:T(8,128)(2,1)S(1)}, bf16[37,16,128]{2,1,0:T(8,128)(2,1)S(1)}, u32[]{:S(2)}, u32[]{:S(2)}) collective-permute-start(bf16[37,16,128]{2,1,0:T(8,128)(2,1)S(1)} %collective-permute-done.2.refs_1_), channel_id=1, source_target_pairs={{0,4},{4,0},{8,12},{12,8},{16,20},{20,16},{24,28},{28,24},{1,5},{5... | collective-permute-start | bytes 454664 | tf_op jit(solution)/shard_map/ppermute | solution.py:710
  22.1 4.6 %collective-permute-start.9 = (bf16[4,16,128]{2,1,0:T(8,128)(2,1)S(1)}, bf16[4,16,128]{2,1,0:T(8,128)(2,1)S(1)}, u32[]{:S(2)}, u32[]{:S(2)}) collective-permute-start(bf16[4,16,128]{2,1,0:T(8,128)(2,1)S(1)} %get-tuple-element.84), channel_id=1, source_target_pairs={{1,2},{2,1},{3,0},{0,3},{5,6},{6,5},{7,4},{4,7},{9,10},{10,9},{11,... | collective-permute-start | bytes 49160 | tf_op jit(solution)/shard_map/ppermute | solution.py:610
  24.4 2.6 %collective-permute-start.10 = (bf16[4,16,128]{2,1,0:T(8,128)(2,1)S(1)}, bf16[4,16,128]{2,1,0:T(8,128)(2,1)S(1)}, u32[]{:S(2)}, u32[]{:S(2)}) collective-permute-start(bf16[4,16,128]{2,1,0:T(8,128)(2,1)S(1)} %get-tuple-element.86), channel_id=1, source_target_pairs={{0,1},{1,0},{2,3},{3,2},{4,5},{5,4},{6,7},{7,6},{8,9},{9,8},{10,11... | collective-permute-start | bytes 49160 | tf_op jit(solution)/shard_map/ppermute | solution.py:610
  27.7 10.1 %collective-permute-start.11 = (bf16[16,32,128]{2,1,0:T(8,128)(2,1)S(1)}, bf16[16,32,128]{2,1,0:T(8,128)(2,1)S(1)}, u32[]{:S(2)}, u32[]{:S(2)}) collective-permute-start(bf16[16,32,128]{2,1,0:T(8,128)(2,1)S(1)} %get-tuple-element.94), channel_id=1, source_target_pairs={{4,8},{8,4},{12,16},{16,12},{20,24},{24,20},{5,9},{9,5},{13,17},{1... | collective-permute-start | bytes 393224 | tf_op jit(solution)/shard_map/ppermute | solution.py:610
  33.7 4.0 %collective-permute-start.12 = (bf16[16,32,128]{2,1,0:T(8,128)(2,1)S(1)}, bf16[16,32,128]{2,1,0:T(8,128)(2,1)S(1)}, u32[]{:S(2)}, u32[]{:S(2)}) collective-permute-start(bf16[16,32,128]{2,1,0:T(8,128)(2,1)S(1)} %get-tuple-element.94), channel_id=1, source_target_pairs={{0,4},{4,0},{8,12},{12,8},{16,20},{20,16},{24,28},{28,24},{1,5},{5... | collective-permute-start | bytes 393224 | tf_op jit(solution)/shard_map/ppermute | solution.py:610

commit v14 on v13

--- a/solution.py
+++ b/solution.py
@@ -775,7 +775,7 @@
         ),
     )
     inner_states, weights = rest[:3], rest[3:]
-    *near, _ = lax.optimization_barrier((*near, profile))
+    *near, far, close, profile = lax.optimization_barrier((*near, far, close, profile))
     for bit in others:
         near = [jnp.concatenate(near, axis=0)]
         near.append(swapped(near[0], 1 << bit))

time: 39.2 us -> 38.8 us (0.990)
  starting transfers between devices: 20.8 us -> 19.9 us
  waiting for transfers between devices: 3.95 us -> 4.45 us
    ppermute x4, starting transfers between devices: 16.2 us -> 14.7 us  [exchange(): lax.ppermute(to_far, axis, far)]
    ppermute x5, starting transfers between devices: 4.41 us -> 5.06 us  [swapped(): return lax.ppermute(part, 'lat', [(i, i ^ apart) for i in range(lat_count)])]
  transfers between devices with their start and end apart: 13 -> 13, of which waited for: 2 -> 3; matrix products, arithmetic and copies ran while one was open for 0% -> 0% of each run, Pallas kernels for 22% -> 22%
where the time goes in v14:
time: 38.8 us; the launch traced here: 38.5 us
  starting transfers between devices  19.9 us (51%)
  Pallas kernels  13.8 us (36%)
  waiting for transfers between devices  4.45 us (11%)
    ppermute x4, starting transfers between devices, exchange(): lax.ppermute(to_far, axis, far)  14.7 us
    ppermute x5, starting transfers between devices, swapped(): return lax.ppermute(part, 'lat', [(i, i ^ apart) for i in range(lat_count)])  5.06 us
    ppermute x4, waiting for transfers between devices, exchange(): lax.ppermute(to_far, axis, far)  3.82 us
    pallas_call x1, Pallas kernels, shards(): call(functools.partial(inner_forward_kernel, per_tile, outer_slots), (sha...  2.63 us
    pallas_call x1, Pallas kernels, shards(): call(functools.partial(outer_backward_kernel, per_tile, len(slabs), recv_...  2.43 us
    pallas_call x1, Pallas kernels, shards(): call(functools.partial(inner_backward_kernel, per_tile, len(slabs), outer...  2.28 us
    pallas_call x1, Pallas kernels, shards(): call(functools.partial(outer_forward_kernel, per_tile), state_shapes(oute...  1.72 us
    pallas_call x1, Pallas kernels, shards(): call(prepare_kernel, (shape((tiles, 24, LANES), f32), shape((tiles, width...  1.16 us
  transfers between devices with their start and end apart: 13, of which 3 were waited for; matrix products, arithmetic and copies ran while one was open for 0% of the time, Pallas kernels for 22%

profile of v14, /device:TPU:1, one launch (start us, length us, event | category | flops | bytes accessed | tf_op | source)
XLA Modules:
  0.0 38.5 jit_solution(14557865227981509845)
XLA Ops:
  0.0 1.1 %slabs_halves.1 = (bf16[37,16,128]{2,1,0:T(8,128)(2,1)S(1)}, bf16[16,32,128]{2,1,0:T(8,128)(2,1)S(1)}, bf16[16,32,128]{2,1,0:T(8,128)(2,1)S(1)}, f32[16,32,128]{2,1,0:T(8,128)S(1)}) custom-call(bf16[36,16,128]{2,1,0:T(8,128)(2,1)} %bitcast.13, s32[1,64]{1,0:T(1,128)} %bitcast.14, s32[1,36]{1,0:T(1,128)} %bitcast.16, f32[16,32,128]{2,1,0:T(8,128)} %control.1), custom_call_target="tpu_custom_call" | custom-call | bytes 1310720 | tf_op jit(solution)/shard_map/slabs_halves/pallas_call | solution.py:648
  1.1 4.5 %collective-permute-start.3 = (bf16[16,32,128]{2,1,0:T(8,128)(2,1)S(1)}, bf16[16,32,128]{2,1,0:T(8,128)(2,1)S(1)}, u32[]{:S(2)}, u32[]{:S(2)}) collective-permute-start(bf16[16,32,128]{2,1,0:T(8,128)(2,1)S(1)} %get-tuple-element.58), channel_id=1, source_target_pairs={{4,8},{8,4},{12,16},{16,12},{20,24},{24,20},{5,9},{9,5},{13,17},{1... | collective-permute-start | bytes 393224 | tf_op jit(solution)/shard_map/ppermute | solution.py:610
  5.6 0.1 collective-permute-start.4
  5.7 1.3 %collective-permute-start = (bf16[37,16,128]{2,1,0:T(8,128)(2,1)S(1)}, bf16[37,16,128]{2,1,0:T(8,128)(2,1)S(1)}, u32[]{:S(2)}, u32[]{:S(2)}) collective-permute-start(bf16[37,16,128]{2,1,0:T(8,128)(2,1)S(1)} %get-tuple-element.71), channel_id=1, source_target_pairs={{0,16},{4,20},{8,24},{12,28},{16,0},{20,4},{24,8},{28,12},{1,17},{... | collective-permute-start | bytes 454664 | tf_op jit(solution)/shard_map/ppermute | solution.py:710
  7.0 0.1 collective-permute-start.1
  7.1 1.3 %collective-permute-start.2 = (bf16[37,16,128]{2,1,0:T(8,128)(2,1)S(1)}, bf16[37,16,128]{2,1,0:T(8,128)(2,1)S(1)}, u32[]{:S(2)}, u32[]{:S(2)}) collective-permute-start(bf16[37,16,128]{2,1,0:T(8,128)(2,1)S(1)} %get-tuple-element.71), channel_id=1, source_target_pairs={{0,24},{4,28},{8,16},{12,20},{16,8},{20,12},{24,0},{28,4},{1,25},{... | collective-permute-start | bytes 454664 | tf_op jit(solution)/shard_map/ppermute | solution.py:710
  8.4 1.2 %taps_background.1 = (f32[4,24,128]{2,1,0:T(8,128)S(1)}, f32[4,128,128]{2,1,0:T(8,128)S(1)}, s32[8,128]{1,0:T(8,128)S(1)}, f32[16,32,128]{2,1,0:T(8,128)S(1)}) custom-call(s32[16]{0:T(128)} %lon_width.1, s32[1,64]{1,0:T(1,128)} %bitcast.17, s32[1,64]{1,0:T(1,128)} %bitcast.15, f32[16,32,128]{2,1,0:T(8,128)} %background.1, ...), custom_call_target="tpu_custom_call" | custom-call | flops 2162688 | bytes 786432 | tf_op jit(solution)/shard_map/taps_background/pallas_call | solution.py:679
  9.6 0.4 %lat_smooth.1 = (f32[4,128,128]{2,1,0:T(8,128)S(1)}, f32[4,16,128]{2,1,0:T(8,128)S(1)}, f32[4,16,128]{2,1,0:T(8,128)S(1)}) custom-call(bf16[16,32,128]{2,1,0:T(8,128)(2,1)S(1)} %collective-permute-done.3.far, bf16[16,32,128]{2,1,0:T(8,128)(2,1)S(1)} %collective-permute-done.4.close, f32[16,32,128]{2,1,0:T(8,128)S(1)} %get-tuple-element.62.own_part), custom_call_target="tpu_custom_call" | custom-call | flops 276824064 | bytes 67108864 | tf_op jit(solution)/shard_map/lat_smooth/pallas_call | solution.py:716
  10.1 3.4 %collective-permute-start.5 = (f32[4,16,128]{2,1,0:T(8,128)S(1)}, f32[4,16,128]{2,1,0:T(8,128)S(1)}, u32[]{:S(2)}, u32[]{:S(2)}) collective-permute-start(f32[4,16,128]{2,1,0:T(8,128)S(1)} %get-tuple-element.63), channel_id=1, source_target_pairs={{1,2},{2,1},{3,0},{0,3},{5,6},{6,5},{7,4},{4,7},{9,10},{10,9},{11,... | collective-permute-start | bytes 98312 | tf_op jit(solution)/shard_map/ppermute | solution.py:610
  13.4 2.6 %inner_forward.1 = (f32[512,128]{1,0:T(8,128)S(1)}, bf16[320,1024]{1,0:T(8,128)(2,1)S(1)}, bf16[320,1024]{1,0:T(8,128)(2,1)S(1)}, f32[320,256]{1,0:T(8,128)S(1)}...) custom-call(s32[8,128]{1,0:T(8,128)S(1)} %get-tuple-element.55.plan,, ...), custom_call_target="tpu_custom_call" | custom-call | flops 9227468800 | bytes 41943040 | tf_op jit(solution)/shard_map/inner_forward/pallas_call | solution.py:740
  16.1 0.6 %collective-permute-done.6.close = f32[4,16,128]{2,1,0:T(8,128)S(1)} collective-permute-done((f32[4,16,128]{2,1,0:T(8,128)S(1)}, f32[4,16,128]{2,1,0:T(8,128)S(1)}, u32[]{:S(2)}, u32[]{:S(2)}) %collective-permute-start.6) | collective-permute-done | bytes 32800 | tf_op jit(solution)/shard_map/ppermute | solution.py:610
  16.8 2.3 %collective-permute-start.7 = (bf16[111,16,128]{2,1,0:T(8,128)(2,1)S(1)}, bf16[111,16,128]{2,1,0:T(8,128)(2,1)S(1)}, u32[]{:S(2)}, u32[]{:S(2)}) collective-permute-start(bf16[111,16,128]{2,1,0:T(8,128)(2,1)S(1)} %constant_dynamic-update-slice_fusion.refs_0_), channel_id=1, source_target_pairs={{0,4},{4,0},{8,12},{12,8},{16,20},{20,16},{24,28},{28,24},{1,5},{5... | collective-permute-start | bytes 1363976 | tf_op jit(solution)/shard_map/ppermute | solution.py:710
  19.1 0.1 collective-permute-start.8
  19.1 1.7 %outer_forward.1 = (bf16[192,1024]{1,0:T(8,128)(2,1)S(1)}, bf16[192,1024]{1,0:T(8,128)(2,1)S(1)}, f32[192,256]{1,0:T(8,128)S(1)}, bf16[320,1024]{1,0:T(8,128)(2,...) custom-call(s32[8,128]{1,0:T(8,128)S(1)} %get-tuple-element.55.plan, ...), custom_call_target="tpu_custom_call" | custom-call | flops 5536481280 | bytes 41943040 | tf_op jit(solution)/shard_map/outer_forward/pallas_call | solution.py:785
  20.9 2.4 %outer_backward.1 = (s32[8,128]{1,0:T(8,128)S(1)}, f32[512,128]{1,0:T(8,128)S(1)}, bf16[4,16,128]{2,1,0:T(8,128)(2,1)S(1)}, bf16[4,16,128]{2,1,0:T(8,128)(2,1)S(1)}) custom-call(s32[8,128]{1,0:T(8,128)S(1)} %get-tuple-element.55.plan, bf16[111,16,128]{2,1,0:T(8,128)(2,1)S(1)} %constant_dynamic-update-slice_fusion.refs_0_, ...), custom_call_target="tpu_custom_call" | custom-call | flops 553648128 | bytes 4194304 | tf_op jit(solution)/shard_map/outer_backward/pallas_call | solution.py:804
  23.3 1.6 %collective-permute-start.9 = (bf16[4,16,128]{2,1,0:T(8,128)(2,1)S(1)}, bf16[4,16,128]{2,1,0:T(8,128)(2,1)S(1)}, u32[]{:S(2)}, u32[]{:S(2)}) collective-permute-start(bf16[4,16,128]{2,1,0:T(8,128)(2,1)S(1)} %get-tuple-element.90), channel_id=1, source_target_pairs={{1,2},{2,1},{3,0},{0,3},{5,6},{6,5},{7,4},{4,7},{9,10},{10,9},{11,... | collective-permute-start | bytes 49160 | tf_op jit(solution)/shard_map/ppermute | solution.py:610
  24.9 2.3 %inner_backward.1.own = f32[4,128,128]{2,1,0:T(8,128)S(1)} custom-call(s32[8,128]{1,0:T(8,128)S(1)} %get-tuple-element.55.plan, s32[8,128]{1,0:T(8,128)S(1)} %get-tuple-element.94.table_rows, f32[512,128]{1,0:T(8,128)S(1)} %get-tuple-element.95.sens, bf16[111,16,128]{2,1,0:T(8,128)(2,1)S(1)} %constant_dynamic-update-slice_fusion.refs_0_, ...), custom_call_target="tpu_custom_call" | custom-call | flops 922746880 | bytes 4194304 | tf_op jit(solution)/shard_map/inner_backward/pallas_call | solution.py:828
  27.2 0.6 %collective-permute-done.9.far = bf16[4,16,128]{2,1,0:T(8,128)(2,1)S(1)} collective-permute-done((bf16[4,16,128]{2,1,0:T(8,128)(2,1)S(1)}, bf16[4,16,128]{2,1,0:T(8,128)(2,1)S(1)}, u32[]{:S(2)}, u32[]{:S(2)}) %collective-permute-start.9) | collective-permute-done | bytes 16416 | tf_op jit(solution)/shard_map/ppermute | solution.py:610
  27.8 0.7 %lon_back.1 = (f32[16,32,128]{2,1,0:T(8,128)S(1)}, bf16[16,32,128]{2,1,0:T(8,128)(2,1)S(1)}) custom-call(bf16[4,16,128]{2,1,0:T(8,128)(2,1)S(1)} %collective-permute-done.9.far, bf16[4,16,128]{2,1,0:T(8,128)(2,1)S(1)} %collective-permute-done.10.close, f32[4,128,128]{2,1,0:T(8,128)S(1)} %inner_backward.1.own, f32[4,24,128]{2,1,0:T(8,128)S(1)} %get-tuple-element.69.taps), custom_call_target="tpu_custom_call" | custom-call | flops 4325376 | bytes 524288 | tf_op jit(solution)/shard_map/lon_back/pallas_call | solution.py:846
  28.5 5.2 %collective-permute-start.11 = (bf16[16,32,128]{2,1,0:T(8,128)(2,1)S(1)}, bf16[16,32,128]{2,1,0:T(8,128)(2,1)S(1)}, u32[]{:S(2)}, u32[]{:S(2)}) collective-permute-start(bf16[16,32,128]{2,1,0:T(8,128)(2,1)S(1)} %get-tuple-element.100), channel_id=1, source_target_pairs={{4,8},{8,4},{12,16},{16,12},{20,24},{24,20},{5,9},{9,5},{13,17},{1... | collective-permute-start | bytes 393224 | tf_op jit(solution)/shard_map/ppermute | solution.py:610
  33.7 0.1 collective-permute-start.12
  33.8 0.3 lat_back_own.1.own_part
  34.1 3.2 %collective-permute-done.11.far = bf16[16,32,128]{2,1,0:T(8,128)(2,1)S(1)} collective-permute-done((bf16[16,32,128]{2,1,0:T(8,128)(2,1)S(1)}, bf16[16,32,128]{2,1,0:T(8,128)(2,1)S(1)}, u32[]{:S(2)}, u32[]{:S(2)}) %collective-permute-start.11) | collective-permute-done | bytes 131104 | tf_op jit(solution)/shard_map/ppermute | solution.py:610
  37.4 1.0 %lat_back.1 = f32[16,32,128]{2,1,0:T(8,128)} custom-call(bf16[16,32,128]{2,1,0:T(8,128)(2,1)S(1)} %collective-permute-done.11.far, bf16[16,32,128]{2,1,0:T(8,128)(2,1)S(1)} %collective-permute-done.12.close, f32[16,32,128]{2,1,0:T(8,128)S(1)} %lat_back_own.1.own_part), custom_call_target="tpu_custom_call" | custom-call | flops 2162688 | bytes 1048576 | tf_op jit(solution)/shard_map/lat_back/pallas_call | solution.py:866
  (15 shorter events, 0.1 us)
Async XLA Ops:
  1.1 8.5 %collective-permute-start.3 = (bf16[16,32,128]{2,1,0:T(8,128)(2,1)S(1)}, bf16[16,32,128]{2,1,0:T(8,128)(2,1)S(1)}, u32[]{:S(2)}, u32[]{:S(2)}) collective-permute-start(bf16[16,32,128]{2,1,0:T(8,128)(2,1)S(1)} %get-tuple-element.58), channel_id=1, source_target_pairs={{4,8},{8,4},{12,16},{16,12},{20,24},{24,20},{5,9},{9,5},{13,17},{1... | collective-permute-start | bytes 393224 | tf_op jit(solution)/shard_map/ppermute | solution.py:610
  5.6 4.0 %collective-permute-start.4 = (bf16[16,32,128]{2,1,0:T(8,128)(2,1)S(1)}, bf16[16,32,128]{2,1,0:T(8,128)(2,1)S(1)}, u32[]{:S(2)}, u32[]{:S(2)}) collective-permute-start(bf16[16,32,128]{2,1,0:T(8,128)(2,1)S(1)} %get-tuple-element.59), channel_id=1, source_target_pairs={{0,4},{4,0},{8,12},{12,8},{16,20},{20,16},{24,28},{28,24},{1,5},{5... | collective-permute-start | bytes 393224 | tf_op jit(solution)/shard_map/ppermute | solution.py:610
  5.7 11.0 %collective-permute-start = (bf16[37,16,128]{2,1,0:T(8,128)(2,1)S(1)}, bf16[37,16,128]{2,1,0:T(8,128)(2,1)S(1)}, u32[]{:S(2)}, u32[]{:S(2)}) collective-permute-start(bf16[37,16,128]{2,1,0:T(8,128)(2,1)S(1)} %get-tuple-element.71), channel_id=1, source_target_pairs={{0,16},{4,20},{8,24},{12,28},{16,0},{20,4},{24,8},{28,12},{1,17},{... | collective-permute-start | bytes 454664 | tf_op jit(solution)/shard_map/ppermute | solution.py:710
  7.0 9.7 %collective-permute-start.1 = (bf16[37,16,128]{2,1,0:T(8,128)(2,1)S(1)}, bf16[37,16,128]{2,1,0:T(8,128)(2,1)S(1)}, u32[]{:S(2)}, u32[]{:S(2)}) collective-permute-start(bf16[37,16,128]{2,1,0:T(8,128)(2,1)S(1)} %get-tuple-element.71), channel_id=1, source_target_pairs={{0,8},{4,12},{8,0},{12,4},{16,24},{20,28},{24,16},{28,20},{1,9},{5... | collective-permute-start | bytes 454664 | tf_op jit(solution)/shard_map/ppermute | solution.py:710
  7.1 9.6 %collective-permute-start.2 = (bf16[37,16,128]{2,1,0:T(8,128)(2,1)S(1)}, bf16[37,16,128]{2,1,0:T(8,128)(2,1)S(1)}, u32[]{:S(2)}, u32[]{:S(2)}) collective-permute-start(bf16[37,16,128]{2,1,0:T(8,128)(2,1)S(1)} %get-tuple-element.71), channel_id=1, source_target_pairs={{0,24},{4,28},{8,16},{12,20},{16,8},{20,12},{24,0},{28,4},{1,25},{... | collective-permute-start | bytes 454664 | tf_op jit(solution)/shard_map/ppermute | solution.py:710
  10.1 6.0 %collective-permute-start.5 = (f32[4,16,128]{2,1,0:T(8,128)S(1)}, f32[4,16,128]{2,1,0:T(8,128)S(1)}, u32[]{:S(2)}, u32[]{:S(2)}) collective-permute-start(f32[4,16,128]{2,1,0:T(8,128)S(1)} %get-tuple-element.63), channel_id=1, source_target_pairs={{1,2},{2,1},{3,0},{0,3},{5,6},{6,5},{7,4},{4,7},{9,10},{10,9},{11,... | collective-permute-start | bytes 98312 | tf_op jit(solution)/shard_map/ppermute | solution.py:610
  13.4 3.3 %collective-permute-start.6 = (f32[4,16,128]{2,1,0:T(8,128)S(1)}, f32[4,16,128]{2,1,0:T(8,128)S(1)}, u32[]{:S(2)}, u32[]{:S(2)}) collective-permute-start(f32[4,16,128]{2,1,0:T(8,128)S(1)} %get-tuple-element.65), channel_id=1, source_target_pairs={{0,1},{1,0},{2,3},{3,2},{4,5},{5,4},{6,7},{7,6},{8,9},{9,8},{10,11... | collective-permute-start | bytes 98312 | tf_op jit(solution)/shard_map/ppermute | solution.py:610
  16.8 4.1 %collective-permute-start.7 = (bf16[111,16,128]{2,1,0:T(8,128)(2,1)S(1)}, bf16[111,16,128]{2,1,0:T(8,128)(2,1)S(1)}, u32[]{:S(2)}, u32[]{:S(2)}) collective-permute-start(bf16[111,16,128]{2,1,0:T(8,128)(2,1)S(1)} %constant_dynamic-update-slice_fusion.refs_0_), channel_id=1, source_target_pairs={{0,4},{4,0},{8,12},{12,8},{16,20},{20,16},{24,28},{28,24},{1,5},{5... | collective-permute-start | bytes 1363976 | tf_op jit(solution)/shard_map/ppermute | solution.py:710
  19.1 1.8 %collective-permute-start.8 = (bf16[37,16,128]{2,1,0:T(8,128)(2,1)S(1)}, bf16[37,16,128]{2,1,0:T(8,128)(2,1)S(1)}, u32[]{:S(2)}, u32[]{:S(2)}) collective-permute-start(bf16[37,16,128]{2,1,0:T(8,128)(2,1)S(1)} %collective-permute-done.2.refs_1_), channel_id=1, source_target_pairs={{0,4},{4,0},{8,12},{12,8},{16,20},{20,16},{24,28},{28,24},{1,5},{5... | collective-permute-start | bytes 454664 | tf_op jit(solution)/shard_map/ppermute | solution.py:710
  23.3 4.5 %collective-permute-start.9 = (bf16[4,16,128]{2,1,0:T(8,128)(2,1)S(1)}, bf16[4,16,128]{2,1,0:T(8,128)(2,1)S(1)}, u32[]{:S(2)}, u32[]{:S(2)}) collective-permute-start(bf16[4,16,128]{2,1,0:T(8,128)(2,1)S(1)} %get-tuple-element.90), channel_id=1, source_target_pairs={{1,2},{2,1},{3,0},{0,3},{5,6},{6,5},{7,4},{4,7},{9,10},{10,9},{11,... | collective-permute-start | bytes 49160 | tf_op jit(solution)/shard_map/ppermute | solution.py:610
  24.9 2.9 %collective-permute-start.10 = (bf16[4,16,128]{2,1,0:T(8,128)(2,1)S(1)}, bf16[4,16,128]{2,1,0:T(8,128)(2,1)S(1)}, u32[]{:S(2)}, u32[]{:S(2)}) collective-permute-start(bf16[4,16,128]{2,1,0:T(8,128)(2,1)S(1)} %get-tuple-element.92), channel_id=1, source_target_pairs={{0,1},{1,0},{2,3},{3,2},{4,5},{5,4},{6,7},{7,6},{8,9},{9,8},{10,11... | collective-permute-start | bytes 49160 | tf_op jit(solution)/shard_map/ppermute | solution.py:610
  28.5 8.8 %collective-permute-start.11 = (bf16[16,32,128]{2,1,0:T(8,128)(2,1)S(1)}, bf16[16,32,128]{2,1,0:T(8,128)(2,1)S(1)}, u32[]{:S(2)}, u32[]{:S(2)}) collective-permute-start(bf16[16,32,128]{2,1,0:T(8,128)(2,1)S(1)} %get-tuple-element.100), channel_id=1, source_target_pairs={{4,8},{8,4},{12,16},{16,12},{20,24},{24,20},{5,9},{9,5},{13,17},{1... | collective-permute-start | bytes 393224 | tf_op jit(solution)/shard_map/ppermute | solution.py:610
  33.7 3.6 %collective-permute-start.12 = (bf16[16,32,128]{2,1,0:T(8,128)(2,1)S(1)}, bf16[16,32,128]{2,1,0:T(8,128)(2,1)S(1)}, u32[]{:S(2)}, u32[]{:S(2)}) collective-permute-start(bf16[16,32,128]{2,1,0:T(8,128)(2,1)S(1)} %get-tuple-element.100), channel_id=1, source_target_pairs={{0,4},{4,0},{8,12},{12,8},{16,20},{20,16},{24,28},{28,24},{1,5},{5... | collective-permute-start | bytes 393224 | tf_op jit(solution)/shard_map/ppermute | solution.py:610

commit v15 on v13

--- a/solution.py
+++ b/solution.py
@@ -673,7 +673,18 @@
             control,
         )
     )
+    lat_count = lax.axis_size("lat")
+    one, two, *others = swap_bits(lat_count)
+
+    def swapped(part, apart):
+        return lax.ppermute(part, "lat", [(i, i ^ apart) for i in range(lat_count)])
+
+    second = swapped(slabs, 1 << two)
     far, close, sent = exchange(to_far, to_close, "lat", False)
+    second, far, close = lax.optimization_barrier((second, far, close))
+    later, _ = lax.optimization_barrier((slabs, sent))
+    near = [slabs, swapped(later, 1 << one), second, swapped(later, (1 << one) + (1 << two))]
+
 
     band = pltpu.VMEM((height, levels, width), f32)
     taps, turned, plan, own_part = call(
@@ -702,15 +713,6 @@
         ),
         held,
     )
-
-    lat_count = lax.axis_size("lat")
-    one, two, *others = swap_bits(lat_count)
-
-    def swapped(part, apart):
-        return lax.ppermute(part, "lat", [(i, i ^ apart) for i in range(lat_count)])
-
-    later, _ = lax.optimization_barrier((slabs, sent))
-    near = [slabs, swapped(later, 1 << one), swapped(later, 1 << two), swapped(slabs, (1 << one) + (1 << two))]
 
     halos = pltpu.VMEM((2, REACH, levels, width), f32)
     smoothed, to_far, to_close = call(

time: 39.2 us -> 39 us (level)
    ppermute x4, starting transfers between devices: 16.2 us -> 12.6 us  [exchange(): lax.ppermute(to_far, axis, far)]
    ppermute x5, starting transfers between devices: 4.41 us -> 7.45 us  [swapped(): return lax.ppermute(part, 'lat', [(i, i ^ apart) for i in range(lat_count)])]
    ppermute x4, starting transfers between devices: 0.15 us -> 0.91 us  [exchange(): lax.ppermute(to_close, axis, close)]
where the time goes in v15:
time: 39 us; the launch traced here: 38.8 us
  starting transfers between devices  20.9 us (54%)
  Pallas kernels  13.8 us (35%)
  waiting for transfers between devices  3.64 us (9%)
    ppermute x4, starting transfers between devices, exchange(): lax.ppermute(to_far, axis, far)  12.6 us
    ppermute x5, starting transfers between devices, swapped(): return lax.ppermute(part, 'lat', [(i, i ^ apart) for i in range(lat_count)])  7.45 us
    ppermute x4, waiting for transfers between devices, exchange(): lax.ppermute(to_far, axis, far)  3.62 us
    pallas_call x1, Pallas kernels, shards(): call(functools.partial(inner_forward_kernel, per_tile, outer_slots), (sha...  2.63 us
    pallas_call x1, Pallas kernels, shards(): call(functools.partial(outer_backward_kernel, per_tile, len(slabs), recv_...  2.43 us
    pallas_call x1, Pallas kernels, shards(): call(functools.partial(inner_backward_kernel, per_tile, len(slabs), outer...  2.28 us
    pallas_call x1, Pallas kernels, shards(): call(functools.partial(outer_forward_kernel, per_tile), state_shapes(oute...  1.72 us
    pallas_call x1, Pallas kernels, shards(): call(prepare_kernel, (shape((tiles, 24, LANES), f32), shape((tiles, width...  1.16 us
  transfers between devices with their start and end apart: 13, of which 2 were waited for; matrix products, arithmetic and copies ran while one was open for 0% of the time, Pallas kernels for 22%

profile of v15, /device:TPU:1, one launch (start us, length us, event | category | flops | bytes accessed | tf_op | source)
XLA Modules:
  0.0 38.8 jit_solution(5849368210952784747)
XLA Ops:
  0.0 1.1 %slabs_halves.1 = (bf16[37,16,128]{2,1,0:T(8,128)(2,1)S(1)}, bf16[16,32,128]{2,1,0:T(8,128)(2,1)S(1)}, bf16[16,32,128]{2,1,0:T(8,128)(2,1)S(1)}, f32[16,32,128]{2,1,0:T(8,128)S(1)}) custom-call(bf16[36,16,128]{2,1,0:T(8,128)(2,1)} %bitcast.13, s32[1,64]{1,0:T(1,128)} %bitcast.14, s32[1,36]{1,0:T(1,128)} %bitcast.16, f32[16,32,128]{2,1,0:T(8,128)} %control.1), custom_call_target="tpu_custom_call" | custom-call | bytes 1310720 | tf_op jit(solution)/shard_map/slabs_halves/pallas_call | solution.py:648
  1.1 2.1 %collective-permute-start.1 = (bf16[37,16,128]{2,1,0:T(8,128)(2,1)S(1)}, bf16[37,16,128]{2,1,0:T(8,128)(2,1)S(1)}, u32[]{:S(2)}, u32[]{:S(2)}) collective-permute-start(bf16[37,16,128]{2,1,0:T(8,128)(2,1)S(1)} %get-tuple-element.70), channel_id=1, source_target_pairs={{0,8},{4,12},{8,0},{12,4},{16,24},{20,28},{24,16},{28,20},{1,9},{5... | collective-permute-start | bytes 454664 | tf_op jit(solution)/shard_map/ppermute | solution.py:680
  3.2 2.5 %collective-permute-start.2 = (bf16[16,32,128]{2,1,0:T(8,128)(2,1)S(1)}, bf16[16,32,128]{2,1,0:T(8,128)(2,1)S(1)}, u32[]{:S(2)}, u32[]{:S(2)}) collective-permute-start(bf16[16,32,128]{2,1,0:T(8,128)(2,1)S(1)} %get-tuple-element.58), channel_id=1, source_target_pairs={{4,8},{8,4},{12,16},{16,12},{20,24},{24,20},{5,9},{9,5},{13,17},{1... | collective-permute-start | bytes 393224 | tf_op jit(solution)/shard_map/ppermute | solution.py:610
  5.7 0.1 collective-permute-start.3
  5.8 1.8 %collective-permute-start = (bf16[37,16,128]{2,1,0:T(8,128)(2,1)S(1)}, bf16[37,16,128]{2,1,0:T(8,128)(2,1)S(1)}, u32[]{:S(2)}, u32[]{:S(2)}) collective-permute-start(bf16[37,16,128]{2,1,0:T(8,128)(2,1)S(1)} %get-tuple-element.70), channel_id=1, source_target_pairs={{0,16},{4,20},{8,24},{12,28},{16,0},{20,4},{24,8},{28,12},{1,17},{... | collective-permute-start | bytes 454664 | tf_op jit(solution)/shard_map/ppermute | solution.py:680
  7.6 2.1 %collective-permute-start.4 = (bf16[37,16,128]{2,1,0:T(8,128)(2,1)S(1)}, bf16[37,16,128]{2,1,0:T(8,128)(2,1)S(1)}, u32[]{:S(2)}, u32[]{:S(2)}) collective-permute-start(bf16[37,16,128]{2,1,0:T(8,128)(2,1)S(1)} %get-tuple-element.70), channel_id=1, source_target_pairs={{0,24},{4,28},{8,16},{12,20},{16,8},{20,12},{24,0},{28,4},{1,25},{... | collective-permute-start | bytes 454664 | tf_op jit(solution)/shard_map/ppermute | solution.py:680
  9.7 1.2 %taps_background.1 = (f32[4,24,128]{2,1,0:T(8,128)S(1)}, f32[4,128,128]{2,1,0:T(8,128)S(1)}, s32[8,128]{1,0:T(8,128)S(1)}, f32[16,32,128]{2,1,0:T(8,128)S(1)}) custom-call(s32[16]{0:T(128)} %lon_width.1, s32[1,64]{1,0:T(1,128)} %bitcast.17, s32[1,64]{1,0:T(1,128)} %bitcast.15, f32[16,32,128]{2,1,0:T(8,128)} %background.1, ...), custom_call_target="tpu_custom_call" | custom-call | flops 2162688 | bytes 786432 | tf_op jit(solution)/shard_map/taps_background/pallas_call | solution.py:690
  10.9 0.4 %lat_smooth.1 = (f32[4,128,128]{2,1,0:T(8,128)S(1)}, f32[4,16,128]{2,1,0:T(8,128)S(1)}, f32[4,16,128]{2,1,0:T(8,128)S(1)}) custom-call(bf16[16,32,128]{2,1,0:T(8,128)(2,1)S(1)} %collective-permute-done.2.far, bf16[16,32,128]{2,1,0:T(8,128)(2,1)S(1)} %collective-permute-done.3.close, f32[16,32,128]{2,1,0:T(8,128)S(1)} %get-tuple-element.65.own_part), custom_call_target="tpu_custom_call" | custom-call | flops 276824064 | bytes 67108864 | tf_op jit(solution)/shard_map/lat_smooth/pallas_call | solution.py:718
  11.4 3.4 %collective-permute-start.7 = (f32[4,16,128]{2,1,0:T(8,128)S(1)}, f32[4,16,128]{2,1,0:T(8,128)S(1)}, u32[]{:S(2)}, u32[]{:S(2)}) collective-permute-start(f32[4,16,128]{2,1,0:T(8,128)S(1)} %get-tuple-element.77), channel_id=1, source_target_pairs={{1,2},{2,1},{3,0},{0,3},{5,6},{6,5},{7,4},{4,7},{9,10},{10,9},{11,... | collective-permute-start | bytes 98312 | tf_op jit(solution)/shard_map/ppermute | solution.py:610
  14.7 2.6 %inner_forward.1 = (f32[512,128]{1,0:T(8,128)S(1)}, bf16[320,1024]{1,0:T(8,128)(2,1)S(1)}, bf16[320,1024]{1,0:T(8,128)(2,1)S(1)}, f32[320,256]{1,0:T(8,128)S(1)}...) custom-call(s32[8,128]{1,0:T(8,128)S(1)} %get-tuple-element.55.plan,, ...), custom_call_target="tpu_custom_call" | custom-call | flops 9227468800 | bytes 41943040 | tf_op jit(solution)/shard_map/inner_forward/pallas_call | solution.py:742
  17.5 1.3 %collective-permute-start.5 = (bf16[111,16,128]{2,1,0:T(8,128)(2,1)S(1)}, bf16[111,16,128]{2,1,0:T(8,128)(2,1)S(1)}, u32[]{:S(2)}, u32[]{:S(2)}) collective-permute-start(bf16[111,16,128]{2,1,0:T(8,128)(2,1)S(1)} %constant_dynamic-update-slice_fusion.refs_0_), channel_id=1, source_target_pairs={{0,4},{4,0},{8,12},{12,8},{16,20},{20,16},{24,28},{28,24},{1,5},{5... | collective-permute-start | bytes 1363976 | tf_op jit(solution)/shard_map/ppermute | solution.py:680
  18.8 0.1 collective-permute-start.6
  18.9 1.7 %outer_forward.1 = (bf16[192,1024]{1,0:T(8,128)(2,1)S(1)}, bf16[192,1024]{1,0:T(8,128)(2,1)S(1)}, f32[192,256]{1,0:T(8,128)S(1)}, bf16[320,1024]{1,0:T(8,128)(2,...) custom-call(s32[8,128]{1,0:T(8,128)S(1)} %get-tuple-element.55.plan, ...), custom_call_target="tpu_custom_call" | custom-call | flops 5536481280 | bytes 41943040 | tf_op jit(solution)/shard_map/outer_forward/pallas_call | solution.py:787
  20.7 2.4 %outer_backward.1 = (s32[8,128]{1,0:T(8,128)S(1)}, f32[512,128]{1,0:T(8,128)S(1)}, bf16[4,16,128]{2,1,0:T(8,128)(2,1)S(1)}, bf16[4,16,128]{2,1,0:T(8,128)(2,1)S(1)}) custom-call(s32[8,128]{1,0:T(8,128)S(1)} %get-tuple-element.55.plan, bf16[111,16,128]{2,1,0:T(8,128)(2,1)S(1)} %constant_dynamic-update-slice_fusion.refs_0_, ...), custom_call_target="tpu_custom_call" | custom-call | flops 553648128 | bytes 4194304 | tf_op jit(solution)/shard_map/outer_backward/pallas_call | solution.py:806
  23.1 1.1 %collective-permute-start.9 = (bf16[4,16,128]{2,1,0:T(8,128)(2,1)S(1)}, bf16[4,16,128]{2,1,0:T(8,128)(2,1)S(1)}, u32[]{:S(2)}, u32[]{:S(2)}) collective-permute-start(bf16[4,16,128]{2,1,0:T(8,128)(2,1)S(1)} %get-tuple-element.90), channel_id=1, source_target_pairs={{1,2},{2,1},{3,0},{0,3},{5,6},{6,5},{7,4},{4,7},{9,10},{10,9},{11,... | collective-permute-start | bytes 49160 | tf_op jit(solution)/shard_map/ppermute | solution.py:610
  24.2 0.8 %collective-permute-start.10 = (bf16[4,16,128]{2,1,0:T(8,128)(2,1)S(1)}, bf16[4,16,128]{2,1,0:T(8,128)(2,1)S(1)}, u32[]{:S(2)}, u32[]{:S(2)}) collective-permute-start(bf16[4,16,128]{2,1,0:T(8,128)(2,1)S(1)} %get-tuple-element.92), channel_id=1, source_target_pairs={{0,1},{1,0},{2,3},{3,2},{4,5},{5,4},{6,7},{7,6},{8,9},{9,8},{10,11... | collective-permute-start | bytes 49160 | tf_op jit(solution)/shard_map/ppermute | solution.py:610
  25.0 2.3 %inner_backward.1.own = f32[4,128,128]{2,1,0:T(8,128)S(1)} custom-call(s32[8,128]{1,0:T(8,128)S(1)} %get-tuple-element.55.plan, s32[8,128]{1,0:T(8,128)S(1)} %get-tuple-element.94.table_rows, f32[512,128]{1,0:T(8,128)S(1)} %get-tuple-element.95.sens, bf16[111,16,128]{2,1,0:T(8,128)(2,1)S(1)} %constant_dynamic-update-slice_fusion.refs_0_, ...), custom_call_target="tpu_custom_call" | custom-call | flops 922746880 | bytes 4194304 | tf_op jit(solution)/shard_map/inner_backward/pallas_call | solution.py:830
  27.3 0.3 collective-permute-done.9.far
  27.6 0.7 %lon_back.1 = (f32[16,32,128]{2,1,0:T(8,128)S(1)}, bf16[16,32,128]{2,1,0:T(8,128)(2,1)S(1)}) custom-call(bf16[4,16,128]{2,1,0:T(8,128)(2,1)S(1)} %collective-permute-done.9.far, bf16[4,16,128]{2,1,0:T(8,128)(2,1)S(1)} %collective-permute-done.10.close, f32[4,128,128]{2,1,0:T(8,128)S(1)} %inner_backward.1.own, f32[4,24,128]{2,1,0:T(8,128)S(1)} %get-tuple-element.68.taps), custom_call_target="tpu_custom_call" | custom-call | flops 4325376 | bytes 524288 | tf_op jit(solution)/shard_map/lon_back/pallas_call | solution.py:848
  28.3 5.6 %collective-permute-start.11 = (bf16[16,32,128]{2,1,0:T(8,128)(2,1)S(1)}, bf16[16,32,128]{2,1,0:T(8,128)(2,1)S(1)}, u32[]{:S(2)}, u32[]{:S(2)}) collective-permute-start(bf16[16,32,128]{2,1,0:T(8,128)(2,1)S(1)} %get-tuple-element.100), channel_id=1, source_target_pairs={{4,8},{8,4},{12,16},{16,12},{20,24},{24,20},{5,9},{9,5},{13,17},{1... | collective-permute-start | bytes 393224 | tf_op jit(solution)/shard_map/ppermute | solution.py:610
  33.9 0.1 collective-permute-start.12
  33.9 0.3 lat_back_own.1.own_part
  34.3 3.3 %collective-permute-done.11.far = bf16[16,32,128]{2,1,0:T(8,128)(2,1)S(1)} collective-permute-done((bf16[16,32,128]{2,1,0:T(8,128)(2,1)S(1)}, bf16[16,32,128]{2,1,0:T(8,128)(2,1)S(1)}, u32[]{:S(2)}, u32[]{:S(2)}) %collective-permute-start.11) | collective-permute-done | bytes 131104 | tf_op jit(solution)/shard_map/ppermute | solution.py:610
  37.6 1.0 %lat_back.1 = f32[16,32,128]{2,1,0:T(8,128)} custom-call(bf16[16,32,128]{2,1,0:T(8,128)(2,1)S(1)} %collective-permute-done.11.far, bf16[16,32,128]{2,1,0:T(8,128)(2,1)S(1)} %collective-permute-done.12.close, f32[16,32,128]{2,1,0:T(8,128)S(1)} %lat_back_own.1.own_part), custom_call_target="tpu_custom_call" | custom-call | flops 2162688 | bytes 1048576 | tf_op jit(solution)/shard_map/lat_back/pallas_call | solution.py:868
  (15 shorter events, 0.1 us)
Async XLA Ops:
  1.1 9.8 %collective-permute-start.1 = (bf16[37,16,128]{2,1,0:T(8,128)(2,1)S(1)}, bf16[37,16,128]{2,1,0:T(8,128)(2,1)S(1)}, u32[]{:S(2)}, u32[]{:S(2)}) collective-permute-start(bf16[37,16,128]{2,1,0:T(8,128)(2,1)S(1)} %get-tuple-element.70), channel_id=1, source_target_pairs={{0,8},{4,12},{8,0},{12,4},{16,24},{20,28},{24,16},{28,20},{1,9},{5... | collective-permute-start | bytes 454664 | tf_op jit(solution)/shard_map/ppermute | solution.py:680
  3.2 7.7 %collective-permute-start.2 = (bf16[16,32,128]{2,1,0:T(8,128)(2,1)S(1)}, bf16[16,32,128]{2,1,0:T(8,128)(2,1)S(1)}, u32[]{:S(2)}, u32[]{:S(2)}) collective-permute-start(bf16[16,32,128]{2,1,0:T(8,128)(2,1)S(1)} %get-tuple-element.58), channel_id=1, source_target_pairs={{4,8},{8,4},{12,16},{16,12},{20,24},{24,20},{5,9},{9,5},{13,17},{1... | collective-permute-start | bytes 393224 | tf_op jit(solution)/shard_map/ppermute | solution.py:610
  5.7 5.2 %collective-permute-start.3 = (bf16[16,32,128]{2,1,0:T(8,128)(2,1)S(1)}, bf16[16,32,128]{2,1,0:T(8,128)(2,1)S(1)}, u32[]{:S(2)}, u32[]{:S(2)}) collective-permute-start(bf16[16,32,128]{2,1,0:T(8,128)(2,1)S(1)} %get-tuple-element.59), channel_id=1, source_target_pairs={{0,4},{4,0},{8,12},{12,8},{16,20},{20,16},{24,28},{28,24},{1,5},{5... | collective-permute-start | bytes 393224 | tf_op jit(solution)/shard_map/ppermute | solution.py:610
  5.8 11.6 %collective-permute-start = (bf16[37,16,128]{2,1,0:T(8,128)(2,1)S(1)}, bf16[37,16,128]{2,1,0:T(8,128)(2,1)S(1)}, u32[]{:S(2)}, u32[]{:S(2)}) collective-permute-start(bf16[37,16,128]{2,1,0:T(8,128)(2,1)S(1)} %get-tuple-element.70), channel_id=1, source_target_pairs={{0,16},{4,20},{8,24},{12,28},{16,0},{20,4},{24,8},{28,12},{1,17},{... | collective-permute-start | bytes 454664 | tf_op jit(solution)/shard_map/ppermute | solution.py:680
  7.6 9.8 %collective-permute-start.4 = (bf16[37,16,128]{2,1,0:T(8,128)(2,1)S(1)}, bf16[37,16,128]{2,1,0:T(8,128)(2,1)S(1)}, u32[]{:S(2)}, u32[]{:S(2)}) collective-permute-start(bf16[37,16,128]{2,1,0:T(8,128)(2,1)S(1)} %get-tuple-element.70), channel_id=1, source_target_pairs={{0,24},{4,28},{8,16},{12,20},{16,8},{20,12},{24,0},{28,4},{1,25},{... | collective-permute-start | bytes 454664 | tf_op jit(solution)/shard_map/ppermute | solution.py:680
  11.4 7.5 %collective-permute-start.7 = (f32[4,16,128]{2,1,0:T(8,128)S(1)}, f32[4,16,128]{2,1,0:T(8,128)S(1)}, u32[]{:S(2)}, u32[]{:S(2)}) collective-permute-start(f32[4,16,128]{2,1,0:T(8,128)S(1)} %get-tuple-element.77), channel_id=1, source_target_pairs={{1,2},{2,1},{3,0},{0,3},{5,6},{6,5},{7,4},{4,7},{9,10},{10,9},{11,... | collective-permute-start | bytes 98312 | tf_op jit(solution)/shard_map/ppermute | solution.py:610
  14.7 4.2 %collective-permute-start.8 = (f32[4,16,128]{2,1,0:T(8,128)S(1)}, f32[4,16,128]{2,1,0:T(8,128)S(1)}, u32[]{:S(2)}, u32[]{:S(2)}) collective-permute-start(f32[4,16,128]{2,1,0:T(8,128)S(1)} %get-tuple-element.79), channel_id=1, source_target_pairs={{0,1},{1,0},{2,3},{3,2},{4,5},{5,4},{6,7},{7,6},{8,9},{9,8},{10,11... | collective-permute-start | bytes 98312 | tf_op jit(solution)/shard_map/ppermute | solution.py:610
  17.5 3.2 %collective-permute-start.5 = (bf16[111,16,128]{2,1,0:T(8,128)(2,1)S(1)}, bf16[111,16,128]{2,1,0:T(8,128)(2,1)S(1)}, u32[]{:S(2)}, u32[]{:S(2)}) collective-permute-start(bf16[111,16,128]{2,1,0:T(8,128)(2,1)S(1)} %constant_dynamic-update-slice_fusion.refs_0_), channel_id=1, source_target_pairs={{0,4},{4,0},{8,12},{12,8},{16,20},{20,16},{24,28},{28,24},{1,5},{5... | collective-permute-start | bytes 1363976 | tf_op jit(solution)/shard_map/ppermute | solution.py:680
  18.8 1.8 %collective-permute-start.6 = (bf16[37,16,128]{2,1,0:T(8,128)(2,1)S(1)}, bf16[37,16,128]{2,1,0:T(8,128)(2,1)S(1)}, u32[]{:S(2)}, u32[]{:S(2)}) collective-permute-start(bf16[37,16,128]{2,1,0:T(8,128)(2,1)S(1)} %collective-permute-done.4.refs_1_), channel_id=1, source_target_pairs={{0,4},{4,0},{8,12},{12,8},{16,20},{20,16},{24,28},{28,24},{1,5},{5... | collective-permute-start | bytes 454664 | tf_op jit(solution)/shard_map/ppermute | solution.py:680
  23.1 4.5 %collective-permute-start.9 = (bf16[4,16,128]{2,1,0:T(8,128)(2,1)S(1)}, bf16[4,16,128]{2,1,0:T(8,128)(2,1)S(1)}, u32[]{:S(2)}, u32[]{:S(2)}) collective-permute-start(bf16[4,16,128]{2,1,0:T(8,128)(2,1)S(1)} %get-tuple-element.90), channel_id=1, source_target_pairs={{1,2},{2,1},{3,0},{0,3},{5,6},{6,5},{7,4},{4,7},{9,10},{10,9},{11,... | collective-permute-start | bytes 49160 | tf_op jit(solution)/shard_map/ppermute | solution.py:610
  24.2 3.3 %collective-permute-start.10 = (bf16[4,16,128]{2,1,0:T(8,128)(2,1)S(1)}, bf16[4,16,128]{2,1,0:T(8,128)(2,1)S(1)}, u32[]{:S(2)}, u32[]{:S(2)}) collective-permute-start(bf16[4,16,128]{2,1,0:T(8,128)(2,1)S(1)} %get-tuple-element.92), channel_id=1, source_target_pairs={{0,1},{1,0},{2,3},{3,2},{4,5},{5,4},{6,7},{7,6},{8,9},{9,8},{10,11... | collective-permute-start | bytes 49160 | tf_op jit(solution)/shard_map/ppermute | solution.py:610
  28.3 9.3 %collective-permute-start.11 = (bf16[16,32,128]{2,1,0:T(8,128)(2,1)S(1)}, bf16[16,32,128]{2,1,0:T(8,128)(2,1)S(1)}, u32[]{:S(2)}, u32[]{:S(2)}) collective-permute-start(bf16[16,32,128]{2,1,0:T(8,128)(2,1)S(1)} %get-tuple-element.100), channel_id=1, source_target_pairs={{4,8},{8,4},{12,16},{16,12},{20,24},{24,20},{5,9},{9,5},{13,17},{1... | collective-permute-start | bytes 393224 | tf_op jit(solution)/shard_map/ppermute | solution.py:610
  33.9 3.7 %collective-permute-start.12 = (bf16[16,32,128]{2,1,0:T(8,128)(2,1)S(1)}, bf16[16,32,128]{2,1,0:T(8,128)(2,1)S(1)}, u32[]{:S(2)}, u32[]{:S(2)}) collective-permute-start(bf16[16,32,128]{2,1,0:T(8,128)(2,1)S(1)} %get-tuple-element.100), channel_id=1, source_target_pairs={{0,4},{4,0},{8,12},{12,8},{16,20},{20,16},{24,28},{28,24},{1,5},{5... | collective-permute-start | bytes 393224 | tf_op jit(solution)/shard_map/ppermute | solution.py:610

commit v16 on v8

--- a/solution.py
+++ b/solution.py
@@ -728,7 +728,7 @@
         ),
     )
     inner_states, weights = rest[:3], rest[3:]
-    *near, _ = lax.optimization_barrier((*near, profile))
+    *near, far, close, profile = lax.optimization_barrier((*near, far, close, profile))
     for bit in others:
         near = [jnp.concatenate(near, axis=0)]
         near.append(swapped(near[0], 1 << bit))

time: 39.2 us -> 38.5 us (0.982)
  waiting for transfers between devices: 2.61 us -> 2.12 us
    ppermute x5, starting transfers between devices: 4.41 us -> 5.06 us  [swapped(): return lax.ppermute(part, 'lat', [(i, i ^ apart) for i in range(lat_count)])]
    ppermute x4, waiting for transfers between devices: 2.58 us -> 1.97 us  [exchange(): lax.ppermute(to_far, axis, far)]
    ppermute x4, starting transfers between devices: 14.2 us -> 13.8 us  [exchange(): lax.ppermute(to_far, axis, far)]
  transfers between devices with their start and end apart: 13 -> 13, of which waited for: 1 -> 2; matrix products, arithmetic and copies ran while one was open for 0% -> 0% of each run, Pallas kernels for 29% -> 30%
where the time goes in v16:
time: 38.5 us; the launch traced here: 38.3 us
  starting transfers between devices  19 us (49%)
  Pallas kernels  16.7 us (43%)
  waiting for transfers between devices  2.12 us (6%)
    ppermute x4, starting transfers between devices, exchange(): lax.ppermute(to_far, axis, far)  13.8 us
    ppermute x5, starting transfers between devices, swapped(): return lax.ppermute(part, 'lat', [(i, i ^ apart) for i in range(lat_count)])  5.06 us
    pallas_call x1, Pallas kernels, shards(): call(functools.partial(inner_backward_kernel, per_tile, len(slabs), outer...  3.37 us
    pallas_call x1, Pallas kernels, shards(): call(functools.partial(inner_forward_kernel, per_tile, outer_slots), (sha...  3.11 us
    pallas_call x1, Pallas kernels, shards(): call(functools.partial(outer_backward_kernel, per_tile, len(slabs), recv_...  2.47 us
    ppermute x4, waiting for transfers between devices, exchange(): lax.ppermute(to_far, axis, far)  1.97 us
    pallas_call x1, Pallas kernels, shards(): call(functools.partial(outer_forward_kernel, per_tile), state_shapes(oute...  1.72 us
    pallas_call x1, Pallas kernels, shards(): call(prepare_kernel, (shape((tiles, 24, LANES), f32), shape((tiles, width...  1.45 us
  transfers between devices with their start and end apart: 13, of which 2 were waited for; matrix products, arithmetic and copies ran while one was open for 0% of the time, Pallas kernels for 30%

profile of v16, /device:TPU:1, one launch (start us, length us, event | category | flops | bytes accessed | tf_op | source)
XLA Modules:
  0.0 38.3 jit_solution(5762481289839243087)
XLA Ops:
  0.0 1.1 %slabs_halves.1 = (bf16[37,16,128]{2,1,0:T(8,128)(2,1)S(1)}, bf16[16,32,128]{2,1,0:T(8,128)(2,1)S(1)}, bf16[16,32,128]{2,1,0:T(8,128)(2,1)S(1)}) custom-call(bf16[36,16,128]{2,1,0:T(8,128)(2,1)} %bitcast.13, s32[1,64]{1,0:T(1,128)} %bitcast.14, s32[1,36]{1,0:T(1,128)} %bitcast.16, f32[16,32,128]{2,1,0:T(8,128)} %control.5), custom_call_target="tpu_custom_call" | custom-call | bytes 1048576 | tf_op jit(solution)/shard_map/slabs_halves/pallas_call | solution.py:609
  1.1 4.5 %collective-permute-start.3 = (bf16[16,32,128]{2,1,0:T(8,128)(2,1)S(1)}, bf16[16,32,128]{2,1,0:T(8,128)(2,1)S(1)}, u32[]{:S(2)}, u32[]{:S(2)}) collective-permute-start(bf16[16,32,128]{2,1,0:T(8,128)(2,1)S(1)} %get-tuple-element.57), channel_id=1, source_target_pairs={{4,8},{8,4},{12,16},{16,12},{20,24},{24,20},{5,9},{9,5},{13,17},{1... | collective-permute-start | bytes 393224 | tf_op jit(solution)/shard_map/ppermute | solution.py:571
  5.6 0.1 collective-permute-start.4
  5.7 1.3 %collective-permute-start = (bf16[37,16,128]{2,1,0:T(8,128)(2,1)S(1)}, bf16[37,16,128]{2,1,0:T(8,128)(2,1)S(1)}, u32[]{:S(2)}, u32[]{:S(2)}) collective-permute-start(bf16[37,16,128]{2,1,0:T(8,128)(2,1)S(1)} %get-tuple-element.70), channel_id=1, source_target_pairs={{0,16},{4,20},{8,24},{12,28},{16,0},{20,4},{24,8},{28,12},{1,17},{... | collective-permute-start | bytes 454664 | tf_op jit(solution)/shard_map/ppermute | solution.py:664
  7.0 0.1 collective-permute-start.1
  7.1 1.3 %collective-permute-start.2 = (bf16[37,16,128]{2,1,0:T(8,128)(2,1)S(1)}, bf16[37,16,128]{2,1,0:T(8,128)(2,1)S(1)}, u32[]{:S(2)}, u32[]{:S(2)}) collective-permute-start(bf16[37,16,128]{2,1,0:T(8,128)(2,1)S(1)} %get-tuple-element.70), channel_id=1, source_target_pairs={{0,24},{4,28},{8,16},{12,20},{16,8},{20,12},{24,0},{28,4},{1,25},{... | collective-permute-start | bytes 454664 | tf_op jit(solution)/shard_map/ppermute | solution.py:664
  8.4 1.5 %taps_background.1 = (f32[4,24,128]{2,1,0:T(8,128)S(1)}, f32[4,128,128]{2,1,0:T(8,128)S(1)}, s32[8,128]{1,0:T(8,128)S(1)}, f32[16,32,128]{2,1,0:T(8,128)S(1)}) custom-call(s32[16]{0:T(128)} %lon_width.1, f32[16,32,128]{2,1,0:T(8,128)} %background.1, s32[1,64]{1,0:T(1,128)} %bitcast.17, s32[1,64]{1,0:T(1,128)} %bitcast.15, f32[16,32,128]{2,1,0:T(8,128)} %control.5), custom_call_target="tpu_custom_call" | custom-call | flops 2162688 | bytes 786432 | tf_op jit(solution)/shard_map/taps_background/pallas_call | solution.py:629
  9.9 0.0 collective-permute-done.4.close
  9.9 0.4 %lat_smooth.1 = (f32[4,128,128]{2,1,0:T(8,128)S(1)}, f32[4,16,128]{2,1,0:T(8,128)S(1)}, f32[4,16,128]{2,1,0:T(8,128)S(1)}) custom-call(bf16[16,32,128]{2,1,0:T(8,128)(2,1)S(1)} %collective-permute-done.3.far, bf16[16,32,128]{2,1,0:T(8,128)(2,1)S(1)} %collective-permute-done.4.close, f32[16,32,128]{2,1,0:T(8,128)S(1)} %get-tuple-element.61.own_part), custom_call_target="tpu_custom_call" | custom-call | flops 4325376 | bytes 1048576 | tf_op jit(solution)/shard_map/lat_smooth/pallas_call | solution.py:670
  10.3 3.4 %collective-permute-start.5 = (f32[4,16,128]{2,1,0:T(8,128)S(1)}, f32[4,16,128]{2,1,0:T(8,128)S(1)}, u32[]{:S(2)}, u32[]{:S(2)}) collective-permute-start(f32[4,16,128]{2,1,0:T(8,128)S(1)} %get-tuple-element.62), channel_id=1, source_target_pairs={{1,2},{2,1},{3,0},{0,3},{5,6},{6,5},{7,4},{4,7},{9,10},{10,9},{11,... | collective-permute-start | bytes 98312 | tf_op jit(solution)/shard_map/ppermute | solution.py:571
  13.7 3.1 %inner_forward.1 = (f32[512,128]{1,0:T(8,128)S(1)}, bf16[320,1024]{1,0:T(8,128)(2,1)S(1)}, bf16[320,1024]{1,0:T(8,128)(2,1)S(1)}, f32[320,256]{1,0:T(8,128)S(1)}...) custom-call(s32[8,128]{1,0:T(8,128)S(1)} %get-tuple-element.54.plan,, ...), custom_call_target="tpu_custom_call" | custom-call | flops 922746880 | bytes 4194304 | tf_op jit(solution)/shard_map/inner_forward/pallas_call | solution.py:693
  16.9 0.1 collective-permute-done.6.close
  17.1 2.3 %collective-permute-start.7 = (bf16[111,16,128]{2,1,0:T(8,128)(2,1)S(1)}, bf16[111,16,128]{2,1,0:T(8,128)(2,1)S(1)}, u32[]{:S(2)}, u32[]{:S(2)}) collective-permute-start(bf16[111,16,128]{2,1,0:T(8,128)(2,1)S(1)} %constant_dynamic-update-slice_fusion.refs_0_), channel_id=1, source_target_pairs={{0,4},{4,0},{8,12},{12,8},{16,20},{20,16},{24,28},{28,24},{1,5},{5... | collective-permute-start | bytes 1363976 | tf_op jit(solution)/shard_map/ppermute | solution.py:664
  19.4 0.1 collective-permute-start.8
  19.4 1.7 %outer_forward.1 = (bf16[192,1024]{1,0:T(8,128)(2,1)S(1)}, bf16[192,1024]{1,0:T(8,128)(2,1)S(1)}, f32[192,256]{1,0:T(8,128)S(1)}, bf16[320,1024]{1,0:T(8,128)(2,...) custom-call(s32[8,128]{1,0:T(8,128)S(1)} %get-tuple-element.54.plan, ...), custom_call_target="tpu_custom_call" | custom-call | flops 5536481280 | bytes 41943040 | tf_op jit(solution)/shard_map/outer_forward/pallas_call | solution.py:738
  21.2 2.5 %outer_backward.1 = (s32[8,128]{1,0:T(8,128)S(1)}, f32[512,128]{1,0:T(8,128)S(1)}, bf16[4,16,128]{2,1,0:T(8,128)(2,1)S(1)}, bf16[4,16,128]{2,1,0:T(8,128)(2,1)S(1)}) custom-call(s32[8,128]{1,0:T(8,128)S(1)} %get-tuple-element.54.plan, bf16[111,16,128]{2,1,0:T(8,128)(2,1)S(1)} %constant_dynamic-update-slice_fusion.refs_0_, ...), custom_call_target="tpu_custom_call" | custom-call | flops 553648128 | bytes 4194304 | tf_op jit(solution)/shard_map/outer_backward/pallas_call | solution.py:757
  23.7 1.6 %collective-permute-start.9 = (bf16[4,16,128]{2,1,0:T(8,128)(2,1)S(1)}, bf16[4,16,128]{2,1,0:T(8,128)(2,1)S(1)}, u32[]{:S(2)}, u32[]{:S(2)}) collective-permute-start(bf16[4,16,128]{2,1,0:T(8,128)(2,1)S(1)} %get-tuple-element.89), channel_id=1, source_target_pairs={{1,2},{2,1},{3,0},{0,3},{5,6},{6,5},{7,4},{4,7},{9,10},{10,9},{11,... | collective-permute-start | bytes 49160 | tf_op jit(solution)/shard_map/ppermute | solution.py:571
  25.3 3.4 %inner_backward.1.own = f32[4,128,128]{2,1,0:T(8,128)S(1)} custom-call(s32[8,128]{1,0:T(8,128)S(1)} %get-tuple-element.54.plan, s32[8,128]{1,0:T(8,128)S(1)} %get-tuple-element.93.table_rows, f32[512,128]{1,0:T(8,128)S(1)} %get-tuple-element.94.sens, bf16[111,16,128]{2,1,0:T(8,128)(2,1)S(1)} %constant_dynamic-update-slice_fusion.refs_0_, ...), custom_call_target="tpu_custom_call" | custom-call | flops 922746880 | bytes 4194304 | tf_op jit(solution)/shard_map/inner_backward/pallas_call | solution.py:785
  28.6 0.8 %lon_back.1 = (f32[16,32,128]{2,1,0:T(8,128)S(1)}, bf16[16,32,128]{2,1,0:T(8,128)(2,1)S(1)}, bf16[16,32,128]{2,1,0:T(8,128)(2,1)S(1)}) custom-call(bf16[4,16,128]{2,1,0:T(8,128)(2,1)S(1)} %collective-permute-done.9.far, bf16[4,16,128]{2,1,0:T(8,128)(2,1)S(1)} %collective-permute-done.10.close, f32[4,128,128]{2,1,0:T(8,128)S(1)} %inner_backward.1.own, ...), custom_call_target="tpu_custom_call" | custom-call | flops 4325376 | bytes 524288 | tf_op jit(solution)/shard_map/lon_back/pallas_call | solution.py:805
  29.4 4.4 %collective-permute-start.11 = (bf16[16,32,128]{2,1,0:T(8,128)(2,1)S(1)}, bf16[16,32,128]{2,1,0:T(8,128)(2,1)S(1)}, u32[]{:S(2)}, u32[]{:S(2)}) collective-permute-start(bf16[16,32,128]{2,1,0:T(8,128)(2,1)S(1)} %get-tuple-element.98), channel_id=1, source_target_pairs={{4,8},{8,4},{12,16},{16,12},{20,24},{24,20},{5,9},{9,5},{13,17},{1... | collective-permute-start | bytes 393224 | tf_op jit(solution)/shard_map/ppermute | solution.py:571
  33.8 0.1 collective-permute-start.12
  33.9 1.3 %lat_back_own.1.own_part = f32[16,32,128]{2,1,0:T(8,128)S(1)} custom-call(f32[16,32,128]{2,1,0:T(8,128)S(1)} %get-tuple-element.102.back, f32[16,32,128]{2,1,0:T(8,128)} %control.5), custom_call_target="tpu_custom_call" | custom-call | flops 2162688 | bytes 786432 | tf_op jit(solution)/shard_map/lat_back_own/pallas_call | solution.py:816
  35.2 2.0 %collective-permute-done.11.far = bf16[16,32,128]{2,1,0:T(8,128)(2,1)S(1)} collective-permute-done((bf16[16,32,128]{2,1,0:T(8,128)(2,1)S(1)}, bf16[16,32,128]{2,1,0:T(8,128)(2,1)S(1)}, u32[]{:S(2)}, u32[]{:S(2)}) %collective-permute-start.11) | collective-permute-done | bytes 131104 | tf_op jit(solution)/shard_map/ppermute | solution.py:571
  37.1 1.0 %lat_back.1 = f32[16,32,128]{2,1,0:T(8,128)} custom-call(bf16[16,32,128]{2,1,0:T(8,128)(2,1)S(1)} %collective-permute-done.11.far, bf16[16,32,128]{2,1,0:T(8,128)(2,1)S(1)} %collective-permute-done.12.close, f32[16,32,128]{2,1,0:T(8,128)S(1)} %lat_back_own.1.own_part), custom_call_target="tpu_custom_call" | custom-call | flops 2162688 | bytes 1048576 | tf_op jit(solution)/shard_map/lat_back/pallas_call | solution.py:827
  (15 shorter events, 0.1 us)
Async XLA Ops:
  1.1 8.8 %collective-permute-start.3 = (bf16[16,32,128]{2,1,0:T(8,128)(2,1)S(1)}, bf16[16,32,128]{2,1,0:T(8,128)(2,1)S(1)}, u32[]{:S(2)}, u32[]{:S(2)}) collective-permute-start(bf16[16,32,128]{2,1,0:T(8,128)(2,1)S(1)} %get-tuple-element.57), channel_id=1, source_target_pairs={{4,8},{8,4},{12,16},{16,12},{20,24},{24,20},{5,9},{9,5},{13,17},{1... | collective-permute-start | bytes 393224 | tf_op jit(solution)/shard_map/ppermute | solution.py:571
  5.6 4.3 %collective-permute-start.4 = (bf16[16,32,128]{2,1,0:T(8,128)(2,1)S(1)}, bf16[16,32,128]{2,1,0:T(8,128)(2,1)S(1)}, u32[]{:S(2)}, u32[]{:S(2)}) collective-permute-start(bf16[16,32,128]{2,1,0:T(8,128)(2,1)S(1)} %get-tuple-element.58), channel_id=1, source_target_pairs={{0,4},{4,0},{8,12},{12,8},{16,20},{20,16},{24,28},{28,24},{1,5},{5... | collective-permute-start | bytes 393224 | tf_op jit(solution)/shard_map/ppermute | solution.py:571
  5.7 11.3 %collective-permute-start = (bf16[37,16,128]{2,1,0:T(8,128)(2,1)S(1)}, bf16[37,16,128]{2,1,0:T(8,128)(2,1)S(1)}, u32[]{:S(2)}, u32[]{:S(2)}) collective-permute-start(bf16[37,16,128]{2,1,0:T(8,128)(2,1)S(1)} %get-tuple-element.70), channel_id=1, source_target_pairs={{0,16},{4,20},{8,24},{12,28},{16,0},{20,4},{24,8},{28,12},{1,17},{... | collective-permute-start | bytes 454664 | tf_op jit(solution)/shard_map/ppermute | solution.py:664
  7.0 10.0 %collective-permute-start.1 = (bf16[37,16,128]{2,1,0:T(8,128)(2,1)S(1)}, bf16[37,16,128]{2,1,0:T(8,128)(2,1)S(1)}, u32[]{:S(2)}, u32[]{:S(2)}) collective-permute-start(bf16[37,16,128]{2,1,0:T(8,128)(2,1)S(1)} %get-tuple-element.70), channel_id=1, source_target_pairs={{0,8},{4,12},{8,0},{12,4},{16,24},{20,28},{24,16},{28,20},{1,9},{5... | collective-permute-start | bytes 454664 | tf_op jit(solution)/shard_map/ppermute | solution.py:664
  7.1 9.9 %collective-permute-start.2 = (bf16[37,16,128]{2,1,0:T(8,128)(2,1)S(1)}, bf16[37,16,128]{2,1,0:T(8,128)(2,1)S(1)}, u32[]{:S(2)}, u32[]{:S(2)}) collective-permute-start(bf16[37,16,128]{2,1,0:T(8,128)(2,1)S(1)} %get-tuple-element.70), channel_id=1, source_target_pairs={{0,24},{4,28},{8,16},{12,20},{16,8},{20,12},{24,0},{28,4},{1,25},{... | collective-permute-start | bytes 454664 | tf_op jit(solution)/shard_map/ppermute | solution.py:664
  10.3 6.5 %collective-permute-start.5 = (f32[4,16,128]{2,1,0:T(8,128)S(1)}, f32[4,16,128]{2,1,0:T(8,128)S(1)}, u32[]{:S(2)}, u32[]{:S(2)}) collective-permute-start(f32[4,16,128]{2,1,0:T(8,128)S(1)} %get-tuple-element.62), channel_id=1, source_target_pairs={{1,2},{2,1},{3,0},{0,3},{5,6},{6,5},{7,4},{4,7},{9,10},{10,9},{11,... | collective-permute-start | bytes 98312 | tf_op jit(solution)/shard_map/ppermute | solution.py:571
  13.7 3.3 %collective-permute-start.6 = (f32[4,16,128]{2,1,0:T(8,128)S(1)}, f32[4,16,128]{2,1,0:T(8,128)S(1)}, u32[]{:S(2)}, u32[]{:S(2)}) collective-permute-start(f32[4,16,128]{2,1,0:T(8,128)S(1)} %get-tuple-element.64), channel_id=1, source_target_pairs={{0,1},{1,0},{2,3},{3,2},{4,5},{5,4},{6,7},{7,6},{8,9},{9,8},{10,11... | collective-permute-start | bytes 98312 | tf_op jit(solution)/shard_map/ppermute | solution.py:571
  17.1 4.1 %collective-permute-start.7 = (bf16[111,16,128]{2,1,0:T(8,128)(2,1)S(1)}, bf16[111,16,128]{2,1,0:T(8,128)(2,1)S(1)}, u32[]{:S(2)}, u32[]{:S(2)}) collective-permute-start(bf16[111,16,128]{2,1,0:T(8,128)(2,1)S(1)} %constant_dynamic-update-slice_fusion.refs_0_), channel_id=1, source_target_pairs={{0,4},{4,0},{8,12},{12,8},{16,20},{20,16},{24,28},{28,24},{1,5},{5... | collective-permute-start | bytes 1363976 | tf_op jit(solution)/shard_map/ppermute | solution.py:664
  19.4 1.8 %collective-permute-start.8 = (bf16[37,16,128]{2,1,0:T(8,128)(2,1)S(1)}, bf16[37,16,128]{2,1,0:T(8,128)(2,1)S(1)}, u32[]{:S(2)}, u32[]{:S(2)}) collective-permute-start(bf16[37,16,128]{2,1,0:T(8,128)(2,1)S(1)} %collective-permute-done.2.refs_1_), channel_id=1, source_target_pairs={{0,4},{4,0},{8,12},{12,8},{16,20},{20,16},{24,28},{28,24},{1,5},{5... | collective-permute-start | bytes 454664 | tf_op jit(solution)/shard_map/ppermute | solution.py:664
  23.7 5.0 %collective-permute-start.9 = (bf16[4,16,128]{2,1,0:T(8,128)(2,1)S(1)}, bf16[4,16,128]{2,1,0:T(8,128)(2,1)S(1)}, u32[]{:S(2)}, u32[]{:S(2)}) collective-permute-start(bf16[4,16,128]{2,1,0:T(8,128)(2,1)S(1)} %get-tuple-element.89), channel_id=1, source_target_pairs={{1,2},{2,1},{3,0},{0,3},{5,6},{6,5},{7,4},{4,7},{9,10},{10,9},{11,... | collective-permute-start | bytes 49160 | tf_op jit(solution)/shard_map/ppermute | solution.py:571
  25.3 3.4 %collective-permute-start.10 = (bf16[4,16,128]{2,1,0:T(8,128)(2,1)S(1)}, bf16[4,16,128]{2,1,0:T(8,128)(2,1)S(1)}, u32[]{:S(2)}, u32[]{:S(2)}) collective-permute-start(bf16[4,16,128]{2,1,0:T(8,128)(2,1)S(1)} %get-tuple-element.91), channel_id=1, source_target_pairs={{0,1},{1,0},{2,3},{3,2},{4,5},{5,4},{6,7},{7,6},{8,9},{9,8},{10,11... | collective-permute-start | bytes 49160 | tf_op jit(solution)/shard_map/ppermute | solution.py:571
  29.4 7.7 %collective-permute-start.11 = (bf16[16,32,128]{2,1,0:T(8,128)(2,1)S(1)}, bf16[16,32,128]{2,1,0:T(8,128)(2,1)S(1)}, u32[]{:S(2)}, u32[]{:S(2)}) collective-permute-start(bf16[16,32,128]{2,1,0:T(8,128)(2,1)S(1)} %get-tuple-element.98), channel_id=1, source_target_pairs={{4,8},{8,4},{12,16},{16,12},{20,24},{24,20},{5,9},{9,5},{13,17},{1... | collective-permute-start | bytes 393224 | tf_op jit(solution)/shard_map/ppermute | solution.py:571
  33.8 3.3 %collective-permute-start.12 = (bf16[16,32,128]{2,1,0:T(8,128)(2,1)S(1)}, bf16[16,32,128]{2,1,0:T(8,128)(2,1)S(1)}, u32[]{:S(2)}, u32[]{:S(2)}) collective-permute-start(bf16[16,32,128]{2,1,0:T(8,128)(2,1)S(1)} %get-tuple-element.100), channel_id=1, source_target_pairs={{0,4},{4,0},{8,12},{12,8},{16,20},{20,16},{24,28},{28,24},{1,5},{5... | collective-permute-start | bytes 393224 | tf_op jit(solution)/shard_map/ppermute | solution.py:571
